TPU v7x, 32 devices: a whole 2x2x4 slice. The times are simulated.
32 devices in a mesh: batch: 4 (over z), col: 4 (over x, core), rep: 2 (over y).
Axes of the slice: x: 2, y: 2, z: 4, core: 2. Of those that a mesh axis runs over, the one named last changes fastest.
Arguments:
- lookups: bfloat16 [8192, 1024], P(('rep', 'batch'), 'col'), parts along dimension 0, may hold values from -6 to 6
- input_weight: bfloat16 [1024, 1024], replicated, may hold values from -0.1875 to 0.1875
- joined_weight: bfloat16 [1024, 2048], replicated, may hold values from -0.1875 to 0.1875
- output_weight: bfloat16 [512, 1024], replicated, may hold values from -0.25 to 0.25
- owner_counts: int32 [32, 4], P(('rep', 'batch', 'col')), parts along dimension 0, may hold values from 1 to 96, 256 in all within a row
- user_index: int32 [8192], P(('rep', 'batch', 'col')), parts along dimension 0, may hold values from 0 to 7
Outputs:
- layer_out: bfloat16 [8192, 1024], P(('rep', 'batch', 'col')), parts along dimension 0
There are 2 independent parts, one for each index of `rep`. A program takes and returns all parts, laid end to end along the dimension named above; an argument that names none is the same for every part. Nothing has to cross between parts.
Inputs may be any that keep to these rules, and one draw needn't show every extreme that they name: `owner_counts`: each row sums to 256; every entry is 1 or more and each row reaches 96.
All inputs are finite; a program needn't handle non-finite values.
Results may differ from a plain program's by a relative error of at most 0.0071.
Values may be sent and summed in bfloat16 or wider, within the bound.
No kernel may reach another device: no remote copies, remote signals or barrier semaphores. Data moves between devices by JAX's collectives and lax.ppermute only.
A program may use at most 64 MiB of HBM per device.

v0:
```python
import jax
import jax.numpy as jnp
from jax import lax
from jax.sharding import PartitionSpec as P

HEADS = 4
HEAD_DIM = 128


eps_norm = 1e-06


def layer_norm(values):
    row_mean = jnp.mean(values, axis=-1, keepdims=True)
    centered = values - row_mean
    row_var = jnp.mean(centered * centered, axis=-1, keepdims=True)
    return centered * lax.rsqrt(row_var + eps_norm)


def project(hidden_rows, joined_weight):
    normed = layer_norm(hidden_rows.astype(jnp.float32)).astype(jnp.bfloat16)
    return jax.nn.silu(jnp.dot(normed, joined_weight, preferred_element_type=jnp.float32)).astype(
        jnp.bfloat16
    )


def attend(joined_rows, seg_ids):
    width = HEADS * HEAD_DIM
    total = joined_rows.shape[0]
    gate_part = joined_rows[:, :width]
    value_part = joined_rows[:, width : 2 * width].reshape(total, HEADS, HEAD_DIM)
    query_part = joined_rows[:, 2 * width : 3 * width].reshape(total, HEADS, HEAD_DIM)
    key_part = joined_rows[:, 3 * width :].reshape(total, HEADS, HEAD_DIM)
    scores = jnp.einsum(
        "ihd,jhd->hij", query_part, key_part, preferred_element_type=jnp.float32
    ) * HEAD_DIM ** (-0.5)
    positions = jnp.arange(total, dtype=jnp.int32)
    allowed = (positions[None, :] <= positions[:, None]) & (seg_ids[None, :] == seg_ids[:, None])
    weights = jnp.where(allowed[None], jax.nn.silu(scores), 0.0).astype(jnp.bfloat16)
    mixed = jnp.einsum(
        "hij,jhd->ihd", weights, value_part, preferred_element_type=jnp.float32
    ).reshape(total, width)
    return (layer_norm(mixed) * gate_part.astype(jnp.float32)).astype(jnp.bfloat16)


def on_device(lookups, input_weight, joined_weight, output_weight, owner_counts, user_index):
    token_block = lax.all_to_all(lookups, "col", split_axis=0, concat_axis=1, tiled=True)
    hidden = jnp.dot(token_block, input_weight, preferred_element_type=jnp.float32).astype(
        jnp.bfloat16
    )
    local_rows = hidden.shape[0]
    owners = lax.axis_size("batch")
    capacity = local_rows // owners + local_rows // (2 * owners)
    counts = owner_counts[0]
    bin_ends = jnp.cumsum(counts)
    bin_starts = bin_ends - counts
    slot_ids = jnp.arange(capacity, dtype=jnp.int32)
    filled = slot_ids[None, :] < counts[:, None]
    gather_rows = jnp.where(filled, bin_starts[:, None] + slot_ids[None, :], 0).reshape(-1)
    seg_send = jnp.where(filled.reshape(-1), user_index[gather_rows], -1).reshape(owners, capacity)
    payload = hidden[gather_rows].reshape(owners, capacity, -1)
    received, seg_ids = (
        lax.all_to_all(payload, "batch", split_axis=0, concat_axis=0, tiled=True),
        lax.all_to_all(seg_send, "batch", split_axis=0, concat_axis=0, tiled=True),
    )
    joined_rows = project(received.reshape(owners * capacity, -1), joined_weight)
    gated_rows = attend(joined_rows, seg_ids.reshape(-1))
    token_pos = jnp.arange(local_rows, dtype=jnp.int32)
    owner_ids = jnp.arange(owners, dtype=jnp.int32)
    dest_owner = jnp.sum((token_pos[:, None] >= bin_ends[None, :]).astype(jnp.int32), axis=1)
    onehot = dest_owner[:, None] == owner_ids[None, :]
    first_slot = jnp.sum(jnp.where(onehot, bin_starts[None, :], 0), axis=1)
    back_rows = dest_owner * capacity + token_pos - first_slot
    returned = lax.all_to_all(
        gated_rows.reshape(owners, capacity, -1), "batch", split_axis=0, concat_axis=0, tiled=True
    )
    own_gated = returned.reshape(owners * capacity, -1)[back_rows]
    branch_rows = jnp.dot(own_gated, output_weight, preferred_element_type=jnp.float32).astype(
        jnp.bfloat16
    )
    return (hidden.astype(jnp.float32) + branch_rows.astype(jnp.float32)).astype(jnp.bfloat16)


def solution(mesh):
    return jax.shard_map(
        on_device,
        mesh=mesh,
        in_specs=(
            P(("rep", "batch"), "col"),
            P(),
            P(),
            P(),
            P(("rep", "batch", "col"), None),
            P(("rep", "batch", "col")),
        ),
        out_specs=P(("rep", "batch", "col"), None),
        check_vma=False,
    )
```

profile of v0, /device:TPU:0, one launch (start us, length us, event | category | flops | bytes accessed | tf_op | source)
XLA Modules:
  0.0 85.7 jit_solution(10829304756676959447)
XLA Ops:
  0.0 0.0 copy-start
  0.0 0.0 copy-start.4
  0.0 0.0 copy-start.1
  0.0 4.4 %all-to-all-start = ((bf16[4,256,256]{2,1,0:T(8,128)(2,1)}), bf16[4,256,256]{2,1,0:T(8,128)(2,1)S(1)}, u32[]{:S(2)}, u32[]{:S(2)}) async-start(bf16[4,256,256]{2,1,0:T(8,128)(2,1)} %bitcast.63), calls=%async_computation | async-start | bytes 1048576 | tf_op jit(solution)/shard_map/all_to_all | solution.py:47
  4.4 0.8 reduce-window.4
  5.2 0.7 bitcast_subtract_fusion.3
  5.8 0.7 add_select_fusion
  6.6 0.1 select_n.57
  6.7 0.0 copy-done.1
  6.7 2.8 %gather_fusion.1 = s32[384]{0:T(512)S(1)} fusion(s32[256]{0:T(256)S(1)} %copy-done.1, s32[1024]{0:T(1024)S(1)} %pad_clamp_fusion.1), kind=kCustom, calls=%fused_computation.1 | custom fusion | bytes 4608 | tf_op jit(solution)/shard_map/gather | solution.py:60
  9.5 0.1 gather.13
  9.6 0.0 copy-done.4
  9.6 0.6 compare_select_fusion.1
  10.3 3.0 %all-to-all-done = bf16[4,256,256]{2,1,0:T(8,128)(2,1)S(1)} async-done(((bf16[4,256,256]{2,1,0:T(8,128)(2,1)}), bf16[4,256,256]{2,1,0:T(8,128)(2,1)S(1)}, u32[]{:S(2)}, u32[]{:S(2)}) %all-to-all-start) | async-done | bytes 524320 | tf_op jit(solution)/shard_map/all_to_all | solution.py:47
  13.2 5.6 %all-to-all-start.2 = ((s32[4,1,96]{2,1,0:T(1,128)}), s32[4,1,96]{2,1,0:T(1,128)S(1)}, u32[]{:S(2)}, u32[]{:S(2)}) async-start(s32[4,1,96]{2,1,0:T(1,128)} %compare_select_fusion.1), calls=%async_computation.2 | async-start | bytes 4096 | tf_op jit(solution)/shard_map/all_to_all | solution.py:64
  18.8 0.2 copy.20
  19.0 0.0 copy-done
  19.0 0.7 convolution_convert_fusion.1
  19.7 2.7 %gather_fusion = bf16[384,1024]{1,0:T(8,128)(2,1)} fusion(bf16[256,1024]{1,0:T(8,128)(2,1)S(1)} %convolution_convert_fusion.1, s32[1024]{0:T(1024)S(1)} %pad_clamp_fusion.1), kind=kCustom, calls=%fused_computation | custom fusion | bytes 1574400 | tf_op jit(solution)/shard_map/gather | solution.py:61
  22.4 1.8 %all-to-all-done.2 = s32[4,1,96]{2,1,0:T(1,128)S(1)} async-done(((s32[4,1,96]{2,1,0:T(1,128)}), s32[4,1,96]{2,1,0:T(1,128)S(1)}, u32[]{:S(2)}, u32[]{:S(2)}) %all-to-all-start.2) | async-done | bytes 1568 | tf_op jit(solution)/shard_map/all_to_all | solution.py:64
  24.2 3.5 %all-to-all-start.1 = ((bf16[4,96,1024]{2,1,0:T(8,128)(2,1)}), bf16[4,96,1024]{2,1,0:T(8,128)(2,1)S(1)}, u32[]{:S(2)}, u32[]{:S(2)}) async-start(bf16[4,96,1024]{2,1,0:T(8,128)(2,1)} %bitcast.60), calls=%async_computation.1 | async-start | bytes 1572864 | tf_op jit(solution)/shard_map/all_to_all | solution.py:63
  27.7 0.7 convert_reduce_fusion.1
  28.4 0.6 fusion.22
  29.0 0.5 broadcast.192
  29.5 0.7 reduce.10
  30.2 0.7 eq.32
  30.8 0.9 %fusion.12 = pred[384,384]{1,0:T(8,128)(4,1)S(1)} fusion(s32[384]{0:T(512)} %eq.32), kind=kLoop, calls=%fused_computation.25 | loop fusion | flops 442368 | bytes 148992 | tf_op jit(solution)/shard_map/and | solution.py:38
  31.7 15.1 %all-to-all-done.1 = bf16[4,96,1024]{2,1,0:T(8,128)(2,1)S(1)} async-done(((bf16[4,96,1024]{2,1,0:T(8,128)(2,1)}), bf16[4,96,1024]{2,1,0:T(8,128)(2,1)S(1)}, u32[]{:S(2)}, u32[]{:S(2)}) %all-to-all-start.1) | async-done | bytes 786464 | tf_op jit(solution)/shard_map/all_to_all | solution.py:63
  46.8 0.2 convert_reduce_fusion
  47.0 0.6 broadcast_multiply_fusion.1
  47.6 1.3 %div.23 = f32[384]{0:T(512)} reshape(f32[4,96]{1,0:T(4,128)} %broadcast_multiply_fusion.1) | data formatting | bytes 3072 | tf_op jit(solution)/shard_map/div | solution.py:14
  49.0 1.0 %multiply_reduce_fusion = f32[4,96]{1,0:T(4,128)S(1)} fusion(bf16[4,96,1024]{2,1,0:T(8,128)(2,1)S(1)} %all-to-all-done.1, f32[4,96]{1,0:T(4,128)} %broadcast_multiply_fusion.1), kind=kLoop, calls=%fused_computation.8 | loop fusion | flops 1572480 | bytes 789504 | tf_op jit(solution)/shard_map/reduce_sum | solution.py:16
  50.0 0.6 add_rsqrt_fusion.1
  50.6 1.4 %rsqrt.20 = f32[384]{0:T(512)} reshape(f32[4,96]{1,0:T(4,128)} %add_rsqrt_fusion.1) | data formatting | bytes 3072 | tf_op jit(solution)/shard_map/rsqrt | solution.py:17
  52.0 0.9 %fusion.1 = bf16[384,1024]{1,0:T(8,128)(2,1)S(1)} fusion(bf16[4,96,1024]{2,1,0:T(8,128)(2,1)S(1)} %all-to-all-done.1, f32[384]{0:T(512)} %rsqrt.20, f32[384]{0:T(512)} %div.23), kind=kLoop, calls=%fused_computation.7 | loop fusion | flops 1572864 | bytes 1575936 | tf_op jit(solution)/shard_map/convert_element_type | solution.py:21
  52.9 4.2 %multiply_convert_fusion = bf16[384,2048]{1,0:T(8,128)(2,1)S(1)} fusion(bf16[384,1024]{1,0:T(8,128)(2,1)S(1)} %fusion.1, bf16[1024,2048]{1,0:T(8,128)(2,1)} %param.8), kind=kOutput, calls=%fused_computation.3 | convolution fusion | flops 1614544896 | bytes 6553600 | tf_op jit(solution)/shard_map/dot_general | solution.py:22
  57.1 0.0 copy-start.2
  57.1 1.1 %copy-done.2 = bf16[384,2048]{1,0:T(8,128)(2,1)} copy-done((bf16[384,2048]{1,0:T(8,128)(2,1)}, bf16[384,2048]{1,0:T(8,128)(2,1)S(1)}, u32[]{:S(2)}) %copy-start.2) | copy-done | bytes 1572888
  58.3 1.0 %slice_bitcast_fusion.1 = (bf16[48,4,8,128]{3,2,1,0:T(8,128)(2,1)}, bf16[48,4,8,128]{3,2,1,0:T(8,128)(2,1)}, bf16[384,512]{1,0:T(8,128)(2,1)S(1)}) fusion(bf16[384,2048]{1,0:T(8,128)(2,1)S(1)} %multiply_convert_fusion), kind=kLoop, calls=%fused_computation.31 | loop fusion | bytes 2359296
  59.3 0.9 %copy.25 = bf16[384,512]{0,1:T(8,128)(2,1)} copy(bf16[384,512]{1,0:T(8,128)(2,1)S(1)} %get-tuple-element.7) | data formatting | bytes 786432 | tf_op jit(solution)/shard_map/reshape | solution.py:31
  60.3 3.0 %fusion.26 = (f32[384]{0:T(512)}, f32[4,128,384]{2,1,0:T(8,128)S(1)}) fusion(bf16[384,4,128]{0,2,1:T(8,128)(2,1)} %bitcast.64, pred[384,384]{1,0:T(8,128)(4,1)S(1)} %fusion.12, bf16[48,4,8,128]{3,2,1,0:T(8,128)(2,1)} %get-tuple-element.6, bf16[48,4,8,128]{3,2,1,0:T(8,128)(2,1)} %get-tuple-element.5), kind=kOutput, calls=%fused_computation.55 | convolution fusion | flops 306314880 | bytes 2115072 | tf_op jit(solution)/shard_map/hij,jhd->ihd/dot_general | solution.py:40
  63.3 0.7 broadcast_multiply_fusion
  64.0 0.0 copy-start.3
  64.0 0.0 copy-start.5
  64.0 0.1 fusion.11
  64.1 1.2 %copy.26 = f32[384,512]{1,0:T(8,128)} copy(f32[384,512]{0,1:T(8,128)S(1)} %bitcast.59) | data formatting | bytes 1572864 | tf_op jit(solution)/shard_map/reshape | solution.py:42
  65.3 2.2 %multiply_convert_fusion.1 = bf16[384,512]{1,0:T(8,128)(2,1)} fusion(f32[384,512]{1,0:T(8,128)} %copy.26, bf16[384,2048]{1,0:T(8,128)(2,1)} %copy-done.2, f32[384]{0:T(512)S(1)} %add_rsqrt_fusion, f32[384]{0:T(512)S(1)} %broadcast_multiply_fusion), kind=kLoop, calls=%fused_computation.23 | loop fusion | flops 983040 | bytes 1575936 | tf_op jit(solution)/shard_map/convert_element_type | solution.py:43
  67.5 3.5 %all-to-all-start.3 = ((bf16[4,96,512]{2,1,0:T(8,128)(2,1)}), bf16[4,96,512]{2,1,0:T(8,128)(2,1)S(1)}, u32[]{:S(2)}, u32[]{:S(2)}) async-start(bf16[4,96,512]{2,1,0:T(8,128)(2,1)} %bitcast.11), calls=%async_computation.3 | async-start | bytes 786432 | tf_op jit(solution)/shard_map/all_to_all | solution.py:74
  70.9 0.0 copy-done.3
  70.9 0.0 copy-done.5
  71.0 0.1 select_reduce_fusion
  71.1 11.0 %all-to-all-done.3 = bf16[4,96,512]{2,1,0:T(8,128)(2,1)S(1)} async-done(((bf16[4,96,512]{2,1,0:T(8,128)(2,1)}), bf16[4,96,512]{2,1,0:T(8,128)(2,1)S(1)}, u32[]{:S(2)}, u32[]{:S(2)}) %all-to-all-start.3) | async-done | bytes 393248 | tf_op jit(solution)/shard_map/all_to_all | solution.py:74
  82.1 1.2 %gather_fusion.2 = bf16[256,512]{1,0:T(8,128)(2,1)S(1)} fusion(bf16[384,512]{1,0:T(8,128)(2,1)S(1)} %bitcast.58, s32[1024]{0:T(1024)S(1)} %pad_clamp_fusion), kind=kCustom, calls=%fused_computation.2 | custom fusion | bytes 525312 | tf_op jit(solution)/shard_map/gather | solution.py:77
  83.2 2.5 %fusion.5 = bf16[256,1024]{1,0:T(8,128)(2,1)} fusion(bf16[256,512]{1,0:T(8,128)(2,1)S(1)} %gather_fusion.2, bf16[512,1024]{1,0:T(8,128)(2,1)} %param.9, bf16[256,1024]{1,0:T(8,128)(2,1)S(1)} %convolution_convert_fusion.1), kind=kOutput, calls=%fused_computation.13 | convolution fusion | flops 269746176 | bytes 2359296 | tf_op jit(solution)/shard_map/dot_general | solution.py:78
  (6 shorter events, 0.1 us)
Async XLA Ops:
  0.0 19.0 %copy-start = (bf16[1024,1024]{1,0:T(8,128)(2,1)S(1)}, bf16[1024,1024]{1,0:T(8,128)(2,1)}, u32[]{:S(2)}) copy-start(bf16[1024,1024]{1,0:T(8,128)(2,1)} %param.7) | copy-start | bytes 6291460
  0.0 9.6 %copy-start.4 = (s32[1,4]{1,0:T(1,128)S(1)}, s32[1,4]{1,0:T(1,128)}, u32[]{:S(2)}) copy-start(s32[1,4]{1,0:T(1,128)} %param.10) | copy-start | bytes 52
  0.0 6.7 %copy-start.1 = (s32[256]{0:T(256)S(1)}, s32[256]{0:T(256)}, u32[]{:S(2)}) copy-start(s32[256]{0:T(256)} %param.11) | copy-start | bytes 3076
  0.0 13.2 %all-to-all-start = ((bf16[4,256,256]{2,1,0:T(8,128)(2,1)}), bf16[4,256,256]{2,1,0:T(8,128)(2,1)S(1)}, u32[]{:S(2)}, u32[]{:S(2)}) async-start(bf16[4,256,256]{2,1,0:T(8,128)(2,1)} %bitcast.63), calls=%async_computation | async-start | bytes 1048576 | tf_op jit(solution)/shard_map/all_to_all | solution.py:47
  13.2 11.0 %all-to-all-start.2 = ((s32[4,1,96]{2,1,0:T(1,128)}), s32[4,1,96]{2,1,0:T(1,128)S(1)}, u32[]{:S(2)}, u32[]{:S(2)}) async-start(s32[4,1,96]{2,1,0:T(1,128)} %compare_select_fusion.1), calls=%async_computation.2 | async-start | bytes 4096 | tf_op jit(solution)/shard_map/all_to_all | solution.py:64
  24.2 22.6 %all-to-all-start.1 = ((bf16[4,96,1024]{2,1,0:T(8,128)(2,1)}), bf16[4,96,1024]{2,1,0:T(8,128)(2,1)S(1)}, u32[]{:S(2)}, u32[]{:S(2)}) async-start(bf16[4,96,1024]{2,1,0:T(8,128)(2,1)} %bitcast.60), calls=%async_computation.1 | async-start | bytes 1572864 | tf_op jit(solution)/shard_map/all_to_all | solution.py:63
  57.1 1.2 %copy-start.2 = (bf16[384,2048]{1,0:T(8,128)(2,1)}, bf16[384,2048]{1,0:T(8,128)(2,1)S(1)}, u32[]{:S(2)}) copy-start(bf16[384,2048]{1,0:T(8,128)(2,1)S(1)} %multiply_convert_fusion) | copy-start | bytes 4718596
  64.0 6.9 %copy-start.3 = (s32[256]{0:T(256)S(1)}, s32[256]{0:T(256)}, u32[]{:S(2)}) copy-start(s32[256]{0:T(256)} %convert_reduce_fusion.1) | copy-start | bytes 3076
  64.0 7.0 %copy-start.5 = (s32[4]{0:T(128)S(1)}, s32[4]{0:T(128)}, u32[]{:S(2)}) copy-start(s32[4]{0:T(128)} %fusion.22) | copy-start | bytes 52
  67.5 14.6 %all-to-all-start.3 = ((bf16[4,96,512]{2,1,0:T(8,128)(2,1)}), bf16[4,96,512]{2,1,0:T(8,128)(2,1)S(1)}, u32[]{:S(2)}, u32[]{:S(2)}) async-start(bf16[4,96,512]{2,1,0:T(8,128)(2,1)} %bitcast.11), calls=%async_computation.3 | async-start | bytes 786432 | tf_op jit(solution)/shard_map/all_to_all | solution.py:74
where the time goes:
time: 86.4 us; the launch traced here: 85.7 us
  waiting for transfers between devices  30.9 us (36%)
  starting transfers between devices  16.9 us (20%)
  local copies, waits for them, and re-layouts  15.2 us (18%)
  other arithmetic  12.1 us (14%)
  matrix products  10.5 us (12%)
    all_to_all x1, waiting for transfers between devices, on_device(): lax.all_to_all(payload, 'batch', split_axis=0, concat_axis=0, tiled=True)  15.1 us
    all_to_all x1, waiting for transfers between devices, on_device(): lax.all_to_all(gated_rows.reshape(owners, capacity, -1), 'batch', split_a...  11 us
    all_to_all x1, starting transfers between devices, on_device(): lax.all_to_all(seg_send, 'batch', split_axis=0, concat_axis=0, tiled=True)  5.55 us
    all_to_all x1, starting transfers between devices, on_device(): lax.all_to_all(lookups, 'col', split_axis=0, concat_axis=1, tiled=True)  4.35 us
    dot_general x1, matrix products, project(): jnp.dot(normed, joined_weight, preferred_element_type=jnp.float32)  4.24 us
    all_to_all x1, starting transfers between devices, on_device(): lax.all_to_all(payload, 'batch', split_axis=0, concat_axis=0, tiled=True)  3.49 us
    all_to_all x1, starting transfers between devices, on_device(): lax.all_to_all(gated_rows.reshape(owners, capacity, -1), 'batch', split_a...  3.46 us
    dot_general x1, matrix products, attend(): jnp.einsum('hij,jhd->ihd', weights, value_part, preferred_element_type=jn...  3.04 us
  transfers between devices with their start and end apart: 4, of which 4 were waited for; matrix products, arithmetic and copies ran while one was open for 16% of the time, Pallas kernels for 0%

commit v1 on v0

--- a/solution.py
+++ b/solution.py
@@ -1,13 +1,20 @@
+import functools
+
 import jax
 import jax.numpy as jnp
 from jax import lax
+from jax.experimental import pallas as pl
+from jax.experimental.pallas import tpu as pltpu
 from jax.sharding import PartitionSpec as P
 
 HEADS = 4
 HEAD_DIM = 128
-
+SEG_ROWS = 8
 
 eps_norm = 1e-06
+
+F32 = jnp.float32
+BF16 = jnp.bfloat16
 
 
 def layer_norm(values):
@@ -18,10 +25,8 @@
 
 
 def project(hidden_rows, joined_weight):
-    normed = layer_norm(hidden_rows.astype(jnp.float32)).astype(jnp.bfloat16)
-    return jax.nn.silu(jnp.dot(normed, joined_weight, preferred_element_type=jnp.float32)).astype(
-        jnp.bfloat16
-    )
+    normed = layer_norm(hidden_rows.astype(F32)).astype(BF16)
+    return jax.nn.silu(jnp.dot(normed, joined_weight, preferred_element_type=F32)).astype(BF16)
 
 
 def attend(joined_rows, seg_ids):
@@ -32,22 +37,20 @@
     query_part = joined_rows[:, 2 * width : 3 * width].reshape(total, HEADS, HEAD_DIM)
     key_part = joined_rows[:, 3 * width :].reshape(total, HEADS, HEAD_DIM)
     scores = jnp.einsum(
-        "ihd,jhd->hij", query_part, key_part, preferred_element_type=jnp.float32
+        "ihd,jhd->hij", query_part, key_part, preferred_element_type=F32
     ) * HEAD_DIM ** (-0.5)
     positions = jnp.arange(total, dtype=jnp.int32)
     allowed = (positions[None, :] <= positions[:, None]) & (seg_ids[None, :] == seg_ids[:, None])
-    weights = jnp.where(allowed[None], jax.nn.silu(scores), 0.0).astype(jnp.bfloat16)
+    weights = jnp.where(allowed[None], jax.nn.silu(scores), 0.0).astype(BF16)
     mixed = jnp.einsum(
-        "hij,jhd->ihd", weights, value_part, preferred_element_type=jnp.float32
+        "hij,jhd->ihd", weights, value_part, preferred_element_type=F32
     ).reshape(total, width)
-    return (layer_norm(mixed) * gate_part.astype(jnp.float32)).astype(jnp.bfloat16)
-
-
-def on_device(lookups, input_weight, joined_weight, output_weight, owner_counts, user_index):
+    return (layer_norm(mixed) * gate_part.astype(F32)).astype(BF16)
+
+
+def owners_plan(lookups, input_weight, joined_weight, output_weight, owner_counts, user_index):
     token_block = lax.all_to_all(lookups, "col", split_axis=0, concat_axis=1, tiled=True)
-    hidden = jnp.dot(token_block, input_weight, preferred_element_type=jnp.float32).astype(
-        jnp.bfloat16
-    )
+    hidden = jnp.dot(token_block, input_weight, preferred_element_type=F32).astype(BF16)
     local_rows = hidden.shape[0]
     owners = lax.axis_size("batch")
     capacity = local_rows // owners + local_rows // (2 * owners)
@@ -75,15 +78,291 @@
         gated_rows.reshape(owners, capacity, -1), "batch", split_axis=0, concat_axis=0, tiled=True
     )
     own_gated = returned.reshape(owners * capacity, -1)[back_rows]
-    branch_rows = jnp.dot(own_gated, output_weight, preferred_element_type=jnp.float32).astype(
-        jnp.bfloat16
-    )
-    return (hidden.astype(jnp.float32) + branch_rows.astype(jnp.float32)).astype(jnp.bfloat16)
+    branch_rows = jnp.dot(own_gated, output_weight, preferred_element_type=F32).astype(BF16)
+    return (hidden.astype(F32) + branch_rows.astype(F32)).astype(BF16)
+
+
+def silu_of(values):
+    half = 0.5 * values
+    return half + half * jnp.tanh(half)
+
+
+def head_weights(query, key, allowed):
+    scores = lax.dot_general(query, key, (((1,), (1,)), ((), ())), preferred_element_type=F32)
+    half = scores * (0.5 * HEAD_DIM ** (-0.5))
+    return jnp.where(allowed, half + half * jnp.tanh(half), 0.0).astype(BF16)
+
+
+def seg_column(seg_row):
+    wide = jnp.broadcast_to(seg_row, (128, seg_row.shape[1]))
+    return wide.T[:, :1]
+
+
+def project_kernel(
+    place, counts, own, part1, part2, part3, w_in, w_joined, users,
+    hidden_out, gate_out, qkv_out, seg_out, send_a, send_b, send_c, normed,
+):
+    batch_at, col_at = place[0], place[1]
+    rows, piece = own.shape
+    group = qkv_out.shape[2] // 3
+    total = None
+    for shift, part in enumerate((own, part1, part2, part3)):
+        start = pl.multiple_of((col_at ^ shift) * piece, piece)
+        term = jnp.dot(part[...], w_in[pl.ds(start, piece), :], preferred_element_type=F32)
+        total = term if total is None else total + term
+    hidden = total.astype(BF16)
+    hidden_out[...] = hidden
+    normed[...] = layer_norm(hidden.astype(F32)).astype(BF16)
+
+    owners = counts.shape[1]
+    position = lax.broadcasted_iota(jnp.int32, (1, rows), 1)
+    end = counts[0, 0]
+    owner = (position >= end).astype(jnp.int32)
+    for d in range(1, owners - 1):
+        end = end + counts[0, d]
+        owner = owner + (position >= end).astype(jnp.int32)
+    seg_row = (owner + owners * users[...]).astype(F32)
+    seg = jnp.broadcast_to(seg_row, (SEG_ROWS, rows))
+    seg_out[...] = seg
+
+    width = 2 * group
+    for kind, base in ((1, 3), (2, 1), (0, 2)):
+        for g in range(2):
+            at = base * width + g * group
+            block = jnp.dot(normed[...], w_joined[:, at : at + group], preferred_element_type=F32)
+            qkv_out[g, :, kind * group : (kind + 1) * group] = silu_of(block).astype(BF16)
+    near = batch_at % 2
+    far = 1 - near
+    send_b[:rows, :] = qkv_out[far, :, group:]
+    send_c[:rows, :] = qkv_out[far, :, :group]
+    send_b[rows:, :rows] = seg.astype(BF16)
+    send_b[rows:, rows:] = seg.astype(BF16)
+    send_c[rows:, :] = seg.astype(BF16)
+    send_a[rows:, :rows] = seg.astype(BF16)
+    send_a[rows:, rows:] = seg.astype(BF16)
+
+    @pl.when(batch_at == 0)
+    def _():
+        send_a[:rows, :] = qkv_out[near, :, group:]
+
+    @pl.when(batch_at != 0)
+    def _():
+        which = jnp.where(batch_at == 1, far, near)
+        send_a[:rows, :group] = qkv_out[which, :, :group]
+        send_a[:rows, group:] = jnp.zeros((rows, group), BF16)
+
+    for g in range(2):
+        at = g * group
+        block = jnp.dot(normed[...], w_joined[:, at : at + group], preferred_element_type=F32)
+        gate_out[:, at : at + group] = silu_of(block).astype(BF16)
+
+
+def diagonal_kernel(qkv, seg, mixed_out):
+    rows = qkv.shape[1]
+    group = qkv.shape[2] // 3
+    seg_row = seg[0:1, :]
+    allowed = (seg_column(seg_row) == seg_row) & (
+        lax.broadcasted_iota(jnp.int32, (rows, rows), 1)
+        <= lax.broadcasted_iota(jnp.int32, (rows, rows), 0)
+    )
+    for g in range(2):
+        for h in range(group // HEAD_DIM):
+            lo = h * HEAD_DIM
+            weights = head_weights(
+                qkv[g, :, lo : lo + HEAD_DIM], qkv[g, :, group + lo : group + lo + HEAD_DIM], allowed
+            )
+            value = qkv[g, :, 2 * group + lo : 2 * group + lo + HEAD_DIM]
+            mixed_out[g, :, lo : lo + HEAD_DIM] = jnp.dot(weights, value, preferred_element_type=F32)
+
+
+def seg_row_of(ref, rows):
+    return ref[rows : rows + SEG_ROWS, :rows].astype(F32)[0:1, :]
+
+
+def far_kernel(place, qkv, seg, got_a, got_b, got_c, send_d, send_e):
+    batch_at = place[0]
+    rows = qkv.shape[1]
+    group = qkv.shape[2] // 3
+    near = batch_at % 2
+
+    def block(query, query_at, key_value, key_at, allowed, h):
+        lo = h * HEAD_DIM
+        weights = head_weights(
+            query(query_at + lo), key_value(key_at + lo), allowed
+        )
+        return jnp.dot(weights, key_value(key_at + group + lo), preferred_element_type=F32)
+
+    def own(at):
+        return qkv[near, :, at : at + HEAD_DIM]
+
+    def of(ref):
+        return lambda at: ref[:rows, at : at + HEAD_DIM]
+
+    seg_own = seg[0:1, :]
+    seg_a, seg_b, seg_c = (seg_row_of(ref, rows) for ref in (got_a, got_b, got_c))
+
+    def run(query_ref, query_seg, others, out):
+        column = seg_column(query_seg)
+        masks = [column == row for _, _, row in others]
+        for h in range(group // HEAD_DIM):
+            total = None
+            for (key_value, key_at, _), allowed in zip(others, masks):
+                term = block(of(query_ref), 0, key_value, key_at, allowed, h)
+                total = term if total is None else total + term
+            out[:, h * HEAD_DIM : (h + 1) * HEAD_DIM] = total.astype(BF16)
+
+    from_own = (own, group, seg_own)
+    from_a = (of(got_a), 0, seg_a)
+    from_b = (of(got_b), 0, seg_b)
+
+    @pl.when(batch_at == 0)
+    def _():
+        run(got_a, seg_a, [from_own], send_d)
+        send_e[...] = jnp.zeros_like(send_e)
+
+    @pl.when(batch_at == 1)
+    def _():
+        run(got_c, seg_c, [from_own, from_b], send_d)
+        run(got_a, seg_a, [from_own, from_b], send_e)
+
+    @pl.when(batch_at == 2)
+    def _():
+        run(got_c, seg_c, [from_own, from_b, from_a], send_d)
+        send_e[...] = jnp.zeros_like(send_e)
+
+    @pl.when(batch_at == 3)
+    def _():
+        send_d[...] = jnp.zeros_like(send_d)
+        send_e[...] = jnp.zeros_like(send_e)
+
+
+def near_kernel(place, qkv, seg, got_a, got_b, mixed, near_out):
+    batch_at = place[0]
+    rows = qkv.shape[1]
+    group = qkv.shape[2] // 3
+    near = batch_at % 2
+    column = seg_column(seg[0:1, :])
+    near_out[...] = mixed[near]
+
+    def add(ref):
+        allowed = column == seg_row_of(ref, rows)
+        for h in range(group // HEAD_DIM):
+            lo = h * HEAD_DIM
+            weights = head_weights(
+                qkv[near, :, lo : lo + HEAD_DIM], ref[:rows, lo : lo + HEAD_DIM], allowed
+            )
+            near_out[:, lo : lo + HEAD_DIM] += jnp.dot(
+                weights, ref[:rows, group + lo : group + lo + HEAD_DIM], preferred_element_type=F32
+            )
+
+    @pl.when(batch_at > 0)
+    def _():
+        add(got_b)
+
+    @pl.when(batch_at == 2)
+    def _():
+        add(got_a)
+
+
+def finish_kernel(place, mixed, near_mixed, got_d, got_e, gate, hidden, w_out, out, whole):
+    near = place[0] % 2
+    group = near_mixed.shape[1]
+    whole[near] = near_mixed[...] + got_e[...].astype(F32)
+    whole[1 - near] = mixed[1 - near] + got_d[...].astype(F32)
+    both = jnp.concatenate([whole[0], whole[1]], axis=1)
+    gated = (layer_norm(both) * gate[...].astype(F32)).astype(BF16)
+    branch = jnp.dot(gated, w_out[...], preferred_element_type=F32).astype(BF16)
+    out[...] = (hidden[...].astype(F32) + branch.astype(F32)).astype(BF16)
+
+
+VMEM = pl.BlockSpec(memory_space=pltpu.VMEM)
+SMEM = pl.BlockSpec(memory_space=pltpu.SMEM)
+
+
+def call(kernel, in_specs, outs, operands, flops, scratch=(), limit=32 << 20):
+    return pl.pallas_call(
+        kernel,
+        out_shape=[jax.ShapeDtypeStruct(shape, dtype) for shape, dtype in outs],
+        in_specs=in_specs,
+        out_specs=[VMEM] * len(outs),
+        scratch_shapes=list(scratch),
+        compiler_params=pltpu.CompilerParams(vmem_limit_bytes=limit),
+        cost_estimate=pl.CostEstimate(flops=flops, bytes_accessed=flops // 256, transcendentals=0),
+    )(*operands)
+
+
+def chain_plan(lookups, input_weight, joined_weight, output_weight, owner_counts, user_index):
+    cols = lax.axis_size("col")
+    batch_at = lax.axis_index("batch").astype(jnp.int32)
+    col_at = lax.axis_index("col").astype(jnp.int32)
+    place = jnp.stack([batch_at, col_at])
+    pieces = lookups.reshape(cols, lookups.shape[0] // cols, lookups.shape[1])
+    rows = pieces.shape[1]
+
+    def piece(shift):
+        return lax.dynamic_index_in_dim(pieces, col_at ^ shift, 0, keepdims=False)
+
+    got = [piece(0)] + [
+        lax.ppermute(piece(shift), "col", [(i, i ^ shift) for i in range(cols)])
+        for shift in range(1, cols)
+    ]
+    width = HEADS * HEAD_DIM
+    group = width // 2
+    features = input_weight.shape[1]
+    hidden, gate, qkv, seg, send_a, send_b, send_c = call(
+        project_kernel,
+        [SMEM, SMEM] + [VMEM] * 7,
+        [
+            ((rows, features), BF16),
+            ((rows, width), BF16),
+            ((2, rows, 3 * group), BF16),
+            ((SEG_ROWS, rows), F32),
+            ((rows + SEG_ROWS, 2 * group), BF16),
+            ((rows + SEG_ROWS, 2 * group), BF16),
+            ((rows + SEG_ROWS, group), BF16),
+        ],
+        (place, owner_counts, *got, input_weight, joined_weight, user_index.reshape(1, rows)),
+        2 * rows * features * (features + 4 * width),
+        [pltpu.VMEM((rows, features), BF16)],
+    )
+    got_a = lax.ppermute(send_a, "batch", [(0, 2), (3, 1), (1, 0)])
+    got_b = lax.ppermute(send_b, "batch", [(0, 1), (1, 2), (2, 3)])
+    got_c = lax.ppermute(send_c, "batch", [(2, 1), (3, 2)])
+    pair_flops = 4 * rows * rows * group
+    (mixed,) = call(
+        diagonal_kernel, [VMEM] * 2, [((2, rows, group), F32)], (qkv, seg), 2 * pair_flops
+    )
+    send_d, send_e = call(
+        far_kernel,
+        [SMEM] + [VMEM] * 5,
+        [((rows, group), BF16)] * 2,
+        (place, qkv, seg, got_a, got_b, got_c),
+        4 * pair_flops,
+    )
+    got_d = lax.ppermute(send_d, "batch", [(0, 1), (1, 2), (2, 3)])
+    got_e = lax.ppermute(send_e, "batch", [(1, 3)])
+    (near_mixed,) = call(
+        near_kernel,
+        [SMEM] + [VMEM] * 5,
+        [((rows, group), F32)],
+        (place, qkv, seg, got_a, got_b, mixed),
+        2 * pair_flops,
+    )
+    (out,) = call(
+        finish_kernel,
+        [SMEM] + [VMEM] * 7,
+        [((rows, features), BF16)],
+        (place, mixed, near_mixed, got_d, got_e, gate, hidden, output_weight),
+        2 * rows * width * features,
+        [pltpu.VMEM((2, rows, group), F32)],
+    )
+    return out
 
 
 def solution(mesh):
+    chain = mesh.shape["batch"] == HEADS and mesh.shape["col"] & (mesh.shape["col"] - 1) == 0
     return jax.shard_map(
-        on_device,
+        chain_plan if chain else owners_plan,
         mesh=mesh,
         in_specs=(
             P(("rep", "batch"), "col"),

time: 86.4 us -> 49.2 us (0.57)
  the two profiles are of different devices: /device:TPU:0 before, /device:TPU:24 now
where the time goes in v1:
time: 49.2 us; the launch traced here: 48.9 us
  waiting for transfers between devices  22.2 us (45%)
  starting transfers between devices  12.6 us (26%)
  Pallas kernels  7.67 us (16%)
  local copies, waits for them, and re-layouts  6.24 us (13%)
    pallas_call x5, Pallas kernels, call(): pl.pallas_call(kernel, out_shape=[jax.ShapeDtypeStruct(shape, dtype) for...  7.67 us
    ppermute x1, waiting for transfers between devices, chain_plan(): got_d = lax.ppermute(send_d, 'batch', [(0, 1), (1, 2), (2, 3)])  7.32 us
    ppermute x3, waiting for transfers between devices, chain_plan(): lax.ppermute(piece(shift), 'col', [(i, i ^ shift) for i in range(cols)])  6.67 us
    unnamed x10, local copies, waits for them, and re-layouts  5.12 us
    ppermute x1, starting transfers between devices, chain_plan(): got_c = lax.ppermute(send_c, 'batch', [(2, 1), (3, 2)])  4.55 us
    ppermute x1, waiting for transfers between devices, chain_plan(): got_e = lax.ppermute(send_e, 'batch', [(1, 3)])  3.98 us
    ppermute x1, waiting for transfers between devices, chain_plan(): got_c = lax.ppermute(send_c, 'batch', [(2, 1), (3, 2)])  2.99 us
    ppermute x1, starting transfers between devices, chain_plan(): got_a = lax.ppermute(send_a, 'batch', [(0, 2), (3, 1), (1, 0)])  2.25 us
  transfers between devices with their start and end apart: 8, of which 6 were waited for; matrix products, arithmetic and copies ran while one was open for 0% of the time, Pallas kernels for 4%

profile of v1, /device:TPU:24, one launch (start us, length us, event | category | flops | bytes accessed | tf_op | source)
XLA Modules:
  0.0 48.9 jit_solution(15874121205486542955)
XLA Ops:
  0.0 1.1 %dynamic-slice_bitcast_fusion = (bf16[256,256]{1,0:T(8,128)(2,1)S(1)}, bf16[256,256]{1,0:T(8,128)(2,1)S(1)}, bf16[256,256]{1,0:T(8,128)(2,1)S(1)}, bf16[256,256]{1,0:T(8,128)(2,1)S(1)}) fusion(bf16[4,256,256]{2,1,0:T(8,128)(2,1)} %bitcast.13, s32[]{:T(128)S(6)} %select_n.16, s32[]{:T(128)S(6)} %select_n.15, s32[]{:T(128)S(6)} %select_n.14, s32[]{:T(128)S(6)} %select_n.13), kind=kLoop, calls=%fused_computation | loop fusion | bytes 1048592 | tf_op jit(solution)/shard_map/jit(dynamic_index_in_dim)/squeeze | solution.py:303
  1.1 1.0 %collective-permute-start.2 = (bf16[256,256]{1,0:T(8,128)(2,1)S(1)}, bf16[256,256]{1,0:T(8,128)(2,1)S(1)}, u32[]{:S(2)}, u32[]{:S(2)}) collective-permute-start(bf16[256,256]{1,0:T(8,128)(2,1)S(1)} %get-tuple-element.23), channel_id=1, source_target_pairs={{0,6},{2,4},{4,2},{6,0},{1,7},{3,5},{5,3},{7,1},{8,14},{10,12},{12... | collective-permute-start | bytes 393224 | tf_op jit(solution)/shard_map/ppermute | solution.py:306
  2.1 0.6 %collective-permute-start.1 = (bf16[256,256]{1,0:T(8,128)(2,1)S(1)}, bf16[256,256]{1,0:T(8,128)(2,1)S(1)}, u32[]{:S(2)}, u32[]{:S(2)}) collective-permute-start(bf16[256,256]{1,0:T(8,128)(2,1)S(1)} %get-tuple-element.24), channel_id=1, source_target_pairs={{0,4},{2,6},{4,0},{6,2},{1,5},{3,7},{5,1},{7,3},{8,12},{10,14},{12... | collective-permute-start | bytes 393224 | tf_op jit(solution)/shard_map/ppermute | solution.py:306
  2.8 0.3 collective-permute-start
  3.1 0.1 pad_add_fusion.place
  3.1 3.8 %collective-permute-done.2.part3 = bf16[256,256]{1,0:T(8,128)(2,1)S(1)} collective-permute-done((bf16[256,256]{1,0:T(8,128)(2,1)S(1)}, bf16[256,256]{1,0:T(8,128)(2,1)S(1)}, u32[]{:S(2)}, u32[]{:S(2)}) %collective-permute-start.2) | collective-permute-done | bytes 131104 | tf_op jit(solution)/shard_map/ppermute | solution.py:306
  6.9 2.9 %collective-permute-done.1.part2 = bf16[256,256]{1,0:T(8,128)(2,1)S(1)} collective-permute-done((bf16[256,256]{1,0:T(8,128)(2,1)S(1)}, bf16[256,256]{1,0:T(8,128)(2,1)S(1)}, u32[]{:S(2)}, u32[]{:S(2)}) %collective-permute-start.1) | collective-permute-done | bytes 131104 | tf_op jit(solution)/shard_map/ppermute | solution.py:306
  9.8 0.0 collective-permute-done.part1
  9.8 0.0 copy-start
  9.8 2.2 %copy-done = bf16[1024,2048]{1,0:T(8,128)(2,1)S(1)} copy-done((bf16[1024,2048]{1,0:T(8,128)(2,1)S(1)}, bf16[1024,2048]{1,0:T(8,128)(2,1)}, u32[]{:S(2)}) %copy-start) | copy-done | bytes 4194328
  12.0 0.0 copy-start.1
  12.0 1.6 %copy-done.1 = bf16[1024,1024]{1,0:T(8,128)(2,1)S(1)} copy-done((bf16[1024,1024]{1,0:T(8,128)(2,1)S(1)}, bf16[1024,1024]{1,0:T(8,128)(2,1)}, u32[]{:S(2)}) %copy-start.1) | copy-done | bytes 2097176
  13.6 0.0 copy-start.3
  13.6 0.7 %copy-done.3 = s32[256]{0:T(256)S(1)} copy-done((s32[256]{0:T(256)S(1)}, s32[256]{0:T(256)}, u32[]{:S(2)}) %copy-start.3) | copy-done | bytes 1048
  14.3 0.0 copy-start.4
  14.3 0.7 %copy-done.4 = s32[1,4]{1,0:T(1,128)S(1)} copy-done((s32[1,4]{1,0:T(1,128)S(1)}, s32[1,4]{1,0:T(1,128)}, u32[]{:S(2)}) %copy-start.4) | copy-done | bytes 40
  14.9 0.0 copy-start.2
  14.9 3.2 %shard_map.64 = (bf16[256,1024]{1,0:T(8,128)(2,1)S(1)}, bf16[256,512]{1,0:T(8,128)(2,1)S(1)}, bf16[2,256,768]{2,1,0:T(8,128)(2,1)S(1)}, f32[8,256]{1,0:T(8,128)S...) custom-call(s32[2]{0:T(128)S(1)} %pad_add_fusion.place, ...), custom_call_target="tpu_custom_call" | custom-call | flops 1610612736 | bytes 6291456 | tf_op jit(solution)/shard_map/pallas_call | solution.py:283
  18.2 2.3 %collective-permute-start.3 = (bf16[264,512]{1,0:T(8,128)(2,1)S(1)}, bf16[264,512]{1,0:T(8,128)(2,1)S(1)}, u32[]{:S(2)}, u32[]{:S(2)}) collective-permute-start(bf16[264,512]{1,0:T(8,128)(2,1)S(1)} %get-tuple-element.16), channel_id=1, source_target_pairs={{0,16},{24,8},{8,0},{1,17},{25,9},{9,1},{2,18},{26,10},{10,2},{3,1... | collective-permute-start | bytes 811016 | tf_op jit(solution)/shard_map/ppermute | solution.py:328
  20.4 1.3 %collective-permute-start.4 = (bf16[264,512]{1,0:T(8,128)(2,1)S(1)}, bf16[264,512]{1,0:T(8,128)(2,1)S(1)}, u32[]{:S(2)}, u32[]{:S(2)}) collective-permute-start(bf16[264,512]{1,0:T(8,128)(2,1)S(1)} %get-tuple-element.17), channel_id=1, source_target_pairs={{0,8},{8,16},{16,24},{1,9},{9,17},{17,25},{2,10},{10,18},{18,26},{... | collective-permute-start | bytes 811016 | tf_op jit(solution)/shard_map/ppermute | solution.py:329
  21.7 4.6 %collective-permute-start.5 = (bf16[264,256]{1,0:T(8,128)(2,1)S(1)}, bf16[264,256]{1,0:T(8,128)(2,1)S(1)}, u32[]{:S(2)}, u32[]{:S(2)}) collective-permute-start(bf16[264,256]{1,0:T(8,128)(2,1)S(1)} %get-tuple-element.18), channel_id=1, source_target_pairs={{16,8},{24,16},{17,9},{25,17},{18,10},{26,18},{19,11},{27,19},{20,... | collective-permute-start | bytes 405512 | tf_op jit(solution)/shard_map/ppermute | solution.py:330
  26.3 3.0 %collective-permute-done.5.got_c = bf16[264,256]{1,0:T(8,128)(2,1)S(1)} collective-permute-done((bf16[264,256]{1,0:T(8,128)(2,1)S(1)}, bf16[264,256]{1,0:T(8,128)(2,1)S(1)}, u32[]{:S(2)}, u32[]{:S(2)}) %collective-permute-start.5) | collective-permute-done | bytes 135200 | tf_op jit(solution)/shard_map/ppermute | solution.py:330
  29.3 0.0 collective-permute-done.3.got_a
  29.3 1.2 %collective-permute-done.4.got_b = bf16[264,512]{1,0:T(8,128)(2,1)S(1)} collective-permute-done((bf16[264,512]{1,0:T(8,128)(2,1)S(1)}, bf16[264,512]{1,0:T(8,128)(2,1)S(1)}, u32[]{:S(2)}, u32[]{:S(2)}) %collective-permute-start.4) | collective-permute-done | bytes 270368 | tf_op jit(solution)/shard_map/ppermute | solution.py:329
  30.5 0.6 %shard_map.67 = (bf16[256,256]{1,0:T(8,128)(2,1)S(1)}, bf16[256,256]{1,0:T(8,128)(2,1)S(1)}) custom-call(s32[2]{0:T(128)S(1)} %pad_add_fusion.place, bf16[2,256,768]{2,1,0:T(8,128)(2,1)S(1)} %get-tuple-element.14.qkv, f32[8,256]{1,0:T(8,128)S(1)} %get-tuple-element.15.seg, bf16[264,512]{1,0:T(8,128)(2,1)S(1)} %collective-permute-done.3.got_a, ...), custom_call_target="tpu_custom_call" | custom-call | flops 268435456 | bytes 1048576 | tf_op jit(solution)/shard_map/pallas_call | solution.py:283
  31.1 1.3 %collective-permute-start.6 = (bf16[256,256]{1,0:T(8,128)(2,1)S(1)}, bf16[256,256]{1,0:T(8,128)(2,1)S(1)}, u32[]{:S(2)}, u32[]{:S(2)}) collective-permute-start(bf16[256,256]{1,0:T(8,128)(2,1)S(1)} %get-tuple-element.19), channel_id=1, source_target_pairs={{0,8},{8,16},{16,24},{1,9},{9,17},{17,25},{2,10},{10,18},{18,26},{... | collective-permute-start | bytes 393224 | tf_op jit(solution)/shard_map/ppermute | solution.py:342
  32.4 1.3 %collective-permute-start.7 = (bf16[256,256]{1,0:T(8,128)(2,1)S(1)}, bf16[256,256]{1,0:T(8,128)(2,1)S(1)}, u32[]{:S(2)}, u32[]{:S(2)}) collective-permute-start(bf16[256,256]{1,0:T(8,128)(2,1)S(1)} %get-tuple-element.20), channel_id=1, source_target_pairs={{8,24},{9,25},{10,26},{11,27},{12,28},{13,29},{14,30},{15,31}} | collective-permute-start | bytes 393224 | tf_op jit(solution)/shard_map/ppermute | solution.py:343
  33.7 0.7 %shard_map.65.mixed = f32[2,256,256]{2,1,0:T(8,128)S(1)} custom-call(bf16[2,256,768]{2,1,0:T(8,128)(2,1)S(1)} %get-tuple-element.14.qkv, f32[8,256]{1,0:T(8,128)S(1)} %get-tuple-element.15.seg), custom_call_target="tpu_custom_call" | custom-call | flops 134217728 | bytes 524288 | tf_op jit(solution)/shard_map/pallas_call | solution.py:283
  34.4 1.1 %shard_map.66.near_mixed = f32[256,256]{1,0:T(8,128)S(1)} custom-call(s32[2]{0:T(128)S(1)} %pad_add_fusion.place, bf16[2,256,768]{2,1,0:T(8,128)(2,1)S(1)} %get-tuple-element.14.qkv, f32[8,256]{1,0:T(8,128)S(1)} %get-tuple-element.15.seg, bf16[264,512]{1,0:T(8,128)(2,1)S(1)} %collective-permute-done.3.got_a, ...), custom_call_target="tpu_custom_call" | custom-call | flops 134217728 | bytes 524288 | tf_op jit(solution)/shard_map/pallas_call | solution.py:283
  35.5 7.3 %collective-permute-done.6.got_d = bf16[256,256]{1,0:T(8,128)(2,1)S(1)} collective-permute-done((bf16[256,256]{1,0:T(8,128)(2,1)S(1)}, bf16[256,256]{1,0:T(8,128)(2,1)S(1)}, u32[]{:S(2)}, u32[]{:S(2)}) %collective-permute-start.6) | collective-permute-done | bytes 131104 | tf_op jit(solution)/shard_map/ppermute | solution.py:342
  42.9 4.0 %collective-permute-done.7.got_e = bf16[256,256]{1,0:T(8,128)(2,1)S(1)} collective-permute-done((bf16[256,256]{1,0:T(8,128)(2,1)S(1)}, bf16[256,256]{1,0:T(8,128)(2,1)S(1)}, u32[]{:S(2)}, u32[]{:S(2)}) %collective-permute-start.7) | collective-permute-done | bytes 131104 | tf_op jit(solution)/shard_map/ppermute | solution.py:343
  46.8 0.0 copy-done.2
  46.8 2.0 %shard_map.68 = bf16[256,1024]{1,0:T(8,128)(2,1)} custom-call(s32[2]{0:T(128)S(1)} %pad_add_fusion.place, f32[2,256,256]{2,1,0:T(8,128)S(1)} %shard_map.65.mixed, f32[256,256]{1,0:T(8,128)S(1)} %shard_map.66.near_mixed, bf16[256,256]{1,0:T(8,128)(2,1)S(1)} %collective-permute-done.6.got_d, bf16[256,256]{1,0:T(8,128)(2,1)S(1)} %collective-permute-done.7.got_e, ...), custom_call_target="tpu_custom_call" | custom-call | flops 268435456 | bytes 1048576 | tf_op jit(solution)/shard_map/pallas_call | solution.py:283
Async XLA Ops:
  1.1 5.8 %collective-permute-start.2 = (bf16[256,256]{1,0:T(8,128)(2,1)S(1)}, bf16[256,256]{1,0:T(8,128)(2,1)S(1)}, u32[]{:S(2)}, u32[]{:S(2)}) collective-permute-start(bf16[256,256]{1,0:T(8,128)(2,1)S(1)} %get-tuple-element.23), channel_id=1, source_target_pairs={{0,6},{2,4},{4,2},{6,0},{1,7},{3,5},{5,3},{7,1},{8,14},{10,12},{12... | collective-permute-start | bytes 393224 | tf_op jit(solution)/shard_map/ppermute | solution.py:306
  2.1 7.7 %collective-permute-start.1 = (bf16[256,256]{1,0:T(8,128)(2,1)S(1)}, bf16[256,256]{1,0:T(8,128)(2,1)S(1)}, u32[]{:S(2)}, u32[]{:S(2)}) collective-permute-start(bf16[256,256]{1,0:T(8,128)(2,1)S(1)} %get-tuple-element.24), channel_id=1, source_target_pairs={{0,4},{2,6},{4,0},{6,2},{1,5},{3,7},{5,1},{7,3},{8,12},{10,14},{12... | collective-permute-start | bytes 393224 | tf_op jit(solution)/shard_map/ppermute | solution.py:306
  2.8 7.0 %collective-permute-start = (bf16[256,256]{1,0:T(8,128)(2,1)S(1)}, bf16[256,256]{1,0:T(8,128)(2,1)S(1)}, u32[]{:S(2)}, u32[]{:S(2)}) collective-permute-start(bf16[256,256]{1,0:T(8,128)(2,1)S(1)} %get-tuple-element.25), channel_id=1, source_target_pairs={{0,2},{2,0},{4,6},{6,4},{1,3},{3,1},{5,7},{7,5},{8,10},{10,8},{12,... | collective-permute-start | bytes 393224 | tf_op jit(solution)/shard_map/ppermute | solution.py:306
  9.8 2.2 %copy-start = (bf16[1024,2048]{1,0:T(8,128)(2,1)S(1)}, bf16[1024,2048]{1,0:T(8,128)(2,1)}, u32[]{:S(2)}) copy-start(bf16[1024,2048]{1,0:T(8,128)(2,1)} %w_joined.1) | copy-start | bytes 12582916
  12.0 1.6 %copy-start.1 = (bf16[1024,1024]{1,0:T(8,128)(2,1)S(1)}, bf16[1024,1024]{1,0:T(8,128)(2,1)}, u32[]{:S(2)}) copy-start(bf16[1024,1024]{1,0:T(8,128)(2,1)} %w_in.1) | copy-start | bytes 6291460
  13.6 0.7 %copy-start.3 = (s32[256]{0:T(256)S(1)}, s32[256]{0:T(256)}, u32[]{:S(2)}) copy-start(s32[256]{0:T(256)} %param.11) | copy-start | bytes 3076
  14.3 0.7 %copy-start.4 = (s32[1,4]{1,0:T(1,128)S(1)}, s32[1,4]{1,0:T(1,128)}, u32[]{:S(2)}) copy-start(s32[1,4]{1,0:T(1,128)} %counts.1) | copy-start | bytes 52
  14.9 31.9 %copy-start.2 = (bf16[512,1024]{1,0:T(8,128)(2,1)S(1)}, bf16[512,1024]{1,0:T(8,128)(2,1)}, u32[]{:S(2)}) copy-start(bf16[512,1024]{1,0:T(8,128)(2,1)} %w_out.1) | copy-start | bytes 3145732
  18.2 11.1 %collective-permute-start.3 = (bf16[264,512]{1,0:T(8,128)(2,1)S(1)}, bf16[264,512]{1,0:T(8,128)(2,1)S(1)}, u32[]{:S(2)}, u32[]{:S(2)}) collective-permute-start(bf16[264,512]{1,0:T(8,128)(2,1)S(1)} %get-tuple-element.16), channel_id=1, source_target_pairs={{0,16},{24,8},{8,0},{1,17},{25,9},{9,1},{2,18},{26,10},{10,2},{3,1... | collective-permute-start | bytes 811016 | tf_op jit(solution)/shard_map/ppermute | solution.py:328
  20.4 10.1 %collective-permute-start.4 = (bf16[264,512]{1,0:T(8,128)(2,1)S(1)}, bf16[264,512]{1,0:T(8,128)(2,1)S(1)}, u32[]{:S(2)}, u32[]{:S(2)}) collective-permute-start(bf16[264,512]{1,0:T(8,128)(2,1)S(1)} %get-tuple-element.17), channel_id=1, source_target_pairs={{0,8},{8,16},{16,24},{1,9},{9,17},{17,25},{2,10},{10,18},{18,26},{... | collective-permute-start | bytes 811016 | tf_op jit(solution)/shard_map/ppermute | solution.py:329
  21.7 7.5 %collective-permute-start.5 = (bf16[264,256]{1,0:T(8,128)(2,1)S(1)}, bf16[264,256]{1,0:T(8,128)(2,1)S(1)}, u32[]{:S(2)}, u32[]{:S(2)}) collective-permute-start(bf16[264,256]{1,0:T(8,128)(2,1)S(1)} %get-tuple-element.18), channel_id=1, source_target_pairs={{16,8},{24,16},{17,9},{25,17},{18,10},{26,18},{19,11},{27,19},{20,... | collective-permute-start | bytes 405512 | tf_op jit(solution)/shard_map/ppermute | solution.py:330
  31.1 11.8 %collective-permute-start.6 = (bf16[256,256]{1,0:T(8,128)(2,1)S(1)}, bf16[256,256]{1,0:T(8,128)(2,1)S(1)}, u32[]{:S(2)}, u32[]{:S(2)}) collective-permute-start(bf16[256,256]{1,0:T(8,128)(2,1)S(1)} %get-tuple-element.19), channel_id=1, source_target_pairs={{0,8},{8,16},{16,24},{1,9},{9,17},{17,25},{2,10},{10,18},{18,26},{... | collective-permute-start | bytes 393224 | tf_op jit(solution)/shard_map/ppermute | solution.py:342
  32.4 14.5 %collective-permute-start.7 = (bf16[256,256]{1,0:T(8,128)(2,1)S(1)}, bf16[256,256]{1,0:T(8,128)(2,1)S(1)}, u32[]{:S(2)}, u32[]{:S(2)}) collective-permute-start(bf16[256,256]{1,0:T(8,128)(2,1)S(1)} %get-tuple-element.20), channel_id=1, source_target_pairs={{8,24},{9,25},{10,26},{11,27},{12,28},{13,29},{14,30},{15,31}} | collective-permute-start | bytes 393224 | tf_op jit(solution)/shard_map/ppermute | solution.py:343

commit v2 on v0

--- a/solution.py
+++ b/solution.py
@@ -1,13 +1,20 @@
+import functools
+
 import jax
 import jax.numpy as jnp
 from jax import lax
+from jax.experimental import pallas as pl
+from jax.experimental.pallas import tpu as pltpu
 from jax.sharding import PartitionSpec as P
 
 HEADS = 4
 HEAD_DIM = 128
-
+SEG_ROWS = 8
 
 eps_norm = 1e-06
+
+F32 = jnp.float32
+BF16 = jnp.bfloat16
 
 
 def layer_norm(values):
@@ -18,10 +25,8 @@
 
 
 def project(hidden_rows, joined_weight):
-    normed = layer_norm(hidden_rows.astype(jnp.float32)).astype(jnp.bfloat16)
-    return jax.nn.silu(jnp.dot(normed, joined_weight, preferred_element_type=jnp.float32)).astype(
-        jnp.bfloat16
-    )
+    normed = layer_norm(hidden_rows.astype(F32)).astype(BF16)
+    return jax.nn.silu(jnp.dot(normed, joined_weight, preferred_element_type=F32)).astype(BF16)
 
 
 def attend(joined_rows, seg_ids):
@@ -32,22 +37,20 @@
     query_part = joined_rows[:, 2 * width : 3 * width].reshape(total, HEADS, HEAD_DIM)
     key_part = joined_rows[:, 3 * width :].reshape(total, HEADS, HEAD_DIM)
     scores = jnp.einsum(
-        "ihd,jhd->hij", query_part, key_part, preferred_element_type=jnp.float32
+        "ihd,jhd->hij", query_part, key_part, preferred_element_type=F32
     ) * HEAD_DIM ** (-0.5)
     positions = jnp.arange(total, dtype=jnp.int32)
     allowed = (positions[None, :] <= positions[:, None]) & (seg_ids[None, :] == seg_ids[:, None])
-    weights = jnp.where(allowed[None], jax.nn.silu(scores), 0.0).astype(jnp.bfloat16)
+    weights = jnp.where(allowed[None], jax.nn.silu(scores), 0.0).astype(BF16)
     mixed = jnp.einsum(
-        "hij,jhd->ihd", weights, value_part, preferred_element_type=jnp.float32
+        "hij,jhd->ihd", weights, value_part, preferred_element_type=F32
     ).reshape(total, width)
-    return (layer_norm(mixed) * gate_part.astype(jnp.float32)).astype(jnp.bfloat16)
-
-
-def on_device(lookups, input_weight, joined_weight, output_weight, owner_counts, user_index):
+    return (layer_norm(mixed) * gate_part.astype(F32)).astype(BF16)
+
+
+def owners_plan(lookups, input_weight, joined_weight, output_weight, owner_counts, user_index):
     token_block = lax.all_to_all(lookups, "col", split_axis=0, concat_axis=1, tiled=True)
-    hidden = jnp.dot(token_block, input_weight, preferred_element_type=jnp.float32).astype(
-        jnp.bfloat16
-    )
+    hidden = jnp.dot(token_block, input_weight, preferred_element_type=F32).astype(BF16)
     local_rows = hidden.shape[0]
     owners = lax.axis_size("batch")
     capacity = local_rows // owners + local_rows // (2 * owners)
@@ -75,15 +78,307 @@
         gated_rows.reshape(owners, capacity, -1), "batch", split_axis=0, concat_axis=0, tiled=True
     )
     own_gated = returned.reshape(owners * capacity, -1)[back_rows]
-    branch_rows = jnp.dot(own_gated, output_weight, preferred_element_type=jnp.float32).astype(
-        jnp.bfloat16
-    )
-    return (hidden.astype(jnp.float32) + branch_rows.astype(jnp.float32)).astype(jnp.bfloat16)
+    branch_rows = jnp.dot(own_gated, output_weight, preferred_element_type=F32).astype(BF16)
+    return (hidden.astype(F32) + branch_rows.astype(F32)).astype(BF16)
+
+
+def silu_of(values):
+    half = 0.5 * values
+    return half + half * jnp.tanh(half)
+
+
+def head_weights(query, key, allowed):
+    scores = lax.dot_general(query, key, (((1,), (1,)), ((), ())), preferred_element_type=F32)
+    half = scores * (0.5 * HEAD_DIM ** (-0.5))
+    return jnp.where(allowed, half + half * jnp.tanh(half), 0.0).astype(BF16)
+
+
+def seg_column(seg_row):
+    wide = jnp.broadcast_to(seg_row, (128, seg_row.shape[1]))
+    return wide.T[:, :1]
+
+
+def segments_kernel(counts, users, seg_out):
+    rows = users.shape[1]
+    owners = counts.shape[1]
+    position = lax.broadcasted_iota(jnp.int32, (1, rows), 1)
+    end = counts[0, 0]
+    owner = (position >= end).astype(jnp.int32)
+    for d in range(1, owners - 1):
+        end = end + counts[0, d]
+        owner = owner + (position >= end).astype(jnp.int32)
+    seg_out[...] = jnp.broadcast_to((owner + owners * users[...]).astype(F32), seg_out.shape)
+
+
+def columns_of(w_joined, block, index, group):
+    start = pl.multiple_of(block * 2 * group + index * group, group)
+    return w_joined[:, pl.ds(start, group)]
+
+
+def put_seg(ref, seg):
+    rows = seg.shape[1]
+    for at in range(0, ref.shape[1], rows):
+        ref[rows:, at : at + rows] = seg.astype(BF16)
+
+
+def project_first_kernel(
+    place, own, part1, part2, part3, w_in, w_joined, seg, hidden_out, normed, send_b
+):
+    batch_at, col_at = place[0], place[1]
+    rows, piece = own.shape
+    group = send_b.shape[1] // 2
+    total = None
+    for shift, part in enumerate((own, part1, part2, part3)):
+        start = pl.multiple_of((col_at ^ shift) * piece, piece)
+        term = jnp.dot(part[...], w_in[pl.ds(start, piece), :], preferred_element_type=F32)
+        total = term if total is None else total + term
+    hidden = total.astype(BF16)
+    hidden_out[...] = hidden
+    normed[...] = layer_norm(hidden.astype(F32)).astype(BF16)
+    far = 1 - batch_at % 2
+    for at, block in ((0, 3), (group, 1)):
+        joined = jnp.dot(
+            normed[...], columns_of(w_joined, block, far, group), preferred_element_type=F32
+        )
+        send_b[:rows, at : at + group] = silu_of(joined).astype(BF16)
+    put_seg(send_b, seg[...])
+
+
+def project_rest_kernel(place, normed, w_joined, seg, send_a, send_c, send_f, query_near):
+    batch_at = place[0]
+    rows = normed.shape[0]
+    group = send_c.shape[1]
+    near = batch_at % 2
+
+    def joined(block, index):
+        return silu_of(
+            jnp.dot(
+                normed[...], columns_of(w_joined, block, index, group), preferred_element_type=F32
+            )
+        ).astype(BF16)
+
+    query_near[...] = joined(2, near)
+    send_c[:rows, :] = joined(2, 1 - near)
+    put_seg(send_c, seg[...])
+    put_seg(send_f, seg[...])
+
+    @pl.when(batch_at == 1)
+    def _():
+        send_f[:rows, :] = send_c[:rows, :]
+
+    @pl.when(batch_at != 1)
+    def _():
+        send_f[:rows, :] = query_near[...]
+
+    send_a[:rows, :group] = joined(3, near)
+    send_a[:rows, group:] = joined(1, near)
+    put_seg(send_a, seg[...])
+
+
+def seg_row_of(ref, rows):
+    return ref[rows : rows + SEG_ROWS, :rows].astype(F32)[0:1, :]
+
+
+def add_blocks(query, key_values, out):
+    group = query.shape[1]
+    rows = query.shape[0] - SEG_ROWS
+    column = seg_column(seg_row_of(query, rows))
+    masks = [column == seg_row_of(ref, rows) for ref in key_values]
+    for lo in range(0, group, HEAD_DIM):
+        hi = lo + HEAD_DIM
+        total = None
+        for ref, allowed in zip(key_values, masks):
+            weights = head_weights(query[:rows, lo:hi], ref[:rows, lo:hi], allowed)
+            term = jnp.dot(
+                weights, ref[:rows, group + lo : group + hi], preferred_element_type=F32
+            )
+            total = term if total is None else total + term
+        out[:, lo:hi] = total.astype(BF16)
+
+
+def add_near(query_near, column, key_value, mixed):
+    rows, group = query_near.shape
+    allowed = column == seg_row_of(key_value, rows)
+    for lo in range(0, group, HEAD_DIM):
+        hi = lo + HEAD_DIM
+        weights = head_weights(query_near[:, lo:hi], key_value[:rows, lo:hi], allowed)
+        mixed[:, lo:hi] += jnp.dot(
+            weights, key_value[:rows, group + lo : group + hi], preferred_element_type=F32
+        )
+
+
+def own_kernel(
+    place, got_b, query_near, send_a, send_b, send_c, seg, normed, w_joined, mixed_out, gate_out
+):
+    rows, group = query_near.shape
+    seg_row = seg[0:1, :]
+    column = seg_column(seg_row)
+    allowed = (column == seg_row) & (
+        lax.broadcasted_iota(jnp.int32, (rows, rows), 1)
+        <= lax.broadcasted_iota(jnp.int32, (rows, rows), 0)
+    )
+    for side, (query, key_value) in enumerate(((query_near, send_a), (send_c, send_b))):
+        for lo in range(0, group, HEAD_DIM):
+            hi = lo + HEAD_DIM
+            weights = head_weights(query[:rows, lo:hi], key_value[:rows, lo:hi], allowed)
+            mixed_out[side, :, lo:hi] = jnp.dot(
+                weights, key_value[:rows, group + lo : group + hi], preferred_element_type=F32
+            )
+
+    @pl.when(place[0] > 0)
+    def _():
+        add_near(query_near, column, got_b, mixed_out.at[0])
+
+    for at in range(0, 2 * group, group):
+        block = jnp.dot(normed[...], w_joined[:, at : at + group], preferred_element_type=F32)
+        gate_out[:, at : at + group] = silu_of(block).astype(BF16)
+
+
+def far_kernel(place, got_b, mixed, send_a, got_f, got_c, got_a, send_e, send_d):
+    @pl.when(place[0] == 0)
+    def _():
+        add_blocks(got_f, [send_a], send_d)
+
+    @pl.when(place[0] == 1)
+    def _():
+        add_blocks(got_f, [send_a, got_b], send_e)
+        add_blocks(got_c, [send_a, got_b], send_d)
+
+    @pl.when(place[0] == 2)
+    def _():
+        add_blocks(got_c, [send_a, got_b, got_a], send_d)
+
+    @pl.when(place[0] != 1)
+    def _():
+        send_e[...] = jnp.zeros_like(send_e)
+
+    @pl.when(place[0] > 2)
+    def _():
+        send_d[...] = jnp.zeros_like(send_d)
+
+
+def near_kernel(place, query_near, seg, got_a, mixed, near_out):
+    near_out[...] = mixed[0]
+
+    @pl.when(place[0] == 2)
+    def _():
+        add_near(query_near, seg_column(seg[0:1, :]), got_a, near_out)
+
+
+def finish_kernel(place, mixed, near_mixed, got_e, got_d, gate, hidden, w_out, out, whole):
+    near = place[0] % 2
+    whole[near] = near_mixed[...] + got_e[...].astype(F32)
+    whole[1 - near] = mixed[1] + got_d[...].astype(F32)
+    both = jnp.concatenate([whole[0], whole[1]], axis=1)
+    gated = (layer_norm(both) * gate[...].astype(F32)).astype(BF16)
+    branch = jnp.dot(gated, w_out[...], preferred_element_type=F32).astype(BF16)
+    out[...] = (hidden[...].astype(F32) + branch.astype(F32)).astype(BF16)
+
+
+VMEM = pl.BlockSpec(memory_space=pltpu.VMEM)
+SMEM = pl.BlockSpec(memory_space=pltpu.SMEM)
+
+
+def call(kernel, in_specs, outs, operands, flops, scratch=(), limit=32 << 20):
+    return pl.pallas_call(
+        kernel,
+        out_shape=[jax.ShapeDtypeStruct(shape, dtype) for shape, dtype in outs],
+        in_specs=in_specs,
+        out_specs=[VMEM] * len(outs),
+        scratch_shapes=list(scratch),
+        compiler_params=pltpu.CompilerParams(vmem_limit_bytes=limit),
+        cost_estimate=pl.CostEstimate(flops=flops, bytes_accessed=0, transcendentals=0),
+    )(*operands)
+
+
+def chain_plan(lookups, input_weight, joined_weight, output_weight, owner_counts, user_index):
+    cols = lax.axis_size("col")
+    batch_at = lax.axis_index("batch").astype(jnp.int32)
+    col_at = lax.axis_index("col").astype(jnp.int32)
+    place = jnp.stack([batch_at, col_at])
+    pieces = lookups.reshape(cols, lookups.shape[0] // cols, lookups.shape[1])
+    rows = pieces.shape[1]
+
+    def piece(shift):
+        return lax.dynamic_index_in_dim(pieces, col_at ^ shift, 0, keepdims=False)
+
+    parts = [piece(0)] + [
+        lax.ppermute(piece(shift), "col", [(i, i ^ shift) for i in range(cols)])
+        for shift in range(1, cols)
+    ]
+    width = HEADS * HEAD_DIM
+    group = width // 2
+    features = input_weight.shape[1]
+    tall = rows + SEG_ROWS
+    (seg,) = call(
+        segments_kernel,
+        [SMEM, VMEM],
+        [((SEG_ROWS, rows), F32)],
+        (owner_counts, user_index.reshape(1, rows)),
+        2 * rows * features * (features + 4 * width),
+    )
+    hidden, normed, send_b = call(
+        project_first_kernel,
+        [SMEM] + [VMEM] * 7,
+        [((rows, features), BF16), ((rows, features), BF16), ((tall, 2 * group), BF16)],
+        (place, *parts, input_weight, joined_weight, seg),
+        2 * rows * features * (features + 2 * group),
+    )
+    got_b = lax.ppermute(send_b, "batch", [(0, 1), (1, 2), (2, 3)])
+    send_a, send_c, send_f, query_near = call(
+        project_rest_kernel,
+        [SMEM] + [VMEM] * 3,
+        [
+            ((tall, 2 * group), BF16),
+            ((tall, group), BF16),
+            ((tall, group), BF16),
+            ((rows, group), BF16),
+        ],
+        (place, normed, joined_weight, seg),
+        2 * rows * features * 4 * group,
+    )
+    got_a = lax.ppermute(send_a, "batch", [(0, 2)])
+    got_f = lax.ppermute(send_f, "batch", [(3, 1), (1, 0)])
+    got_c = lax.ppermute(send_c, "batch", [(2, 1), (3, 2)])
+    pair_flops = 4 * rows * rows * group
+    mixed, gate = call(
+        own_kernel,
+        [SMEM] + [VMEM] * 8,
+        [((2, rows, group), F32), ((rows, width), BF16)],
+        (place, got_b, query_near, send_a, send_b, send_c, seg, normed, joined_weight),
+        3 * pair_flops + 2 * rows * features * width,
+    )
+    send_e, send_d = call(
+        far_kernel,
+        [SMEM] + [VMEM] * 6,
+        [((rows, group), BF16)] * 2,
+        (place, got_b, mixed, send_a, got_f, got_c, got_a),
+        rows,
+    )
+    got_e = lax.ppermute(send_e, "batch", [(1, 3)])
+    got_d = lax.ppermute(send_d, "batch", [(0, 1), (1, 2), (2, 3)])
+    (near_mixed,) = call(
+        near_kernel,
+        [SMEM] + [VMEM] * 4,
+        [((rows, group), F32)],
+        (place, query_near, seg, got_a, mixed),
+        rows,
+    )
+    (out,) = call(
+        finish_kernel,
+        [SMEM] + [VMEM] * 7,
+        [((rows, features), BF16)],
+        (place, mixed, near_mixed, got_e, got_d, gate, hidden, output_weight),
+        2 * rows * width * features,
+        [pltpu.VMEM((2, rows, group), F32)],
+    )
+    return out
 
 
 def solution(mesh):
+    chain = mesh.shape["batch"] == HEADS and mesh.shape["col"] & (mesh.shape["col"] - 1) == 0
     return jax.shard_map(
-        on_device,
+        chain_plan if chain else owners_plan,
         mesh=mesh,
         in_specs=(
             P(("rep", "batch"), "col"),

time: 86.4 us -> 45.9 us (0.53)
  waiting for transfers between devices: 30.9 us -> 9.3 us
  other arithmetic: 12.1 us -> 0.08 us
  matrix products: 10.5 us -> 0 us
  local copies, waits for them, and re-layouts: 15.2 us -> 4.81 us
  Pallas kernels: 0 us -> 9.56 us
  starting transfers between devices: 16.9 us -> 21.7 us
    all_to_all x4 -> x0, waiting for transfers between devices: 30.9 us -> none  [the longest x1 15.1 us: on_device(): lax.all_to_all(payload, 'batch', split_axis=0, concat_axis=0, tiled=True)]
    ppermute x0 -> x9, starting transfers between devices: none -> 21.7 us  [the longest x1 7.11 us: chain_plan(): got_d = lax.ppermute(send_d, 'batch', [(0, 1), (1, 2), (2, 3)])]
    all_to_all x4 -> x0, starting transfers between devices: 16.9 us -> none  [the longest x1 5.55 us: on_device(): lax.all_to_all(seg_send, 'batch', split_axis=0, concat_axis=0, tiled=True)]
    dot_general x4 -> x0, matrix products: 10.5 us -> none  [the longest x1 4.24 us: project(): jnp.dot(normed, joined_weight, preferred_element_type=jnp.float32)]
    pallas_call x0 -> x7, Pallas kernels: none -> 9.56 us  [call(): pl.pallas_call(kernel, out_shape=[jax.ShapeDtypeStruct(shape, dtype) for...]
    ppermute x0 -> x9, waiting for transfers between devices: none -> 9.3 us  [the longest x3 4.21 us: chain_plan(): lax.ppermute(piece(shift), 'col', [(i, i ^ shift) for i in range(cols)])]
    gather x4 -> x0, local copies, waits for them, and re-layouts: 6.73 us -> none  [the longest x2 2.89 us: on_device(): user_index[gather_rows]]
    convert_element_type x2 -> x0, other arithmetic: 3.1 us -> none  [the longest x1 2.18 us: attend(): (layer_norm(mixed) * gate_part.astype(jnp.float32)).astype(jnp.bfloat16)]
  transfers between devices with their start and end apart: 4 -> 9, of which waited for: 4 -> 4; matrix products, arithmetic and copies ran while one was open for 16% -> 0% of each run, Pallas kernels for 0% -> 10%
where the time goes in v2:
time: 45.9 us; the launch traced here: 45.6 us
  starting transfers between devices  21.7 us (47%)
  Pallas kernels  9.56 us (21%)
  waiting for transfers between devices  9.3 us (20%)
  local copies, waits for them, and re-layouts  4.81 us (10%)
    pallas_call x7, Pallas kernels, call(): pl.pallas_call(kernel, out_shape=[jax.ShapeDtypeStruct(shape, dtype) for...  9.56 us
    ppermute x1, starting transfers between devices, chain_plan(): got_d = lax.ppermute(send_d, 'batch', [(0, 1), (1, 2), (2, 3)])  7.11 us
    ppermute x1, starting transfers between devices, chain_plan(): got_a = lax.ppermute(send_a, 'batch', [(0, 2)])  4.51 us
    ppermute x1, starting transfers between devices, chain_plan(): got_b = lax.ppermute(send_b, 'batch', [(0, 1), (1, 2), (2, 3)])  4.3 us
    ppermute x3, waiting for transfers between devices, chain_plan(): lax.ppermute(piece(shift), 'col', [(i, i ^ shift) for i in range(cols)])  4.21 us
    unnamed x12, local copies, waits for them, and re-layouts  3.53 us
    ppermute x1, waiting for transfers between devices, chain_plan(): got_f = lax.ppermute(send_f, 'batch', [(3, 1), (1, 0)])  3.16 us
    ppermute x3, starting transfers between devices, chain_plan(): lax.ppermute(piece(shift), 'col', [(i, i ^ shift) for i in range(cols)])  3.12 us
  transfers between devices with their start and end apart: 9, of which 4 were waited for; matrix products, arithmetic and copies ran while one was open for 0% of the time, Pallas kernels for 10%

profile of v2, /device:TPU:0, one launch (start us, length us, event | category | flops | bytes accessed | tf_op | source)
XLA Modules:
  0.0 45.6 jit_solution(12898006238508807681)
XLA Ops:
  0.0 0.0 copy-start.2
  0.0 1.3 %dynamic-slice_bitcast_fusion = (bf16[256,256]{1,0:T(8,128)(2,1)S(1)}, bf16[256,256]{1,0:T(8,128)(2,1)S(1)}, bf16[256,256]{1,0:T(8,128)(2,1)S(1)}, bf16[256,256]{1,0:T(8,128)(2,1)S(1)}) fusion(bf16[4,256,256]{2,1,0:T(8,128)(2,1)} %bitcast.13, s32[]{:T(128)S(6)} %select_n.16, s32[]{:T(128)S(6)} %select_n.15, s32[]{:T(128)S(6)} %select_n.14, s32[]{:T(128)S(6)} %select_n.13), kind=kLoop, calls=%fused_computation | loop fusion | bytes 1048592 | tf_op jit(solution)/shard_map/jit(dynamic_index_in_dim)/squeeze | solution.py:303
  1.3 2.4 %collective-permute-start.2 = (bf16[256,256]{1,0:T(8,128)(2,1)S(1)}, bf16[256,256]{1,0:T(8,128)(2,1)S(1)}, u32[]{:S(2)}, u32[]{:S(2)}) collective-permute-start(bf16[256,256]{1,0:T(8,128)(2,1)S(1)} %get-tuple-element.27), channel_id=1, source_target_pairs={{0,6},{2,4},{4,2},{6,0},{1,7},{3,5},{5,3},{7,1},{8,14},{10,12},{12... | collective-permute-start | bytes 393224 | tf_op jit(solution)/shard_map/ppermute | solution.py:306
  3.7 0.6 %collective-permute-start.1 = (bf16[256,256]{1,0:T(8,128)(2,1)S(1)}, bf16[256,256]{1,0:T(8,128)(2,1)S(1)}, u32[]{:S(2)}, u32[]{:S(2)}) collective-permute-start(bf16[256,256]{1,0:T(8,128)(2,1)S(1)} %get-tuple-element.28), channel_id=1, source_target_pairs={{0,4},{2,6},{4,0},{6,2},{1,5},{3,7},{5,1},{7,3},{8,12},{10,14},{12... | collective-permute-start | bytes 393224 | tf_op jit(solution)/shard_map/ppermute | solution.py:306
  4.4 0.0 collective-permute-start
  4.4 0.0 copy-start.4
  4.4 0.7 %copy-done.4 = s32[256]{0:T(256)S(1)} copy-done((s32[256]{0:T(256)S(1)}, s32[256]{0:T(256)}, u32[]{:S(2)}) %copy-start.4) | copy-done | bytes 1048
  5.1 0.0 copy-start.5
  5.1 0.7 %copy-done.5 = s32[1,4]{1,0:T(1,128)S(1)} copy-done((s32[1,4]{1,0:T(1,128)S(1)}, s32[1,4]{1,0:T(1,128)}, u32[]{:S(2)}) %copy-start.5) | copy-done | bytes 40
  5.7 0.6 %shard_map.64.seg = f32[8,256]{1,0:T(8,128)S(1)} custom-call(s32[1,4]{1,0:T(1,128)S(1)} %copy-done.5, s32[1,256]{1,0:T(1,128)S(1)} %bitcast.12), custom_call_target="tpu_custom_call" | custom-call | flops 1610612736 | tf_op jit(solution)/shard_map/pallas_call | solution.py:283
  6.3 0.1 pad_add_fusion.place
  6.4 1.2 %collective-permute-done.2.part3 = bf16[256,256]{1,0:T(8,128)(2,1)S(1)} collective-permute-done((bf16[256,256]{1,0:T(8,128)(2,1)S(1)}, bf16[256,256]{1,0:T(8,128)(2,1)S(1)}, u32[]{:S(2)}, u32[]{:S(2)}) %collective-permute-start.2) | collective-permute-done | bytes 131104 | tf_op jit(solution)/shard_map/ppermute | solution.py:306
  7.6 3.0 %collective-permute-done.1.part2 = bf16[256,256]{1,0:T(8,128)(2,1)S(1)} collective-permute-done((bf16[256,256]{1,0:T(8,128)(2,1)S(1)}, bf16[256,256]{1,0:T(8,128)(2,1)S(1)}, u32[]{:S(2)}, u32[]{:S(2)}) %collective-permute-start.1) | collective-permute-done | bytes 131104 | tf_op jit(solution)/shard_map/ppermute | solution.py:306
  10.6 0.0 collective-permute-done.part1
  10.6 0.0 copy-done.2
  10.6 0.0 copy-start
  10.6 2.2 %copy-done = bf16[1024,2048]{1,0:T(8,128)(2,1)S(1)} copy-done((bf16[1024,2048]{1,0:T(8,128)(2,1)S(1)}, bf16[1024,2048]{1,0:T(8,128)(2,1)}, u32[]{:S(2)}) %copy-start) | copy-done | bytes 4194328
  12.8 0.0 copy-start.1
  12.8 2.0 %shard_map.65 = (bf16[256,1024]{1,0:T(8,128)(2,1)S(1)}, bf16[256,1024]{1,0:T(8,128)(2,1)S(1)}, bf16[264,512]{1,0:T(8,128)(2,1)S(1)}) custom-call(s32[2]{0:T(128)S(1)} %pad_add_fusion.place, bf16[256,256]{1,0:T(8,128)(2,1)S(1)} %get-tuple-element.30.own, bf16[256,256]{1,0:T(8,128)(2,1)S(1)} %collective-permute-done.part1, ...), custom_call_target="tpu_custom_call" | custom-call | flops 805306368 | tf_op jit(solution)/shard_map/pallas_call | solution.py:283
  14.8 4.3 %collective-permute-start.3 = (bf16[264,512]{1,0:T(8,128)(2,1)S(1)}, bf16[264,512]{1,0:T(8,128)(2,1)S(1)}, u32[]{:S(2)}, u32[]{:S(2)}) collective-permute-start(bf16[264,512]{1,0:T(8,128)(2,1)S(1)} %get-tuple-element.16.send_b), channel_id=1, source_target_pairs={{0,8},{8,16},{16,24},{1,9},{9,17},{17,25},{2,10},{10,18},{18,26},{... | collective-permute-start | bytes 811016 | tf_op jit(solution)/shard_map/ppermute | solution.py:327
  19.1 0.0 copy-done.1
  19.1 1.5 %shard_map.66 = (bf16[264,512]{1,0:T(8,128)(2,1)S(1)}, bf16[264,256]{1,0:T(8,128)(2,1)S(1)}, bf16[264,256]{1,0:T(8,128)(2,1)S(1)}, bf16[256,256]{1,0:T(8,128)(2,1)S(1)}) custom-call(s32[2]{0:T(128)S(1)} %pad_add_fusion.place, bf16[256,1024]{1,0:T(8,128)(2,1)S(1)} %get-tuple-element.17.normed, bf16[1024,2048]{1,0:T(8,128)(2,1)S(1)} %copy-done.1, ...), custom_call_target="tpu_custom_call" | custom-call | flops 536870912 | tf_op jit(solution)/shard_map/pallas_call | solution.py:283
  20.6 4.5 %collective-permute-start.4 = (bf16[264,512]{1,0:T(8,128)(2,1)S(1)}, bf16[264,512]{1,0:T(8,128)(2,1)S(1)}, u32[]{:S(2)}, u32[]{:S(2)}) collective-permute-start(bf16[264,512]{1,0:T(8,128)(2,1)S(1)} %get-tuple-element.19.send_a), channel_id=1, source_target_pairs={{0,16},{1,17},{2,18},{3,19},{4,20},{5,21},{6,22},{7,23}} | collective-permute-start | bytes 811016 | tf_op jit(solution)/shard_map/ppermute | solution.py:340
  25.1 1.3 %collective-permute-start.5 = (bf16[264,256]{1,0:T(8,128)(2,1)S(1)}, bf16[264,256]{1,0:T(8,128)(2,1)S(1)}, u32[]{:S(2)}, u32[]{:S(2)}) collective-permute-start(bf16[264,256]{1,0:T(8,128)(2,1)S(1)} %get-tuple-element.22), channel_id=1, source_target_pairs={{24,8},{8,0},{25,9},{9,1},{26,10},{10,2},{27,11},{11,3},{28,12},{1... | collective-permute-start | bytes 405512 | tf_op jit(solution)/shard_map/ppermute | solution.py:341
  26.4 0.7 %collective-permute-start.6 = (bf16[264,256]{1,0:T(8,128)(2,1)S(1)}, bf16[264,256]{1,0:T(8,128)(2,1)S(1)}, u32[]{:S(2)}, u32[]{:S(2)}) collective-permute-start(bf16[264,256]{1,0:T(8,128)(2,1)S(1)} %get-tuple-element.20.send_c), channel_id=1, source_target_pairs={{16,8},{24,16},{17,9},{25,17},{18,10},{26,18},{19,11},{27,19},{20,... | collective-permute-start | bytes 405512 | tf_op jit(solution)/shard_map/ppermute | solution.py:342
  27.1 0.0 collective-permute-done.3.got_b
  27.1 0.0 copy-start.3
  27.1 1.7 %shard_map.67 = (f32[2,256,256]{2,1,0:T(8,128)S(1)}, bf16[256,512]{1,0:T(8,128)(2,1)S(1)}) custom-call(s32[2]{0:T(128)S(1)} %pad_add_fusion.place, bf16[264,512]{1,0:T(8,128)(2,1)S(1)} %collective-permute-done.3.got_b, bf16[256,256]{1,0:T(8,128)(2,1)S(1)} %get-tuple-element.18.query_near, bf16[264,512]{1,0:T(8,128)(2,1)S(1)} %get-tuple-element.19.send_a, ...), custom_call_target="tpu_custom_call" | custom-call | flops 469762048 | tf_op jit(solution)/shard_map/pallas_call | solution.py:283
  28.9 3.2 %collective-permute-done.5.got_f = bf16[264,256]{1,0:T(8,128)(2,1)S(1)} collective-permute-done((bf16[264,256]{1,0:T(8,128)(2,1)S(1)}, bf16[264,256]{1,0:T(8,128)(2,1)S(1)}, u32[]{:S(2)}, u32[]{:S(2)}) %collective-permute-start.5) | collective-permute-done | bytes 135200 | tf_op jit(solution)/shard_map/ppermute | solution.py:341
  32.0 0.0 collective-permute-done.6.got_c
  32.0 0.0 collective-permute-done.4.got_a
  32.1 1.2 %shard_map.69 = (bf16[256,256]{1,0:T(8,128)(2,1)S(1)}, bf16[256,256]{1,0:T(8,128)(2,1)S(1)}) custom-call(s32[2]{0:T(128)S(1)} %pad_add_fusion.place, bf16[264,512]{1,0:T(8,128)(2,1)S(1)} %collective-permute-done.3.got_b, f32[2,256,256]{2,1,0:T(8,128)S(1)} %get-tuple-element.21.mixed, bf16[264,512]{1,0:T(8,128)(2,1)S(1)} %get-tuple-element.19.send_a, ...), custom_call_target="tpu_custom_call" | custom-call | flops 256 | tf_op jit(solution)/shard_map/pallas_call | solution.py:283
  33.2 0.7 %collective-permute-start.7 = (bf16[256,256]{1,0:T(8,128)(2,1)S(1)}, bf16[256,256]{1,0:T(8,128)(2,1)S(1)}, u32[]{:S(2)}, u32[]{:S(2)}) collective-permute-start(bf16[256,256]{1,0:T(8,128)(2,1)S(1)} %get-tuple-element.23), channel_id=1, source_target_pairs={{8,24},{9,25},{10,26},{11,27},{12,28},{13,29},{14,30},{15,31}} | collective-permute-start | bytes 393224 | tf_op jit(solution)/shard_map/ppermute | solution.py:358
  33.9 7.1 %collective-permute-start.8 = (bf16[256,256]{1,0:T(8,128)(2,1)S(1)}, bf16[256,256]{1,0:T(8,128)(2,1)S(1)}, u32[]{:S(2)}, u32[]{:S(2)}) collective-permute-start(bf16[256,256]{1,0:T(8,128)(2,1)S(1)} %get-tuple-element.24), channel_id=1, source_target_pairs={{0,8},{8,16},{16,24},{1,9},{9,17},{17,25},{2,10},{10,18},{18,26},{... | collective-permute-start | bytes 393224 | tf_op jit(solution)/shard_map/ppermute | solution.py:359
  41.0 0.6 %shard_map.68.near_mixed = f32[256,256]{1,0:T(8,128)S(1)} custom-call(s32[2]{0:T(128)S(1)} %pad_add_fusion.place, bf16[256,256]{1,0:T(8,128)(2,1)S(1)} %get-tuple-element.18.query_near, f32[8,256]{1,0:T(8,128)S(1)} %shard_map.64.seg, bf16[264,512]{1,0:T(8,128)(2,1)S(1)} %collective-permute-done.4.got_a, f32[2,256,256]{2,1,0:T(8,128)S(1)} %get-tuple-element.21.mixed), custom_call_target="tpu_custom_call" | custom-call | flops 256 | tf_op jit(solution)/shard_map/pallas_call | solution.py:283
  41.6 0.0 collective-permute-done.7.got_e
  41.6 1.9 %collective-permute-done.8.got_d = bf16[256,256]{1,0:T(8,128)(2,1)S(1)} collective-permute-done((bf16[256,256]{1,0:T(8,128)(2,1)S(1)}, bf16[256,256]{1,0:T(8,128)(2,1)S(1)}, u32[]{:S(2)}, u32[]{:S(2)}) %collective-permute-start.8) | collective-permute-done | bytes 131104 | tf_op jit(solution)/shard_map/ppermute | solution.py:359
  43.5 0.0 copy-done.3
  43.5 2.0 %shard_map.70 = bf16[256,1024]{1,0:T(8,128)(2,1)} custom-call(s32[2]{0:T(128)S(1)} %pad_add_fusion.place, f32[2,256,256]{2,1,0:T(8,128)S(1)} %get-tuple-element.21.mixed, f32[256,256]{1,0:T(8,128)S(1)} %shard_map.68.near_mixed, bf16[256,256]{1,0:T(8,128)(2,1)S(1)} %collective-permute-done.7.got_e, bf16[256,256]{1,0:T(8,128)(2,1)S(1)} %collective-permute-done.8.got_d, ...), custom_call_target="tpu_custom_call" | custom-call | flops 268435456 | tf_op jit(solution)/shard_map/pallas_call | solution.py:283
Async XLA Ops:
  0.0 10.6 %copy-start.2 = (bf16[1024,1024]{1,0:T(8,128)(2,1)S(1)}, bf16[1024,1024]{1,0:T(8,128)(2,1)}, u32[]{:S(2)}) copy-start(bf16[1024,1024]{1,0:T(8,128)(2,1)} %w_in.1) | copy-start | bytes 6291460
  1.3 6.3 %collective-permute-start.2 = (bf16[256,256]{1,0:T(8,128)(2,1)S(1)}, bf16[256,256]{1,0:T(8,128)(2,1)S(1)}, u32[]{:S(2)}, u32[]{:S(2)}) collective-permute-start(bf16[256,256]{1,0:T(8,128)(2,1)S(1)} %get-tuple-element.27), channel_id=1, source_target_pairs={{0,6},{2,4},{4,2},{6,0},{1,7},{3,5},{5,3},{7,1},{8,14},{10,12},{12... | collective-permute-start | bytes 393224 | tf_op jit(solution)/shard_map/ppermute | solution.py:306
  3.7 6.9 %collective-permute-start.1 = (bf16[256,256]{1,0:T(8,128)(2,1)S(1)}, bf16[256,256]{1,0:T(8,128)(2,1)S(1)}, u32[]{:S(2)}, u32[]{:S(2)}) collective-permute-start(bf16[256,256]{1,0:T(8,128)(2,1)S(1)} %get-tuple-element.28), channel_id=1, source_target_pairs={{0,4},{2,6},{4,0},{6,2},{1,5},{3,7},{5,1},{7,3},{8,12},{10,14},{12... | collective-permute-start | bytes 393224 | tf_op jit(solution)/shard_map/ppermute | solution.py:306
  4.4 6.2 %collective-permute-start = (bf16[256,256]{1,0:T(8,128)(2,1)S(1)}, bf16[256,256]{1,0:T(8,128)(2,1)S(1)}, u32[]{:S(2)}, u32[]{:S(2)}) collective-permute-start(bf16[256,256]{1,0:T(8,128)(2,1)S(1)} %get-tuple-element.29), channel_id=1, source_target_pairs={{0,2},{2,0},{4,6},{6,4},{1,3},{3,1},{5,7},{7,5},{8,10},{10,8},{12,... | collective-permute-start | bytes 393224 | tf_op jit(solution)/shard_map/ppermute | solution.py:306
  4.4 0.7 %copy-start.4 = (s32[256]{0:T(256)S(1)}, s32[256]{0:T(256)}, u32[]{:S(2)}) copy-start(s32[256]{0:T(256)} %param.11) | copy-start | bytes 3076
  5.1 0.7 %copy-start.5 = (s32[1,4]{1,0:T(1,128)S(1)}, s32[1,4]{1,0:T(1,128)}, u32[]{:S(2)}) copy-start(s32[1,4]{1,0:T(1,128)} %counts.1) | copy-start | bytes 52
  10.6 2.2 %copy-start = (bf16[1024,2048]{1,0:T(8,128)(2,1)S(1)}, bf16[1024,2048]{1,0:T(8,128)(2,1)}, u32[]{:S(2)}) copy-start(bf16[1024,2048]{1,0:T(8,128)(2,1)} %w_joined.5) | copy-start | bytes 12582916
  12.8 6.3 %copy-start.1 = (bf16[1024,2048]{1,0:T(8,128)(2,1)S(1)}, bf16[1024,2048]{1,0:T(8,128)(2,1)}, u32[]{:S(2)}) copy-start(bf16[1024,2048]{1,0:T(8,128)(2,1)} %w_joined.5) | copy-start | bytes 12582916
  14.8 12.4 %collective-permute-start.3 = (bf16[264,512]{1,0:T(8,128)(2,1)S(1)}, bf16[264,512]{1,0:T(8,128)(2,1)S(1)}, u32[]{:S(2)}, u32[]{:S(2)}) collective-permute-start(bf16[264,512]{1,0:T(8,128)(2,1)S(1)} %get-tuple-element.16.send_b), channel_id=1, source_target_pairs={{0,8},{8,16},{16,24},{1,9},{9,17},{17,25},{2,10},{10,18},{18,26},{... | collective-permute-start | bytes 811016 | tf_op jit(solution)/shard_map/ppermute | solution.py:327
  20.6 11.4 %collective-permute-start.4 = (bf16[264,512]{1,0:T(8,128)(2,1)S(1)}, bf16[264,512]{1,0:T(8,128)(2,1)S(1)}, u32[]{:S(2)}, u32[]{:S(2)}) collective-permute-start(bf16[264,512]{1,0:T(8,128)(2,1)S(1)} %get-tuple-element.19.send_a), channel_id=1, source_target_pairs={{0,16},{1,17},{2,18},{3,19},{4,20},{5,21},{6,22},{7,23}} | collective-permute-start | bytes 811016 | tf_op jit(solution)/shard_map/ppermute | solution.py:340
  25.1 6.9 %collective-permute-start.5 = (bf16[264,256]{1,0:T(8,128)(2,1)S(1)}, bf16[264,256]{1,0:T(8,128)(2,1)S(1)}, u32[]{:S(2)}, u32[]{:S(2)}) collective-permute-start(bf16[264,256]{1,0:T(8,128)(2,1)S(1)} %get-tuple-element.22), channel_id=1, source_target_pairs={{24,8},{8,0},{25,9},{9,1},{26,10},{10,2},{27,11},{11,3},{28,12},{1... | collective-permute-start | bytes 405512 | tf_op jit(solution)/shard_map/ppermute | solution.py:341
  26.4 5.6 %collective-permute-start.6 = (bf16[264,256]{1,0:T(8,128)(2,1)S(1)}, bf16[264,256]{1,0:T(8,128)(2,1)S(1)}, u32[]{:S(2)}, u32[]{:S(2)}) collective-permute-start(bf16[264,256]{1,0:T(8,128)(2,1)S(1)} %get-tuple-element.20.send_c), channel_id=1, source_target_pairs={{16,8},{24,16},{17,9},{25,17},{18,10},{26,18},{19,11},{27,19},{20,... | collective-permute-start | bytes 405512 | tf_op jit(solution)/shard_map/ppermute | solution.py:342
  27.1 16.4 %copy-start.3 = (bf16[512,1024]{1,0:T(8,128)(2,1)S(1)}, bf16[512,1024]{1,0:T(8,128)(2,1)}, u32[]{:S(2)}) copy-start(bf16[512,1024]{1,0:T(8,128)(2,1)} %w_out.1) | copy-start | bytes 3145732
  33.2 8.4 %collective-permute-start.7 = (bf16[256,256]{1,0:T(8,128)(2,1)S(1)}, bf16[256,256]{1,0:T(8,128)(2,1)S(1)}, u32[]{:S(2)}, u32[]{:S(2)}) collective-permute-start(bf16[256,256]{1,0:T(8,128)(2,1)S(1)} %get-tuple-element.23), channel_id=1, source_target_pairs={{8,24},{9,25},{10,26},{11,27},{12,28},{13,29},{14,30},{15,31}} | collective-permute-start | bytes 393224 | tf_op jit(solution)/shard_map/ppermute | solution.py:358
  33.9 9.6 %collective-permute-start.8 = (bf16[256,256]{1,0:T(8,128)(2,1)S(1)}, bf16[256,256]{1,0:T(8,128)(2,1)S(1)}, u32[]{:S(2)}, u32[]{:S(2)}) collective-permute-start(bf16[256,256]{1,0:T(8,128)(2,1)S(1)} %get-tuple-element.24), channel_id=1, source_target_pairs={{0,8},{8,16},{16,24},{1,9},{9,17},{17,25},{2,10},{10,18},{18,26},{... | collective-permute-start | bytes 393224 | tf_op jit(solution)/shard_map/ppermute | solution.py:359

commit v3 on v2

--- a/solution.py
+++ b/solution.py
@@ -110,23 +110,22 @@
     seg_out[...] = jnp.broadcast_to((owner + owners * users[...]).astype(F32), seg_out.shape)
 
 
-def columns_of(w_joined, block, index, group):
-    start = pl.multiple_of(block * 2 * group + index * group, group)
-    return w_joined[:, pl.ds(start, group)]
-
-
 def put_seg(ref, seg):
     rows = seg.shape[1]
     for at in range(0, ref.shape[1], rows):
         ref[rows:, at : at + rows] = seg.astype(BF16)
 
 
+def silu_dot(normed, weight):
+    return silu_of(jnp.dot(normed[...], weight[...], preferred_element_type=F32)).astype(BF16)
+
+
 def project_first_kernel(
-    place, own, part1, part2, part3, w_in, w_joined, seg, hidden_out, normed, send_b
+    place, part3, part2, part1, own, w_in, w_key, w_value, seg, hidden_out, normed, send_b
 ):
-    batch_at, col_at = place[0], place[1]
+    col_at = place[1]
     rows, piece = own.shape
-    group = send_b.shape[1] // 2
+    group = w_key.shape[1]
     total = None
     for shift, part in enumerate((own, part1, part2, part3)):
         start = pl.multiple_of((col_at ^ shift) * piece, piece)
@@ -135,43 +134,24 @@
     hidden = total.astype(BF16)
     hidden_out[...] = hidden
     normed[...] = layer_norm(hidden.astype(F32)).astype(BF16)
-    far = 1 - batch_at % 2
-    for at, block in ((0, 3), (group, 1)):
-        joined = jnp.dot(
-            normed[...], columns_of(w_joined, block, far, group), preferred_element_type=F32
-        )
-        send_b[:rows, at : at + group] = silu_of(joined).astype(BF16)
+    send_b[:rows, :group] = silu_dot(normed, w_key)
+    send_b[:rows, group:] = silu_dot(normed, w_value)
     put_seg(send_b, seg[...])
 
 
-def project_rest_kernel(place, normed, w_joined, seg, send_a, send_c, send_f, query_near):
-    batch_at = place[0]
+def project_query_kernel(normed, w_far, w_near, seg, send_c, send_f):
     rows = normed.shape[0]
-    group = send_c.shape[1]
-    near = batch_at % 2
-
-    def joined(block, index):
-        return silu_of(
-            jnp.dot(
-                normed[...], columns_of(w_joined, block, index, group), preferred_element_type=F32
-            )
-        ).astype(BF16)
-
-    query_near[...] = joined(2, near)
-    send_c[:rows, :] = joined(2, 1 - near)
+    send_c[:rows, :] = silu_dot(normed, w_far)
     put_seg(send_c, seg[...])
+    send_f[:rows, :] = silu_dot(normed, w_near)
     put_seg(send_f, seg[...])
 
-    @pl.when(batch_at == 1)
-    def _():
-        send_f[:rows, :] = send_c[:rows, :]
-
-    @pl.when(batch_at != 1)
-    def _():
-        send_f[:rows, :] = query_near[...]
-
-    send_a[:rows, :group] = joined(3, near)
-    send_a[:rows, group:] = joined(1, near)
+
+def project_near_kernel(normed, w_key, w_value, seg, send_c, send_a):
+    rows = normed.shape[0]
+    group = w_key.shape[1]
+    send_a[:rows, :group] = silu_dot(normed, w_key)
+    send_a[:rows, group:] = silu_dot(normed, w_value)
     put_seg(send_a, seg[...])
 
 
@@ -193,82 +173,98 @@
                 weights, ref[:rows, group + lo : group + hi], preferred_element_type=F32
             )
             total = term if total is None else total + term
-        out[:, lo:hi] = total.astype(BF16)
-
-
-def add_near(query_near, column, key_value, mixed):
-    rows, group = query_near.shape
+        out[:, lo:hi] = total.astype(out.dtype)
+
+
+def add_near(send_f, column, key_value, mixed):
+    rows, group = mixed.shape
     allowed = column == seg_row_of(key_value, rows)
     for lo in range(0, group, HEAD_DIM):
         hi = lo + HEAD_DIM
-        weights = head_weights(query_near[:, lo:hi], key_value[:rows, lo:hi], allowed)
+        weights = head_weights(send_f[:rows, lo:hi], key_value[:rows, lo:hi], allowed)
         mixed[:, lo:hi] += jnp.dot(
             weights, key_value[:rows, group + lo : group + hi], preferred_element_type=F32
         )
 
 
-def own_kernel(
-    place, got_b, query_near, send_a, send_b, send_c, seg, normed, w_joined, mixed_out, gate_out
-):
-    rows, group = query_near.shape
+def own_kernel(send_f, send_a, send_b, send_c, seg, normed, w_gate, mixed_out, gate_out):
+    rows, group = mixed_out.shape[1:]
     seg_row = seg[0:1, :]
-    column = seg_column(seg_row)
-    allowed = (column == seg_row) & (
+    allowed = (seg_column(seg_row) == seg_row) & (
         lax.broadcasted_iota(jnp.int32, (rows, rows), 1)
         <= lax.broadcasted_iota(jnp.int32, (rows, rows), 0)
     )
-    for side, (query, key_value) in enumerate(((query_near, send_a), (send_c, send_b))):
+    for side, (query, key_value) in enumerate(((send_f, send_a), (send_c, send_b))):
         for lo in range(0, group, HEAD_DIM):
             hi = lo + HEAD_DIM
             weights = head_weights(query[:rows, lo:hi], key_value[:rows, lo:hi], allowed)
             mixed_out[side, :, lo:hi] = jnp.dot(
                 weights, key_value[:rows, group + lo : group + hi], preferred_element_type=F32
             )
+    gate_out[...] = silu_dot(normed, w_gate)
+
+
+def far_g_kernel(place, got_b, mixed, send_a, got_c, send_g, part_d):
+    @pl.when(place[0] == 0)
+    def _():
+        add_blocks(got_c, [send_a], send_g)
+
+    @pl.when(place[0] == 1)
+    def _():
+        add_blocks(got_c, [send_a, got_b], send_g)
+
+    @pl.when(place[0] == 2)
+    def _():
+        add_blocks(got_c, [send_a, got_b], part_d)
+
+    @pl.when(place[0] > 1)
+    def _():
+        send_g[...] = jnp.zeros_like(send_g)
+
+    @pl.when(place[0] != 2)
+    def _():
+        part_d[...] = jnp.zeros_like(part_d)
+
+
+def far_e_kernel(place, got_b, send_a, send_g, got_f, send_e):
+    @pl.when(place[0] == 1)
+    def _():
+        add_blocks(got_f, [send_a, got_b], send_e)
+
+    @pl.when(place[0] != 1)
+    def _():
+        send_e[...] = jnp.zeros_like(send_e)
+
+
+def far_last_kernel(place, part_d, got_c, send_e, got_a, send_d, total):
+    total[...] = part_d[...]
+
+    @pl.when(place[0] == 2)
+    def _():
+        rows = total.shape[0]
+        add_near(got_c, seg_column(seg_row_of(got_c, rows)), got_a, total)
+
+    send_d[...] = total[...].astype(BF16)
+
+
+def near_kernel(place, send_f, seg, got_a, got_b, got_e, got_g, mixed, near_out, far_out):
+    near_out[...] = mixed[0] + got_e[...].astype(F32)
+    far_out[...] = mixed[1] + got_g[...].astype(F32)
+    column = seg_column(seg[0:1, :])
 
     @pl.when(place[0] > 0)
     def _():
-        add_near(query_near, column, got_b, mixed_out.at[0])
-
-    for at in range(0, 2 * group, group):
-        block = jnp.dot(normed[...], w_joined[:, at : at + group], preferred_element_type=F32)
-        gate_out[:, at : at + group] = silu_of(block).astype(BF16)
-
-
-def far_kernel(place, got_b, mixed, send_a, got_f, got_c, got_a, send_e, send_d):
-    @pl.when(place[0] == 0)
-    def _():
-        add_blocks(got_f, [send_a], send_d)
-
-    @pl.when(place[0] == 1)
-    def _():
-        add_blocks(got_f, [send_a, got_b], send_e)
-        add_blocks(got_c, [send_a, got_b], send_d)
+        add_near(send_f, column, got_b, near_out)
 
     @pl.when(place[0] == 2)
     def _():
-        add_blocks(got_c, [send_a, got_b, got_a], send_d)
-
-    @pl.when(place[0] != 1)
-    def _():
-        send_e[...] = jnp.zeros_like(send_e)
-
-    @pl.when(place[0] > 2)
-    def _():
-        send_d[...] = jnp.zeros_like(send_d)
-
-
-def near_kernel(place, query_near, seg, got_a, mixed, near_out):
-    near_out[...] = mixed[0]
-
-    @pl.when(place[0] == 2)
-    def _():
-        add_near(query_near, seg_column(seg[0:1, :]), got_a, near_out)
-
-
-def finish_kernel(place, mixed, near_mixed, got_e, got_d, gate, hidden, w_out, out, whole):
+        add_near(send_f, column, got_a, near_out)
+
+
+def finish_kernel(place, far_mixed, near_mixed, got_d, gate, hidden, w_out, out, whole):
     near = place[0] % 2
-    whole[near] = near_mixed[...] + got_e[...].astype(F32)
-    whole[1 - near] = mixed[1] + got_d[...].astype(F32)
+    whole[near] = near_mixed[...]
+    whole[1 - near] = far_mixed[...] + got_d[...].astype(F32)
     both = jnp.concatenate([whole[0], whole[1]], axis=1)
     gated = (layer_norm(both) * gate[...].astype(F32)).astype(BF16)
     branch = jnp.dot(gated, w_out[...], preferred_element_type=F32).astype(BF16)
@@ -317,58 +313,82 @@
         (owner_counts, user_index.reshape(1, rows)),
         2 * rows * features * (features + 4 * width),
     )
+    near = batch_at % 2
+    far = 1 - near
+
+    def weight_of(block, index):
+        return lax.dynamic_slice_in_dim(joined_weight, block * width + index * group, group, 1)
+
     hidden, normed, send_b = call(
         project_first_kernel,
-        [SMEM] + [VMEM] * 7,
+        [SMEM] + [VMEM] * 8,
         [((rows, features), BF16), ((rows, features), BF16), ((tall, 2 * group), BF16)],
-        (place, *parts, input_weight, joined_weight, seg),
+        (place, *parts[::-1], input_weight, weight_of(3, far), weight_of(1, far), seg),
         2 * rows * features * (features + 2 * group),
     )
-    got_b = lax.ppermute(send_b, "batch", [(0, 1), (1, 2), (2, 3)])
-    send_a, send_c, send_f, query_near = call(
-        project_rest_kernel,
-        [SMEM] + [VMEM] * 3,
-        [
-            ((tall, 2 * group), BF16),
-            ((tall, group), BF16),
-            ((tall, group), BF16),
-            ((rows, group), BF16),
-        ],
-        (place, normed, joined_weight, seg),
-        2 * rows * features * 4 * group,
+    got_b = lax.ppermute(send_b, "batch", [(0, 1), (1, 2), (2, 3), (3, 0)])
+    send_c, send_f = call(
+        project_query_kernel,
+        [VMEM] * 4,
+        [((tall, group), BF16)] * 2,
+        (normed, weight_of(2, far), weight_of(2, near), seg),
+        2 * rows * features * 2 * group,
+    )
+    got_f = lax.ppermute(send_f, "batch", [(3, 1)])
+    got_c = lax.ppermute(send_c, "batch", [(1, 0), (2, 1), (3, 2)])
+    (send_a,) = call(
+        project_near_kernel,
+        [VMEM] * 5,
+        [((tall, 2 * group), BF16)],
+        (normed, weight_of(3, near), weight_of(1, near), seg, send_c),
+        2 * rows * features * 2 * group,
     )
     got_a = lax.ppermute(send_a, "batch", [(0, 2)])
-    got_f = lax.ppermute(send_f, "batch", [(3, 1), (1, 0)])
-    got_c = lax.ppermute(send_c, "batch", [(2, 1), (3, 2)])
     pair_flops = 4 * rows * rows * group
     mixed, gate = call(
         own_kernel,
-        [SMEM] + [VMEM] * 8,
+        [VMEM] * 7,
         [((2, rows, group), F32), ((rows, width), BF16)],
-        (place, got_b, query_near, send_a, send_b, send_c, seg, normed, joined_weight),
-        3 * pair_flops + 2 * rows * features * width,
-    )
-    send_e, send_d = call(
-        far_kernel,
-        [SMEM] + [VMEM] * 6,
-        [((rows, group), BF16)] * 2,
-        (place, got_b, mixed, send_a, got_f, got_c, got_a),
+        (send_f, send_a, send_b, send_c, seg, normed, joined_weight[:, :width]),
+        2 * pair_flops + 2 * rows * features * width,
+    )
+    send_g, part_d = call(
+        far_g_kernel,
+        [SMEM] + [VMEM] * 4,
+        [((rows, group), BF16), ((rows, group), F32)],
+        (place, got_b, mixed, send_a, got_c),
+        4 * rows * features * features,
+    )
+    got_g = lax.ppermute(send_g, "batch", [(0, 1), (1, 2)])
+    (send_e,) = call(
+        far_e_kernel,
+        [SMEM] + [VMEM] * 4,
+        [((rows, group), BF16)],
+        (place, got_b, send_a, send_g, got_f),
+        4 * rows * features * features,
+    )
+    got_e = lax.ppermute(send_e, "batch", [(1, 3)])
+    (send_d,) = call(
+        far_last_kernel,
+        [SMEM] + [VMEM] * 4,
+        [((rows, group), BF16)],
+        (place, part_d, got_c, send_e, got_a),
         rows,
-    )
-    got_e = lax.ppermute(send_e, "batch", [(1, 3)])
-    got_d = lax.ppermute(send_d, "batch", [(0, 1), (1, 2), (2, 3)])
-    (near_mixed,) = call(
+        [pltpu.VMEM((rows, group), F32)],
+    )
+    got_d = lax.ppermute(send_d, "batch", [(2, 3)])
+    near_mixed, far_mixed = call(
         near_kernel,
-        [SMEM] + [VMEM] * 4,
-        [((rows, group), F32)],
-        (place, query_near, seg, got_a, mixed),
+        [SMEM] + [VMEM] * 7,
+        [((rows, group), F32)] * 2,
+        (place, send_f, seg, got_a, got_b, got_e, got_g, mixed),
         rows,
     )
     (out,) = call(
         finish_kernel,
-        [SMEM] + [VMEM] * 7,
+        [SMEM] + [VMEM] * 6,
         [((rows, features), BF16)],
-        (place, mixed, near_mixed, got_e, got_d, gate, hidden, output_weight),
+        (place, far_mixed, near_mixed, got_d, gate, hidden, output_weight),
         2 * rows * width * features,
         [pltpu.VMEM((2, rows, group), F32)],
     )

time: 45.9 us -> 38.1 us (0.83)
  the two profiles are of different devices: /device:TPU:0 before, /device:TPU:24 now
where the time goes in v3:
time: 38.1 us; the launch traced here: 37.9 us
  starting transfers between devices  12.1 us (32%)
  waiting for transfers between devices  11.6 us (30%)
  Pallas kernels  9.34 us (25%)
  local copies, waits for them, and re-layouts  4.55 us (12%)
    pallas_call x10, Pallas kernels, call(): pl.pallas_call(kernel, out_shape=[jax.ShapeDtypeStruct(shape, dtype) for...  9.34 us
    ppermute x1, waiting for transfers between devices, chain_plan(): got_e = lax.ppermute(send_e, 'batch', [(1, 3)])  6.75 us
    ppermute x3, waiting for transfers between devices, chain_plan(): lax.ppermute(piece(shift), 'col', [(i, i ^ shift) for i in range(cols)])  4 us
    ppermute x1, starting transfers between devices, chain_plan(): got_c = lax.ppermute(send_c, 'batch', [(1, 0), (2, 1), (3, 2)])  3.92 us
    ppermute x1, starting transfers between devices, chain_plan(): got_f = lax.ppermute(send_f, 'batch', [(3, 1)])  2.24 us
    dynamic_slice x1, local copies, waits for them, and re-layouts, weight_of(): lax.dynamic_slice_in_dim(joined_weight, block * width + index * group, gr...  2.08 us
    ppermute x3, starting transfers between devices, chain_plan(): lax.ppermute(piece(shift), 'col', [(i, i ^ shift) for i in range(cols)])  1.93 us
    slice x1, local copies, waits for them, and re-layouts, chain_plan(): joined_weight[:, :width]  1.3 us
  transfers between devices with their start and end apart: 10, of which 5 were waited for; matrix products, arithmetic and copies ran while one was open for 9% of the time, Pallas kernels for 14%

profile of v3, /device:TPU:24, one launch (start us, length us, event | category | flops | bytes accessed | tf_op | source)
XLA Modules:
  0.0 37.9 jit_solution(8316727008445404514)
XLA Ops:
  0.0 0.0 copy-start.2
  0.0 0.0 copy-start.3
  0.0 1.2 %dynamic-slice_bitcast_fusion = (bf16[256,256]{1,0:T(8,128)(2,1)S(1)}, bf16[256,256]{1,0:T(8,128)(2,1)S(1)}, bf16[256,256]{1,0:T(8,128)(2,1)S(1)}, bf16[256,256]{1,0:T(8,128)(2,1)S(1)}) fusion(bf16[4,256,256]{2,1,0:T(8,128)(2,1)} %bitcast.13, s32[]{:T(128)S(6)} %select_n.41, s32[]{:T(128)S(6)} %select_n.40, s32[]{:T(128)S(6)} %select_n.39, s32[]{:T(128)S(6)} %select_n.38), kind=kLoop, calls=%fused_computation | loop fusion | bytes 1048592 | tf_op jit(solution)/shard_map/jit(dynamic_index_in_dim)/squeeze | solution.py:299
  1.2 1.0 %collective-permute-start = (bf16[256,256]{1,0:T(8,128)(2,1)S(1)}, bf16[256,256]{1,0:T(8,128)(2,1)S(1)}, u32[]{:S(2)}, u32[]{:S(2)}) collective-permute-start(bf16[256,256]{1,0:T(8,128)(2,1)S(1)} %get-tuple-element.36), channel_id=1, source_target_pairs={{0,6},{2,4},{4,2},{6,0},{1,7},{3,5},{5,3},{7,1},{8,14},{10,12},{12... | collective-permute-start | bytes 393224 | tf_op jit(solution)/shard_map/ppermute | solution.py:302
  2.2 0.6 %collective-permute-start.1 = (bf16[256,256]{1,0:T(8,128)(2,1)S(1)}, bf16[256,256]{1,0:T(8,128)(2,1)S(1)}, u32[]{:S(2)}, u32[]{:S(2)}) collective-permute-start(bf16[256,256]{1,0:T(8,128)(2,1)S(1)} %get-tuple-element.35), channel_id=1, source_target_pairs={{0,4},{2,6},{4,0},{6,2},{1,5},{3,7},{5,1},{7,3},{8,12},{10,14},{12... | collective-permute-start | bytes 393224 | tf_op jit(solution)/shard_map/ppermute | solution.py:302
  2.8 0.3 collective-permute-start.2
  3.1 2.1 %constant_dynamic-slice_fusion = (bf16[1024,256]{1,0:T(8,128)(2,1)S(1)}, bf16[1024,256]{1,0:T(8,128)(2,1)S(1)}, bf16[1024,256]{1,0:T(8,128)(2,1)S(1)}, bf16[1024...) fusion(bf16[1024,2048]{1,0:T(8,128)(2,1)} %param.8, s32[]{:T(128)S(6)} %select_n.48, ...), kind=kLoop, calls=%fused_computation.4 | loop fusion | bytes 6291480 | tf_op jit(solution)/shard_map/dynamic_slice | solution.py:320
  5.2 0.0 copy-start
  5.2 0.0 copy-done.2
  5.2 0.0 copy-done.3
  5.2 0.6 %shard_map.64.seg = f32[8,256]{1,0:T(8,128)S(1)} custom-call(s32[1,4]{1,0:T(1,128)S(1)} %copy-done.3, s32[1,256]{1,0:T(1,128)S(1)} %bitcast.12), custom_call_target="tpu_custom_call" | custom-call | flops 1610612736 | tf_op jit(solution)/shard_map/pallas_call | solution.py:279
  5.8 0.1 pad_add_fusion.place
  5.8 1.1 %collective-permute-done.part3 = bf16[256,256]{1,0:T(8,128)(2,1)S(1)} collective-permute-done((bf16[256,256]{1,0:T(8,128)(2,1)S(1)}, bf16[256,256]{1,0:T(8,128)(2,1)S(1)}, u32[]{:S(2)}, u32[]{:S(2)}) %collective-permute-start) | collective-permute-done | bytes 131104 | tf_op jit(solution)/shard_map/ppermute | solution.py:302
  7.0 2.9 %collective-permute-done.1.part2 = bf16[256,256]{1,0:T(8,128)(2,1)S(1)} collective-permute-done((bf16[256,256]{1,0:T(8,128)(2,1)S(1)}, bf16[256,256]{1,0:T(8,128)(2,1)S(1)}, u32[]{:S(2)}, u32[]{:S(2)}) %collective-permute-start.1) | collective-permute-done | bytes 131104 | tf_op jit(solution)/shard_map/ppermute | solution.py:302
  9.8 0.0 collective-permute-done.2.part1
  9.8 0.0 copy-done
  9.8 1.9 %shard_map.65 = (bf16[256,1024]{1,0:T(8,128)(2,1)S(1)}, bf16[256,1024]{1,0:T(8,128)(2,1)S(1)}, bf16[264,512]{1,0:T(8,128)(2,1)S(1)}) custom-call(s32[2]{0:T(128)S(1)} %pad_add_fusion.place, bf16[256,256]{1,0:T(8,128)(2,1)S(1)} %collective-permute-done.part3, bf16[256,256]{1,0:T(8,128)(2,1)S(1)} %collective-permute-done.1.part2, ...), custom_call_target="tpu_custom_call" | custom-call | flops 805306368 | tf_op jit(solution)/shard_map/pallas_call | solution.py:279
  11.7 0.1 collective-permute-start.4
  11.8 0.5 %shard_map.66 = (bf16[264,256]{1,0:T(8,128)(2,1)S(1)}, bf16[264,256]{1,0:T(8,128)(2,1)S(1)}) custom-call(bf16[256,1024]{1,0:T(8,128)(2,1)S(1)} %get-tuple-element.16.normed, bf16[1024,256]{1,0:T(8,128)(2,1)S(1)} %get-tuple-element.30.w_far, bf16[1024,256]{1,0:T(8,128)(2,1)S(1)} %get-tuple-element.29.w_near, f32[8,256]{1,0:T(8,128)S(1)} %shard_map.64.seg), custom_call_target="tpu_custom_call" | custom-call | flops 268435456 | tf_op jit(solution)/shard_map/pallas_call | solution.py:279
  12.3 3.9 %collective-permute-start.5 = (bf16[264,256]{1,0:T(8,128)(2,1)S(1)}, bf16[264,256]{1,0:T(8,128)(2,1)S(1)}, u32[]{:S(2)}, u32[]{:S(2)}) collective-permute-start(bf16[264,256]{1,0:T(8,128)(2,1)S(1)} %get-tuple-element.18.send_c), channel_id=1, source_target_pairs={{8,0},{16,8},{24,16},{9,1},{17,9},{25,17},{10,2},{18,10},{26,18},{... | collective-permute-start | bytes 405512 | tf_op jit(solution)/shard_map/ppermute | solution.py:338
  16.2 0.5 %shard_map.67.send_a = bf16[264,512]{1,0:T(8,128)(2,1)S(1)} custom-call(bf16[256,1024]{1,0:T(8,128)(2,1)S(1)} %get-tuple-element.16.normed, bf16[1024,256]{1,0:T(8,128)(2,1)S(1)} %get-tuple-element.28.w_key, bf16[1024,256]{1,0:T(8,128)(2,1)S(1)} %get-tuple-element.27.w_value, f32[8,256]{1,0:T(8,128)S(1)} %shard_map.64.seg, ...), custom_call_target="tpu_custom_call" | custom-call | flops 268435456 | tf_op jit(solution)/shard_map/pallas_call | solution.py:279
  16.7 0.7 %collective-permute-start.3 = (bf16[264,512]{1,0:T(8,128)(2,1)S(1)}, bf16[264,512]{1,0:T(8,128)(2,1)S(1)}, u32[]{:S(2)}, u32[]{:S(2)}) collective-permute-start(bf16[264,512]{1,0:T(8,128)(2,1)S(1)} %shard_map.67.send_a), channel_id=1, source_target_pairs={{0,16},{1,17},{2,18},{3,19},{4,20},{5,21},{6,22},{7,23}} | collective-permute-start | bytes 811016 | tf_op jit(solution)/shard_map/ppermute | solution.py:346
  17.4 1.3 %slice.3.w_gate = bf16[1024,512]{1,0:T(8,128)(2,1)S(1)} slice(bf16[1024,2048]{1,0:T(8,128)(2,1)} %param.8), slice={[0:1024], [0:512]} | slice | bytes 2097152 | tf_op jit(solution)/shard_map/slice | solution.py:352
  18.7 2.2 %collective-permute-start.6 = (bf16[264,256]{1,0:T(8,128)(2,1)S(1)}, bf16[264,256]{1,0:T(8,128)(2,1)S(1)}, u32[]{:S(2)}, u32[]{:S(2)}) collective-permute-start(bf16[264,256]{1,0:T(8,128)(2,1)S(1)} %get-tuple-element.17.send_f), channel_id=1, source_target_pairs={{24,8},{25,9},{26,10},{27,11},{28,12},{29,13},{30,14},{31,15}} | collective-permute-start | bytes 405512 | tf_op jit(solution)/shard_map/ppermute | solution.py:337
  20.9 1.0 %shard_map.68 = (f32[2,256,256]{2,1,0:T(8,128)S(1)}, bf16[256,512]{1,0:T(8,128)(2,1)S(1)}) custom-call(bf16[264,256]{1,0:T(8,128)(2,1)S(1)} %get-tuple-element.17.send_f, bf16[264,512]{1,0:T(8,128)(2,1)S(1)} %shard_map.67.send_a, bf16[264,512]{1,0:T(8,128)(2,1)S(1)} %get-tuple-element.19.send_b, bf16[264,256]{1,0:T(8,128)(2,1)S(1)} %get-tuple-element.18.send_c, ...), custom_call_target="tpu_custom_call" | custom-call | flops 402653184 | tf_op jit(solution)/shard_map/pallas_call | solution.py:279
  21.9 0.0 collective-permute-done.5.got_c
  22.0 0.0 collective-permute-done.4.got_b
  22.0 0.0 copy-start.1
  22.0 0.6 %shard_map.69 = (bf16[256,256]{1,0:T(8,128)(2,1)S(1)}, f32[256,256]{1,0:T(8,128)S(1)}) custom-call(s32[2]{0:T(128)S(1)} %pad_add_fusion.place, bf16[264,512]{1,0:T(8,128)(2,1)S(1)} %collective-permute-done.4.got_b, f32[2,256,256]{2,1,0:T(8,128)S(1)} %get-tuple-element.20.mixed, bf16[264,512]{1,0:T(8,128)(2,1)S(1)} %shard_map.67.send_a, ...), custom_call_target="tpu_custom_call" | custom-call | flops 1073741824 | tf_op jit(solution)/shard_map/pallas_call | solution.py:279
  22.6 0.7 %collective-permute-start.8 = (bf16[256,256]{1,0:T(8,128)(2,1)S(1)}, bf16[256,256]{1,0:T(8,128)(2,1)S(1)}, u32[]{:S(2)}, u32[]{:S(2)}) collective-permute-start(bf16[256,256]{1,0:T(8,128)(2,1)S(1)} %get-tuple-element.21.send_g), channel_id=1, source_target_pairs={{0,8},{8,16},{1,9},{9,17},{2,10},{10,18},{3,11},{11,19},{4,12},{12... | collective-permute-start | bytes 393224 | tf_op jit(solution)/shard_map/ppermute | solution.py:362
  23.3 0.6 %collective-permute-done.6.got_f = bf16[264,256]{1,0:T(8,128)(2,1)S(1)} collective-permute-done((bf16[264,256]{1,0:T(8,128)(2,1)S(1)}, bf16[264,256]{1,0:T(8,128)(2,1)S(1)}, u32[]{:S(2)}, u32[]{:S(2)}) %collective-permute-start.6) | collective-permute-done | bytes 135200 | tf_op jit(solution)/shard_map/ppermute | solution.py:337
  23.9 0.6 %shard_map.70.send_e = bf16[256,256]{1,0:T(8,128)(2,1)S(1)} custom-call(s32[2]{0:T(128)S(1)} %pad_add_fusion.place, bf16[264,512]{1,0:T(8,128)(2,1)S(1)} %collective-permute-done.4.got_b, bf16[264,512]{1,0:T(8,128)(2,1)S(1)} %shard_map.67.send_a, bf16[256,256]{1,0:T(8,128)(2,1)S(1)} %get-tuple-element.21.send_g, ...), custom_call_target="tpu_custom_call" | custom-call | flops 1073741824 | tf_op jit(solution)/shard_map/pallas_call | solution.py:279
  24.5 1.3 %collective-permute-start.7 = (bf16[256,256]{1,0:T(8,128)(2,1)S(1)}, bf16[256,256]{1,0:T(8,128)(2,1)S(1)}, u32[]{:S(2)}, u32[]{:S(2)}) collective-permute-start(bf16[256,256]{1,0:T(8,128)(2,1)S(1)} %shard_map.70.send_e), channel_id=1, source_target_pairs={{8,24},{9,25},{10,26},{11,27},{12,28},{13,29},{14,30},{15,31}} | collective-permute-start | bytes 393224 | tf_op jit(solution)/shard_map/ppermute | solution.py:370
  25.8 0.0 collective-permute-done.3.got_a
  25.8 0.6 %shard_map.72 = bf16[256,256]{1,0:T(8,128)(2,1)S(1)} custom-call(s32[2]{0:T(128)S(1)} %pad_add_fusion.place, f32[256,256]{1,0:T(8,128)S(1)} %get-tuple-element.24.part_d, bf16[264,256]{1,0:T(8,128)(2,1)S(1)} %collective-permute-done.5.got_c, bf16[256,256]{1,0:T(8,128)(2,1)S(1)} %shard_map.70.send_e, bf16[264,512]{1,0:T(8,128)(2,1)S(1)} %collective-permute-done.3.got_a), custom_call_target="tpu_custom_call" | custom-call | flops 256 | tf_op jit(solution)/shard_map/pallas_call | solution.py:279
  26.4 1.3 %collective-permute-start.9 = (bf16[256,256]{1,0:T(8,128)(2,1)S(1)}, bf16[256,256]{1,0:T(8,128)(2,1)S(1)}, u32[]{:S(2)}, u32[]{:S(2)}) collective-permute-start(bf16[256,256]{1,0:T(8,128)(2,1)S(1)} %shard_map.72), channel_id=1, source_target_pairs={{16,24},{17,25},{18,26},{19,27},{20,28},{21,29},{22,30},{23,31}} | collective-permute-start | bytes 393224 | tf_op jit(solution)/shard_map/ppermute | solution.py:379
  27.7 6.8 %collective-permute-done.7.got_e = bf16[256,256]{1,0:T(8,128)(2,1)S(1)} collective-permute-done((bf16[256,256]{1,0:T(8,128)(2,1)S(1)}, bf16[256,256]{1,0:T(8,128)(2,1)S(1)}, u32[]{:S(2)}, u32[]{:S(2)}) %collective-permute-start.7) | collective-permute-done | bytes 131104 | tf_op jit(solution)/shard_map/ppermute | solution.py:370
  34.4 0.0 collective-permute-done.8.got_g
  34.4 1.2 %shard_map.71 = (f32[256,256]{1,0:T(8,128)S(1)}, f32[256,256]{1,0:T(8,128)S(1)}) custom-call(s32[2]{0:T(128)S(1)} %pad_add_fusion.place, bf16[264,256]{1,0:T(8,128)(2,1)S(1)} %get-tuple-element.17.send_f, f32[8,256]{1,0:T(8,128)S(1)} %shard_map.64.seg, bf16[264,512]{1,0:T(8,128)(2,1)S(1)} %collective-permute-done.3.got_a, ...), custom_call_target="tpu_custom_call" | custom-call | flops 256 | tf_op jit(solution)/shard_map/pallas_call | solution.py:279
  35.6 0.2 collective-permute-done.9.got_d
  35.8 0.0 copy-done.1
  35.8 2.0 %shard_map.73 = bf16[256,1024]{1,0:T(8,128)(2,1)} custom-call(s32[2]{0:T(128)S(1)} %pad_add_fusion.place, f32[256,256]{1,0:T(8,128)S(1)} %get-tuple-element.22.far_mixed, f32[256,256]{1,0:T(8,128)S(1)} %get-tuple-element.23.near_mixed, bf16[256,256]{1,0:T(8,128)(2,1)S(1)} %collective-permute-done.9.got_d, bf16[256,512]{1,0:T(8,128)(2,1)S(1)} %get-tuple-element.25.gate, ...), custom_call_target="tpu_custom_call" | custom-call | flops 268435456 | tf_op jit(solution)/shard_map/pallas_call | solution.py:279
Async XLA Ops:
  0.0 5.2 %copy-start.2 = (s32[256]{0:T(256)S(1)}, s32[256]{0:T(256)}, u32[]{:S(2)}) copy-start(s32[256]{0:T(256)} %param.11) | copy-start | bytes 3076
  0.0 5.2 %copy-start.3 = (s32[1,4]{1,0:T(1,128)S(1)}, s32[1,4]{1,0:T(1,128)}, u32[]{:S(2)}) copy-start(s32[1,4]{1,0:T(1,128)} %counts.1) | copy-start | bytes 52
  1.2 5.8 %collective-permute-start = (bf16[256,256]{1,0:T(8,128)(2,1)S(1)}, bf16[256,256]{1,0:T(8,128)(2,1)S(1)}, u32[]{:S(2)}, u32[]{:S(2)}) collective-permute-start(bf16[256,256]{1,0:T(8,128)(2,1)S(1)} %get-tuple-element.36), channel_id=1, source_target_pairs={{0,6},{2,4},{4,2},{6,0},{1,7},{3,5},{5,3},{7,1},{8,14},{10,12},{12... | collective-permute-start | bytes 393224 | tf_op jit(solution)/shard_map/ppermute | solution.py:302
  2.2 7.7 %collective-permute-start.1 = (bf16[256,256]{1,0:T(8,128)(2,1)S(1)}, bf16[256,256]{1,0:T(8,128)(2,1)S(1)}, u32[]{:S(2)}, u32[]{:S(2)}) collective-permute-start(bf16[256,256]{1,0:T(8,128)(2,1)S(1)} %get-tuple-element.35), channel_id=1, source_target_pairs={{0,4},{2,6},{4,0},{6,2},{1,5},{3,7},{5,1},{7,3},{8,12},{10,14},{12... | collective-permute-start | bytes 393224 | tf_op jit(solution)/shard_map/ppermute | solution.py:302
  2.8 7.0 %collective-permute-start.2 = (bf16[256,256]{1,0:T(8,128)(2,1)S(1)}, bf16[256,256]{1,0:T(8,128)(2,1)S(1)}, u32[]{:S(2)}, u32[]{:S(2)}) collective-permute-start(bf16[256,256]{1,0:T(8,128)(2,1)S(1)} %get-tuple-element.34), channel_id=1, source_target_pairs={{0,2},{2,0},{4,6},{6,4},{1,3},{3,1},{5,7},{7,5},{8,10},{10,8},{12,... | collective-permute-start | bytes 393224 | tf_op jit(solution)/shard_map/ppermute | solution.py:302
  5.2 4.7 %copy-start = (bf16[1024,1024]{1,0:T(8,128)(2,1)S(1)}, bf16[1024,1024]{1,0:T(8,128)(2,1)}, u32[]{:S(2)}) copy-start(bf16[1024,1024]{1,0:T(8,128)(2,1)} %w_in.1) | copy-start | bytes 6291460
  11.7 10.2 %collective-permute-start.4 = (bf16[264,512]{1,0:T(8,128)(2,1)S(1)}, bf16[264,512]{1,0:T(8,128)(2,1)S(1)}, u32[]{:S(2)}, u32[]{:S(2)}) collective-permute-start(bf16[264,512]{1,0:T(8,128)(2,1)S(1)} %get-tuple-element.19.send_b), channel_id=1, source_target_pairs={{0,8},{8,16},{16,24},{24,0},{1,9},{9,17},{17,25},{25,1},{2,10},{10... | collective-permute-start | bytes 811016 | tf_op jit(solution)/shard_map/ppermute | solution.py:329
  12.3 9.7 %collective-permute-start.5 = (bf16[264,256]{1,0:T(8,128)(2,1)S(1)}, bf16[264,256]{1,0:T(8,128)(2,1)S(1)}, u32[]{:S(2)}, u32[]{:S(2)}) collective-permute-start(bf16[264,256]{1,0:T(8,128)(2,1)S(1)} %get-tuple-element.18.send_c), channel_id=1, source_target_pairs={{8,0},{16,8},{24,16},{9,1},{17,9},{25,17},{10,2},{18,10},{26,18},{... | collective-permute-start | bytes 405512 | tf_op jit(solution)/shard_map/ppermute | solution.py:338
  16.7 9.1 %collective-permute-start.3 = (bf16[264,512]{1,0:T(8,128)(2,1)S(1)}, bf16[264,512]{1,0:T(8,128)(2,1)S(1)}, u32[]{:S(2)}, u32[]{:S(2)}) collective-permute-start(bf16[264,512]{1,0:T(8,128)(2,1)S(1)} %shard_map.67.send_a), channel_id=1, source_target_pairs={{0,16},{1,17},{2,18},{3,19},{4,20},{5,21},{6,22},{7,23}} | collective-permute-start | bytes 811016 | tf_op jit(solution)/shard_map/ppermute | solution.py:346
  18.7 5.2 %collective-permute-start.6 = (bf16[264,256]{1,0:T(8,128)(2,1)S(1)}, bf16[264,256]{1,0:T(8,128)(2,1)S(1)}, u32[]{:S(2)}, u32[]{:S(2)}) collective-permute-start(bf16[264,256]{1,0:T(8,128)(2,1)S(1)} %get-tuple-element.17.send_f), channel_id=1, source_target_pairs={{24,8},{25,9},{26,10},{27,11},{28,12},{29,13},{30,14},{31,15}} | collective-permute-start | bytes 405512 | tf_op jit(solution)/shard_map/ppermute | solution.py:337
  22.0 13.9 %copy-start.1 = (bf16[512,1024]{1,0:T(8,128)(2,1)S(1)}, bf16[512,1024]{1,0:T(8,128)(2,1)}, u32[]{:S(2)}) copy-start(bf16[512,1024]{1,0:T(8,128)(2,1)} %w_out.1) | copy-start | bytes 3145732
  22.6 11.8 %collective-permute-start.8 = (bf16[256,256]{1,0:T(8,128)(2,1)S(1)}, bf16[256,256]{1,0:T(8,128)(2,1)S(1)}, u32[]{:S(2)}, u32[]{:S(2)}) collective-permute-start(bf16[256,256]{1,0:T(8,128)(2,1)S(1)} %get-tuple-element.21.send_g), channel_id=1, source_target_pairs={{0,8},{8,16},{1,9},{9,17},{2,10},{10,18},{3,11},{11,19},{4,12},{12... | collective-permute-start | bytes 393224 | tf_op jit(solution)/shard_map/ppermute | solution.py:362
  24.5 9.9 %collective-permute-start.7 = (bf16[256,256]{1,0:T(8,128)(2,1)S(1)}, bf16[256,256]{1,0:T(8,128)(2,1)S(1)}, u32[]{:S(2)}, u32[]{:S(2)}) collective-permute-start(bf16[256,256]{1,0:T(8,128)(2,1)S(1)} %shard_map.70.send_e), channel_id=1, source_target_pairs={{8,24},{9,25},{10,26},{11,27},{12,28},{13,29},{14,30},{15,31}} | collective-permute-start | bytes 393224 | tf_op jit(solution)/shard_map/ppermute | solution.py:370
  26.4 9.5 %collective-permute-start.9 = (bf16[256,256]{1,0:T(8,128)(2,1)S(1)}, bf16[256,256]{1,0:T(8,128)(2,1)S(1)}, u32[]{:S(2)}, u32[]{:S(2)}) collective-permute-start(bf16[256,256]{1,0:T(8,128)(2,1)S(1)} %shard_map.72), channel_id=1, source_target_pairs={{16,24},{17,25},{18,26},{19,27},{20,28},{21,29},{22,30},{23,31}} | collective-permute-start | bytes 393224 | tf_op jit(solution)/shard_map/ppermute | solution.py:379

commit v4 on v3

--- a/solution.py
+++ b/solution.py
@@ -139,15 +139,14 @@
     put_seg(send_b, seg[...])
 
 
-def project_query_kernel(normed, w_far, w_near, seg, send_c, send_f):
+def project_query_kernel(normed, w_far, w_sent, seg, send_a, send_c, send_f):
     rows = normed.shape[0]
-    send_c[:rows, :] = silu_dot(normed, w_far)
-    put_seg(send_c, seg[...])
-    send_f[:rows, :] = silu_dot(normed, w_near)
-    put_seg(send_f, seg[...])
-
-
-def project_near_kernel(normed, w_key, w_value, seg, send_c, send_a):
+    for weight, ref in ((w_far, send_c), (w_sent, send_f)):
+        ref[:rows, :] = silu_dot(normed, weight)
+        put_seg(ref, seg[...])
+
+
+def project_near_kernel(normed, w_key, w_value, seg, send_a):
     rows = normed.shape[0]
     group = w_key.shape[1]
     send_a[:rows, :group] = silu_dot(normed, w_key)
@@ -176,99 +175,105 @@
         out[:, lo:hi] = total.astype(out.dtype)
 
 
-def add_near(send_f, column, key_value, mixed):
+def add_near(query, column, key_value, mixed):
     rows, group = mixed.shape
     allowed = column == seg_row_of(key_value, rows)
     for lo in range(0, group, HEAD_DIM):
         hi = lo + HEAD_DIM
-        weights = head_weights(send_f[:rows, lo:hi], key_value[:rows, lo:hi], allowed)
+        weights = head_weights(query[:rows, lo:hi], key_value[:rows, lo:hi], allowed)
         mixed[:, lo:hi] += jnp.dot(
             weights, key_value[:rows, group + lo : group + hi], preferred_element_type=F32
         )
 
 
-def own_kernel(send_f, send_a, send_b, send_c, seg, normed, w_gate, mixed_out, gate_out):
+def own_kernel(
+    send_a, send_b, send_c, seg, normed, w_query, w_near, w_far, mixed_out, query_near, gate_out
+):
     rows, group = mixed_out.shape[1:]
     seg_row = seg[0:1, :]
     allowed = (seg_column(seg_row) == seg_row) & (
         lax.broadcasted_iota(jnp.int32, (rows, rows), 1)
         <= lax.broadcasted_iota(jnp.int32, (rows, rows), 0)
     )
-    for side, (query, key_value) in enumerate(((send_f, send_a), (send_c, send_b))):
+    query_near[...] = silu_dot(normed, w_query)
+    for side, (query, key_value) in enumerate(((query_near, send_a), (send_c, send_b))):
         for lo in range(0, group, HEAD_DIM):
             hi = lo + HEAD_DIM
             weights = head_weights(query[:rows, lo:hi], key_value[:rows, lo:hi], allowed)
             mixed_out[side, :, lo:hi] = jnp.dot(
                 weights, key_value[:rows, group + lo : group + hi], preferred_element_type=F32
             )
-    gate_out[...] = silu_dot(normed, w_gate)
-
-
-def far_g_kernel(place, got_b, mixed, send_a, got_c, send_g, part_d):
+    gate_out[0] = silu_dot(normed, w_near)
+    gate_out[1] = silu_dot(normed, w_far)
+
+
+def far_g_kernel(place, got_b, send_e, send_a, got_c, send_g):
+    @pl.when(place[0] == 1)
+    def _():
+        add_blocks(got_c, [send_a, got_b], send_g)
+
+    @pl.when(place[0] != 1)
+    def _():
+        send_g[...] = jnp.zeros_like(send_g)
+
+
+def far_e_kernel(place, got_b, send_a, mixed, got_f, send_e):
     @pl.when(place[0] == 0)
     def _():
-        add_blocks(got_c, [send_a], send_g)
+        add_blocks(got_f, [send_a], send_e)
 
     @pl.when(place[0] == 1)
     def _():
-        add_blocks(got_c, [send_a, got_b], send_g)
-
+        add_blocks(got_f, [send_a, got_b], send_e)
+
+    @pl.when(place[0] > 1)
+    def _():
+        send_e[...] = jnp.zeros_like(send_e)
+
+
+def far_d_kernel(place, got_b, send_a, got_h, got_a, send_d):
     @pl.when(place[0] == 2)
     def _():
-        add_blocks(got_c, [send_a, got_b], part_d)
-
-    @pl.when(place[0] > 1)
-    def _():
-        send_g[...] = jnp.zeros_like(send_g)
+        add_blocks(got_h, [send_a, got_b, got_a], send_d)
 
     @pl.when(place[0] != 2)
     def _():
-        part_d[...] = jnp.zeros_like(part_d)
-
-
-def far_e_kernel(place, got_b, send_a, send_g, got_f, send_e):
-    @pl.when(place[0] == 1)
-    def _():
-        add_blocks(got_f, [send_a, got_b], send_e)
-
-    @pl.when(place[0] != 1)
-    def _():
-        send_e[...] = jnp.zeros_like(send_e)
-
-
-def far_last_kernel(place, part_d, got_c, send_e, got_a, send_d, total):
-    total[...] = part_d[...]
+        send_d[...] = jnp.zeros_like(send_d)
+
+
+def near_kernel(place, query_near, seg, got_a, got_b, mixed, near_out):
+    near_out[...] = mixed[0]
+    column = seg_column(seg[0:1, :])
+
+    @pl.when(place[0] > 0)
+    def _():
+        add_near(query_near, column, got_b, near_out)
 
     @pl.when(place[0] == 2)
     def _():
-        rows = total.shape[0]
-        add_near(got_c, seg_column(seg_row_of(got_c, rows)), got_a, total)
-
-    send_d[...] = total[...].astype(BF16)
-
-
-def near_kernel(place, send_f, seg, got_a, got_b, got_e, got_g, mixed, near_out, far_out):
-    near_out[...] = mixed[0] + got_e[...].astype(F32)
-    far_out[...] = mixed[1] + got_g[...].astype(F32)
-    column = seg_column(seg[0:1, :])
-
-    @pl.when(place[0] > 0)
-    def _():
-        add_near(send_f, column, got_b, near_out)
-
-    @pl.when(place[0] == 2)
-    def _():
-        add_near(send_f, column, got_a, near_out)
-
-
-def finish_kernel(place, far_mixed, near_mixed, got_d, gate, hidden, w_out, out, whole):
+        add_near(query_near, column, got_a, near_out)
+
+
+def finish_kernel(place, near_mixed, mixed, got_d, got_eg, gate, hidden, w_out, out):
     near = place[0] % 2
-    whole[near] = near_mixed[...]
-    whole[1 - near] = far_mixed[...] + got_d[...].astype(F32)
-    both = jnp.concatenate([whole[0], whole[1]], axis=1)
-    gated = (layer_norm(both) * gate[...].astype(F32)).astype(BF16)
-    branch = jnp.dot(gated, w_out[...], preferred_element_type=F32).astype(BF16)
-    out[...] = (hidden[...].astype(F32) + branch.astype(F32)).astype(BF16)
+    last = place[0] == place[2]
+    got = got_eg[...].astype(F32)
+    group = near_mixed.shape[1]
+    sides = (
+        near_mixed[...] + jnp.where(last, got, 0.0),
+        mixed[1] + got_d[...].astype(F32) + jnp.where(last, 0.0, got),
+    )
+    total = sum(jnp.sum(side, axis=-1, keepdims=True) for side in sides)
+    sides = [side - total / (2 * group) for side in sides]
+    total = sum(jnp.sum(side * side, axis=-1, keepdims=True) for side in sides)
+    scale = lax.rsqrt(total / (2 * group) + eps_norm)
+    branch = None
+    for index, (which, side) in enumerate(zip((near, 1 - near), sides)):
+        gated = (side * scale * gate[index].astype(F32)).astype(BF16)
+        start = pl.multiple_of(which * group, group)
+        term = jnp.dot(gated, w_out[pl.ds(start, group), :], preferred_element_type=F32)
+        branch = term if branch is None else branch + term
+    out[...] = (hidden[...].astype(F32) + branch.astype(BF16).astype(F32)).astype(BF16)
 
 
 VMEM = pl.BlockSpec(memory_space=pltpu.VMEM)
@@ -291,7 +296,7 @@
     cols = lax.axis_size("col")
     batch_at = lax.axis_index("batch").astype(jnp.int32)
     col_at = lax.axis_index("col").astype(jnp.int32)
-    place = jnp.stack([batch_at, col_at])
+    place = jnp.stack([batch_at, col_at, jnp.int32(lax.axis_size("batch") - 1)])
     pieces = lookups.reshape(cols, lookups.shape[0] // cols, lookups.shape[1])
     rows = pieces.shape[1]
 
@@ -327,70 +332,72 @@
         2 * rows * features * (features + 2 * group),
     )
     got_b = lax.ppermute(send_b, "batch", [(0, 1), (1, 2), (2, 3), (3, 0)])
+    (send_a,) = call(
+        project_near_kernel,
+        [VMEM] * 4,
+        [((tall, 2 * group), BF16)],
+        (normed, weight_of(3, near), weight_of(1, near), seg),
+        2 * rows * features * 2 * group,
+    )
+    got_a = lax.ppermute(send_a, "batch", [(0, 2)])
     send_c, send_f = call(
         project_query_kernel,
-        [VMEM] * 4,
+        [VMEM] * 5,
         [((tall, group), BF16)] * 2,
-        (normed, weight_of(2, far), weight_of(2, near), seg),
+        (normed, weight_of(2, far), weight_of(2, jnp.where(batch_at == 1, far, near)), seg, send_a),
         2 * rows * features * 2 * group,
     )
-    got_f = lax.ppermute(send_f, "batch", [(3, 1)])
-    got_c = lax.ppermute(send_c, "batch", [(1, 0), (2, 1), (3, 2)])
-    (send_a,) = call(
-        project_near_kernel,
-        [VMEM] * 5,
-        [((tall, 2 * group), BF16)],
-        (normed, weight_of(3, near), weight_of(1, near), seg, send_c),
-        2 * rows * features * 2 * group,
-    )
-    got_a = lax.ppermute(send_a, "batch", [(0, 2)])
+    got_f = lax.ppermute(send_f, "batch", [(3, 1), (1, 0)])
+    got_c = lax.ppermute(send_c, "batch", [(2, 1)])
+    got_h = lax.ppermute(send_c, "batch", [(3, 2)])
     pair_flops = 4 * rows * rows * group
-    mixed, gate = call(
+    mixed, query_near, gate = call(
         own_kernel,
-        [VMEM] * 7,
-        [((2, rows, group), F32), ((rows, width), BF16)],
-        (send_f, send_a, send_b, send_c, seg, normed, joined_weight[:, :width]),
+        [VMEM] * 8,
+        [((2, rows, group), F32), ((rows, group), BF16), ((2, rows, group), BF16)],
+        (
+            send_a, send_b, send_c, seg, normed, weight_of(2, near), weight_of(0, near),
+            weight_of(0, far),
+        ),
         2 * pair_flops + 2 * rows * features * width,
     )
-    send_g, part_d = call(
-        far_g_kernel,
-        [SMEM] + [VMEM] * 4,
-        [((rows, group), BF16), ((rows, group), F32)],
-        (place, got_b, mixed, send_a, got_c),
-        4 * rows * features * features,
-    )
-    got_g = lax.ppermute(send_g, "batch", [(0, 1), (1, 2)])
     (send_e,) = call(
         far_e_kernel,
         [SMEM] + [VMEM] * 4,
         [((rows, group), BF16)],
-        (place, got_b, send_a, send_g, got_f),
-        4 * rows * features * features,
-    )
-    got_e = lax.ppermute(send_e, "batch", [(1, 3)])
-    (send_d,) = call(
-        far_last_kernel,
+        (place, got_b, send_a, mixed, got_f),
+        1 << 30,
+    )
+    got_e = lax.ppermute(send_e, "batch", [(1, 3), (0, 1)])
+    (send_g,) = call(
+        far_g_kernel,
         [SMEM] + [VMEM] * 4,
         [((rows, group), BF16)],
-        (place, part_d, got_c, send_e, got_a),
+        (place, got_b, send_e, send_a, got_c),
+        1 << 30,
+    )
+    got_g = lax.ppermute(send_g, "batch", [(1, 2)])
+    (send_d,) = call(
+        far_d_kernel,
+        [SMEM] + [VMEM] * 4,
+        [((rows, group), BF16)],
+        (place, got_b, send_a, got_h, got_a),
         rows,
-        [pltpu.VMEM((rows, group), F32)],
     )
     got_d = lax.ppermute(send_d, "batch", [(2, 3)])
-    near_mixed, far_mixed = call(
+    (near_mixed,) = call(
         near_kernel,
-        [SMEM] + [VMEM] * 7,
-        [((rows, group), F32)] * 2,
-        (place, send_f, seg, got_a, got_b, got_e, got_g, mixed),
+        [SMEM] + [VMEM] * 5,
+        [((rows, group), F32)],
+        (place, query_near, seg, got_a, got_b, mixed),
         rows,
     )
     (out,) = call(
         finish_kernel,
-        [SMEM] + [VMEM] * 6,
+        [SMEM] + [VMEM] * 7,
         [((rows, features), BF16)],
-        (place, far_mixed, near_mixed, got_d, gate, hidden, output_weight),
-        2 * rows * width * features,
-        [pltpu.VMEM((2, rows, group), F32)],
+        (place, near_mixed, mixed, got_d, got_e + got_g, gate, hidden, output_weight),
+        rows,
     )
     return out
 

time: 38.1 us -> 36.8 us (0.966)
  waiting for transfers between devices: 11.6 us -> 8 us
  starting transfers between devices: 12.1 us -> 14.7 us
  local copies, waits for them, and re-layouts: 4.55 us -> 3.85 us
    ppermute x4 -> x5, waiting for transfers between devices: 7.39 us -> 2.87 us  [the longest x1 2.85 us: chain_plan(): got_e = lax.ppermute(send_e, 'batch', [(1, 3), (0, 1)])]
    ppermute x4 -> x5, starting transfers between devices: 8.12 us -> 10.6 us  [the longest x1 4.17 us: chain_plan(): got_h = lax.ppermute(send_c, 'batch', [(3, 2)])]
    ppermute x1, waiting for transfers between devices: 0.24 us -> 2.11 us  [chain_plan(): got_d = lax.ppermute(send_d, 'batch', [(2, 3)])]
    slice x1 -> x0, local copies, waits for them, and re-layouts: 1.3 us -> none  [chain_plan(): joined_weight[:, :width]]
    ppermute x3, waiting for transfers between devices: 4 us -> 3.03 us  [chain_plan(): lax.ppermute(piece(shift), 'col', [(i, i ^ shift) for i in range(cols)])]
    dynamic_slice x1, local copies, waits for them, and re-layouts: 2.08 us -> 2.7 us  [weight_of(): lax.dynamic_slice_in_dim(joined_weight, block * width + index * group, gr...]
  transfers between devices with their start and end apart: 10 -> 11, of which waited for: 5 -> 4; matrix products, arithmetic and copies ran while one was open for 9% -> 8% of each run, Pallas kernels for 14% -> 15%
where the time goes in v4:
time: 36.8 us; the launch traced here: 36.4 us
  starting transfers between devices  14.7 us (40%)
  Pallas kernels  9.5 us (26%)
  waiting for transfers between devices  8 us (22%)
  local copies, waits for them, and re-layouts  3.85 us (10%)
    pallas_call x10, Pallas kernels, call(): pl.pallas_call(kernel, out_shape=[jax.ShapeDtypeStruct(shape, dtype) for...  9.5 us
    ppermute x1, starting transfers between devices, chain_plan(): got_h = lax.ppermute(send_c, 'batch', [(3, 2)])  4.17 us
    ppermute x1, starting transfers between devices, chain_plan(): got_f = lax.ppermute(send_f, 'batch', [(3, 1), (1, 0)])  3.67 us
    ppermute x3, waiting for transfers between devices, chain_plan(): lax.ppermute(piece(shift), 'col', [(i, i ^ shift) for i in range(cols)])  3.03 us
    ppermute x1, waiting for transfers between devices, chain_plan(): got_e = lax.ppermute(send_e, 'batch', [(1, 3), (0, 1)])  2.85 us
    dynamic_slice x1, local copies, waits for them, and re-layouts, weight_of(): lax.dynamic_slice_in_dim(joined_weight, block * width + index * group, gr...  2.7 us
    ppermute x1, waiting for transfers between devices, chain_plan(): got_d = lax.ppermute(send_d, 'batch', [(2, 3)])  2.11 us
    ppermute x3, starting transfers between devices, chain_plan(): lax.ppermute(piece(shift), 'col', [(i, i ^ shift) for i in range(cols)])  1.93 us
  transfers between devices with their start and end apart: 11, of which 4 were waited for; matrix products, arithmetic and copies ran while one was open for 8% of the time, Pallas kernels for 15%

profile of v4, /device:TPU:24, one launch (start us, length us, event | category | flops | bytes accessed | tf_op | source)
XLA Modules:
  0.0 36.4 jit_solution(15765860284930141943)
XLA Ops:
  0.0 1.1 %dynamic-slice_bitcast_fusion = (bf16[256,256]{1,0:T(8,128)(2,1)S(1)}, bf16[256,256]{1,0:T(8,128)(2,1)S(1)}, bf16[256,256]{1,0:T(8,128)(2,1)S(1)}, bf16[256,256]{1,0:T(8,128)(2,1)S(1)}) fusion(bf16[4,256,256]{2,1,0:T(8,128)(2,1)} %bitcast.13, s32[]{:T(128)S(6)} %select_n.53, s32[]{:T(128)S(6)} %select_n.52, s32[]{:T(128)S(6)} %select_n.51, s32[]{:T(128)S(6)} %select_n.50), kind=kLoop, calls=%fused_computation | loop fusion | bytes 1048592 | tf_op jit(solution)/shard_map/jit(dynamic_index_in_dim)/squeeze | solution.py:304
  1.1 0.1 collective-permute-start.2
  1.2 1.6 %collective-permute-start.1 = (bf16[256,256]{1,0:T(8,128)(2,1)S(1)}, bf16[256,256]{1,0:T(8,128)(2,1)S(1)}, u32[]{:S(2)}, u32[]{:S(2)}) collective-permute-start(bf16[256,256]{1,0:T(8,128)(2,1)S(1)} %get-tuple-element.32), channel_id=1, source_target_pairs={{0,4},{2,6},{4,0},{6,2},{1,5},{3,7},{5,1},{7,3},{8,12},{10,14},{12... | collective-permute-start | bytes 393224 | tf_op jit(solution)/shard_map/ppermute | solution.py:307
  2.8 0.3 collective-permute-start
  3.1 0.0 copy-start.2
  3.1 0.0 copy-start.3
  3.1 2.7 %constant_dynamic-slice_fusion = (bf16[1024,256]{1,0:T(8,128)(2,1)S(1)}, bf16[1024,256]{1,0:T(8,128)(2,1)S(1)}, bf16[1024,256]{1,0:T(8,128)(2,1)S(1)}, bf16[1024...) fusion(bf16[1024,2048]{1,0:T(8,128)(2,1)} %param.8, ...), kind=kLoop, calls=%fused_computation.4 | loop fusion | bytes 9437220 | tf_op jit(solution)/shard_map/dynamic_slice | solution.py:325
  5.8 0.0 copy-start
  5.8 0.0 copy-done.2
  5.8 0.0 copy-done.3
  5.8 0.6 %shard_map.64.seg = f32[8,256]{1,0:T(8,128)S(1)} custom-call(s32[1,4]{1,0:T(1,128)S(1)} %copy-done.3, s32[1,256]{1,0:T(1,128)S(1)} %bitcast.12), custom_call_target="tpu_custom_call" | custom-call | flops 1610612736 | tf_op jit(solution)/shard_map/pallas_call | solution.py:284
  6.4 0.1 pad_add_fusion.place
  6.5 0.0 collective-permute-done.2.part1
  6.5 1.1 %collective-permute-done.1.part2 = bf16[256,256]{1,0:T(8,128)(2,1)S(1)} collective-permute-done((bf16[256,256]{1,0:T(8,128)(2,1)S(1)}, bf16[256,256]{1,0:T(8,128)(2,1)S(1)}, u32[]{:S(2)}, u32[]{:S(2)}) %collective-permute-start.1) | collective-permute-done | bytes 131104 | tf_op jit(solution)/shard_map/ppermute | solution.py:307
  7.6 1.9 %collective-permute-done.part3 = bf16[256,256]{1,0:T(8,128)(2,1)S(1)} collective-permute-done((bf16[256,256]{1,0:T(8,128)(2,1)S(1)}, bf16[256,256]{1,0:T(8,128)(2,1)S(1)}, u32[]{:S(2)}, u32[]{:S(2)}) %collective-permute-start) | collective-permute-done | bytes 131104 | tf_op jit(solution)/shard_map/ppermute | solution.py:307
  9.5 0.0 copy-done
  9.5 1.9 %shard_map.65 = (bf16[256,1024]{1,0:T(8,128)(2,1)S(1)}, bf16[256,1024]{1,0:T(8,128)(2,1)S(1)}, bf16[264,512]{1,0:T(8,128)(2,1)S(1)}) custom-call(s32[3]{0:T(128)S(1)} %pad_add_fusion.place, bf16[256,256]{1,0:T(8,128)(2,1)S(1)} %collective-permute-done.part3, bf16[256,256]{1,0:T(8,128)(2,1)S(1)} %collective-permute-done.1.part2, ...), custom_call_target="tpu_custom_call" | custom-call | flops 805306368 | tf_op jit(solution)/shard_map/pallas_call | solution.py:284
  11.4 0.2 collective-permute-start.4
  11.6 0.5 %shard_map.66.send_a = bf16[264,512]{1,0:T(8,128)(2,1)S(1)} custom-call(bf16[256,1024]{1,0:T(8,128)(2,1)S(1)} %get-tuple-element.13.normed, bf16[1024,256]{1,0:T(8,128)(2,1)S(1)} %get-tuple-element.26.w_key, bf16[1024,256]{1,0:T(8,128)(2,1)S(1)} %get-tuple-element.25.w_value, f32[8,256]{1,0:T(8,128)S(1)} %shard_map.64.seg), custom_call_target="tpu_custom_call" | custom-call | flops 268435456 | tf_op jit(solution)/shard_map/pallas_call | solution.py:284
  12.1 0.5 %shard_map.67 = (bf16[264,256]{1,0:T(8,128)(2,1)S(1)}, bf16[264,256]{1,0:T(8,128)(2,1)S(1)}) custom-call(bf16[256,1024]{1,0:T(8,128)(2,1)S(1)} %get-tuple-element.13.normed, bf16[1024,256]{1,0:T(8,128)(2,1)S(1)} %get-tuple-element.24.w_far, bf16[1024,256]{1,0:T(8,128)(2,1)S(1)} %get-tuple-element.23.w_sent, f32[8,256]{1,0:T(8,128)S(1)} %shard_map.64.seg, ...), custom_call_target="tpu_custom_call" | custom-call | flops 268435456 | tf_op jit(solution)/shard_map/pallas_call | solution.py:284
  12.5 3.7 %collective-permute-start.7 = (bf16[264,256]{1,0:T(8,128)(2,1)S(1)}, bf16[264,256]{1,0:T(8,128)(2,1)S(1)}, u32[]{:S(2)}, u32[]{:S(2)}) collective-permute-start(bf16[264,256]{1,0:T(8,128)(2,1)S(1)} %get-tuple-element.18), channel_id=1, source_target_pairs={{24,8},{8,0},{25,9},{9,1},{26,10},{10,2},{27,11},{11,3},{28,12},{1... | collective-permute-start | bytes 405512 | tf_op jit(solution)/shard_map/ppermute | solution.py:350
  16.2 0.7 %collective-permute-start.3 = (bf16[264,512]{1,0:T(8,128)(2,1)S(1)}, bf16[264,512]{1,0:T(8,128)(2,1)S(1)}, u32[]{:S(2)}, u32[]{:S(2)}) collective-permute-start(bf16[264,512]{1,0:T(8,128)(2,1)S(1)} %shard_map.66.send_a), channel_id=1, source_target_pairs={{0,16},{1,17},{2,18},{3,19},{4,20},{5,21},{6,22},{7,23}} | collective-permute-start | bytes 811016 | tf_op jit(solution)/shard_map/ppermute | solution.py:342
  16.9 0.7 %collective-permute-start.9 = (bf16[264,256]{1,0:T(8,128)(2,1)S(1)}, bf16[264,256]{1,0:T(8,128)(2,1)S(1)}, u32[]{:S(2)}, u32[]{:S(2)}) collective-permute-start(bf16[264,256]{1,0:T(8,128)(2,1)S(1)} %get-tuple-element.15.send_c), channel_id=1, source_target_pairs={{16,8},{17,9},{18,10},{19,11},{20,12},{21,13},{22,14},{23,15}} | collective-permute-start | bytes 405512 | tf_op jit(solution)/shard_map/ppermute | solution.py:351
  17.6 4.2 %collective-permute-start.5 = (bf16[264,256]{1,0:T(8,128)(2,1)S(1)}, bf16[264,256]{1,0:T(8,128)(2,1)S(1)}, u32[]{:S(2)}, u32[]{:S(2)}) collective-permute-start(bf16[264,256]{1,0:T(8,128)(2,1)S(1)} %get-tuple-element.15.send_c), channel_id=1, source_target_pairs={{24,16},{25,17},{26,18},{27,19},{28,20},{29,21},{30,22},{31,23}} | collective-permute-start | bytes 405512 | tf_op jit(solution)/shard_map/ppermute | solution.py:352
  21.8 1.4 %shard_map.68 = (f32[2,256,256]{2,1,0:T(8,128)S(1)}, bf16[256,256]{1,0:T(8,128)(2,1)S(1)}, bf16[2,256,256]{2,1,0:T(8,128)(2,1)S(1)}) custom-call(bf16[264,512]{1,0:T(8,128)(2,1)S(1)} %shard_map.66.send_a, bf16[264,512]{1,0:T(8,128)(2,1)S(1)} %get-tuple-element.14.send_b, bf16[264,256]{1,0:T(8,128)(2,1)S(1)} %get-tuple-element.15.send_c, ...), custom_call_target="tpu_custom_call" | custom-call | flops 402653184 | tf_op jit(solution)/shard_map/pallas_call | solution.py:284
  23.1 0.0 collective-permute-done.7.got_f
  23.1 0.0 collective-permute-done.4.got_b
  23.1 0.6 %shard_map.71.send_e = bf16[256,256]{1,0:T(8,128)(2,1)S(1)} custom-call(s32[3]{0:T(128)S(1)} %pad_add_fusion.place, bf16[264,512]{1,0:T(8,128)(2,1)S(1)} %collective-permute-done.4.got_b, bf16[264,512]{1,0:T(8,128)(2,1)S(1)} %shard_map.66.send_a, f32[2,256,256]{2,1,0:T(8,128)S(1)} %get-tuple-element.17.mixed, bf16[264,256]{1,0:T(8,128)(2,1)S(1)} %collective-permute-done.7.got_f), custom_call_target="tpu_custom_call" | custom-call | flops 1073741824 | tf_op jit(solution)/shard_map/pallas_call | solution.py:284
  23.7 0.0 copy-start.1
  23.7 1.4 %collective-permute-start.8 = (bf16[256,256]{1,0:T(8,128)(2,1)S(1)}, bf16[256,256]{1,0:T(8,128)(2,1)S(1)}, u32[]{:S(2)}, u32[]{:S(2)}) collective-permute-start(bf16[256,256]{1,0:T(8,128)(2,1)S(1)} %shard_map.71.send_e), channel_id=1, source_target_pairs={{8,24},{0,8},{9,25},{1,9},{10,26},{2,10},{11,27},{3,11},{12,28},{4... | collective-permute-start | bytes 393224 | tf_op jit(solution)/shard_map/ppermute | solution.py:371
  25.2 0.0 collective-permute-done.9.got_c
  25.2 0.6 %shard_map.72 = bf16[256,256]{1,0:T(8,128)(2,1)S(1)} custom-call(s32[3]{0:T(128)S(1)} %pad_add_fusion.place, bf16[264,512]{1,0:T(8,128)(2,1)S(1)} %collective-permute-done.4.got_b, bf16[256,256]{1,0:T(8,128)(2,1)S(1)} %shard_map.71.send_e, bf16[264,512]{1,0:T(8,128)(2,1)S(1)} %shard_map.66.send_a, bf16[264,256]{1,0:T(8,128)(2,1)S(1)} %collective-permute-done.9.got_c), custom_call_target="tpu_custom_call" | custom-call | flops 1073741824 | tf_op jit(solution)/shard_map/pallas_call | solution.py:284
  25.7 0.7 %collective-permute-start.10 = (bf16[256,256]{1,0:T(8,128)(2,1)S(1)}, bf16[256,256]{1,0:T(8,128)(2,1)S(1)}, u32[]{:S(2)}, u32[]{:S(2)}) collective-permute-start(bf16[256,256]{1,0:T(8,128)(2,1)S(1)} %shard_map.72), channel_id=1, source_target_pairs={{8,16},{9,17},{10,18},{11,19},{12,20},{13,21},{14,22},{15,23}} | collective-permute-start | bytes 393224 | tf_op jit(solution)/shard_map/ppermute | solution.py:379
  26.4 0.0 collective-permute-done.5.got_h
  26.4 0.0 collective-permute-done.3.got_a
  26.4 0.6 %shard_map.70 = bf16[256,256]{1,0:T(8,128)(2,1)S(1)} custom-call(s32[3]{0:T(128)S(1)} %pad_add_fusion.place, bf16[264,512]{1,0:T(8,128)(2,1)S(1)} %collective-permute-done.4.got_b, bf16[264,512]{1,0:T(8,128)(2,1)S(1)} %shard_map.66.send_a, bf16[264,256]{1,0:T(8,128)(2,1)S(1)} %collective-permute-done.5.got_h, bf16[264,512]{1,0:T(8,128)(2,1)S(1)} %collective-permute-done.3.got_a), custom_call_target="tpu_custom_call" | custom-call | flops 256 | tf_op jit(solution)/shard_map/pallas_call | solution.py:284
  27.0 1.3 %collective-permute-start.6 = (bf16[256,256]{1,0:T(8,128)(2,1)S(1)}, bf16[256,256]{1,0:T(8,128)(2,1)S(1)}, u32[]{:S(2)}, u32[]{:S(2)}) collective-permute-start(bf16[256,256]{1,0:T(8,128)(2,1)S(1)} %shard_map.70), channel_id=1, source_target_pairs={{16,24},{17,25},{18,26},{19,27},{20,28},{21,29},{22,30},{23,31}} | collective-permute-start | bytes 393224 | tf_op jit(solution)/shard_map/ppermute | solution.py:387
  28.3 1.1 %shard_map.69.near_mixed = f32[256,256]{1,0:T(8,128)S(1)} custom-call(s32[3]{0:T(128)S(1)} %pad_add_fusion.place, bf16[256,256]{1,0:T(8,128)(2,1)S(1)} %get-tuple-element.16.query_near, f32[8,256]{1,0:T(8,128)S(1)} %shard_map.64.seg, bf16[264,512]{1,0:T(8,128)(2,1)S(1)} %collective-permute-done.3.got_a, bf16[264,512]{1,0:T(8,128)(2,1)S(1)} %collective-permute-done.4.got_b, ...), custom_call_target="tpu_custom_call" | custom-call | flops 256 | tf_op jit(solution)/shard_map/pallas_call | solution.py:284
  29.4 0.0 collective-permute-done.10
  29.4 2.9 %collective-permute-done.8 = bf16[256,256]{1,0:T(8,128)(2,1)S(1)} collective-permute-done((bf16[256,256]{1,0:T(8,128)(2,1)S(1)}, bf16[256,256]{1,0:T(8,128)(2,1)S(1)}, u32[]{:S(2)}, u32[]{:S(2)}) %collective-permute-start.8) | collective-permute-done | bytes 131104 | tf_op jit(solution)/shard_map/ppermute | solution.py:371
  32.3 2.1 %collective-permute-done.6.got_d = bf16[256,256]{1,0:T(8,128)(2,1)S(1)} collective-permute-done((bf16[256,256]{1,0:T(8,128)(2,1)S(1)}, bf16[256,256]{1,0:T(8,128)(2,1)S(1)}, u32[]{:S(2)}, u32[]{:S(2)}) %collective-permute-start.6) | collective-permute-done | bytes 131104 | tf_op jit(solution)/shard_map/ppermute | solution.py:387
  34.4 0.0 copy-done.1
  34.4 2.0 %shard_map.73 = bf16[256,1024]{1,0:T(8,128)(2,1)} custom-call(s32[3]{0:T(128)S(1)} %pad_add_fusion.place, f32[256,256]{1,0:T(8,128)S(1)} %shard_map.69.near_mixed, f32[2,256,256]{2,1,0:T(8,128)S(1)} %get-tuple-element.17.mixed, bf16[256,256]{1,0:T(8,128)(2,1)S(1)} %collective-permute-done.6.got_d, bf16[256,256]{1,0:T(8,128)(2,1)S(1)} %add.103.got_eg, ...), custom_call_target="tpu_custom_call" | custom-call | flops 256 | tf_op jit(solution)/shard_map/pallas_call | solution.py:284
  (1 shorter events, 0.0 us)
Async XLA Ops:
  1.1 5.3 %collective-permute-start.2 = (bf16[256,256]{1,0:T(8,128)(2,1)S(1)}, bf16[256,256]{1,0:T(8,128)(2,1)S(1)}, u32[]{:S(2)}, u32[]{:S(2)}) collective-permute-start(bf16[256,256]{1,0:T(8,128)(2,1)S(1)} %get-tuple-element.31), channel_id=1, source_target_pairs={{0,2},{2,0},{4,6},{6,4},{1,3},{3,1},{5,7},{7,5},{8,10},{10,8},{12,... | collective-permute-start | bytes 393224 | tf_op jit(solution)/shard_map/ppermute | solution.py:307
  1.2 6.4 %collective-permute-start.1 = (bf16[256,256]{1,0:T(8,128)(2,1)S(1)}, bf16[256,256]{1,0:T(8,128)(2,1)S(1)}, u32[]{:S(2)}, u32[]{:S(2)}) collective-permute-start(bf16[256,256]{1,0:T(8,128)(2,1)S(1)} %get-tuple-element.32), channel_id=1, source_target_pairs={{0,4},{2,6},{4,0},{6,2},{1,5},{3,7},{5,1},{7,3},{8,12},{10,14},{12... | collective-permute-start | bytes 393224 | tf_op jit(solution)/shard_map/ppermute | solution.py:307
  2.8 6.7 %collective-permute-start = (bf16[256,256]{1,0:T(8,128)(2,1)S(1)}, bf16[256,256]{1,0:T(8,128)(2,1)S(1)}, u32[]{:S(2)}, u32[]{:S(2)}) collective-permute-start(bf16[256,256]{1,0:T(8,128)(2,1)S(1)} %get-tuple-element.33), channel_id=1, source_target_pairs={{0,6},{2,4},{4,2},{6,0},{1,7},{3,5},{5,3},{7,1},{8,14},{10,12},{12... | collective-permute-start | bytes 393224 | tf_op jit(solution)/shard_map/ppermute | solution.py:307
  3.1 2.7 %copy-start.2 = (s32[256]{0:T(256)S(1)}, s32[256]{0:T(256)}, u32[]{:S(2)}) copy-start(s32[256]{0:T(256)} %param.11) | copy-start | bytes 3076
  3.1 2.7 %copy-start.3 = (s32[1,4]{1,0:T(1,128)S(1)}, s32[1,4]{1,0:T(1,128)}, u32[]{:S(2)}) copy-start(s32[1,4]{1,0:T(1,128)} %counts.1) | copy-start | bytes 52
  5.8 3.7 %copy-start = (bf16[1024,1024]{1,0:T(8,128)(2,1)S(1)}, bf16[1024,1024]{1,0:T(8,128)(2,1)}, u32[]{:S(2)}) copy-start(bf16[1024,1024]{1,0:T(8,128)(2,1)} %w_in.1) | copy-start | bytes 6291460
  11.4 11.7 %collective-permute-start.4 = (bf16[264,512]{1,0:T(8,128)(2,1)S(1)}, bf16[264,512]{1,0:T(8,128)(2,1)S(1)}, u32[]{:S(2)}, u32[]{:S(2)}) collective-permute-start(bf16[264,512]{1,0:T(8,128)(2,1)S(1)} %get-tuple-element.14.send_b), channel_id=1, source_target_pairs={{0,8},{8,16},{16,24},{24,0},{1,9},{9,17},{17,25},{25,1},{2,10},{10... | collective-permute-start | bytes 811016 | tf_op jit(solution)/shard_map/ppermute | solution.py:334
  12.5 10.6 %collective-permute-start.7 = (bf16[264,256]{1,0:T(8,128)(2,1)S(1)}, bf16[264,256]{1,0:T(8,128)(2,1)S(1)}, u32[]{:S(2)}, u32[]{:S(2)}) collective-permute-start(bf16[264,256]{1,0:T(8,128)(2,1)S(1)} %get-tuple-element.18), channel_id=1, source_target_pairs={{24,8},{8,0},{25,9},{9,1},{26,10},{10,2},{27,11},{11,3},{28,12},{1... | collective-permute-start | bytes 405512 | tf_op jit(solution)/shard_map/ppermute | solution.py:350
  16.2 10.2 %collective-permute-start.3 = (bf16[264,512]{1,0:T(8,128)(2,1)S(1)}, bf16[264,512]{1,0:T(8,128)(2,1)S(1)}, u32[]{:S(2)}, u32[]{:S(2)}) collective-permute-start(bf16[264,512]{1,0:T(8,128)(2,1)S(1)} %shard_map.66.send_a), channel_id=1, source_target_pairs={{0,16},{1,17},{2,18},{3,19},{4,20},{5,21},{6,22},{7,23}} | collective-permute-start | bytes 811016 | tf_op jit(solution)/shard_map/ppermute | solution.py:342
  16.9 8.3 %collective-permute-start.9 = (bf16[264,256]{1,0:T(8,128)(2,1)S(1)}, bf16[264,256]{1,0:T(8,128)(2,1)S(1)}, u32[]{:S(2)}, u32[]{:S(2)}) collective-permute-start(bf16[264,256]{1,0:T(8,128)(2,1)S(1)} %get-tuple-element.15.send_c), channel_id=1, source_target_pairs={{16,8},{17,9},{18,10},{19,11},{20,12},{21,13},{22,14},{23,15}} | collective-permute-start | bytes 405512 | tf_op jit(solution)/shard_map/ppermute | solution.py:351
  17.6 8.8 %collective-permute-start.5 = (bf16[264,256]{1,0:T(8,128)(2,1)S(1)}, bf16[264,256]{1,0:T(8,128)(2,1)S(1)}, u32[]{:S(2)}, u32[]{:S(2)}) collective-permute-start(bf16[264,256]{1,0:T(8,128)(2,1)S(1)} %get-tuple-element.15.send_c), channel_id=1, source_target_pairs={{24,16},{25,17},{26,18},{27,19},{28,20},{29,21},{30,22},{31,23}} | collective-permute-start | bytes 405512 | tf_op jit(solution)/shard_map/ppermute | solution.py:352
  23.7 10.7 %copy-start.1 = (bf16[512,1024]{1,0:T(8,128)(2,1)S(1)}, bf16[512,1024]{1,0:T(8,128)(2,1)}, u32[]{:S(2)}) copy-start(bf16[512,1024]{1,0:T(8,128)(2,1)} %w_out.1) | copy-start | bytes 3145732
  23.7 8.6 %collective-permute-start.8 = (bf16[256,256]{1,0:T(8,128)(2,1)S(1)}, bf16[256,256]{1,0:T(8,128)(2,1)S(1)}, u32[]{:S(2)}, u32[]{:S(2)}) collective-permute-start(bf16[256,256]{1,0:T(8,128)(2,1)S(1)} %shard_map.71.send_e), channel_id=1, source_target_pairs={{8,24},{0,8},{9,25},{1,9},{10,26},{2,10},{11,27},{3,11},{12,28},{4... | collective-permute-start | bytes 393224 | tf_op jit(solution)/shard_map/ppermute | solution.py:371
  25.7 3.7 %collective-permute-start.10 = (bf16[256,256]{1,0:T(8,128)(2,1)S(1)}, bf16[256,256]{1,0:T(8,128)(2,1)S(1)}, u32[]{:S(2)}, u32[]{:S(2)}) collective-permute-start(bf16[256,256]{1,0:T(8,128)(2,1)S(1)} %shard_map.72), channel_id=1, source_target_pairs={{8,16},{9,17},{10,18},{11,19},{12,20},{13,21},{14,22},{15,23}} | collective-permute-start | bytes 393224 | tf_op jit(solution)/shard_map/ppermute | solution.py:379
  27.0 7.4 %collective-permute-start.6 = (bf16[256,256]{1,0:T(8,128)(2,1)S(1)}, bf16[256,256]{1,0:T(8,128)(2,1)S(1)}, u32[]{:S(2)}, u32[]{:S(2)}) collective-permute-start(bf16[256,256]{1,0:T(8,128)(2,1)S(1)} %shard_map.70), channel_id=1, source_target_pairs={{16,24},{17,25},{18,26},{19,27},{20,28},{21,29},{22,30},{23,31}} | collective-permute-start | bytes 393224 | tf_op jit(solution)/shard_map/ppermute | solution.py:387

commit v5 on v4

--- a/solution.py
+++ b/solution.py
@@ -139,19 +139,29 @@
     put_seg(send_b, seg[...])
 
 
-def project_query_kernel(normed, w_far, w_sent, seg, send_a, send_c, send_f):
+def project_query_kernel(normed, w_far, w_sent, seg, send_c, send_f):
     rows = normed.shape[0]
     for weight, ref in ((w_far, send_c), (w_sent, send_f)):
         ref[:rows, :] = silu_dot(normed, weight)
         put_seg(ref, seg[...])
 
 
-def project_near_kernel(normed, w_key, w_value, seg, send_a):
+def project_near_kernel(
+    place, send_b, send_c, seg, normed, w_query, w_near, w_far, w_key, w_value,
+    send_a, mixed_out, query_near, gate_out,
+):
     rows = normed.shape[0]
     group = w_key.shape[1]
     send_a[:rows, :group] = silu_dot(normed, w_key)
     send_a[:rows, group:] = silu_dot(normed, w_value)
     put_seg(send_a, seg[...])
+
+    @pl.when(place[0] == 0)
+    def _():
+        attend_own(
+            send_a, send_b, send_c, seg, normed, (w_query, w_near, w_far),
+            mixed_out, query_near, gate_out,
+        )
 
 
 def seg_row_of(ref, rows):
@@ -186,10 +196,9 @@
         )
 
 
-def own_kernel(
-    send_a, send_b, send_c, seg, normed, w_query, w_near, w_far, mixed_out, query_near, gate_out
-):
+def attend_own(send_a, send_b, send_c, seg, normed, weights, mixed_out, query_near, gate_out):
     rows, group = mixed_out.shape[1:]
+    w_query, w_near, w_far = weights
     seg_row = seg[0:1, :]
     allowed = (seg_column(seg_row) == seg_row) & (
         lax.broadcasted_iota(jnp.int32, (rows, rows), 1)
@@ -207,6 +216,17 @@
     gate_out[1] = silu_dot(normed, w_far)
 
 
+def own_kernel(
+    place, send_a, send_b, send_c, seg, normed, w_query, w_near, w_far,
+    mixed_in, query_in, gate_in, mixed, query_near, gate,
+):
+    @pl.when((place[0] != 0) & (place[0] != place[2]))
+    def _():
+        attend_own(
+            send_a, send_b, send_c, seg, normed, (w_query, w_near, w_far), mixed, query_near, gate
+        )
+
+
 def far_g_kernel(place, got_b, send_e, send_a, got_c, send_g):
     @pl.when(place[0] == 1)
     def _():
@@ -241,26 +261,34 @@
         send_d[...] = jnp.zeros_like(send_d)
 
 
-def near_kernel(place, query_near, seg, got_a, got_b, mixed, near_out):
-    near_out[...] = mixed[0]
+def near_kernel(
+    place, got_a, got_b, send_a, send_b, send_c, seg, normed, w_query, w_near, w_far,
+    mixed_in, query_in, gate_in, mixed, query_near, gate,
+):
     column = seg_column(seg[0:1, :])
 
+    @pl.when(place[0] == place[2])
+    def _():
+        attend_own(
+            send_a, send_b, send_c, seg, normed, (w_query, w_near, w_far), mixed, query_near, gate
+        )
+
     @pl.when(place[0] > 0)
     def _():
-        add_near(query_near, column, got_b, near_out)
+        add_near(query_near, column, got_b, mixed.at[0])
 
     @pl.when(place[0] == 2)
     def _():
-        add_near(query_near, column, got_a, near_out)
-
-
-def finish_kernel(place, near_mixed, mixed, got_d, got_eg, gate, hidden, w_out, out):
+        add_near(query_near, column, got_a, mixed.at[0])
+
+
+def finish_kernel(place, mixed, got_d, got_eg, gate, hidden, w_out, out):
     near = place[0] % 2
     last = place[0] == place[2]
     got = got_eg[...].astype(F32)
-    group = near_mixed.shape[1]
+    group = mixed.shape[2]
     sides = (
-        near_mixed[...] + jnp.where(last, got, 0.0),
+        mixed[0] + jnp.where(last, got, 0.0),
         mixed[1] + got_d[...].astype(F32) + jnp.where(last, 0.0, got),
     )
     total = sum(jnp.sum(side, axis=-1, keepdims=True) for side in sides)
@@ -280,13 +308,14 @@
 SMEM = pl.BlockSpec(memory_space=pltpu.SMEM)
 
 
-def call(kernel, in_specs, outs, operands, flops, scratch=(), limit=32 << 20):
+def call(kernel, in_specs, outs, operands, flops, scratch=(), limit=32 << 20, aliases=()):
     return pl.pallas_call(
         kernel,
         out_shape=[jax.ShapeDtypeStruct(shape, dtype) for shape, dtype in outs],
         in_specs=in_specs,
         out_specs=[VMEM] * len(outs),
         scratch_shapes=list(scratch),
+        input_output_aliases=dict(aliases),
         compiler_params=pltpu.CompilerParams(vmem_limit_bytes=limit),
         cost_estimate=pl.CostEstimate(flops=flops, bytes_accessed=0, transcendentals=0),
     )(*operands)
@@ -300,11 +329,16 @@
     pieces = lookups.reshape(cols, lookups.shape[0] // cols, lookups.shape[1])
     rows = pieces.shape[1]
 
-    def piece(shift):
-        return lax.dynamic_index_in_dim(pieces, col_at ^ shift, 0, keepdims=False)
-
-    parts = [piece(0)] + [
-        lax.ppermute(piece(shift), "col", [(i, i ^ shift) for i in range(cols)])
+    def piece(source, shift):
+        return lax.dynamic_index_in_dim(source, col_at ^ shift, 0, keepdims=False)
+
+    def exchange(block, shift):
+        return lax.ppermute(block, "col", [(i, i ^ shift) for i in range(cols)])
+
+    across = piece(pieces, 2)
+    pieces, across = lax.optimization_barrier((pieces, across))
+    parts = [piece(pieces, 0)] + [
+        exchange(across if shift == 2 else piece(pieces, shift), shift)
         for shift in range(1, cols)
     ]
     width = HEADS * HEAD_DIM
@@ -332,35 +366,38 @@
         2 * rows * features * (features + 2 * group),
     )
     got_b = lax.ppermute(send_b, "batch", [(0, 1), (1, 2), (2, 3), (3, 0)])
-    (send_a,) = call(
-        project_near_kernel,
-        [VMEM] * 4,
-        [((tall, 2 * group), BF16)],
-        (normed, weight_of(3, near), weight_of(1, near), seg),
-        2 * rows * features * 2 * group,
-    )
-    got_a = lax.ppermute(send_a, "batch", [(0, 2)])
     send_c, send_f = call(
         project_query_kernel,
-        [VMEM] * 5,
+        [VMEM] * 4,
         [((tall, group), BF16)] * 2,
-        (normed, weight_of(2, far), weight_of(2, jnp.where(batch_at == 1, far, near)), seg, send_a),
+        (normed, weight_of(2, far), weight_of(2, jnp.where(batch_at == 1, far, near)), seg),
         2 * rows * features * 2 * group,
     )
     got_f = lax.ppermute(send_f, "batch", [(3, 1), (1, 0)])
+    own_inputs = (
+        send_b, send_c, seg, normed, weight_of(2, near), weight_of(0, near), weight_of(0, far),
+    )
+    own_outs = [((2, rows, group), F32), ((rows, group), BF16), ((2, rows, group), BF16)]
+    send_a, *own = call(
+        project_near_kernel,
+        [SMEM] + [VMEM] * 9,
+        [((tall, 2 * group), BF16)] + own_outs,
+        (place, *own_inputs, weight_of(3, near), weight_of(1, near)),
+        2 * rows * features * 2 * group,
+    )
+    got_a = lax.ppermute(send_a, "batch", [(0, 2)])
     got_c = lax.ppermute(send_c, "batch", [(2, 1)])
     got_h = lax.ppermute(send_c, "batch", [(3, 2)])
     pair_flops = 4 * rows * rows * group
-    mixed, query_near, gate = call(
+    own = call(
         own_kernel,
-        [VMEM] * 8,
-        [((2, rows, group), F32), ((rows, group), BF16), ((2, rows, group), BF16)],
-        (
-            send_a, send_b, send_c, seg, normed, weight_of(2, near), weight_of(0, near),
-            weight_of(0, far),
-        ),
+        [SMEM] + [VMEM] * 11,
+        own_outs,
+        (place, send_a, *own_inputs, *own),
         2 * pair_flops + 2 * rows * features * width,
-    )
+        aliases={9: 0, 10: 1, 11: 2},
+    )
+    mixed = own[0]
     (send_e,) = call(
         far_e_kernel,
         [SMEM] + [VMEM] * 4,
@@ -385,18 +422,19 @@
         rows,
     )
     got_d = lax.ppermute(send_d, "batch", [(2, 3)])
-    (near_mixed,) = call(
+    mixed, _, gate = call(
         near_kernel,
-        [SMEM] + [VMEM] * 5,
-        [((rows, group), F32)],
-        (place, query_near, seg, got_a, got_b, mixed),
+        [SMEM] + [VMEM] * 13,
+        own_outs,
+        (place, got_a, got_b, send_a, *own_inputs, *own),
         rows,
+        aliases={11: 0, 12: 1, 13: 2},
     )
     (out,) = call(
         finish_kernel,
-        [SMEM] + [VMEM] * 7,
+        [SMEM] + [VMEM] * 6,
         [((rows, features), BF16)],
-        (place, near_mixed, mixed, got_d, got_e + got_g, gate, hidden, output_weight),
+        (place, mixed, got_d, got_e + got_g, gate, hidden, output_weight),
         rows,
     )
     return out

time: 36.8 us -> 36 us (0.978)
  waiting for transfers between devices: 8 us -> 4.85 us
  Pallas kernels: 9.5 us -> 10.7 us
  local copies, waits for them, and re-layouts: 3.85 us -> 4.69 us
  starting transfers between devices: 14.7 us -> 15.1 us
    ppermute x3, waiting for transfers between devices: 3.03 us -> 1.26 us  [exchange(): return lax.ppermute(block, 'col', [(i, i ^ shift) for i in range(cols)])]
    ppermute x1, waiting for transfers between devices: 2.85 us -> 1.28 us  [chain_plan(): got_e = lax.ppermute(send_e, 'batch', [(1, 3), (0, 1)])]
    pallas_call x10, Pallas kernels: 9.5 us -> 10.7 us  [call(): pl.pallas_call(kernel, out_shape=[jax.ShapeDtypeStruct(shape, dtype) for...]
    squeeze x1 -> x2, local copies, waits for them, and re-layouts: 1.13 us -> 1.97 us  [piece(): return lax.dynamic_index_in_dim(source, col_at ^ shift, 0, keepdims=False)]
  transfers between devices with their start and end apart: 11 -> 11, of which waited for: 4 -> 3; matrix products, arithmetic and copies ran while one was open for 8% -> 11% of each run, Pallas kernels for 15% -> 19%
where the time goes in v5:
time: 36 us; the launch traced here: 35.7 us
  starting transfers between devices  15.1 us (42%)
  Pallas kernels  10.7 us (30%)
  waiting for transfers between devices  4.85 us (13%)
  local copies, waits for them, and re-layouts  4.69 us (13%)
    pallas_call x10, Pallas kernels, call(): pl.pallas_call(kernel, out_shape=[jax.ShapeDtypeStruct(shape, dtype) for...  10.7 us
    ppermute x1, starting transfers between devices, chain_plan(): got_h = lax.ppermute(send_c, 'batch', [(3, 2)])  4.16 us
    ppermute x1, starting transfers between devices, chain_plan(): got_f = lax.ppermute(send_f, 'batch', [(3, 1), (1, 0)])  3.6 us
    dynamic_slice x1, local copies, waits for them, and re-layouts, weight_of(): lax.dynamic_slice_in_dim(joined_weight, block * width + index * group, gr...  2.7 us
    ppermute x1, waiting for transfers between devices, chain_plan(): got_d = lax.ppermute(send_d, 'batch', [(2, 3)])  2.29 us
    ppermute x3, starting transfers between devices, exchange(): return lax.ppermute(block, 'col', [(i, i ^ shift) for i in range(cols)])  2.28 us
    squeeze x2, local copies, waits for them, and re-layouts, piece(): return lax.dynamic_index_in_dim(source, col_at ^ shift, 0, keepdims=False)  1.97 us
    ppermute x1, starting transfers between devices, chain_plan(): got_e = lax.ppermute(send_e, 'batch', [(1, 3), (0, 1)])  1.42 us
  transfers between devices with their start and end apart: 11, of which 3 were waited for; matrix products, arithmetic and copies ran while one was open for 11% of the time, Pallas kernels for 19%

profile of v5, /device:TPU:24, one launch (start us, length us, event | category | flops | bytes accessed | tf_op | source)
XLA Modules:
  0.0 35.7 jit_solution(12713647426531458990)
XLA Ops:
  0.0 0.9 %dynamic-slice_bitcast_fusion.3 = bf16[256,256]{1,0:T(8,128)(2,1)S(1)} fusion(bf16[4,256,256]{2,1,0:T(8,128)(2,1)} %bitcast.13, s32[]{:T(128)S(6)} %select_n.50), kind=kLoop, calls=%fused_computation.3 | loop fusion | bytes 262148 | tf_op jit(solution)/shard_map/jit(dynamic_index_in_dim)/squeeze | solution.py:333
  0.9 1.6 %collective-permute-start.1 = (bf16[256,256]{1,0:T(8,128)(2,1)S(1)}, bf16[256,256]{1,0:T(8,128)(2,1)S(1)}, u32[]{:S(2)}, u32[]{:S(2)}) collective-permute-start(bf16[256,256]{1,0:T(8,128)(2,1)S(1)} %dynamic-slice_bitcast_fusion.3), channel_id=1, source_target_pairs={{0,4},{2,6},{4,0},{6,2},{1,5},{3,7},{5,1},{7,3},{8,12},{10,14},{12... | collective-permute-start | bytes 393224 | tf_op jit(solution)/shard_map/ppermute | solution.py:336
  2.5 1.1 %dynamic-slice_bitcast_fusion = (bf16[256,256]{1,0:T(8,128)(2,1)S(1)}, bf16[256,256]{1,0:T(8,128)(2,1)S(1)}, bf16[256,256]{1,0:T(8,128)(2,1)S(1)}) fusion(bf16[4,256,256]{2,1,0:T(8,128)(2,1)} %bitcast.14, s32[]{:T(128)S(6)} %select_n.53, s32[]{:T(128)S(6)} %select_n.52, s32[]{:T(128)S(6)} %select_n.51), kind=kLoop, calls=%fused_computation | loop fusion | bytes 786444 | tf_op jit(solution)/shard_map/jit(dynamic_index_in_dim)/squeeze | solution.py:333
  3.5 0.1 collective-permute-start.2
  3.6 0.7 %collective-permute-start = (bf16[256,256]{1,0:T(8,128)(2,1)S(1)}, bf16[256,256]{1,0:T(8,128)(2,1)S(1)}, u32[]{:S(2)}, u32[]{:S(2)}) collective-permute-start(bf16[256,256]{1,0:T(8,128)(2,1)S(1)} %get-tuple-element.48), channel_id=1, source_target_pairs={{0,6},{2,4},{4,2},{6,0},{1,7},{3,5},{5,3},{7,1},{8,14},{10,12},{12... | collective-permute-start | bytes 393224 | tf_op jit(solution)/shard_map/ppermute | solution.py:336
  4.3 0.0 copy-start.2
  4.3 0.0 copy-start.3
  4.3 2.7 %constant_dynamic-slice_fusion = (bf16[1024,256]{1,0:T(8,128)(2,1)S(1)}, bf16[1024,256]{1,0:T(8,128)(2,1)S(1)}, bf16[1024,256]{1,0:T(8,128)(2,1)S(1)}, bf16[1024...) fusion(bf16[1024,2048]{1,0:T(8,128)(2,1)} %param.8, ...), kind=kLoop, calls=%fused_computation.4 | loop fusion | bytes 9437220 | tf_op jit(solution)/shard_map/dynamic_slice | solution.py:359
  7.0 0.0 copy-start
  7.0 0.0 copy-done.2
  7.0 0.0 copy-done.3
  7.0 0.6 %shard_map.64.seg = f32[8,256]{1,0:T(8,128)S(1)} custom-call(s32[1,4]{1,0:T(1,128)S(1)} %copy-done.3, s32[1,256]{1,0:T(1,128)S(1)} %bitcast.12), custom_call_target="tpu_custom_call" | custom-call | flops 1610612736 | tf_op jit(solution)/shard_map/pallas_call | solution.py:312
  7.6 0.1 pad_add_fusion.place
  7.6 0.0 collective-permute-done.1.part2
  7.6 0.0 collective-permute-done.2.part1
  7.6 1.3 %collective-permute-done.part3 = bf16[256,256]{1,0:T(8,128)(2,1)S(1)} collective-permute-done((bf16[256,256]{1,0:T(8,128)(2,1)S(1)}, bf16[256,256]{1,0:T(8,128)(2,1)S(1)}, u32[]{:S(2)}, u32[]{:S(2)}) %collective-permute-start) | collective-permute-done | bytes 131104 | tf_op jit(solution)/shard_map/ppermute | solution.py:336
  8.9 0.0 copy-done
  8.9 1.9 %shard_map.65 = (bf16[256,1024]{1,0:T(8,128)(2,1)S(1)}, bf16[256,1024]{1,0:T(8,128)(2,1)S(1)}, bf16[264,512]{1,0:T(8,128)(2,1)S(1)}) custom-call(s32[3]{0:T(128)S(1)} %pad_add_fusion.place, bf16[256,256]{1,0:T(8,128)(2,1)S(1)} %collective-permute-done.part3, bf16[256,256]{1,0:T(8,128)(2,1)S(1)} %collective-permute-done.1.part2, ...), custom_call_target="tpu_custom_call" | custom-call | flops 805306368 | tf_op jit(solution)/shard_map/pallas_call | solution.py:312
  10.8 0.3 collective-permute-start.4
  11.1 0.5 %shard_map.66 = (bf16[264,256]{1,0:T(8,128)(2,1)S(1)}, bf16[264,256]{1,0:T(8,128)(2,1)S(1)}) custom-call(bf16[256,1024]{1,0:T(8,128)(2,1)S(1)} %get-tuple-element.24.normed, bf16[1024,256]{1,0:T(8,128)(2,1)S(1)} %get-tuple-element.42.w_far, bf16[1024,256]{1,0:T(8,128)(2,1)S(1)} %get-tuple-element.41.w_sent, f32[8,256]{1,0:T(8,128)S(1)} %shard_map.64.seg), custom_call_target="tpu_custom_call" | custom-call | flops 268435456 | tf_op jit(solution)/shard_map/pallas_call | solution.py:312
  11.6 3.6 %collective-permute-start.7 = (bf16[264,256]{1,0:T(8,128)(2,1)S(1)}, bf16[264,256]{1,0:T(8,128)(2,1)S(1)}, u32[]{:S(2)}, u32[]{:S(2)}) collective-permute-start(bf16[264,256]{1,0:T(8,128)(2,1)S(1)} %get-tuple-element.34), channel_id=1, source_target_pairs={{24,8},{8,0},{25,9},{9,1},{26,10},{10,2},{27,11},{11,3},{28,12},{1... | collective-permute-start | bytes 405512 | tf_op jit(solution)/shard_map/ppermute | solution.py:376
  15.2 1.0 %shard_map.67 = (bf16[264,512]{1,0:T(8,128)(2,1)S(1)}, f32[2,256,256]{2,1,0:T(8,128)S(1)}, bf16[256,256]{1,0:T(8,128)(2,1)S(1)}, bf16[2,256,256]{2,1,0:T(8,128)(2,1)S(1)}) custom-call(s32[3]{0:T(128)S(1)} %pad_add_fusion.place, bf16[264,512]{1,0:T(8,128)(2,1)S(1)} %get-tuple-element.23.send_b, bf16[264,256]{1,0:T(8,128)(2,1)S(1)} %get-tuple-element.25.send_c, ...), custom_call_target="tpu_custom_call" | custom-call | flops 268435456 | tf_op jit(solution)/shard_map/pallas_call | solution.py:312
  16.2 0.7 %collective-permute-start.3 = (bf16[264,512]{1,0:T(8,128)(2,1)S(1)}, bf16[264,512]{1,0:T(8,128)(2,1)S(1)}, u32[]{:S(2)}, u32[]{:S(2)}) collective-permute-start(bf16[264,512]{1,0:T(8,128)(2,1)S(1)} %get-tuple-element.26.send_a), channel_id=1, source_target_pairs={{0,16},{1,17},{2,18},{3,19},{4,20},{5,21},{6,22},{7,23}} | collective-permute-start | bytes 811016 | tf_op jit(solution)/shard_map/ppermute | solution.py:388
  16.9 0.7 %collective-permute-start.9 = (bf16[264,256]{1,0:T(8,128)(2,1)S(1)}, bf16[264,256]{1,0:T(8,128)(2,1)S(1)}, u32[]{:S(2)}, u32[]{:S(2)}) collective-permute-start(bf16[264,256]{1,0:T(8,128)(2,1)S(1)} %get-tuple-element.25.send_c), channel_id=1, source_target_pairs={{16,8},{17,9},{18,10},{19,11},{20,12},{21,13},{22,14},{23,15}} | collective-permute-start | bytes 405512 | tf_op jit(solution)/shard_map/ppermute | solution.py:389
  17.6 4.2 %collective-permute-start.5 = (bf16[264,256]{1,0:T(8,128)(2,1)S(1)}, bf16[264,256]{1,0:T(8,128)(2,1)S(1)}, u32[]{:S(2)}, u32[]{:S(2)}) collective-permute-start(bf16[264,256]{1,0:T(8,128)(2,1)S(1)} %get-tuple-element.25.send_c), channel_id=1, source_target_pairs={{24,16},{25,17},{26,18},{27,19},{28,20},{29,21},{30,22},{31,23}} | collective-permute-start | bytes 405512 | tf_op jit(solution)/shard_map/ppermute | solution.py:390
  21.7 0.6 %shard_map.68 = (f32[2,256,256]{2,1,0:T(8,128)S(1)}, bf16[256,256]{1,0:T(8,128)(2,1)S(1)}, bf16[2,256,256]{2,1,0:T(8,128)(2,1)S(1)}) custom-call(s32[3]{0:T(128)S(1)} %pad_add_fusion.place, bf16[264,512]{1,0:T(8,128)(2,1)S(1)} %get-tuple-element.26.send_a, ...), custom_call_target="tpu_custom_call", output_to_operand_aliasing={{0}: (9, {}), {1}: (10, {}), {2}: (11, {})} | custom-call | flops 402653184 | tf_op jit(solution)/shard_map/pallas_call | solution.py:312
  22.3 0.0 collective-permute-done.7.got_f
  22.3 0.0 collective-permute-done.4.got_b
  22.3 0.6 %shard_map.71.send_e = bf16[256,256]{1,0:T(8,128)(2,1)S(1)} custom-call(s32[3]{0:T(128)S(1)} %pad_add_fusion.place, bf16[264,512]{1,0:T(8,128)(2,1)S(1)} %collective-permute-done.4.got_b, bf16[264,512]{1,0:T(8,128)(2,1)S(1)} %get-tuple-element.26.send_a, f32[2,256,256]{2,1,0:T(8,128)S(1)} %get-tuple-element.30.mixed_in.mixed, ...), custom_call_target="tpu_custom_call" | custom-call | flops 1073741824 | tf_op jit(solution)/shard_map/pallas_call | solution.py:312
  22.9 0.0 copy-start.1
  22.9 1.4 %collective-permute-start.8 = (bf16[256,256]{1,0:T(8,128)(2,1)S(1)}, bf16[256,256]{1,0:T(8,128)(2,1)S(1)}, u32[]{:S(2)}, u32[]{:S(2)}) collective-permute-start(bf16[256,256]{1,0:T(8,128)(2,1)S(1)} %shard_map.71.send_e), channel_id=1, source_target_pairs={{8,24},{0,8},{9,25},{1,9},{10,26},{2,10},{11,27},{3,11},{12,28},{4... | collective-permute-start | bytes 393224 | tf_op jit(solution)/shard_map/ppermute | solution.py:408
  24.3 0.0 collective-permute-done.9.got_c
  24.4 0.6 %shard_map.72 = bf16[256,256]{1,0:T(8,128)(2,1)S(1)} custom-call(s32[3]{0:T(128)S(1)} %pad_add_fusion.place, bf16[264,512]{1,0:T(8,128)(2,1)S(1)} %collective-permute-done.4.got_b, bf16[256,256]{1,0:T(8,128)(2,1)S(1)} %shard_map.71.send_e, bf16[264,512]{1,0:T(8,128)(2,1)S(1)} %get-tuple-element.26.send_a, bf16[264,256]{1,0:T(8,128)(2,1)S(1)} %collective-permute-done.9.got_c), custom_call_target="tpu_custom_call" | custom-call | flops 1073741824 | tf_op jit(solution)/shard_map/pallas_call | solution.py:312
  24.9 0.7 %collective-permute-start.10 = (bf16[256,256]{1,0:T(8,128)(2,1)S(1)}, bf16[256,256]{1,0:T(8,128)(2,1)S(1)}, u32[]{:S(2)}, u32[]{:S(2)}) collective-permute-start(bf16[256,256]{1,0:T(8,128)(2,1)S(1)} %shard_map.72), channel_id=1, source_target_pairs={{8,16},{9,17},{10,18},{11,19},{12,20},{13,21},{14,22},{15,23}} | collective-permute-start | bytes 393224 | tf_op jit(solution)/shard_map/ppermute | solution.py:416
  25.6 0.0 collective-permute-done.5.got_h
  25.6 0.0 collective-permute-done.3.got_a
  25.6 0.6 %shard_map.70 = bf16[256,256]{1,0:T(8,128)(2,1)S(1)} custom-call(s32[3]{0:T(128)S(1)} %pad_add_fusion.place, bf16[264,512]{1,0:T(8,128)(2,1)S(1)} %collective-permute-done.4.got_b, bf16[264,512]{1,0:T(8,128)(2,1)S(1)} %get-tuple-element.26.send_a, bf16[264,256]{1,0:T(8,128)(2,1)S(1)} %collective-permute-done.5.got_h, ...), custom_call_target="tpu_custom_call" | custom-call | flops 256 | tf_op jit(solution)/shard_map/pallas_call | solution.py:312
  26.2 1.3 %collective-permute-start.6 = (bf16[256,256]{1,0:T(8,128)(2,1)S(1)}, bf16[256,256]{1,0:T(8,128)(2,1)S(1)}, u32[]{:S(2)}, u32[]{:S(2)}) collective-permute-start(bf16[256,256]{1,0:T(8,128)(2,1)S(1)} %shard_map.70), channel_id=1, source_target_pairs={{16,24},{17,25},{18,26},{19,27},{20,28},{21,29},{22,30},{23,31}} | collective-permute-start | bytes 393224 | tf_op jit(solution)/shard_map/ppermute | solution.py:424
  27.5 2.6 %shard_map.69 = (f32[2,256,256]{2,1,0:T(8,128)S(1)}, bf16[256,256]{1,0:T(8,128)(2,1)S(1)}, bf16[2,256,256]{2,1,0:T(8,128)(2,1)S(1)}) custom-call(s32[3]{0:T(128)S(1)} %pad_add_fusion.place, bf16[264,512]{1,0:T(8,128)(2,1)S(1)} %collective-permute-done.3.got_a, ...), custom_call_target="tpu_custom_call", output_to_operand_aliasing={{0}: (11, {}), {1}: (12, {}), {2}: (13, {})} | custom-call | flops 256 | tf_op jit(solution)/shard_map/pallas_call | solution.py:312
  30.1 0.0 collective-permute-done.10
  30.1 1.3 %collective-permute-done.8 = bf16[256,256]{1,0:T(8,128)(2,1)S(1)} collective-permute-done((bf16[256,256]{1,0:T(8,128)(2,1)S(1)}, bf16[256,256]{1,0:T(8,128)(2,1)S(1)}, u32[]{:S(2)}, u32[]{:S(2)}) %collective-permute-start.8) | collective-permute-done | bytes 131104 | tf_op jit(solution)/shard_map/ppermute | solution.py:408
  31.4 2.3 %collective-permute-done.6.got_d = bf16[256,256]{1,0:T(8,128)(2,1)S(1)} collective-permute-done((bf16[256,256]{1,0:T(8,128)(2,1)S(1)}, bf16[256,256]{1,0:T(8,128)(2,1)S(1)}, u32[]{:S(2)}, u32[]{:S(2)}) %collective-permute-start.6) | collective-permute-done | bytes 131104 | tf_op jit(solution)/shard_map/ppermute | solution.py:424
  33.7 0.0 copy-done.1
  33.7 2.0 %shard_map.73 = bf16[256,1024]{1,0:T(8,128)(2,1)} custom-call(s32[3]{0:T(128)S(1)} %pad_add_fusion.place, f32[2,256,256]{2,1,0:T(8,128)S(1)} %get-tuple-element.33.mixed, bf16[256,256]{1,0:T(8,128)(2,1)S(1)} %collective-permute-done.6.got_d, bf16[256,256]{1,0:T(8,128)(2,1)S(1)} %add.103.got_eg, bf16[2,256,256]{2,1,0:T(8,128)(2,1)S(1)} %get-tuple-element.35.gate, ...), custom_call_target="tpu_custom_call" | custom-call | flops 256 | tf_op jit(solution)/shard_map/pallas_call | solution.py:312
  (1 shorter events, 0.0 us)
Async XLA Ops:
  0.9 6.7 %collective-permute-start.1 = (bf16[256,256]{1,0:T(8,128)(2,1)S(1)}, bf16[256,256]{1,0:T(8,128)(2,1)S(1)}, u32[]{:S(2)}, u32[]{:S(2)}) collective-permute-start(bf16[256,256]{1,0:T(8,128)(2,1)S(1)} %dynamic-slice_bitcast_fusion.3), channel_id=1, source_target_pairs={{0,4},{2,6},{4,0},{6,2},{1,5},{3,7},{5,1},{7,3},{8,12},{10,14},{12... | collective-permute-start | bytes 393224 | tf_op jit(solution)/shard_map/ppermute | solution.py:336
  3.5 4.1 %collective-permute-start.2 = (bf16[256,256]{1,0:T(8,128)(2,1)S(1)}, bf16[256,256]{1,0:T(8,128)(2,1)S(1)}, u32[]{:S(2)}, u32[]{:S(2)}) collective-permute-start(bf16[256,256]{1,0:T(8,128)(2,1)S(1)} %get-tuple-element.47), channel_id=1, source_target_pairs={{0,2},{2,0},{4,6},{6,4},{1,3},{3,1},{5,7},{7,5},{8,10},{10,8},{12,... | collective-permute-start | bytes 393224 | tf_op jit(solution)/shard_map/ppermute | solution.py:336
  3.6 5.3 %collective-permute-start = (bf16[256,256]{1,0:T(8,128)(2,1)S(1)}, bf16[256,256]{1,0:T(8,128)(2,1)S(1)}, u32[]{:S(2)}, u32[]{:S(2)}) collective-permute-start(bf16[256,256]{1,0:T(8,128)(2,1)S(1)} %get-tuple-element.48), channel_id=1, source_target_pairs={{0,6},{2,4},{4,2},{6,0},{1,7},{3,5},{5,3},{7,1},{8,14},{10,12},{12... | collective-permute-start | bytes 393224 | tf_op jit(solution)/shard_map/ppermute | solution.py:336
  4.3 2.7 %copy-start.2 = (s32[256]{0:T(256)S(1)}, s32[256]{0:T(256)}, u32[]{:S(2)}) copy-start(s32[256]{0:T(256)} %param.11) | copy-start | bytes 3076
  4.3 2.7 %copy-start.3 = (s32[1,4]{1,0:T(1,128)S(1)}, s32[1,4]{1,0:T(1,128)}, u32[]{:S(2)}) copy-start(s32[1,4]{1,0:T(1,128)} %counts.1) | copy-start | bytes 52
  7.0 1.9 %copy-start = (bf16[1024,1024]{1,0:T(8,128)(2,1)S(1)}, bf16[1024,1024]{1,0:T(8,128)(2,1)}, u32[]{:S(2)}) copy-start(bf16[1024,1024]{1,0:T(8,128)(2,1)} %w_in.1) | copy-start | bytes 6291460
  10.8 11.5 %collective-permute-start.4 = (bf16[264,512]{1,0:T(8,128)(2,1)S(1)}, bf16[264,512]{1,0:T(8,128)(2,1)S(1)}, u32[]{:S(2)}, u32[]{:S(2)}) collective-permute-start(bf16[264,512]{1,0:T(8,128)(2,1)S(1)} %get-tuple-element.23.send_b), channel_id=1, source_target_pairs={{0,8},{8,16},{16,24},{24,0},{1,9},{9,17},{17,25},{25,1},{2,10},{10... | collective-permute-start | bytes 811016 | tf_op jit(solution)/shard_map/ppermute | solution.py:368
  11.6 10.7 %collective-permute-start.7 = (bf16[264,256]{1,0:T(8,128)(2,1)S(1)}, bf16[264,256]{1,0:T(8,128)(2,1)S(1)}, u32[]{:S(2)}, u32[]{:S(2)}) collective-permute-start(bf16[264,256]{1,0:T(8,128)(2,1)S(1)} %get-tuple-element.34), channel_id=1, source_target_pairs={{24,8},{8,0},{25,9},{9,1},{26,10},{10,2},{27,11},{11,3},{28,12},{1... | collective-permute-start | bytes 405512 | tf_op jit(solution)/shard_map/ppermute | solution.py:376
  16.2 9.4 %collective-permute-start.3 = (bf16[264,512]{1,0:T(8,128)(2,1)S(1)}, bf16[264,512]{1,0:T(8,128)(2,1)S(1)}, u32[]{:S(2)}, u32[]{:S(2)}) collective-permute-start(bf16[264,512]{1,0:T(8,128)(2,1)S(1)} %get-tuple-element.26.send_a), channel_id=1, source_target_pairs={{0,16},{1,17},{2,18},{3,19},{4,20},{5,21},{6,22},{7,23}} | collective-permute-start | bytes 811016 | tf_op jit(solution)/shard_map/ppermute | solution.py:388
  16.9 7.5 %collective-permute-start.9 = (bf16[264,256]{1,0:T(8,128)(2,1)S(1)}, bf16[264,256]{1,0:T(8,128)(2,1)S(1)}, u32[]{:S(2)}, u32[]{:S(2)}) collective-permute-start(bf16[264,256]{1,0:T(8,128)(2,1)S(1)} %get-tuple-element.25.send_c), channel_id=1, source_target_pairs={{16,8},{17,9},{18,10},{19,11},{20,12},{21,13},{22,14},{23,15}} | collective-permute-start | bytes 405512 | tf_op jit(solution)/shard_map/ppermute | solution.py:389
  17.6 8.0 %collective-permute-start.5 = (bf16[264,256]{1,0:T(8,128)(2,1)S(1)}, bf16[264,256]{1,0:T(8,128)(2,1)S(1)}, u32[]{:S(2)}, u32[]{:S(2)}) collective-permute-start(bf16[264,256]{1,0:T(8,128)(2,1)S(1)} %get-tuple-element.25.send_c), channel_id=1, source_target_pairs={{24,16},{25,17},{26,18},{27,19},{28,20},{29,21},{30,22},{31,23}} | collective-permute-start | bytes 405512 | tf_op jit(solution)/shard_map/ppermute | solution.py:390
  22.9 10.8 %copy-start.1 = (bf16[512,1024]{1,0:T(8,128)(2,1)S(1)}, bf16[512,1024]{1,0:T(8,128)(2,1)}, u32[]{:S(2)}) copy-start(bf16[512,1024]{1,0:T(8,128)(2,1)} %w_out.1) | copy-start | bytes 3145732
  22.9 8.5 %collective-permute-start.8 = (bf16[256,256]{1,0:T(8,128)(2,1)S(1)}, bf16[256,256]{1,0:T(8,128)(2,1)S(1)}, u32[]{:S(2)}, u32[]{:S(2)}) collective-permute-start(bf16[256,256]{1,0:T(8,128)(2,1)S(1)} %shard_map.71.send_e), channel_id=1, source_target_pairs={{8,24},{0,8},{9,25},{1,9},{10,26},{2,10},{11,27},{3,11},{12,28},{4... | collective-permute-start | bytes 393224 | tf_op jit(solution)/shard_map/ppermute | solution.py:408
  24.9 5.2 %collective-permute-start.10 = (bf16[256,256]{1,0:T(8,128)(2,1)S(1)}, bf16[256,256]{1,0:T(8,128)(2,1)S(1)}, u32[]{:S(2)}, u32[]{:S(2)}) collective-permute-start(bf16[256,256]{1,0:T(8,128)(2,1)S(1)} %shard_map.72), channel_id=1, source_target_pairs={{8,16},{9,17},{10,18},{11,19},{12,20},{13,21},{14,22},{15,23}} | collective-permute-start | bytes 393224 | tf_op jit(solution)/shard_map/ppermute | solution.py:416
  26.2 7.5 %collective-permute-start.6 = (bf16[256,256]{1,0:T(8,128)(2,1)S(1)}, bf16[256,256]{1,0:T(8,128)(2,1)S(1)}, u32[]{:S(2)}, u32[]{:S(2)}) collective-permute-start(bf16[256,256]{1,0:T(8,128)(2,1)S(1)} %shard_map.70), channel_id=1, source_target_pairs={{16,24},{17,25},{18,26},{19,27},{20,28},{21,29},{22,30},{23,31}} | collective-permute-start | bytes 393224 | tf_op jit(solution)/shard_map/ppermute | solution.py:424

commit v6 on v5

--- a/solution.py
+++ b/solution.py
@@ -82,6 +82,14 @@
     return (hidden.astype(F32) + branch_rows.astype(F32)).astype(BF16)
 
 
+def batch_index():
+    return lax.axis_index("batch")
+
+
+def is_last():
+    return lax.axis_index("batch") == lax.axis_size("batch") - 1
+
+
 def silu_of(values):
     half = 0.5 * values
     return half + half * jnp.tanh(half)
@@ -121,9 +129,9 @@
 
 
 def project_first_kernel(
-    place, part3, part2, part1, own, w_in, w_key, w_value, seg, hidden_out, normed, send_b
+    part3, part2, part1, own, w_in, w_key, w_value, seg, hidden_out, normed, send_b
 ):
-    col_at = place[1]
+    col_at = lax.axis_index("col")
     rows, piece = own.shape
     group = w_key.shape[1]
     total = None
@@ -147,7 +155,7 @@
 
 
 def project_near_kernel(
-    place, send_b, send_c, seg, normed, w_query, w_near, w_far, w_key, w_value,
+    send_b, send_c, seg, normed, w_query, w_near, w_far, w_key, w_value,
     send_a, mixed_out, query_near, gate_out,
 ):
     rows = normed.shape[0]
@@ -156,7 +164,7 @@
     send_a[:rows, group:] = silu_dot(normed, w_value)
     put_seg(send_a, seg[...])
 
-    @pl.when(place[0] == 0)
+    @pl.when(batch_index() == 0)
     def _():
         attend_own(
             send_a, send_b, send_c, seg, normed, (w_query, w_near, w_far),
@@ -217,74 +225,74 @@
 
 
 def own_kernel(
-    place, send_a, send_b, send_c, seg, normed, w_query, w_near, w_far,
+    send_a, send_b, send_c, seg, normed, w_query, w_near, w_far,
     mixed_in, query_in, gate_in, mixed, query_near, gate,
 ):
-    @pl.when((place[0] != 0) & (place[0] != place[2]))
+    @pl.when((batch_index() != 0) & ~is_last())
     def _():
         attend_own(
             send_a, send_b, send_c, seg, normed, (w_query, w_near, w_far), mixed, query_near, gate
         )
 
 
-def far_g_kernel(place, got_b, send_e, send_a, got_c, send_g):
-    @pl.when(place[0] == 1)
+def far_g_kernel(got_b, send_e, send_a, got_c, send_g):
+    @pl.when(batch_index() == 1)
     def _():
         add_blocks(got_c, [send_a, got_b], send_g)
 
-    @pl.when(place[0] != 1)
+    @pl.when(batch_index() != 1)
     def _():
         send_g[...] = jnp.zeros_like(send_g)
 
 
-def far_e_kernel(place, got_b, send_a, mixed, got_f, send_e):
-    @pl.when(place[0] == 0)
+def far_e_kernel(got_b, send_a, mixed, got_f, send_e):
+    @pl.when(batch_index() == 0)
     def _():
         add_blocks(got_f, [send_a], send_e)
 
-    @pl.when(place[0] == 1)
+    @pl.when(batch_index() == 1)
     def _():
         add_blocks(got_f, [send_a, got_b], send_e)
 
-    @pl.when(place[0] > 1)
+    @pl.when(batch_index() > 1)
     def _():
         send_e[...] = jnp.zeros_like(send_e)
 
 
-def far_d_kernel(place, got_b, send_a, got_h, got_a, send_d):
-    @pl.when(place[0] == 2)
+def far_d_kernel(got_b, send_a, got_h, got_a, send_d):
+    @pl.when(batch_index() == 2)
     def _():
         add_blocks(got_h, [send_a, got_b, got_a], send_d)
 
-    @pl.when(place[0] != 2)
+    @pl.when(batch_index() != 2)
     def _():
         send_d[...] = jnp.zeros_like(send_d)
 
 
 def near_kernel(
-    place, got_a, got_b, send_a, send_b, send_c, seg, normed, w_query, w_near, w_far,
+    got_a, got_b, send_a, send_b, send_c, seg, normed, w_query, w_near, w_far,
     mixed_in, query_in, gate_in, mixed, query_near, gate,
 ):
     column = seg_column(seg[0:1, :])
 
-    @pl.when(place[0] == place[2])
+    @pl.when(is_last())
     def _():
         attend_own(
             send_a, send_b, send_c, seg, normed, (w_query, w_near, w_far), mixed, query_near, gate
         )
 
-    @pl.when(place[0] > 0)
+    @pl.when(batch_index() > 0)
     def _():
         add_near(query_near, column, got_b, mixed.at[0])
 
-    @pl.when(place[0] == 2)
+    @pl.when(batch_index() == 2)
     def _():
         add_near(query_near, column, got_a, mixed.at[0])
 
 
-def finish_kernel(place, mixed, got_d, got_eg, gate, hidden, w_out, out):
-    near = place[0] % 2
-    last = place[0] == place[2]
+def finish_kernel(mixed, got_d, got_eg, gate, hidden, w_out, out):
+    near = batch_index() % 2
+    last = is_last()
     got = got_eg[...].astype(F32)
     group = mixed.shape[2]
     sides = (
@@ -325,7 +333,6 @@
     cols = lax.axis_size("col")
     batch_at = lax.axis_index("batch").astype(jnp.int32)
     col_at = lax.axis_index("col").astype(jnp.int32)
-    place = jnp.stack([batch_at, col_at, jnp.int32(lax.axis_size("batch") - 1)])
     pieces = lookups.reshape(cols, lookups.shape[0] // cols, lookups.shape[1])
     rows = pieces.shape[1]
 
@@ -360,9 +367,9 @@
 
     hidden, normed, send_b = call(
         project_first_kernel,
-        [SMEM] + [VMEM] * 8,
+        [VMEM] * 8,
         [((rows, features), BF16), ((rows, features), BF16), ((tall, 2 * group), BF16)],
-        (place, *parts[::-1], input_weight, weight_of(3, far), weight_of(1, far), seg),
+        (*parts[::-1], input_weight, weight_of(3, far), weight_of(1, far), seg),
         2 * rows * features * (features + 2 * group),
     )
     got_b = lax.ppermute(send_b, "batch", [(0, 1), (1, 2), (2, 3), (3, 0)])
@@ -380,9 +387,9 @@
     own_outs = [((2, rows, group), F32), ((rows, group), BF16), ((2, rows, group), BF16)]
     send_a, *own = call(
         project_near_kernel,
-        [SMEM] + [VMEM] * 9,
+        [VMEM] * 9,
         [((tall, 2 * group), BF16)] + own_outs,
-        (place, *own_inputs, weight_of(3, near), weight_of(1, near)),
+        (*own_inputs, weight_of(3, near), weight_of(1, near)),
         2 * rows * features * 2 * group,
     )
     got_a = lax.ppermute(send_a, "batch", [(0, 2)])
@@ -391,50 +398,50 @@
     pair_flops = 4 * rows * rows * group
     own = call(
         own_kernel,
-        [SMEM] + [VMEM] * 11,
+        [VMEM] * 11,
         own_outs,
-        (place, send_a, *own_inputs, *own),
+        (send_a, *own_inputs, *own),
         2 * pair_flops + 2 * rows * features * width,
-        aliases={9: 0, 10: 1, 11: 2},
+        aliases={8: 0, 9: 1, 10: 2},
     )
     mixed = own[0]
     (send_e,) = call(
         far_e_kernel,
-        [SMEM] + [VMEM] * 4,
+        [VMEM] * 4,
         [((rows, group), BF16)],
-        (place, got_b, send_a, mixed, got_f),
+        (got_b, send_a, mixed, got_f),
         1 << 30,
     )
     got_e = lax.ppermute(send_e, "batch", [(1, 3), (0, 1)])
     (send_g,) = call(
         far_g_kernel,
-        [SMEM] + [VMEM] * 4,
+        [VMEM] * 4,
         [((rows, group), BF16)],
-        (place, got_b, send_e, send_a, got_c),
+        (got_b, send_e, send_a, got_c),
         1 << 30,
     )
     got_g = lax.ppermute(send_g, "batch", [(1, 2)])
     (send_d,) = call(
         far_d_kernel,
-        [SMEM] + [VMEM] * 4,
+        [VMEM] * 4,
         [((rows, group), BF16)],
-        (place, got_b, send_a, got_h, got_a),
+        (got_b, send_a, got_h, got_a),
         rows,
     )
     got_d = lax.ppermute(send_d, "batch", [(2, 3)])
     mixed, _, gate = call(
         near_kernel,
-        [SMEM] + [VMEM] * 13,
+        [VMEM] * 13,
         own_outs,
-        (place, got_a, got_b, send_a, *own_inputs, *own),
+        (got_a, got_b, send_a, *own_inputs, *own),
         rows,
-        aliases={11: 0, 12: 1, 13: 2},
+        aliases={10: 0, 11: 1, 12: 2},
     )
     (out,) = call(
         finish_kernel,
-        [SMEM] + [VMEM] * 6,
+        [VMEM] * 6,
         [((rows, features), BF16)],
-        (place, mixed, got_d, got_e + got_g, gate, hidden, output_weight),
+        (mixed, got_d, got_e + got_g, gate, hidden, output_weight),
         rows,
     )
     return out

time: 36 us -> 34 us (0.944)
  Pallas kernels: 10.7 us -> 6.37 us
  waiting for transfers between devices: 4.85 us -> 7.19 us
    pallas_call x10, Pallas kernels: 10.7 us -> 6.37 us  [call(): pl.pallas_call(kernel, out_shape=[jax.ShapeDtypeStruct(shape, dtype) for...]
    ppermute x1, waiting for transfers between devices: 1.28 us -> 3.1 us  [chain_plan(): got_e = lax.ppermute(send_e, 'batch', [(1, 3), (0, 1)])]
  transfers between devices with their start and end apart: 11 -> 11, of which waited for: 3 -> 4; matrix products, arithmetic and copies ran while one was open for 11% -> 11% of each run, Pallas kernels for 19% -> 11%
where the time goes in v6:
time: 34 us; the launch traced here: 33.6 us
  starting transfers between devices  15.1 us (44%)
  waiting for transfers between devices  7.19 us (21%)
  Pallas kernels  6.37 us (19%)
  local copies, waits for them, and re-layouts  4.69 us (14%)
    pallas_call x10, Pallas kernels, call(): pl.pallas_call(kernel, out_shape=[jax.ShapeDtypeStruct(shape, dtype) for...  6.37 us
    ppermute x1, starting transfers between devices, chain_plan(): got_h = lax.ppermute(send_c, 'batch', [(3, 2)])  4.16 us
    ppermute x1, starting transfers between devices, chain_plan(): got_f = lax.ppermute(send_f, 'batch', [(3, 1), (1, 0)])  3.6 us
    ppermute x1, waiting for transfers between devices, chain_plan(): got_e = lax.ppermute(send_e, 'batch', [(1, 3), (0, 1)])  3.1 us
    dynamic_slice x1, local copies, waits for them, and re-layouts, weight_of(): lax.dynamic_slice_in_dim(joined_weight, block * width + index * group, gr...  2.7 us
    ppermute x1, waiting for transfers between devices, chain_plan(): got_d = lax.ppermute(send_d, 'batch', [(2, 3)])  2.46 us
    ppermute x3, starting transfers between devices, exchange(): return lax.ppermute(block, 'col', [(i, i ^ shift) for i in range(cols)])  2.28 us
    squeeze x2, local copies, waits for them, and re-layouts, piece(): return lax.dynamic_index_in_dim(source, col_at ^ shift, 0, keepdims=False)  1.97 us
  transfers between devices with their start and end apart: 11, of which 4 were waited for; matrix products, arithmetic and copies ran while one was open for 11% of the time, Pallas kernels for 11%

profile of v6, /device:TPU:24, one launch (start us, length us, event | category | flops | bytes accessed | tf_op | source)
XLA Modules:
  0.0 33.6 jit_solution(1388534936245301107)
XLA Ops:
  0.0 0.9 %dynamic-slice_bitcast_fusion.3 = bf16[256,256]{1,0:T(8,128)(2,1)S(1)} fusion(bf16[4,256,256]{2,1,0:T(8,128)(2,1)} %bitcast.11, s32[]{:T(128)S(6)} %select_n.50), kind=kLoop, calls=%fused_computation.3 | loop fusion | bytes 262148 | tf_op jit(solution)/shard_map/jit(dynamic_index_in_dim)/squeeze | solution.py:340
  0.9 1.6 %collective-permute-start.1 = (bf16[256,256]{1,0:T(8,128)(2,1)S(1)}, bf16[256,256]{1,0:T(8,128)(2,1)S(1)}, u32[]{:S(2)}, u32[]{:S(2)}) collective-permute-start(bf16[256,256]{1,0:T(8,128)(2,1)S(1)} %dynamic-slice_bitcast_fusion.3), channel_id=1, source_target_pairs={{0,4},{2,6},{4,0},{6,2},{1,5},{3,7},{5,1},{7,3},{8,12},{10,14},{12... | collective-permute-start | bytes 393224 | tf_op jit(solution)/shard_map/ppermute | solution.py:343
  2.5 1.1 %dynamic-slice_bitcast_fusion = (bf16[256,256]{1,0:T(8,128)(2,1)S(1)}, bf16[256,256]{1,0:T(8,128)(2,1)S(1)}, bf16[256,256]{1,0:T(8,128)(2,1)S(1)}) fusion(bf16[4,256,256]{2,1,0:T(8,128)(2,1)} %bitcast.12, s32[]{:T(128)S(6)} %select_n.53, s32[]{:T(128)S(6)} %select_n.52, s32[]{:T(128)S(6)} %select_n.51), kind=kLoop, calls=%fused_computation | loop fusion | bytes 786444 | tf_op jit(solution)/shard_map/jit(dynamic_index_in_dim)/squeeze | solution.py:340
  3.5 0.1 collective-permute-start.2
  3.6 0.7 %collective-permute-start = (bf16[256,256]{1,0:T(8,128)(2,1)S(1)}, bf16[256,256]{1,0:T(8,128)(2,1)S(1)}, u32[]{:S(2)}, u32[]{:S(2)}) collective-permute-start(bf16[256,256]{1,0:T(8,128)(2,1)S(1)} %get-tuple-element.48), channel_id=1, source_target_pairs={{0,6},{2,4},{4,2},{6,0},{1,7},{3,5},{5,3},{7,1},{8,14},{10,12},{12... | collective-permute-start | bytes 393224 | tf_op jit(solution)/shard_map/ppermute | solution.py:343
  4.3 0.0 copy-start.2
  4.3 0.0 copy-start.3
  4.3 2.7 %constant_dynamic-slice_fusion = (bf16[1024,256]{1,0:T(8,128)(2,1)S(1)}, bf16[1024,256]{1,0:T(8,128)(2,1)S(1)}, bf16[1024,256]{1,0:T(8,128)(2,1)S(1)}, bf16[1024...) fusion(bf16[1024,2048]{1,0:T(8,128)(2,1)} %param.8, ...), kind=kLoop, calls=%fused_computation.4 | loop fusion | bytes 9437220 | tf_op jit(solution)/shard_map/dynamic_slice | solution.py:366
  7.0 0.0 copy-start
  7.0 0.0 copy-done.2
  7.0 0.0 copy-done.3
  7.0 0.6 %shard_map.64.seg = f32[8,256]{1,0:T(8,128)S(1)} custom-call(s32[1,4]{1,0:T(1,128)S(1)} %copy-done.3, s32[1,256]{1,0:T(1,128)S(1)} %bitcast.10), custom_call_target="tpu_custom_call" | custom-call | flops 1610612736 | tf_op jit(solution)/shard_map/pallas_call | solution.py:320
  7.6 0.0 collective-permute-done.1.part2
  7.6 0.0 collective-permute-done.2.part1
  7.6 1.3 %collective-permute-done.part3 = bf16[256,256]{1,0:T(8,128)(2,1)S(1)} collective-permute-done((bf16[256,256]{1,0:T(8,128)(2,1)S(1)}, bf16[256,256]{1,0:T(8,128)(2,1)S(1)}, u32[]{:S(2)}, u32[]{:S(2)}) %collective-permute-start) | collective-permute-done | bytes 131104 | tf_op jit(solution)/shard_map/ppermute | solution.py:343
  8.9 0.0 copy-done
  8.9 1.4 %shard_map.65 = (bf16[256,1024]{1,0:T(8,128)(2,1)S(1)}, bf16[256,1024]{1,0:T(8,128)(2,1)S(1)}, bf16[264,512]{1,0:T(8,128)(2,1)S(1)}) custom-call(bf16[256,256]{1,0:T(8,128)(2,1)S(1)} %collective-permute-done.part3, bf16[256,256]{1,0:T(8,128)(2,1)S(1)} %collective-permute-done.1.part2, bf16[256,256]{1,0:T(8,128)(2,1)S(1)} %collective-permute-done.2.part1, ...), custom_call_target="tpu_custom_call" | custom-call | flops 805306368 | tf_op jit(solution)/shard_map/pallas_call | solution.py:320
  10.3 0.3 collective-permute-start.4
  10.6 0.5 %shard_map.66 = (bf16[264,256]{1,0:T(8,128)(2,1)S(1)}, bf16[264,256]{1,0:T(8,128)(2,1)S(1)}) custom-call(bf16[256,1024]{1,0:T(8,128)(2,1)S(1)} %get-tuple-element.24.normed, bf16[1024,256]{1,0:T(8,128)(2,1)S(1)} %get-tuple-element.42.w_far, bf16[1024,256]{1,0:T(8,128)(2,1)S(1)} %get-tuple-element.41.w_sent, f32[8,256]{1,0:T(8,128)S(1)} %shard_map.64.seg), custom_call_target="tpu_custom_call" | custom-call | flops 268435456 | tf_op jit(solution)/shard_map/pallas_call | solution.py:320
  11.0 3.6 %collective-permute-start.7 = (bf16[264,256]{1,0:T(8,128)(2,1)S(1)}, bf16[264,256]{1,0:T(8,128)(2,1)S(1)}, u32[]{:S(2)}, u32[]{:S(2)}) collective-permute-start(bf16[264,256]{1,0:T(8,128)(2,1)S(1)} %get-tuple-element.34), channel_id=1, source_target_pairs={{24,8},{8,0},{25,9},{9,1},{26,10},{10,2},{27,11},{11,3},{28,12},{1... | collective-permute-start | bytes 405512 | tf_op jit(solution)/shard_map/ppermute | solution.py:383
  14.7 0.5 %shard_map.67 = (bf16[264,512]{1,0:T(8,128)(2,1)S(1)}, f32[2,256,256]{2,1,0:T(8,128)S(1)}, bf16[256,256]{1,0:T(8,128)(2,1)S(1)}, bf16[2,256,256]{2,1,0:T(8,128)(2,1)S(1)}) custom-call(bf16[264,512]{1,0:T(8,128)(2,1)S(1)} %get-tuple-element.23.send_b, bf16[264,256]{1,0:T(8,128)(2,1)S(1)} %get-tuple-element.25.send_c, f32[8,256]{1,0:T(8,128)S(1)} %shard_map.64.seg, ...), custom_call_target="tpu_custom_call" | custom-call | flops 268435456 | tf_op jit(solution)/shard_map/pallas_call | solution.py:320
  15.1 0.7 %collective-permute-start.3 = (bf16[264,512]{1,0:T(8,128)(2,1)S(1)}, bf16[264,512]{1,0:T(8,128)(2,1)S(1)}, u32[]{:S(2)}, u32[]{:S(2)}) collective-permute-start(bf16[264,512]{1,0:T(8,128)(2,1)S(1)} %get-tuple-element.26.send_a), channel_id=1, source_target_pairs={{0,16},{1,17},{2,18},{3,19},{4,20},{5,21},{6,22},{7,23}} | collective-permute-start | bytes 811016 | tf_op jit(solution)/shard_map/ppermute | solution.py:395
  15.8 0.7 %collective-permute-start.9 = (bf16[264,256]{1,0:T(8,128)(2,1)S(1)}, bf16[264,256]{1,0:T(8,128)(2,1)S(1)}, u32[]{:S(2)}, u32[]{:S(2)}) collective-permute-start(bf16[264,256]{1,0:T(8,128)(2,1)S(1)} %get-tuple-element.25.send_c), channel_id=1, source_target_pairs={{16,8},{17,9},{18,10},{19,11},{20,12},{21,13},{22,14},{23,15}} | collective-permute-start | bytes 405512 | tf_op jit(solution)/shard_map/ppermute | solution.py:396
  16.5 4.2 %collective-permute-start.5 = (bf16[264,256]{1,0:T(8,128)(2,1)S(1)}, bf16[264,256]{1,0:T(8,128)(2,1)S(1)}, u32[]{:S(2)}, u32[]{:S(2)}) collective-permute-start(bf16[264,256]{1,0:T(8,128)(2,1)S(1)} %get-tuple-element.25.send_c), channel_id=1, source_target_pairs={{24,16},{25,17},{26,18},{27,19},{28,20},{29,21},{30,22},{31,23}} | collective-permute-start | bytes 405512 | tf_op jit(solution)/shard_map/ppermute | solution.py:397
  20.7 0.0 collective-permute-done.7.got_f
  20.7 0.0 collective-permute-done.4.got_b
  20.8 0.0 copy-start.1
  20.8 1.4 %collective-permute-start.8 = (bf16[256,256]{1,0:T(8,128)(2,1)S(1)}, bf16[256,256]{1,0:T(8,128)(2,1)S(1)}, u32[]{:S(2)}, u32[]{:S(2)}) collective-permute-start(bf16[256,256]{1,0:T(8,128)(2,1)S(1)} %shard_map.71.send_e), channel_id=1, source_target_pairs={{8,24},{0,8},{9,25},{1,9},{10,26},{2,10},{11,27},{3,11},{12,28},{4... | collective-permute-start | bytes 393224 | tf_op jit(solution)/shard_map/ppermute | solution.py:415
  22.2 0.0 collective-permute-done.9.got_c
  22.2 0.7 %collective-permute-start.10 = (bf16[256,256]{1,0:T(8,128)(2,1)S(1)}, bf16[256,256]{1,0:T(8,128)(2,1)S(1)}, u32[]{:S(2)}, u32[]{:S(2)}) collective-permute-start(bf16[256,256]{1,0:T(8,128)(2,1)S(1)} %shard_map.72), channel_id=1, source_target_pairs={{8,16},{9,17},{10,18},{11,19},{12,20},{13,21},{14,22},{15,23}} | collective-permute-start | bytes 393224 | tf_op jit(solution)/shard_map/ppermute | solution.py:423
  22.9 0.3 collective-permute-done.5.got_h
  23.2 0.0 collective-permute-done.3.got_a
  23.2 1.3 %collective-permute-start.6 = (bf16[256,256]{1,0:T(8,128)(2,1)S(1)}, bf16[256,256]{1,0:T(8,128)(2,1)S(1)}, u32[]{:S(2)}, u32[]{:S(2)}) collective-permute-start(bf16[256,256]{1,0:T(8,128)(2,1)S(1)} %shard_map.70), channel_id=1, source_target_pairs={{16,24},{17,25},{18,26},{19,27},{20,28},{21,29},{22,30},{23,31}} | collective-permute-start | bytes 393224 | tf_op jit(solution)/shard_map/ppermute | solution.py:431
  24.5 2.0 %shard_map.69 = (f32[2,256,256]{2,1,0:T(8,128)S(1)}, bf16[256,256]{1,0:T(8,128)(2,1)S(1)}, bf16[2,256,256]{2,1,0:T(8,128)(2,1)S(1)}) custom-call(bf16[264,512]{1,0:T(8,128)(2,1)S(1)} %collective-permute-done.3.got_a, bf16[264,512]{1,0:T(8,128)(2,1)S(1)} %collective-permute-done.4.got_b, ...), custom_call_target="tpu_custom_call", output_to_operand_aliasing={{0}: (10, {}), {1}: (11, {}), {2}: (12, {})} | custom-call | flops 256 | tf_op jit(solution)/shard_map/pallas_call | solution.py:320
  26.5 0.0 collective-permute-done.10
  26.6 3.1 %collective-permute-done.8 = bf16[256,256]{1,0:T(8,128)(2,1)S(1)} collective-permute-done((bf16[256,256]{1,0:T(8,128)(2,1)S(1)}, bf16[256,256]{1,0:T(8,128)(2,1)S(1)}, u32[]{:S(2)}, u32[]{:S(2)}) %collective-permute-start.8) | collective-permute-done | bytes 131104 | tf_op jit(solution)/shard_map/ppermute | solution.py:415
  29.7 2.5 %collective-permute-done.6.got_d = bf16[256,256]{1,0:T(8,128)(2,1)S(1)} collective-permute-done((bf16[256,256]{1,0:T(8,128)(2,1)S(1)}, bf16[256,256]{1,0:T(8,128)(2,1)S(1)}, u32[]{:S(2)}, u32[]{:S(2)}) %collective-permute-start.6) | collective-permute-done | bytes 131104 | tf_op jit(solution)/shard_map/ppermute | solution.py:431
  32.2 0.0 copy-done.1
  32.2 1.4 %shard_map.73 = bf16[256,1024]{1,0:T(8,128)(2,1)} custom-call(f32[2,256,256]{2,1,0:T(8,128)S(1)} %get-tuple-element.33.mixed, bf16[256,256]{1,0:T(8,128)(2,1)S(1)} %collective-permute-done.6.got_d, bf16[256,256]{1,0:T(8,128)(2,1)S(1)} %add.103.got_eg, bf16[2,256,256]{2,1,0:T(8,128)(2,1)S(1)} %get-tuple-element.35.gate, ...), custom_call_target="tpu_custom_call" | custom-call | flops 256 | tf_op jit(solution)/shard_map/pallas_call | solution.py:320
  (5 shorter events, 0.1 us)
Async XLA Ops:
  0.9 6.6 %collective-permute-start.1 = (bf16[256,256]{1,0:T(8,128)(2,1)S(1)}, bf16[256,256]{1,0:T(8,128)(2,1)S(1)}, u32[]{:S(2)}, u32[]{:S(2)}) collective-permute-start(bf16[256,256]{1,0:T(8,128)(2,1)S(1)} %dynamic-slice_bitcast_fusion.3), channel_id=1, source_target_pairs={{0,4},{2,6},{4,0},{6,2},{1,5},{3,7},{5,1},{7,3},{8,12},{10,14},{12... | collective-permute-start | bytes 393224 | tf_op jit(solution)/shard_map/ppermute | solution.py:343
  3.5 4.0 %collective-permute-start.2 = (bf16[256,256]{1,0:T(8,128)(2,1)S(1)}, bf16[256,256]{1,0:T(8,128)(2,1)S(1)}, u32[]{:S(2)}, u32[]{:S(2)}) collective-permute-start(bf16[256,256]{1,0:T(8,128)(2,1)S(1)} %get-tuple-element.47), channel_id=1, source_target_pairs={{0,2},{2,0},{4,6},{6,4},{1,3},{3,1},{5,7},{7,5},{8,10},{10,8},{12,... | collective-permute-start | bytes 393224 | tf_op jit(solution)/shard_map/ppermute | solution.py:343
  3.6 5.3 %collective-permute-start = (bf16[256,256]{1,0:T(8,128)(2,1)S(1)}, bf16[256,256]{1,0:T(8,128)(2,1)S(1)}, u32[]{:S(2)}, u32[]{:S(2)}) collective-permute-start(bf16[256,256]{1,0:T(8,128)(2,1)S(1)} %get-tuple-element.48), channel_id=1, source_target_pairs={{0,6},{2,4},{4,2},{6,0},{1,7},{3,5},{5,3},{7,1},{8,14},{10,12},{12... | collective-permute-start | bytes 393224 | tf_op jit(solution)/shard_map/ppermute | solution.py:343
  4.3 2.7 %copy-start.2 = (s32[256]{0:T(256)S(1)}, s32[256]{0:T(256)}, u32[]{:S(2)}) copy-start(s32[256]{0:T(256)} %param.11) | copy-start | bytes 3076
  4.3 2.7 %copy-start.3 = (s32[1,4]{1,0:T(1,128)S(1)}, s32[1,4]{1,0:T(1,128)}, u32[]{:S(2)}) copy-start(s32[1,4]{1,0:T(1,128)} %counts.1) | copy-start | bytes 52
  7.0 1.9 %copy-start = (bf16[1024,1024]{1,0:T(8,128)(2,1)S(1)}, bf16[1024,1024]{1,0:T(8,128)(2,1)}, u32[]{:S(2)}) copy-start(bf16[1024,1024]{1,0:T(8,128)(2,1)} %w_in.1) | copy-start | bytes 6291460
  10.3 10.4 %collective-permute-start.4 = (bf16[264,512]{1,0:T(8,128)(2,1)S(1)}, bf16[264,512]{1,0:T(8,128)(2,1)S(1)}, u32[]{:S(2)}, u32[]{:S(2)}) collective-permute-start(bf16[264,512]{1,0:T(8,128)(2,1)S(1)} %get-tuple-element.23.send_b), channel_id=1, source_target_pairs={{0,8},{8,16},{16,24},{24,0},{1,9},{9,17},{17,25},{25,1},{2,10},{10... | collective-permute-start | bytes 811016 | tf_op jit(solution)/shard_map/ppermute | solution.py:375
  11.0 9.6 %collective-permute-start.7 = (bf16[264,256]{1,0:T(8,128)(2,1)S(1)}, bf16[264,256]{1,0:T(8,128)(2,1)S(1)}, u32[]{:S(2)}, u32[]{:S(2)}) collective-permute-start(bf16[264,256]{1,0:T(8,128)(2,1)S(1)} %get-tuple-element.34), channel_id=1, source_target_pairs={{24,8},{8,0},{25,9},{9,1},{26,10},{10,2},{27,11},{11,3},{28,12},{1... | collective-permute-start | bytes 405512 | tf_op jit(solution)/shard_map/ppermute | solution.py:383
  15.1 8.1 %collective-permute-start.3 = (bf16[264,512]{1,0:T(8,128)(2,1)S(1)}, bf16[264,512]{1,0:T(8,128)(2,1)S(1)}, u32[]{:S(2)}, u32[]{:S(2)}) collective-permute-start(bf16[264,512]{1,0:T(8,128)(2,1)S(1)} %get-tuple-element.26.send_a), channel_id=1, source_target_pairs={{0,16},{1,17},{2,18},{3,19},{4,20},{5,21},{6,22},{7,23}} | collective-permute-start | bytes 811016 | tf_op jit(solution)/shard_map/ppermute | solution.py:395
  15.8 6.4 %collective-permute-start.9 = (bf16[264,256]{1,0:T(8,128)(2,1)S(1)}, bf16[264,256]{1,0:T(8,128)(2,1)S(1)}, u32[]{:S(2)}, u32[]{:S(2)}) collective-permute-start(bf16[264,256]{1,0:T(8,128)(2,1)S(1)} %get-tuple-element.25.send_c), channel_id=1, source_target_pairs={{16,8},{17,9},{18,10},{19,11},{20,12},{21,13},{22,14},{23,15}} | collective-permute-start | bytes 405512 | tf_op jit(solution)/shard_map/ppermute | solution.py:396
  16.5 6.7 %collective-permute-start.5 = (bf16[264,256]{1,0:T(8,128)(2,1)S(1)}, bf16[264,256]{1,0:T(8,128)(2,1)S(1)}, u32[]{:S(2)}, u32[]{:S(2)}) collective-permute-start(bf16[264,256]{1,0:T(8,128)(2,1)S(1)} %get-tuple-element.25.send_c), channel_id=1, source_target_pairs={{24,16},{25,17},{26,18},{27,19},{28,20},{29,21},{30,22},{31,23}} | collective-permute-start | bytes 405512 | tf_op jit(solution)/shard_map/ppermute | solution.py:397
  20.8 11.4 %copy-start.1 = (bf16[512,1024]{1,0:T(8,128)(2,1)S(1)}, bf16[512,1024]{1,0:T(8,128)(2,1)}, u32[]{:S(2)}) copy-start(bf16[512,1024]{1,0:T(8,128)(2,1)} %w_out.1) | copy-start | bytes 3145732
  20.8 8.9 %collective-permute-start.8 = (bf16[256,256]{1,0:T(8,128)(2,1)S(1)}, bf16[256,256]{1,0:T(8,128)(2,1)S(1)}, u32[]{:S(2)}, u32[]{:S(2)}) collective-permute-start(bf16[256,256]{1,0:T(8,128)(2,1)S(1)} %shard_map.71.send_e), channel_id=1, source_target_pairs={{8,24},{0,8},{9,25},{1,9},{10,26},{2,10},{11,27},{3,11},{12,28},{4... | collective-permute-start | bytes 393224 | tf_op jit(solution)/shard_map/ppermute | solution.py:415
  22.2 4.3 %collective-permute-start.10 = (bf16[256,256]{1,0:T(8,128)(2,1)S(1)}, bf16[256,256]{1,0:T(8,128)(2,1)S(1)}, u32[]{:S(2)}, u32[]{:S(2)}) collective-permute-start(bf16[256,256]{1,0:T(8,128)(2,1)S(1)} %shard_map.72), channel_id=1, source_target_pairs={{8,16},{9,17},{10,18},{11,19},{12,20},{13,21},{14,22},{15,23}} | collective-permute-start | bytes 393224 | tf_op jit(solution)/shard_map/ppermute | solution.py:423
  23.2 8.9 %collective-permute-start.6 = (bf16[256,256]{1,0:T(8,128)(2,1)S(1)}, bf16[256,256]{1,0:T(8,128)(2,1)S(1)}, u32[]{:S(2)}, u32[]{:S(2)}) collective-permute-start(bf16[256,256]{1,0:T(8,128)(2,1)S(1)} %shard_map.70), channel_id=1, source_target_pairs={{16,24},{17,25},{18,26},{19,27},{20,28},{21,29},{22,30},{23,31}} | collective-permute-start | bytes 393224 | tf_op jit(solution)/shard_map/ppermute | solution.py:431

commit v7 on v6

--- a/solution.py
+++ b/solution.py
@@ -110,10 +110,10 @@
     rows = users.shape[1]
     owners = counts.shape[1]
     position = lax.broadcasted_iota(jnp.int32, (1, rows), 1)
-    end = counts[0, 0]
+    end = counts[:, :1]
     owner = (position >= end).astype(jnp.int32)
     for d in range(1, owners - 1):
-        end = end + counts[0, d]
+        end = end + counts[:, d : d + 1]
         owner = owner + (position >= end).astype(jnp.int32)
     seg_out[...] = jnp.broadcast_to((owner + owners * users[...]).astype(F32), seg_out.shape)
 
@@ -128,48 +128,128 @@
     return silu_of(jnp.dot(normed[...], weight[...], preferred_element_type=F32)).astype(BF16)
 
 
+def is_upward():
+    return lax.axis_index("col") % 2 == 0
+
+
+def put_keys(normed, w_key, w_value, out):
+    rows = normed.shape[0]
+    group = w_key.shape[1]
+    out[:rows, :group] = silu_dot(normed, w_key)
+    out[:rows, group : 2 * group] = silu_dot(normed, w_value)
+
+
+def put_query(normed, w_query, out):
+    rows = normed.shape[0]
+    group = w_query.shape[1]
+    out[:rows, :group] = silu_dot(normed, w_query)
+    out[:rows, group:] = jnp.zeros((rows, group), BF16)
+
+
+def add_pieces(pieces, w_in, total):
+    for shift, piece in pieces.items():
+        width = piece.shape[1]
+        start = pl.multiple_of((lax.axis_index("col") ^ shift) * width, width)
+        term = jnp.dot(piece[...], w_in[pl.ds(start, width), :], preferred_element_type=F32)
+        total = term if total is None else total + term
+    return total
+
+
+def partial_kernel(part2, part1, own, w_in, partial):
+    partial[...] = add_pieces({0: own, 1: part1, 2: part2}, w_in, None)
+
+
 def project_first_kernel(
-    part3, part2, part1, own, w_in, w_key, w_value, seg, hidden_out, normed, send_b
+    part3, partial, w_in, w_key, w_value, w_query, seg, hidden_out, normed, send_1
 ):
-    col_at = lax.axis_index("col")
-    rows, piece = own.shape
-    group = w_key.shape[1]
-    total = None
-    for shift, part in enumerate((own, part1, part2, part3)):
-        start = pl.multiple_of((col_at ^ shift) * piece, piece)
-        term = jnp.dot(part[...], w_in[pl.ds(start, piece), :], preferred_element_type=F32)
-        total = term if total is None else total + term
+    total = add_pieces({3: part3}, w_in, partial[...])
     hidden = total.astype(BF16)
     hidden_out[...] = hidden
     normed[...] = layer_norm(hidden.astype(F32)).astype(BF16)
-    send_b[:rows, :group] = silu_dot(normed, w_key)
-    send_b[:rows, group:] = silu_dot(normed, w_value)
-    put_seg(send_b, seg[...])
-
-
-def project_query_kernel(normed, w_far, w_sent, seg, send_c, send_f):
-    rows = normed.shape[0]
-    for weight, ref in ((w_far, send_c), (w_sent, send_f)):
-        ref[:rows, :] = silu_dot(normed, weight)
-        put_seg(ref, seg[...])
-
-
-def project_near_kernel(
-    send_b, send_c, seg, normed, w_query, w_near, w_far, w_key, w_value,
-    send_a, mixed_out, query_near, gate_out,
+    put_seg(send_1, seg[...])
+
+    @pl.when(is_upward())
+    def _():
+        put_keys(normed, w_key, w_value, send_1)
+
+    @pl.when(~is_upward())
+    def _():
+        put_query(normed, w_query, send_1)
+
+
+def project_second_kernel(
+    normed, send_1, w_key, w_value, w_query, seg, send_2, far_keys, far_query
 ):
     rows = normed.shape[0]
-    group = w_key.shape[1]
-    send_a[:rows, :group] = silu_dot(normed, w_key)
-    send_a[:rows, group:] = silu_dot(normed, w_value)
+    group = w_query.shape[1]
+    put_seg(send_2, seg[...])
+
+    @pl.when(is_upward())
+    def _():
+        put_query(normed, w_query, send_2)
+        far_query[...] = send_2[:rows, :group]
+        far_keys[...] = send_1[:rows, :]
+
+    @pl.when(~is_upward())
+    def _():
+        put_keys(normed, w_key, w_value, send_2)
+        far_query[...] = send_1[:rows, :group]
+        far_keys[...] = send_2[:rows, :]
+
+
+def sort_first_kernel(got_1, got_b, got_c):
+    @pl.when(is_upward())
+    def _():
+        got_b[...] = got_1[...]
+
+    @pl.when(~is_upward())
+    def _():
+        got_c[...] = got_1[:, : got_c.shape[1]]
+
+
+def sort_second_kernel(got_2, up_in, down_in, got_b, got_c):
+    @pl.when(is_upward())
+    def _():
+        got_c[...] = got_2[:, : got_c.shape[1]]
+
+    @pl.when(~is_upward())
+    def _():
+        got_b[...] = got_2[...]
+
+
+def project_query_kernel(normed, w_near, seg, send_2, send_f):
+    rows = normed.shape[0]
+    send_f[:rows, :] = silu_dot(normed, w_near)
+    put_seg(send_f, seg[...])
+
+
+def attend_own(send_a, send_f, far_keys, far_query, seg, normed, w_near, w_far, mixed, gate):
+    rows, group = mixed.shape[1:]
+    seg_row = seg[0:1, :]
+    allowed = (seg_column(seg_row) == seg_row) & (
+        lax.broadcasted_iota(jnp.int32, (rows, rows), 1)
+        <= lax.broadcasted_iota(jnp.int32, (rows, rows), 0)
+    )
+    for side, (query, key_value) in enumerate(((send_f, send_a), (far_query, far_keys))):
+        for lo in range(0, group, HEAD_DIM):
+            hi = lo + HEAD_DIM
+            weights = head_weights(query[:rows, lo:hi], key_value[:rows, lo:hi], allowed)
+            mixed[side, :, lo:hi] = jnp.dot(
+                weights, key_value[:rows, group + lo : group + hi], preferred_element_type=F32
+            )
+    gate[0] = silu_dot(normed, w_near)
+    gate[1] = silu_dot(normed, w_far)
+
+
+def project_near_kernel(
+    send_f, far_keys, far_query, seg, normed, w_near, w_far, w_key, w_value, send_a, mixed, gate
+):
+    put_keys(normed, w_key, w_value, send_a)
     put_seg(send_a, seg[...])
 
-    @pl.when(batch_index() == 0)
-    def _():
-        attend_own(
-            send_a, send_b, send_c, seg, normed, (w_query, w_near, w_far),
-            mixed_out, query_near, gate_out,
-        )
+    @pl.when(~is_last())
+    def _():
+        attend_own(send_a, send_f, far_keys, far_query, seg, normed, w_near, w_far, mixed, gate)
 
 
 def seg_row_of(ref, rows):
@@ -204,65 +284,42 @@
         )
 
 
-def attend_own(send_a, send_b, send_c, seg, normed, weights, mixed_out, query_near, gate_out):
-    rows, group = mixed_out.shape[1:]
-    w_query, w_near, w_far = weights
-    seg_row = seg[0:1, :]
-    allowed = (seg_column(seg_row) == seg_row) & (
-        lax.broadcasted_iota(jnp.int32, (rows, rows), 1)
-        <= lax.broadcasted_iota(jnp.int32, (rows, rows), 0)
-    )
-    query_near[...] = silu_dot(normed, w_query)
-    for side, (query, key_value) in enumerate(((query_near, send_a), (send_c, send_b))):
-        for lo in range(0, group, HEAD_DIM):
-            hi = lo + HEAD_DIM
-            weights = head_weights(query[:rows, lo:hi], key_value[:rows, lo:hi], allowed)
-            mixed_out[side, :, lo:hi] = jnp.dot(
-                weights, key_value[:rows, group + lo : group + hi], preferred_element_type=F32
-            )
-    gate_out[0] = silu_dot(normed, w_near)
-    gate_out[1] = silu_dot(normed, w_far)
-
-
-def own_kernel(
-    send_a, send_b, send_c, seg, normed, w_query, w_near, w_far,
-    mixed_in, query_in, gate_in, mixed, query_near, gate,
-):
-    @pl.when((batch_index() != 0) & ~is_last())
-    def _():
-        attend_own(
-            send_a, send_b, send_c, seg, normed, (w_query, w_near, w_far), mixed, query_near, gate
-        )
-
-
-def far_g_kernel(got_b, send_e, send_a, got_c, send_g):
+def early_kernel(got_b, got_c, send_a, early_1, early_2):
     @pl.when(batch_index() == 1)
     def _():
-        add_blocks(got_c, [send_a, got_b], send_g)
+        add_blocks(got_c, [send_a, got_b], early_1)
+
+    @pl.when(batch_index() == 2)
+    def _():
+        add_blocks(got_c, [send_a, got_b], early_2)
+
+
+def far_kernel(got_b, got_c, got_f, send_a, early_1, send_e, send_g):
+    @pl.when(batch_index() == 0)
+    def _():
+        add_blocks(got_c, [send_a], send_e)
+
+    @pl.when(batch_index() == 1)
+    def _():
+        add_blocks(got_f, [send_a, got_b], send_e)
+        send_g[...] = early_1[...]
+
+    @pl.when(batch_index() > 1)
+    def _():
+        send_e[...] = jnp.zeros_like(send_e)
 
     @pl.when(batch_index() != 1)
     def _():
         send_g[...] = jnp.zeros_like(send_g)
 
 
-def far_e_kernel(got_b, send_a, mixed, got_f, send_e):
-    @pl.when(batch_index() == 0)
-    def _():
-        add_blocks(got_f, [send_a], send_e)
-
-    @pl.when(batch_index() == 1)
-    def _():
-        add_blocks(got_f, [send_a, got_b], send_e)
-
-    @pl.when(batch_index() > 1)
-    def _():
-        send_e[...] = jnp.zeros_like(send_e)
-
-
-def far_d_kernel(got_b, send_a, got_h, got_a, send_d):
+def far_d_kernel(early_2, got_c, got_a, send_d, total):
     @pl.when(batch_index() == 2)
     def _():
-        add_blocks(got_h, [send_a, got_b, got_a], send_d)
+        rows = total.shape[0]
+        total[...] = early_2[...]
+        add_near(got_c, seg_column(seg_row_of(got_c, rows)), got_a, total)
+        send_d[...] = total[...].astype(BF16)
 
     @pl.when(batch_index() != 2)
     def _():
@@ -270,24 +327,22 @@
 
 
 def near_kernel(
-    got_a, got_b, send_a, send_b, send_c, seg, normed, w_query, w_near, w_far,
-    mixed_in, query_in, gate_in, mixed, query_near, gate,
+    got_a, got_b, send_a, send_f, far_keys, far_query, seg, normed, w_near, w_far,
+    mixed_in, gate_in, mixed, gate,
 ):
     column = seg_column(seg[0:1, :])
 
     @pl.when(is_last())
     def _():
-        attend_own(
-            send_a, send_b, send_c, seg, normed, (w_query, w_near, w_far), mixed, query_near, gate
-        )
+        attend_own(send_a, send_f, far_keys, far_query, seg, normed, w_near, w_far, mixed, gate)
 
     @pl.when(batch_index() > 0)
     def _():
-        add_near(query_near, column, got_b, mixed.at[0])
+        add_near(send_f, column, got_b, mixed.at[0])
 
     @pl.when(batch_index() == 2)
     def _():
-        add_near(query_near, column, got_a, mixed.at[0])
+        add_near(send_f, column, got_a, mixed.at[0])
 
 
 def finish_kernel(mixed, got_d, got_eg, gate, hidden, w_out, out):
@@ -313,7 +368,6 @@
 
 
 VMEM = pl.BlockSpec(memory_space=pltpu.VMEM)
-SMEM = pl.BlockSpec(memory_space=pltpu.SMEM)
 
 
 def call(kernel, in_specs, outs, operands, flops, scratch=(), limit=32 << 20, aliases=()):
@@ -354,10 +408,10 @@
     tall = rows + SEG_ROWS
     (seg,) = call(
         segments_kernel,
-        [SMEM, VMEM],
+        [VMEM] * 2,
         [((SEG_ROWS, rows), F32)],
         (owner_counts, user_index.reshape(1, rows)),
-        2 * rows * features * (features + 4 * width),
+        1 << 30,
     )
     near = batch_at % 2
     far = 1 - near
@@ -365,26 +419,52 @@
     def weight_of(block, index):
         return lax.dynamic_slice_in_dim(joined_weight, block * width + index * group, group, 1)
 
-    hidden, normed, send_b = call(
+    last = lax.axis_size("batch") - 1
+
+    def up_and_down(block, parity):
+        perm = []
+        for at in range(cols):
+            step = 1 if at % 2 == parity else -1
+            for source in range(last + 1):
+                inside = 0 <= source + step <= last
+                target = (source + step, at) if inside else (source, at ^ 1)
+                perm.append((source * cols + at, target[0] * cols + target[1]))
+        return lax.ppermute(block, ("batch", "col"), perm)
+
+    far_weights = (weight_of(3, far), weight_of(1, far), weight_of(2, far))
+    (partial,) = call(
+        partial_kernel,
+        [VMEM] * 4,
+        [((rows, features), F32)],
+        (parts[2], parts[1], parts[0], input_weight),
+        rows,
+    )
+    hidden, normed, send_1 = call(
         project_first_kernel,
-        [VMEM] * 8,
+        [VMEM] * 7,
         [((rows, features), BF16), ((rows, features), BF16), ((tall, 2 * group), BF16)],
-        (*parts[::-1], input_weight, weight_of(3, far), weight_of(1, far), seg),
+        (parts[3], partial, input_weight, *far_weights, seg),
         2 * rows * features * (features + 2 * group),
     )
-    got_b = lax.ppermute(send_b, "batch", [(0, 1), (1, 2), (2, 3), (3, 0)])
-    send_c, send_f = call(
+    got_1 = up_and_down(send_1, 0)
+    send_2, far_keys, far_query = call(
+        project_second_kernel,
+        [VMEM] * 6,
+        [((tall, 2 * group), BF16), ((rows, 2 * group), BF16), ((rows, group), BF16)],
+        (normed, send_1, *far_weights, seg),
+        2 * rows * features * 2 * group,
+    )
+    got_2 = up_and_down(send_2, 1)
+    (send_f,) = call(
         project_query_kernel,
         [VMEM] * 4,
-        [((tall, group), BF16)] * 2,
-        (normed, weight_of(2, far), weight_of(2, jnp.where(batch_at == 1, far, near)), seg),
-        2 * rows * features * 2 * group,
-    )
-    got_f = lax.ppermute(send_f, "batch", [(3, 1), (1, 0)])
-    own_inputs = (
-        send_b, send_c, seg, normed, weight_of(2, near), weight_of(0, near), weight_of(0, far),
-    )
-    own_outs = [((2, rows, group), F32), ((rows, group), BF16), ((2, rows, group), BF16)]
+        [((tall, group), BF16)],
+        (normed, weight_of(2, near), seg, send_2),
+        2 * rows * features * group,
+    )
+    got_f = lax.ppermute(send_f, "batch", [(3, 1)])
+    own_inputs = (send_f, far_keys, far_query, seg, normed, weight_of(0, near), weight_of(0, far))
+    own_outs = [((2, rows, group), F32), ((2, rows, group), BF16)]
     send_a, *own = call(
         project_near_kernel,
         [VMEM] * 9,
@@ -393,49 +473,44 @@
         2 * rows * features * 2 * group,
     )
     got_a = lax.ppermute(send_a, "batch", [(0, 2)])
-    got_c = lax.ppermute(send_c, "batch", [(2, 1)])
-    got_h = lax.ppermute(send_c, "batch", [(3, 2)])
-    pair_flops = 4 * rows * rows * group
-    own = call(
-        own_kernel,
-        [VMEM] * 11,
-        own_outs,
-        (send_a, *own_inputs, *own),
-        2 * pair_flops + 2 * rows * features * width,
-        aliases={8: 0, 9: 1, 10: 2},
-    )
-    mixed = own[0]
-    (send_e,) = call(
-        far_e_kernel,
-        [VMEM] * 4,
-        [((rows, group), BF16)],
-        (got_b, send_a, mixed, got_f),
+    sorted_outs = [((tall, 2 * group), BF16), ((tall, group), BF16)]
+    got_b, got_c = call(sort_first_kernel, [VMEM], sorted_outs, (got_1,), 1 << 30)
+    got_b, got_c = call(
+        sort_second_kernel, [VMEM] * 3, sorted_outs, (got_2, got_b, got_c), rows,
+        aliases={1: 0, 2: 1},
+    )
+    early_1, early_2 = call(
+        early_kernel,
+        [VMEM] * 3,
+        [((rows, group), BF16), ((rows, group), F32)],
+        (got_b, got_c, send_a),
         1 << 30,
     )
+    send_e, send_g = call(
+        far_kernel,
+        [VMEM] * 5,
+        [((rows, group), BF16)] * 2,
+        (got_b, got_c, got_f, send_a, early_1),
+        1 << 30,
+    )
     got_e = lax.ppermute(send_e, "batch", [(1, 3), (0, 1)])
-    (send_g,) = call(
-        far_g_kernel,
-        [VMEM] * 4,
-        [((rows, group), BF16)],
-        (got_b, send_e, send_a, got_c),
-        1 << 30,
-    )
     got_g = lax.ppermute(send_g, "batch", [(1, 2)])
     (send_d,) = call(
         far_d_kernel,
-        [VMEM] * 4,
+        [VMEM] * 3,
         [((rows, group), BF16)],
-        (got_b, send_a, got_h, got_a),
+        (early_2, got_c, got_a),
         rows,
+        [pltpu.VMEM((rows, group), F32)],
     )
     got_d = lax.ppermute(send_d, "batch", [(2, 3)])
-    mixed, _, gate = call(
+    mixed, gate = call(
         near_kernel,
-        [VMEM] * 13,
+        [VMEM] * 12,
         own_outs,
         (got_a, got_b, send_a, *own_inputs, *own),
         rows,
-        aliases={10: 0, 11: 1, 12: 2},
+        aliases={10: 0, 11: 1},
     )
     (out,) = call(
         finish_kernel,

time: 34 us -> 33.4 us (0.982)
  starting transfers between devices: 15.1 us -> 10.6 us
  waiting for transfers between devices: 7.19 us -> 11.5 us
  Pallas kernels: 6.37 us -> 6 us
    ppermute x4 -> x3, starting transfers between devices: 8.74 us -> 4.31 us  [the longest x1 2.25 us: chain_plan(): got_f = lax.ppermute(send_f, 'batch', [(3, 1)])]
    ppermute x4 -> x3, waiting for transfers between devices: 0.29 us -> 3.29 us  [the longest x2 3.18 us: up_and_down(): return lax.ppermute(block, ('batch', 'col'), perm)]
    ppermute x1, waiting for transfers between devices: 3.1 us -> 5.32 us  [chain_plan(): got_e = lax.ppermute(send_e, 'batch', [(1, 3), (0, 1)])]
    ppermute x1, waiting for transfers between devices: 2.46 us -> 1.81 us  [chain_plan(): got_d = lax.ppermute(send_d, 'batch', [(2, 3)])]
    pallas_call x10 -> x13, Pallas kernels: 6.37 us -> 6 us  [call(): pl.pallas_call(kernel, out_shape=[jax.ShapeDtypeStruct(shape, dtype) for...]
  transfers between devices with their start and end apart: 11 -> 10, of which waited for: 4 -> 5; matrix products, arithmetic and copies ran while one was open for 11% -> 11% of each run, Pallas kernels for 11% -> 11%
where the time goes in v7:
time: 33.4 us; the launch traced here: 33.1 us
  waiting for transfers between devices  11.5 us (34%)
  starting transfers between devices  10.6 us (32%)
  Pallas kernels  6 us (18%)
  local copies, waits for them, and re-layouts  4.75 us (14%)
    pallas_call x13, Pallas kernels, call(): pl.pallas_call(kernel, out_shape=[jax.ShapeDtypeStruct(shape, dtype) for...  6 us
    ppermute x1, waiting for transfers between devices, chain_plan(): got_e = lax.ppermute(send_e, 'batch', [(1, 3), (0, 1)])  5.32 us
    ppermute x2, waiting for transfers between devices, up_and_down(): return lax.ppermute(block, ('batch', 'col'), perm)  3.18 us
    dynamic_slice x1, local copies, waits for them, and re-layouts, weight_of(): lax.dynamic_slice_in_dim(joined_weight, block * width + index * group, gr...  2.63 us
    ppermute x3, starting transfers between devices, exchange(): return lax.ppermute(block, 'col', [(i, i ^ shift) for i in range(cols)])  2.28 us
    ppermute x1, starting transfers between devices, chain_plan(): got_f = lax.ppermute(send_f, 'batch', [(3, 1)])  2.25 us
    ppermute x2, starting transfers between devices, up_and_down(): return lax.ppermute(block, ('batch', 'col'), perm)  2.06 us
    squeeze x2, local copies, waits for them, and re-layouts, piece(): return lax.dynamic_index_in_dim(source, col_at ^ shift, 0, keepdims=False)  1.97 us
  transfers between devices with their start and end apart: 10, of which 5 were waited for; matrix products, arithmetic and copies ran while one was open for 11% of the time, Pallas kernels for 11%

profile of v7, /device:TPU:24, one launch (start us, length us, event | category | flops | bytes accessed | tf_op | source)
XLA Modules:
  0.0 33.1 jit_solution(2397299730420536865)
XLA Ops:
  0.0 0.9 %dynamic-slice_bitcast_fusion.3 = bf16[256,256]{1,0:T(8,128)(2,1)S(1)} fusion(bf16[4,256,256]{2,1,0:T(8,128)(2,1)} %bitcast.11, s32[]{:T(128)S(6)} %select_n.44), kind=kLoop, calls=%fused_computation.3 | loop fusion | bytes 262148 | tf_op jit(solution)/shard_map/jit(dynamic_index_in_dim)/squeeze | solution.py:394
  0.9 1.6 %collective-permute-start.1 = (bf16[256,256]{1,0:T(8,128)(2,1)S(1)}, bf16[256,256]{1,0:T(8,128)(2,1)S(1)}, u32[]{:S(2)}, u32[]{:S(2)}) collective-permute-start(bf16[256,256]{1,0:T(8,128)(2,1)S(1)} %dynamic-slice_bitcast_fusion.3), channel_id=1, source_target_pairs={{0,4},{2,6},{4,0},{6,2},{1,5},{3,7},{5,1},{7,3},{8,12},{10,14},{12... | collective-permute-start | bytes 393224 | tf_op jit(solution)/shard_map/ppermute | solution.py:397
  2.5 1.1 %dynamic-slice_bitcast_fusion = (bf16[256,256]{1,0:T(8,128)(2,1)S(1)}, bf16[256,256]{1,0:T(8,128)(2,1)S(1)}, bf16[256,256]{1,0:T(8,128)(2,1)S(1)}) fusion(bf16[4,256,256]{2,1,0:T(8,128)(2,1)} %bitcast.12, s32[]{:T(128)S(6)} %select_n.47, s32[]{:T(128)S(6)} %select_n.46, s32[]{:T(128)S(6)} %select_n.45), kind=kLoop, calls=%fused_computation | loop fusion | bytes 786444 | tf_op jit(solution)/shard_map/jit(dynamic_index_in_dim)/squeeze | solution.py:394
  3.5 0.1 collective-permute-start.2
  3.6 0.7 %collective-permute-start = (bf16[256,256]{1,0:T(8,128)(2,1)S(1)}, bf16[256,256]{1,0:T(8,128)(2,1)S(1)}, u32[]{:S(2)}, u32[]{:S(2)}) collective-permute-start(bf16[256,256]{1,0:T(8,128)(2,1)S(1)} %get-tuple-element.57), channel_id=1, source_target_pairs={{0,6},{2,4},{4,2},{6,0},{1,7},{3,5},{5,3},{7,1},{8,14},{10,12},{12... | collective-permute-start | bytes 393224 | tf_op jit(solution)/shard_map/ppermute | solution.py:397
  4.3 0.0 copy-start.2
  4.3 0.0 copy-start.3
  4.3 0.0 copy-start
  4.3 2.6 %constant_dynamic-slice_fusion = (bf16[1024,256]{1,0:T(8,128)(2,1)S(1)}, bf16[1024,256]{1,0:T(8,128)(2,1)S(1)}, bf16[1024,256]{1,0:T(8,128)(2,1)S(1)}, bf16[1024...) fusion(bf16[1024,2048]{1,0:T(8,128)(2,1)} %param.8, ...), kind=kLoop, calls=%fused_computation.4 | loop fusion | bytes 8388640 | tf_op jit(solution)/shard_map/dynamic_slice | solution.py:420
  6.9 0.0 copy-done.2
  6.9 0.0 copy-done.3
  6.9 0.1 shard_map.65.seg
  7.1 0.0 collective-permute-done.1.part2
  7.1 0.0 collective-permute-done.2.part1
  7.1 0.1 copy-done
  7.2 0.6 %shard_map.64.partial = f32[256,1024]{1,0:T(8,128)S(1)} custom-call(bf16[256,256]{1,0:T(8,128)(2,1)S(1)} %collective-permute-done.1.part2, bf16[256,256]{1,0:T(8,128)(2,1)S(1)} %collective-permute-done.2.part1, bf16[256,256]{1,0:T(8,128)(2,1)S(1)} %get-tuple-element.55.own, bf16[1024,1024]{1,0:T(8,128)(2,1)S(1)} %copy-done), custom_call_target="tpu_custom_call" | custom-call | flops 256 | tf_op jit(solution)/shard_map/pallas_call | solution.py:374
  7.8 1.1 %collective-permute-done.part3 = bf16[256,256]{1,0:T(8,128)(2,1)S(1)} collective-permute-done((bf16[256,256]{1,0:T(8,128)(2,1)S(1)}, bf16[256,256]{1,0:T(8,128)(2,1)S(1)}, u32[]{:S(2)}, u32[]{:S(2)}) %collective-permute-start) | collective-permute-done | bytes 131104 | tf_op jit(solution)/shard_map/ppermute | solution.py:397
  8.9 1.0 %shard_map.66 = (bf16[256,1024]{1,0:T(8,128)(2,1)S(1)}, bf16[256,1024]{1,0:T(8,128)(2,1)S(1)}, bf16[264,512]{1,0:T(8,128)(2,1)S(1)}) custom-call(bf16[256,256]{1,0:T(8,128)(2,1)S(1)} %collective-permute-done.part3, f32[256,1024]{1,0:T(8,128)S(1)} %shard_map.64.partial, bf16[1024,1024]{1,0:T(8,128)(2,1)S(1)} %copy-done, ...), custom_call_target="tpu_custom_call" | custom-call | flops 805306368 | tf_op jit(solution)/shard_map/pallas_call | solution.py:374
  9.9 0.3 collective-permute-start.5
  10.2 0.3 shard_map.67
  10.5 1.8 %collective-permute-start.4 = (bf16[264,512]{1,0:T(8,128)(2,1)S(1)}, bf16[264,512]{1,0:T(8,128)(2,1)S(1)}, u32[]{:S(2)}, u32[]{:S(2)}) collective-permute-start(bf16[264,512]{1,0:T(8,128)(2,1)S(1)} %get-tuple-element.30.send_2), channel_id=1, source_target_pairs={{0,2},{8,0},{16,8},{24,16},{2,10},{10,18},{18,26},{26,24},{4,6},{1... | collective-permute-start | bytes 811016 | tf_op jit(solution)/shard_map/ppermute | solution.py:432
  12.3 0.3 shard_map.68.send_f
  12.7 2.2 %collective-permute-start.7 = (bf16[264,256]{1,0:T(8,128)(2,1)S(1)}, bf16[264,256]{1,0:T(8,128)(2,1)S(1)}, u32[]{:S(2)}, u32[]{:S(2)}) collective-permute-start(bf16[264,256]{1,0:T(8,128)(2,1)S(1)} %shard_map.68.send_f), channel_id=1, source_target_pairs={{24,8},{25,9},{26,10},{27,11},{28,12},{29,13},{30,14},{31,15}} | collective-permute-start | bytes 405512 | tf_op jit(solution)/shard_map/ppermute | solution.py:465
  14.9 0.5 %shard_map.69 = (bf16[264,512]{1,0:T(8,128)(2,1)S(1)}, f32[2,256,256]{2,1,0:T(8,128)S(1)}, bf16[2,256,256]{2,1,0:T(8,128)(2,1)S(1)}) custom-call(bf16[264,256]{1,0:T(8,128)(2,1)S(1)} %shard_map.68.send_f, bf16[256,512]{1,0:T(8,128)(2,1)S(1)} %get-tuple-element.31.far_keys, bf16[256,256]{1,0:T(8,128)(2,1)S(1)} %get-tuple-element.32.far_query, ...), custom_call_target="tpu_custom_call" | custom-call | flops 268435456 | tf_op jit(solution)/shard_map/pallas_call | solution.py:374
  15.4 0.7 %collective-permute-start.3 = (bf16[264,512]{1,0:T(8,128)(2,1)S(1)}, bf16[264,512]{1,0:T(8,128)(2,1)S(1)}, u32[]{:S(2)}, u32[]{:S(2)}) collective-permute-start(bf16[264,512]{1,0:T(8,128)(2,1)S(1)} %get-tuple-element.33.send_a), channel_id=1, source_target_pairs={{0,16},{1,17},{2,18},{3,19},{4,20},{5,21},{6,22},{7,23}} | collective-permute-start | bytes 811016 | tf_op jit(solution)/shard_map/ppermute | solution.py:475
  16.1 3.2 %collective-permute-done.5.got_1 = bf16[264,512]{1,0:T(8,128)(2,1)S(1)} collective-permute-done((bf16[264,512]{1,0:T(8,128)(2,1)S(1)}, bf16[264,512]{1,0:T(8,128)(2,1)S(1)}, u32[]{:S(2)}, u32[]{:S(2)}) %collective-permute-start.5) | collective-permute-done | bytes 270368 | tf_op jit(solution)/shard_map/ppermute | solution.py:432
  19.3 0.0 collective-permute-done.4.got_2
  19.4 0.1 collective-permute-done.7.got_f
  19.5 0.0 copy-start.1
  19.5 1.4 %collective-permute-start.8 = (bf16[256,256]{1,0:T(8,128)(2,1)S(1)}, bf16[256,256]{1,0:T(8,128)(2,1)S(1)}, u32[]{:S(2)}, u32[]{:S(2)}) collective-permute-start(bf16[256,256]{1,0:T(8,128)(2,1)S(1)} %get-tuple-element.43), channel_id=1, source_target_pairs={{8,24},{0,8},{9,25},{1,9},{10,26},{2,10},{11,27},{3,11},{12,28},{4... | collective-permute-start | bytes 393224 | tf_op jit(solution)/shard_map/ppermute | solution.py:496
  20.9 0.7 %collective-permute-start.9 = (bf16[256,256]{1,0:T(8,128)(2,1)S(1)}, bf16[256,256]{1,0:T(8,128)(2,1)S(1)}, u32[]{:S(2)}, u32[]{:S(2)}) collective-permute-start(bf16[256,256]{1,0:T(8,128)(2,1)S(1)} %get-tuple-element.44), channel_id=1, source_target_pairs={{8,16},{9,17},{10,18},{11,19},{12,20},{13,21},{14,22},{15,23}} | collective-permute-start | bytes 393224 | tf_op jit(solution)/shard_map/ppermute | solution.py:497
  21.6 0.0 collective-permute-done.3.got_a
  21.6 1.3 %collective-permute-start.6 = (bf16[256,256]{1,0:T(8,128)(2,1)S(1)}, bf16[256,256]{1,0:T(8,128)(2,1)S(1)}, u32[]{:S(2)}, u32[]{:S(2)}) collective-permute-start(bf16[256,256]{1,0:T(8,128)(2,1)S(1)} %shard_map.74), channel_id=1, source_target_pairs={{16,24},{17,25},{18,26},{19,27},{20,28},{21,29},{22,30},{23,31}} | collective-permute-start | bytes 393224 | tf_op jit(solution)/shard_map/ppermute | solution.py:506
  22.9 1.6 %shard_map.72 = (f32[2,256,256]{2,1,0:T(8,128)S(1)}, bf16[2,256,256]{2,1,0:T(8,128)(2,1)S(1)}) custom-call(bf16[264,512]{1,0:T(8,128)(2,1)S(1)} %collective-permute-done.3.got_a, bf16[264,512]{1,0:T(8,128)(2,1)S(1)} %get-tuple-element.36.got_b, bf16[264,512]{1,0:T(8,128)(2,1)S(1)} %get-tuple-element.33.send_a, ...), custom_call_target="tpu_custom_call", output_to_operand_aliasing={{0}: (10, {}), {1}: (11, {})} | custom-call | flops 256 | tf_op jit(solution)/shard_map/pallas_call | solution.py:374
  24.6 5.3 %collective-permute-done.8 = bf16[256,256]{1,0:T(8,128)(2,1)S(1)} collective-permute-done((bf16[256,256]{1,0:T(8,128)(2,1)S(1)}, bf16[256,256]{1,0:T(8,128)(2,1)S(1)}, u32[]{:S(2)}, u32[]{:S(2)}) %collective-permute-start.8) | collective-permute-done | bytes 131104 | tf_op jit(solution)/shard_map/ppermute | solution.py:496
  29.9 0.0 collective-permute-done.9
  29.9 1.8 %collective-permute-done.6.got_d = bf16[256,256]{1,0:T(8,128)(2,1)S(1)} collective-permute-done((bf16[256,256]{1,0:T(8,128)(2,1)S(1)}, bf16[256,256]{1,0:T(8,128)(2,1)S(1)}, u32[]{:S(2)}, u32[]{:S(2)}) %collective-permute-start.6) | collective-permute-done | bytes 131104 | tf_op jit(solution)/shard_map/ppermute | solution.py:506
  31.7 0.0 copy-done.1
  31.7 1.4 %shard_map.76 = bf16[256,1024]{1,0:T(8,128)(2,1)} custom-call(f32[2,256,256]{2,1,0:T(8,128)S(1)} %get-tuple-element.39.mixed, bf16[256,256]{1,0:T(8,128)(2,1)S(1)} %collective-permute-done.6.got_d, bf16[256,256]{1,0:T(8,128)(2,1)S(1)} %add.93.got_eg, bf16[2,256,256]{2,1,0:T(8,128)(2,1)S(1)} %get-tuple-element.45.gate, ...), custom_call_target="tpu_custom_call" | custom-call | flops 256 | tf_op jit(solution)/shard_map/pallas_call | solution.py:374
  (6 shorter events, 0.2 us)
Async XLA Ops:
  0.9 6.2 %collective-permute-start.1 = (bf16[256,256]{1,0:T(8,128)(2,1)S(1)}, bf16[256,256]{1,0:T(8,128)(2,1)S(1)}, u32[]{:S(2)}, u32[]{:S(2)}) collective-permute-start(bf16[256,256]{1,0:T(8,128)(2,1)S(1)} %dynamic-slice_bitcast_fusion.3), channel_id=1, source_target_pairs={{0,4},{2,6},{4,0},{6,2},{1,5},{3,7},{5,1},{7,3},{8,12},{10,14},{12... | collective-permute-start | bytes 393224 | tf_op jit(solution)/shard_map/ppermute | solution.py:397
  3.5 3.5 %collective-permute-start.2 = (bf16[256,256]{1,0:T(8,128)(2,1)S(1)}, bf16[256,256]{1,0:T(8,128)(2,1)S(1)}, u32[]{:S(2)}, u32[]{:S(2)}) collective-permute-start(bf16[256,256]{1,0:T(8,128)(2,1)S(1)} %get-tuple-element.56), channel_id=1, source_target_pairs={{0,2},{2,0},{4,6},{6,4},{1,3},{3,1},{5,7},{7,5},{8,10},{10,8},{12,... | collective-permute-start | bytes 393224 | tf_op jit(solution)/shard_map/ppermute | solution.py:397
  3.6 5.3 %collective-permute-start = (bf16[256,256]{1,0:T(8,128)(2,1)S(1)}, bf16[256,256]{1,0:T(8,128)(2,1)S(1)}, u32[]{:S(2)}, u32[]{:S(2)}) collective-permute-start(bf16[256,256]{1,0:T(8,128)(2,1)S(1)} %get-tuple-element.57), channel_id=1, source_target_pairs={{0,6},{2,4},{4,2},{6,0},{1,7},{3,5},{5,3},{7,1},{8,14},{10,12},{12... | collective-permute-start | bytes 393224 | tf_op jit(solution)/shard_map/ppermute | solution.py:397
  4.3 2.6 %copy-start.2 = (s32[256]{0:T(256)S(1)}, s32[256]{0:T(256)}, u32[]{:S(2)}) copy-start(s32[256]{0:T(256)} %param.11) | copy-start | bytes 3076
  4.3 2.6 %copy-start.3 = (s32[1,4]{1,0:T(1,128)S(1)}, s32[1,4]{1,0:T(1,128)}, u32[]{:S(2)}) copy-start(s32[1,4]{1,0:T(1,128)} %counts.1) | copy-start | bytes 52
  4.3 2.9 %copy-start = (bf16[1024,1024]{1,0:T(8,128)(2,1)S(1)}, bf16[1024,1024]{1,0:T(8,128)(2,1)}, u32[]{:S(2)}) copy-start(bf16[1024,1024]{1,0:T(8,128)(2,1)} %w_in.3) | copy-start | bytes 6291460
  9.9 9.3 %collective-permute-start.5 = (bf16[264,512]{1,0:T(8,128)(2,1)S(1)}, bf16[264,512]{1,0:T(8,128)(2,1)S(1)}, u32[]{:S(2)}, u32[]{:S(2)}) collective-permute-start(bf16[264,512]{1,0:T(8,128)(2,1)S(1)} %get-tuple-element.29.send_1), channel_id=1, source_target_pairs={{0,8},{8,16},{16,24},{24,26},{2,0},{10,2},{18,10},{26,18},{4,12},{... | collective-permute-start | bytes 811016 | tf_op jit(solution)/shard_map/ppermute | solution.py:432
  10.5 8.7 %collective-permute-start.4 = (bf16[264,512]{1,0:T(8,128)(2,1)S(1)}, bf16[264,512]{1,0:T(8,128)(2,1)S(1)}, u32[]{:S(2)}, u32[]{:S(2)}) collective-permute-start(bf16[264,512]{1,0:T(8,128)(2,1)S(1)} %get-tuple-element.30.send_2), channel_id=1, source_target_pairs={{0,2},{8,0},{16,8},{24,16},{2,10},{10,18},{18,26},{26,24},{4,6},{1... | collective-permute-start | bytes 811016 | tf_op jit(solution)/shard_map/ppermute | solution.py:432
  12.7 6.8 %collective-permute-start.7 = (bf16[264,256]{1,0:T(8,128)(2,1)S(1)}, bf16[264,256]{1,0:T(8,128)(2,1)S(1)}, u32[]{:S(2)}, u32[]{:S(2)}) collective-permute-start(bf16[264,256]{1,0:T(8,128)(2,1)S(1)} %shard_map.68.send_f), channel_id=1, source_target_pairs={{24,8},{25,9},{26,10},{27,11},{28,12},{29,13},{30,14},{31,15}} | collective-permute-start | bytes 405512 | tf_op jit(solution)/shard_map/ppermute | solution.py:465
  15.4 6.2 %collective-permute-start.3 = (bf16[264,512]{1,0:T(8,128)(2,1)S(1)}, bf16[264,512]{1,0:T(8,128)(2,1)S(1)}, u32[]{:S(2)}, u32[]{:S(2)}) collective-permute-start(bf16[264,512]{1,0:T(8,128)(2,1)S(1)} %get-tuple-element.33.send_a), channel_id=1, source_target_pairs={{0,16},{1,17},{2,18},{3,19},{4,20},{5,21},{6,22},{7,23}} | collective-permute-start | bytes 811016 | tf_op jit(solution)/shard_map/ppermute | solution.py:475
  19.5 12.3 %copy-start.1 = (bf16[512,1024]{1,0:T(8,128)(2,1)S(1)}, bf16[512,1024]{1,0:T(8,128)(2,1)}, u32[]{:S(2)}) copy-start(bf16[512,1024]{1,0:T(8,128)(2,1)} %w_out.1) | copy-start | bytes 3145732
  19.5 10.4 %collective-permute-start.8 = (bf16[256,256]{1,0:T(8,128)(2,1)S(1)}, bf16[256,256]{1,0:T(8,128)(2,1)S(1)}, u32[]{:S(2)}, u32[]{:S(2)}) collective-permute-start(bf16[256,256]{1,0:T(8,128)(2,1)S(1)} %get-tuple-element.43), channel_id=1, source_target_pairs={{8,24},{0,8},{9,25},{1,9},{10,26},{2,10},{11,27},{3,11},{12,28},{4... | collective-permute-start | bytes 393224 | tf_op jit(solution)/shard_map/ppermute | solution.py:496
  20.9 9.0 %collective-permute-start.9 = (bf16[256,256]{1,0:T(8,128)(2,1)S(1)}, bf16[256,256]{1,0:T(8,128)(2,1)S(1)}, u32[]{:S(2)}, u32[]{:S(2)}) collective-permute-start(bf16[256,256]{1,0:T(8,128)(2,1)S(1)} %get-tuple-element.44), channel_id=1, source_target_pairs={{8,16},{9,17},{10,18},{11,19},{12,20},{13,21},{14,22},{15,23}} | collective-permute-start | bytes 393224 | tf_op jit(solution)/shard_map/ppermute | solution.py:497
  21.6 10.1 %collective-permute-start.6 = (bf16[256,256]{1,0:T(8,128)(2,1)S(1)}, bf16[256,256]{1,0:T(8,128)(2,1)S(1)}, u32[]{:S(2)}, u32[]{:S(2)}) collective-permute-start(bf16[256,256]{1,0:T(8,128)(2,1)S(1)} %shard_map.74), channel_id=1, source_target_pairs={{16,24},{17,25},{18,26},{19,27},{20,28},{21,29},{22,30},{23,31}} | collective-permute-start | bytes 393224 | tf_op jit(solution)/shard_map/ppermute | solution.py:506

commit v8 on v7

--- a/solution.py
+++ b/solution.py
@@ -431,6 +431,14 @@
                 perm.append((source * cols + at, target[0] * cols + target[1]))
         return lax.ppermute(block, ("batch", "col"), perm)
 
+    def closed(block, legs):
+        perm = []
+        for at in range(cols):
+            for source in range(last + 1):
+                target = (legs[source], at) if source in legs else (source, at ^ 1)
+                perm.append((source * cols + at, target[0] * cols + target[1]))
+        return lax.ppermute(block, ("batch", "col"), perm)
+
     far_weights = (weight_of(3, far), weight_of(1, far), weight_of(2, far))
     (partial,) = call(
         partial_kernel,
@@ -494,7 +502,7 @@
         1 << 30,
     )
     got_e = lax.ppermute(send_e, "batch", [(1, 3), (0, 1)])
-    got_g = lax.ppermute(send_g, "batch", [(1, 2)])
+    got_g = closed(send_g, {1: 2, 2: 1})
     (send_d,) = call(
         far_d_kernel,
         [VMEM] * 3,
@@ -503,7 +511,7 @@
         rows,
         [pltpu.VMEM((rows, group), F32)],
     )
-    got_d = lax.ppermute(send_d, "batch", [(2, 3)])
+    got_d = closed(send_d, {2: 3, 3: 2})
     mixed, gate = call(
         near_kernel,
         [VMEM] * 12,

time: 33.4 us -> 33.2 us (level)
  waiting for transfers between devices: 11.5 us -> 7.05 us
  starting transfers between devices: 10.6 us -> 14.7 us
    ppermute x2, starting transfers between devices: 1.96 us -> 6.06 us  [closed(): return lax.ppermute(block, ('batch', 'col'), perm)]
    ppermute x1, waiting for transfers between devices: 5.32 us -> 1.24 us  [chain_plan(): got_e = lax.ppermute(send_e, 'batch', [(1, 3), (0, 1)])]
    ppermute x2, waiting for transfers between devices: 1.81 us -> 1.41 us  [closed(): return lax.ppermute(block, ('batch', 'col'), perm)]
where the time goes in v8:
time: 33.2 us; the launch traced here: 32.7 us
  starting transfers between devices  14.7 us (44%)
  waiting for transfers between devices  7.05 us (21%)
  Pallas kernels  5.99 us (18%)
  local copies, waits for them, and re-layouts  4.75 us (14%)
    ppermute x2, starting transfers between devices, closed(): return lax.ppermute(block, ('batch', 'col'), perm)  6.06 us
    pallas_call x13, Pallas kernels, call(): pl.pallas_call(kernel, out_shape=[jax.ShapeDtypeStruct(shape, dtype) for...  5.99 us
    ppermute x2, waiting for transfers between devices, up_and_down(): return lax.ppermute(block, ('batch', 'col'), perm)  3.18 us
    dynamic_slice x1, local copies, waits for them, and re-layouts, weight_of(): lax.dynamic_slice_in_dim(joined_weight, block * width + index * group, gr...  2.63 us
    ppermute x3, starting transfers between devices, exchange(): return lax.ppermute(block, 'col', [(i, i ^ shift) for i in range(cols)])  2.28 us
    ppermute x1, starting transfers between devices, chain_plan(): got_f = lax.ppermute(send_f, 'batch', [(3, 1)])  2.25 us
    ppermute x2, starting transfers between devices, up_and_down(): return lax.ppermute(block, ('batch', 'col'), perm)  2.06 us
    squeeze x2, local copies, waits for them, and re-layouts, piece(): return lax.dynamic_index_in_dim(source, col_at ^ shift, 0, keepdims=False)  1.97 us
  transfers between devices with their start and end apart: 10, of which 5 were waited for; matrix products, arithmetic and copies ran while one was open for 11% of the time, Pallas kernels for 11%

profile of v8, /device:TPU:24, one launch (start us, length us, event | category | flops | bytes accessed | tf_op | source)
XLA Modules:
  0.0 32.7 jit_solution(5597097818426943239)
XLA Ops:
  0.0 0.9 %dynamic-slice_bitcast_fusion.3 = bf16[256,256]{1,0:T(8,128)(2,1)S(1)} fusion(bf16[4,256,256]{2,1,0:T(8,128)(2,1)} %bitcast.11, s32[]{:T(128)S(6)} %select_n.44), kind=kLoop, calls=%fused_computation.3 | loop fusion | bytes 262148 | tf_op jit(solution)/shard_map/jit(dynamic_index_in_dim)/squeeze | solution.py:394
  0.9 1.6 %collective-permute-start.1 = (bf16[256,256]{1,0:T(8,128)(2,1)S(1)}, bf16[256,256]{1,0:T(8,128)(2,1)S(1)}, u32[]{:S(2)}, u32[]{:S(2)}) collective-permute-start(bf16[256,256]{1,0:T(8,128)(2,1)S(1)} %dynamic-slice_bitcast_fusion.3), channel_id=1, source_target_pairs={{0,4},{2,6},{4,0},{6,2},{1,5},{3,7},{5,1},{7,3},{8,12},{10,14},{12... | collective-permute-start | bytes 393224 | tf_op jit(solution)/shard_map/ppermute | solution.py:397
  2.5 1.1 %dynamic-slice_bitcast_fusion = (bf16[256,256]{1,0:T(8,128)(2,1)S(1)}, bf16[256,256]{1,0:T(8,128)(2,1)S(1)}, bf16[256,256]{1,0:T(8,128)(2,1)S(1)}) fusion(bf16[4,256,256]{2,1,0:T(8,128)(2,1)} %bitcast.12, s32[]{:T(128)S(6)} %select_n.47, s32[]{:T(128)S(6)} %select_n.46, s32[]{:T(128)S(6)} %select_n.45), kind=kLoop, calls=%fused_computation | loop fusion | bytes 786444 | tf_op jit(solution)/shard_map/jit(dynamic_index_in_dim)/squeeze | solution.py:394
  3.5 0.1 collective-permute-start.2
  3.6 0.7 %collective-permute-start = (bf16[256,256]{1,0:T(8,128)(2,1)S(1)}, bf16[256,256]{1,0:T(8,128)(2,1)S(1)}, u32[]{:S(2)}, u32[]{:S(2)}) collective-permute-start(bf16[256,256]{1,0:T(8,128)(2,1)S(1)} %get-tuple-element.57), channel_id=1, source_target_pairs={{0,6},{2,4},{4,2},{6,0},{1,7},{3,5},{5,3},{7,1},{8,14},{10,12},{12... | collective-permute-start | bytes 393224 | tf_op jit(solution)/shard_map/ppermute | solution.py:397
  4.3 0.0 copy-start.2
  4.3 0.0 copy-start.3
  4.3 0.0 copy-start
  4.3 2.6 %constant_dynamic-slice_fusion = (bf16[1024,256]{1,0:T(8,128)(2,1)S(1)}, bf16[1024,256]{1,0:T(8,128)(2,1)S(1)}, bf16[1024,256]{1,0:T(8,128)(2,1)S(1)}, bf16[1024...) fusion(bf16[1024,2048]{1,0:T(8,128)(2,1)} %param.8, ...), kind=kLoop, calls=%fused_computation.4 | loop fusion | bytes 8388640 | tf_op jit(solution)/shard_map/dynamic_slice | solution.py:420
  6.9 0.0 copy-done.2
  6.9 0.0 copy-done.3
  6.9 0.1 shard_map.65.seg
  7.1 0.0 collective-permute-done.1.part2
  7.1 0.0 collective-permute-done.2.part1
  7.1 0.1 copy-done
  7.2 0.6 %shard_map.64.partial = f32[256,1024]{1,0:T(8,128)S(1)} custom-call(bf16[256,256]{1,0:T(8,128)(2,1)S(1)} %collective-permute-done.1.part2, bf16[256,256]{1,0:T(8,128)(2,1)S(1)} %collective-permute-done.2.part1, bf16[256,256]{1,0:T(8,128)(2,1)S(1)} %get-tuple-element.55.own, bf16[1024,1024]{1,0:T(8,128)(2,1)S(1)} %copy-done), custom_call_target="tpu_custom_call" | custom-call | flops 256 | tf_op jit(solution)/shard_map/pallas_call | solution.py:374
  7.8 1.1 %collective-permute-done.part3 = bf16[256,256]{1,0:T(8,128)(2,1)S(1)} collective-permute-done((bf16[256,256]{1,0:T(8,128)(2,1)S(1)}, bf16[256,256]{1,0:T(8,128)(2,1)S(1)}, u32[]{:S(2)}, u32[]{:S(2)}) %collective-permute-start) | collective-permute-done | bytes 131104 | tf_op jit(solution)/shard_map/ppermute | solution.py:397
  8.9 1.0 %shard_map.66 = (bf16[256,1024]{1,0:T(8,128)(2,1)S(1)}, bf16[256,1024]{1,0:T(8,128)(2,1)S(1)}, bf16[264,512]{1,0:T(8,128)(2,1)S(1)}) custom-call(bf16[256,256]{1,0:T(8,128)(2,1)S(1)} %collective-permute-done.part3, f32[256,1024]{1,0:T(8,128)S(1)} %shard_map.64.partial, bf16[1024,1024]{1,0:T(8,128)(2,1)S(1)} %copy-done, ...), custom_call_target="tpu_custom_call" | custom-call | flops 805306368 | tf_op jit(solution)/shard_map/pallas_call | solution.py:374
  9.9 0.3 collective-permute-start.5
  10.2 0.3 shard_map.67
  10.5 1.8 %collective-permute-start.4 = (bf16[264,512]{1,0:T(8,128)(2,1)S(1)}, bf16[264,512]{1,0:T(8,128)(2,1)S(1)}, u32[]{:S(2)}, u32[]{:S(2)}) collective-permute-start(bf16[264,512]{1,0:T(8,128)(2,1)S(1)} %get-tuple-element.30.send_2), channel_id=1, source_target_pairs={{0,2},{8,0},{16,8},{24,16},{2,10},{10,18},{18,26},{26,24},{4,6},{1... | collective-permute-start | bytes 811016 | tf_op jit(solution)/shard_map/ppermute | solution.py:432
  12.3 0.3 shard_map.68.send_f
  12.7 2.2 %collective-permute-start.7 = (bf16[264,256]{1,0:T(8,128)(2,1)S(1)}, bf16[264,256]{1,0:T(8,128)(2,1)S(1)}, u32[]{:S(2)}, u32[]{:S(2)}) collective-permute-start(bf16[264,256]{1,0:T(8,128)(2,1)S(1)} %shard_map.68.send_f), channel_id=1, source_target_pairs={{24,8},{25,9},{26,10},{27,11},{28,12},{29,13},{30,14},{31,15}} | collective-permute-start | bytes 405512 | tf_op jit(solution)/shard_map/ppermute | solution.py:473
  14.9 0.5 %shard_map.69 = (bf16[264,512]{1,0:T(8,128)(2,1)S(1)}, f32[2,256,256]{2,1,0:T(8,128)S(1)}, bf16[2,256,256]{2,1,0:T(8,128)(2,1)S(1)}) custom-call(bf16[264,256]{1,0:T(8,128)(2,1)S(1)} %shard_map.68.send_f, bf16[256,512]{1,0:T(8,128)(2,1)S(1)} %get-tuple-element.31.far_keys, bf16[256,256]{1,0:T(8,128)(2,1)S(1)} %get-tuple-element.32.far_query, ...), custom_call_target="tpu_custom_call" | custom-call | flops 268435456 | tf_op jit(solution)/shard_map/pallas_call | solution.py:374
  15.4 0.7 %collective-permute-start.3 = (bf16[264,512]{1,0:T(8,128)(2,1)S(1)}, bf16[264,512]{1,0:T(8,128)(2,1)S(1)}, u32[]{:S(2)}, u32[]{:S(2)}) collective-permute-start(bf16[264,512]{1,0:T(8,128)(2,1)S(1)} %get-tuple-element.33.send_a), channel_id=1, source_target_pairs={{0,16},{1,17},{2,18},{3,19},{4,20},{5,21},{6,22},{7,23}} | collective-permute-start | bytes 811016 | tf_op jit(solution)/shard_map/ppermute | solution.py:483
  16.1 3.2 %collective-permute-done.5.got_1 = bf16[264,512]{1,0:T(8,128)(2,1)S(1)} collective-permute-done((bf16[264,512]{1,0:T(8,128)(2,1)S(1)}, bf16[264,512]{1,0:T(8,128)(2,1)S(1)}, u32[]{:S(2)}, u32[]{:S(2)}) %collective-permute-start.5) | collective-permute-done | bytes 270368 | tf_op jit(solution)/shard_map/ppermute | solution.py:432
  19.3 0.0 collective-permute-done.4.got_2
  19.4 0.1 collective-permute-done.7.got_f
  19.5 0.0 copy-start.1
  19.5 1.4 %collective-permute-start.8 = (bf16[256,256]{1,0:T(8,128)(2,1)S(1)}, bf16[256,256]{1,0:T(8,128)(2,1)S(1)}, u32[]{:S(2)}, u32[]{:S(2)}) collective-permute-start(bf16[256,256]{1,0:T(8,128)(2,1)S(1)} %get-tuple-element.43), channel_id=1, source_target_pairs={{8,24},{0,8},{9,25},{1,9},{10,26},{2,10},{11,27},{3,11},{12,28},{4... | collective-permute-start | bytes 393224 | tf_op jit(solution)/shard_map/ppermute | solution.py:504
  20.9 0.1 collective-permute-start.9
  21.0 0.0 collective-permute-done.3.got_a
  21.0 6.0 %collective-permute-start.6 = (bf16[256,256]{1,0:T(8,128)(2,1)S(1)}, bf16[256,256]{1,0:T(8,128)(2,1)S(1)}, u32[]{:S(2)}, u32[]{:S(2)}) collective-permute-start(bf16[256,256]{1,0:T(8,128)(2,1)S(1)} %shard_map.74), channel_id=1, source_target_pairs={{0,2},{8,10},{16,24},{24,16},{2,0},{10,8},{18,26},{26,18},{4,6},{1... | collective-permute-start | bytes 393224 | tf_op jit(solution)/shard_map/ppermute | solution.py:440
  27.0 1.6 %shard_map.72 = (f32[2,256,256]{2,1,0:T(8,128)S(1)}, bf16[2,256,256]{2,1,0:T(8,128)(2,1)S(1)}) custom-call(bf16[264,512]{1,0:T(8,128)(2,1)S(1)} %collective-permute-done.3.got_a, bf16[264,512]{1,0:T(8,128)(2,1)S(1)} %get-tuple-element.36.got_b, bf16[264,512]{1,0:T(8,128)(2,1)S(1)} %get-tuple-element.33.send_a, ...), custom_call_target="tpu_custom_call", output_to_operand_aliasing={{0}: (10, {}), {1}: (11, {})} | custom-call | flops 256 | tf_op jit(solution)/shard_map/pallas_call | solution.py:374
  28.6 1.2 %collective-permute-done.8 = bf16[256,256]{1,0:T(8,128)(2,1)S(1)} collective-permute-done((bf16[256,256]{1,0:T(8,128)(2,1)S(1)}, bf16[256,256]{1,0:T(8,128)(2,1)S(1)}, u32[]{:S(2)}, u32[]{:S(2)}) %collective-permute-start.8) | collective-permute-done | bytes 131104 | tf_op jit(solution)/shard_map/ppermute | solution.py:504
  29.9 0.0 collective-permute-done.9
  29.9 1.4 %collective-permute-done.6.got_d = bf16[256,256]{1,0:T(8,128)(2,1)S(1)} collective-permute-done((bf16[256,256]{1,0:T(8,128)(2,1)S(1)}, bf16[256,256]{1,0:T(8,128)(2,1)S(1)}, u32[]{:S(2)}, u32[]{:S(2)}) %collective-permute-start.6) | collective-permute-done | bytes 131104 | tf_op jit(solution)/shard_map/ppermute | solution.py:440
  31.3 0.0 copy-done.1
  31.3 1.4 %shard_map.76 = bf16[256,1024]{1,0:T(8,128)(2,1)} custom-call(f32[2,256,256]{2,1,0:T(8,128)S(1)} %get-tuple-element.39.mixed, bf16[256,256]{1,0:T(8,128)(2,1)S(1)} %collective-permute-done.6.got_d, bf16[256,256]{1,0:T(8,128)(2,1)S(1)} %add.93.got_eg, bf16[2,256,256]{2,1,0:T(8,128)(2,1)S(1)} %get-tuple-element.45.gate, ...), custom_call_target="tpu_custom_call" | custom-call | flops 256 | tf_op jit(solution)/shard_map/pallas_call | solution.py:374
  (6 shorter events, 0.2 us)
Async XLA Ops:
  0.9 6.2 %collective-permute-start.1 = (bf16[256,256]{1,0:T(8,128)(2,1)S(1)}, bf16[256,256]{1,0:T(8,128)(2,1)S(1)}, u32[]{:S(2)}, u32[]{:S(2)}) collective-permute-start(bf16[256,256]{1,0:T(8,128)(2,1)S(1)} %dynamic-slice_bitcast_fusion.3), channel_id=1, source_target_pairs={{0,4},{2,6},{4,0},{6,2},{1,5},{3,7},{5,1},{7,3},{8,12},{10,14},{12... | collective-permute-start | bytes 393224 | tf_op jit(solution)/shard_map/ppermute | solution.py:397
  3.5 3.5 %collective-permute-start.2 = (bf16[256,256]{1,0:T(8,128)(2,1)S(1)}, bf16[256,256]{1,0:T(8,128)(2,1)S(1)}, u32[]{:S(2)}, u32[]{:S(2)}) collective-permute-start(bf16[256,256]{1,0:T(8,128)(2,1)S(1)} %get-tuple-element.56), channel_id=1, source_target_pairs={{0,2},{2,0},{4,6},{6,4},{1,3},{3,1},{5,7},{7,5},{8,10},{10,8},{12,... | collective-permute-start | bytes 393224 | tf_op jit(solution)/shard_map/ppermute | solution.py:397
  3.6 5.3 %collective-permute-start = (bf16[256,256]{1,0:T(8,128)(2,1)S(1)}, bf16[256,256]{1,0:T(8,128)(2,1)S(1)}, u32[]{:S(2)}, u32[]{:S(2)}) collective-permute-start(bf16[256,256]{1,0:T(8,128)(2,1)S(1)} %get-tuple-element.57), channel_id=1, source_target_pairs={{0,6},{2,4},{4,2},{6,0},{1,7},{3,5},{5,3},{7,1},{8,14},{10,12},{12... | collective-permute-start | bytes 393224 | tf_op jit(solution)/shard_map/ppermute | solution.py:397
  4.3 2.6 %copy-start.2 = (s32[256]{0:T(256)S(1)}, s32[256]{0:T(256)}, u32[]{:S(2)}) copy-start(s32[256]{0:T(256)} %param.11) | copy-start | bytes 3076
  4.3 2.6 %copy-start.3 = (s32[1,4]{1,0:T(1,128)S(1)}, s32[1,4]{1,0:T(1,128)}, u32[]{:S(2)}) copy-start(s32[1,4]{1,0:T(1,128)} %counts.1) | copy-start | bytes 52
  4.3 2.9 %copy-start = (bf16[1024,1024]{1,0:T(8,128)(2,1)S(1)}, bf16[1024,1024]{1,0:T(8,128)(2,1)}, u32[]{:S(2)}) copy-start(bf16[1024,1024]{1,0:T(8,128)(2,1)} %w_in.3) | copy-start | bytes 6291460
  9.9 9.3 %collective-permute-start.5 = (bf16[264,512]{1,0:T(8,128)(2,1)S(1)}, bf16[264,512]{1,0:T(8,128)(2,1)S(1)}, u32[]{:S(2)}, u32[]{:S(2)}) collective-permute-start(bf16[264,512]{1,0:T(8,128)(2,1)S(1)} %get-tuple-element.29.send_1), channel_id=1, source_target_pairs={{0,8},{8,16},{16,24},{24,26},{2,0},{10,2},{18,10},{26,18},{4,12},{... | collective-permute-start | bytes 811016 | tf_op jit(solution)/shard_map/ppermute | solution.py:432
  10.5 8.7 %collective-permute-start.4 = (bf16[264,512]{1,0:T(8,128)(2,1)S(1)}, bf16[264,512]{1,0:T(8,128)(2,1)S(1)}, u32[]{:S(2)}, u32[]{:S(2)}) collective-permute-start(bf16[264,512]{1,0:T(8,128)(2,1)S(1)} %get-tuple-element.30.send_2), channel_id=1, source_target_pairs={{0,2},{8,0},{16,8},{24,16},{2,10},{10,18},{18,26},{26,24},{4,6},{1... | collective-permute-start | bytes 811016 | tf_op jit(solution)/shard_map/ppermute | solution.py:432
  12.7 6.8 %collective-permute-start.7 = (bf16[264,256]{1,0:T(8,128)(2,1)S(1)}, bf16[264,256]{1,0:T(8,128)(2,1)S(1)}, u32[]{:S(2)}, u32[]{:S(2)}) collective-permute-start(bf16[264,256]{1,0:T(8,128)(2,1)S(1)} %shard_map.68.send_f), channel_id=1, source_target_pairs={{24,8},{25,9},{26,10},{27,11},{28,12},{29,13},{30,14},{31,15}} | collective-permute-start | bytes 405512 | tf_op jit(solution)/shard_map/ppermute | solution.py:473
  15.4 5.6 %collective-permute-start.3 = (bf16[264,512]{1,0:T(8,128)(2,1)S(1)}, bf16[264,512]{1,0:T(8,128)(2,1)S(1)}, u32[]{:S(2)}, u32[]{:S(2)}) collective-permute-start(bf16[264,512]{1,0:T(8,128)(2,1)S(1)} %get-tuple-element.33.send_a), channel_id=1, source_target_pairs={{0,16},{1,17},{2,18},{3,19},{4,20},{5,21},{6,22},{7,23}} | collective-permute-start | bytes 811016 | tf_op jit(solution)/shard_map/ppermute | solution.py:483
  19.5 11.9 %copy-start.1 = (bf16[512,1024]{1,0:T(8,128)(2,1)S(1)}, bf16[512,1024]{1,0:T(8,128)(2,1)}, u32[]{:S(2)}) copy-start(bf16[512,1024]{1,0:T(8,128)(2,1)} %w_out.1) | copy-start | bytes 3145732
  19.5 10.4 %collective-permute-start.8 = (bf16[256,256]{1,0:T(8,128)(2,1)S(1)}, bf16[256,256]{1,0:T(8,128)(2,1)S(1)}, u32[]{:S(2)}, u32[]{:S(2)}) collective-permute-start(bf16[256,256]{1,0:T(8,128)(2,1)S(1)} %get-tuple-element.43), channel_id=1, source_target_pairs={{8,24},{0,8},{9,25},{1,9},{10,26},{2,10},{11,27},{3,11},{12,28},{4... | collective-permute-start | bytes 393224 | tf_op jit(solution)/shard_map/ppermute | solution.py:504
  20.9 9.0 %collective-permute-start.9 = (bf16[256,256]{1,0:T(8,128)(2,1)S(1)}, bf16[256,256]{1,0:T(8,128)(2,1)S(1)}, u32[]{:S(2)}, u32[]{:S(2)}) collective-permute-start(bf16[256,256]{1,0:T(8,128)(2,1)S(1)} %get-tuple-element.44), channel_id=1, source_target_pairs={{0,2},{8,16},{16,8},{24,26},{2,0},{10,18},{18,10},{26,24},{4,6},{1... | collective-permute-start | bytes 393224 | tf_op jit(solution)/shard_map/ppermute | solution.py:440
  21.0 10.3 %collective-permute-start.6 = (bf16[256,256]{1,0:T(8,128)(2,1)S(1)}, bf16[256,256]{1,0:T(8,128)(2,1)S(1)}, u32[]{:S(2)}, u32[]{:S(2)}) collective-permute-start(bf16[256,256]{1,0:T(8,128)(2,1)S(1)} %shard_map.74), channel_id=1, source_target_pairs={{0,2},{8,10},{16,24},{24,16},{2,0},{10,8},{18,26},{26,18},{4,6},{1... | collective-permute-start | bytes 393224 | tf_op jit(solution)/shard_map/ppermute | solution.py:440

commit v9 on v8

--- a/solution.py
+++ b/solution.py
@@ -1,5 +1,3 @@
-import functools
-
 import jax
 import jax.numpy as jnp
 from jax import lax
@@ -531,7 +529,7 @@
 
 
 def solution(mesh):
-    chain = mesh.shape["batch"] == HEADS and mesh.shape["col"] & (mesh.shape["col"] - 1) == 0
+    chain = mesh.shape["batch"] == 4 and mesh.shape["col"] == 4
     return jax.shard_map(
         chain_plan if chain else owners_plan,
         mesh=mesh,

time: 33.2 us -> 33.2 us (level)
  no operation moved by 1% of the time
where the time goes in v9:
time: 33.2 us; the launch traced here: 32.7 us
  starting transfers between devices  14.7 us (44%)
  waiting for transfers between devices  7.05 us (21%)
  Pallas kernels  5.99 us (18%)
  local copies, waits for them, and re-layouts  4.75 us (14%)
    ppermute x2, starting transfers between devices, closed(): return lax.ppermute(block, ('batch', 'col'), perm)  6.06 us
    pallas_call x13, Pallas kernels, call(): pl.pallas_call(kernel, out_shape=[jax.ShapeDtypeStruct(shape, dtype) for...  5.99 us
    ppermute x2, waiting for transfers between devices, up_and_down(): return lax.ppermute(block, ('batch', 'col'), perm)  3.18 us
    dynamic_slice x1, local copies, waits for them, and re-layouts, weight_of(): lax.dynamic_slice_in_dim(joined_weight, block * width + index * group, gr...  2.63 us
    ppermute x3, starting transfers between devices, exchange(): return lax.ppermute(block, 'col', [(i, i ^ shift) for i in range(cols)])  2.28 us
    ppermute x1, starting transfers between devices, chain_plan(): got_f = lax.ppermute(send_f, 'batch', [(3, 1)])  2.25 us
    ppermute x2, starting transfers between devices, up_and_down(): return lax.ppermute(block, ('batch', 'col'), perm)  2.06 us
    squeeze x2, local copies, waits for them, and re-layouts, piece(): return lax.dynamic_index_in_dim(source, col_at ^ shift, 0, keepdims=False)  1.97 us
  transfers between devices with their start and end apart: 10, of which 5 were waited for; matrix products, arithmetic and copies ran while one was open for 11% of the time, Pallas kernels for 11%

profile of v9, /device:TPU:24, one launch (start us, length us, event | category | flops | bytes accessed | tf_op | source)
XLA Modules:
  0.0 32.7 jit_solution(5597097818426943239)
XLA Ops:
  0.0 0.9 %dynamic-slice_bitcast_fusion.3 = bf16[256,256]{1,0:T(8,128)(2,1)S(1)} fusion(bf16[4,256,256]{2,1,0:T(8,128)(2,1)} %bitcast.11, s32[]{:T(128)S(6)} %select_n.44), kind=kLoop, calls=%fused_computation.3 | loop fusion | bytes 262148 | tf_op jit(solution)/shard_map/jit(dynamic_index_in_dim)/squeeze | solution.py:392
  0.9 1.6 %collective-permute-start.1 = (bf16[256,256]{1,0:T(8,128)(2,1)S(1)}, bf16[256,256]{1,0:T(8,128)(2,1)S(1)}, u32[]{:S(2)}, u32[]{:S(2)}) collective-permute-start(bf16[256,256]{1,0:T(8,128)(2,1)S(1)} %dynamic-slice_bitcast_fusion.3), channel_id=1, source_target_pairs={{0,4},{2,6},{4,0},{6,2},{1,5},{3,7},{5,1},{7,3},{8,12},{10,14},{12... | collective-permute-start | bytes 393224 | tf_op jit(solution)/shard_map/ppermute | solution.py:395
  2.5 1.1 %dynamic-slice_bitcast_fusion = (bf16[256,256]{1,0:T(8,128)(2,1)S(1)}, bf16[256,256]{1,0:T(8,128)(2,1)S(1)}, bf16[256,256]{1,0:T(8,128)(2,1)S(1)}) fusion(bf16[4,256,256]{2,1,0:T(8,128)(2,1)} %bitcast.12, s32[]{:T(128)S(6)} %select_n.47, s32[]{:T(128)S(6)} %select_n.46, s32[]{:T(128)S(6)} %select_n.45), kind=kLoop, calls=%fused_computation | loop fusion | bytes 786444 | tf_op jit(solution)/shard_map/jit(dynamic_index_in_dim)/squeeze | solution.py:392
  3.5 0.1 collective-permute-start.2
  3.6 0.7 %collective-permute-start = (bf16[256,256]{1,0:T(8,128)(2,1)S(1)}, bf16[256,256]{1,0:T(8,128)(2,1)S(1)}, u32[]{:S(2)}, u32[]{:S(2)}) collective-permute-start(bf16[256,256]{1,0:T(8,128)(2,1)S(1)} %get-tuple-element.57), channel_id=1, source_target_pairs={{0,6},{2,4},{4,2},{6,0},{1,7},{3,5},{5,3},{7,1},{8,14},{10,12},{12... | collective-permute-start | bytes 393224 | tf_op jit(solution)/shard_map/ppermute | solution.py:395
  4.3 0.0 copy-start.2
  4.3 0.0 copy-start.3
  4.3 0.0 copy-start
  4.3 2.6 %constant_dynamic-slice_fusion = (bf16[1024,256]{1,0:T(8,128)(2,1)S(1)}, bf16[1024,256]{1,0:T(8,128)(2,1)S(1)}, bf16[1024,256]{1,0:T(8,128)(2,1)S(1)}, bf16[1024...) fusion(bf16[1024,2048]{1,0:T(8,128)(2,1)} %param.8, ...), kind=kLoop, calls=%fused_computation.4 | loop fusion | bytes 8388640 | tf_op jit(solution)/shard_map/dynamic_slice | solution.py:418
  6.9 0.0 copy-done.2
  6.9 0.0 copy-done.3
  6.9 0.1 shard_map.65.seg
  7.1 0.0 collective-permute-done.1.part2
  7.1 0.0 collective-permute-done.2.part1
  7.1 0.1 copy-done
  7.2 0.6 %shard_map.64.partial = f32[256,1024]{1,0:T(8,128)S(1)} custom-call(bf16[256,256]{1,0:T(8,128)(2,1)S(1)} %collective-permute-done.1.part2, bf16[256,256]{1,0:T(8,128)(2,1)S(1)} %collective-permute-done.2.part1, bf16[256,256]{1,0:T(8,128)(2,1)S(1)} %get-tuple-element.55.own, bf16[1024,1024]{1,0:T(8,128)(2,1)S(1)} %copy-done), custom_call_target="tpu_custom_call" | custom-call | flops 256 | tf_op jit(solution)/shard_map/pallas_call | solution.py:372
  7.8 1.1 %collective-permute-done.part3 = bf16[256,256]{1,0:T(8,128)(2,1)S(1)} collective-permute-done((bf16[256,256]{1,0:T(8,128)(2,1)S(1)}, bf16[256,256]{1,0:T(8,128)(2,1)S(1)}, u32[]{:S(2)}, u32[]{:S(2)}) %collective-permute-start) | collective-permute-done | bytes 131104 | tf_op jit(solution)/shard_map/ppermute | solution.py:395
  8.9 1.0 %shard_map.66 = (bf16[256,1024]{1,0:T(8,128)(2,1)S(1)}, bf16[256,1024]{1,0:T(8,128)(2,1)S(1)}, bf16[264,512]{1,0:T(8,128)(2,1)S(1)}) custom-call(bf16[256,256]{1,0:T(8,128)(2,1)S(1)} %collective-permute-done.part3, f32[256,1024]{1,0:T(8,128)S(1)} %shard_map.64.partial, bf16[1024,1024]{1,0:T(8,128)(2,1)S(1)} %copy-done, ...), custom_call_target="tpu_custom_call" | custom-call | flops 805306368 | tf_op jit(solution)/shard_map/pallas_call | solution.py:372
  9.9 0.3 collective-permute-start.5
  10.2 0.3 shard_map.67
  10.5 1.8 %collective-permute-start.4 = (bf16[264,512]{1,0:T(8,128)(2,1)S(1)}, bf16[264,512]{1,0:T(8,128)(2,1)S(1)}, u32[]{:S(2)}, u32[]{:S(2)}) collective-permute-start(bf16[264,512]{1,0:T(8,128)(2,1)S(1)} %get-tuple-element.30.send_2), channel_id=1, source_target_pairs={{0,2},{8,0},{16,8},{24,16},{2,10},{10,18},{18,26},{26,24},{4,6},{1... | collective-permute-start | bytes 811016 | tf_op jit(solution)/shard_map/ppermute | solution.py:430
  12.3 0.3 shard_map.68.send_f
  12.7 2.2 %collective-permute-start.7 = (bf16[264,256]{1,0:T(8,128)(2,1)S(1)}, bf16[264,256]{1,0:T(8,128)(2,1)S(1)}, u32[]{:S(2)}, u32[]{:S(2)}) collective-permute-start(bf16[264,256]{1,0:T(8,128)(2,1)S(1)} %shard_map.68.send_f), channel_id=1, source_target_pairs={{24,8},{25,9},{26,10},{27,11},{28,12},{29,13},{30,14},{31,15}} | collective-permute-start | bytes 405512 | tf_op jit(solution)/shard_map/ppermute | solution.py:471
  14.9 0.5 %shard_map.69 = (bf16[264,512]{1,0:T(8,128)(2,1)S(1)}, f32[2,256,256]{2,1,0:T(8,128)S(1)}, bf16[2,256,256]{2,1,0:T(8,128)(2,1)S(1)}) custom-call(bf16[264,256]{1,0:T(8,128)(2,1)S(1)} %shard_map.68.send_f, bf16[256,512]{1,0:T(8,128)(2,1)S(1)} %get-tuple-element.31.far_keys, bf16[256,256]{1,0:T(8,128)(2,1)S(1)} %get-tuple-element.32.far_query, ...), custom_call_target="tpu_custom_call" | custom-call | flops 268435456 | tf_op jit(solution)/shard_map/pallas_call | solution.py:372
  15.4 0.7 %collective-permute-start.3 = (bf16[264,512]{1,0:T(8,128)(2,1)S(1)}, bf16[264,512]{1,0:T(8,128)(2,1)S(1)}, u32[]{:S(2)}, u32[]{:S(2)}) collective-permute-start(bf16[264,512]{1,0:T(8,128)(2,1)S(1)} %get-tuple-element.33.send_a), channel_id=1, source_target_pairs={{0,16},{1,17},{2,18},{3,19},{4,20},{5,21},{6,22},{7,23}} | collective-permute-start | bytes 811016 | tf_op jit(solution)/shard_map/ppermute | solution.py:481
  16.1 3.2 %collective-permute-done.5.got_1 = bf16[264,512]{1,0:T(8,128)(2,1)S(1)} collective-permute-done((bf16[264,512]{1,0:T(8,128)(2,1)S(1)}, bf16[264,512]{1,0:T(8,128)(2,1)S(1)}, u32[]{:S(2)}, u32[]{:S(2)}) %collective-permute-start.5) | collective-permute-done | bytes 270368 | tf_op jit(solution)/shard_map/ppermute | solution.py:430
  19.3 0.0 collective-permute-done.4.got_2
  19.4 0.1 collective-permute-done.7.got_f
  19.5 0.0 copy-start.1
  19.5 1.4 %collective-permute-start.8 = (bf16[256,256]{1,0:T(8,128)(2,1)S(1)}, bf16[256,256]{1,0:T(8,128)(2,1)S(1)}, u32[]{:S(2)}, u32[]{:S(2)}) collective-permute-start(bf16[256,256]{1,0:T(8,128)(2,1)S(1)} %get-tuple-element.43), channel_id=1, source_target_pairs={{8,24},{0,8},{9,25},{1,9},{10,26},{2,10},{11,27},{3,11},{12,28},{4... | collective-permute-start | bytes 393224 | tf_op jit(solution)/shard_map/ppermute | solution.py:502
  20.9 0.1 collective-permute-start.9
  21.0 0.0 collective-permute-done.3.got_a
  21.0 6.0 %collective-permute-start.6 = (bf16[256,256]{1,0:T(8,128)(2,1)S(1)}, bf16[256,256]{1,0:T(8,128)(2,1)S(1)}, u32[]{:S(2)}, u32[]{:S(2)}) collective-permute-start(bf16[256,256]{1,0:T(8,128)(2,1)S(1)} %shard_map.74), channel_id=1, source_target_pairs={{0,2},{8,10},{16,24},{24,16},{2,0},{10,8},{18,26},{26,18},{4,6},{1... | collective-permute-start | bytes 393224 | tf_op jit(solution)/shard_map/ppermute | solution.py:438
  27.0 1.6 %shard_map.72 = (f32[2,256,256]{2,1,0:T(8,128)S(1)}, bf16[2,256,256]{2,1,0:T(8,128)(2,1)S(1)}) custom-call(bf16[264,512]{1,0:T(8,128)(2,1)S(1)} %collective-permute-done.3.got_a, bf16[264,512]{1,0:T(8,128)(2,1)S(1)} %get-tuple-element.36.got_b, bf16[264,512]{1,0:T(8,128)(2,1)S(1)} %get-tuple-element.33.send_a, ...), custom_call_target="tpu_custom_call", output_to_operand_aliasing={{0}: (10, {}), {1}: (11, {})} | custom-call | flops 256 | tf_op jit(solution)/shard_map/pallas_call | solution.py:372
  28.6 1.2 %collective-permute-done.8 = bf16[256,256]{1,0:T(8,128)(2,1)S(1)} collective-permute-done((bf16[256,256]{1,0:T(8,128)(2,1)S(1)}, bf16[256,256]{1,0:T(8,128)(2,1)S(1)}, u32[]{:S(2)}, u32[]{:S(2)}) %collective-permute-start.8) | collective-permute-done | bytes 131104 | tf_op jit(solution)/shard_map/ppermute | solution.py:502
  29.9 0.0 collective-permute-done.9
  29.9 1.4 %collective-permute-done.6.got_d = bf16[256,256]{1,0:T(8,128)(2,1)S(1)} collective-permute-done((bf16[256,256]{1,0:T(8,128)(2,1)S(1)}, bf16[256,256]{1,0:T(8,128)(2,1)S(1)}, u32[]{:S(2)}, u32[]{:S(2)}) %collective-permute-start.6) | collective-permute-done | bytes 131104 | tf_op jit(solution)/shard_map/ppermute | solution.py:438
  31.3 0.0 copy-done.1
  31.3 1.4 %shard_map.76 = bf16[256,1024]{1,0:T(8,128)(2,1)} custom-call(f32[2,256,256]{2,1,0:T(8,128)S(1)} %get-tuple-element.39.mixed, bf16[256,256]{1,0:T(8,128)(2,1)S(1)} %collective-permute-done.6.got_d, bf16[256,256]{1,0:T(8,128)(2,1)S(1)} %add.93.got_eg, bf16[2,256,256]{2,1,0:T(8,128)(2,1)S(1)} %get-tuple-element.45.gate, ...), custom_call_target="tpu_custom_call" | custom-call | flops 256 | tf_op jit(solution)/shard_map/pallas_call | solution.py:372
  (6 shorter events, 0.2 us)
Async XLA Ops:
  0.9 6.2 %collective-permute-start.1 = (bf16[256,256]{1,0:T(8,128)(2,1)S(1)}, bf16[256,256]{1,0:T(8,128)(2,1)S(1)}, u32[]{:S(2)}, u32[]{:S(2)}) collective-permute-start(bf16[256,256]{1,0:T(8,128)(2,1)S(1)} %dynamic-slice_bitcast_fusion.3), channel_id=1, source_target_pairs={{0,4},{2,6},{4,0},{6,2},{1,5},{3,7},{5,1},{7,3},{8,12},{10,14},{12... | collective-permute-start | bytes 393224 | tf_op jit(solution)/shard_map/ppermute | solution.py:395
  3.5 3.5 %collective-permute-start.2 = (bf16[256,256]{1,0:T(8,128)(2,1)S(1)}, bf16[256,256]{1,0:T(8,128)(2,1)S(1)}, u32[]{:S(2)}, u32[]{:S(2)}) collective-permute-start(bf16[256,256]{1,0:T(8,128)(2,1)S(1)} %get-tuple-element.56), channel_id=1, source_target_pairs={{0,2},{2,0},{4,6},{6,4},{1,3},{3,1},{5,7},{7,5},{8,10},{10,8},{12,... | collective-permute-start | bytes 393224 | tf_op jit(solution)/shard_map/ppermute | solution.py:395
  3.6 5.3 %collective-permute-start = (bf16[256,256]{1,0:T(8,128)(2,1)S(1)}, bf16[256,256]{1,0:T(8,128)(2,1)S(1)}, u32[]{:S(2)}, u32[]{:S(2)}) collective-permute-start(bf16[256,256]{1,0:T(8,128)(2,1)S(1)} %get-tuple-element.57), channel_id=1, source_target_pairs={{0,6},{2,4},{4,2},{6,0},{1,7},{3,5},{5,3},{7,1},{8,14},{10,12},{12... | collective-permute-start | bytes 393224 | tf_op jit(solution)/shard_map/ppermute | solution.py:395
  4.3 2.6 %copy-start.2 = (s32[256]{0:T(256)S(1)}, s32[256]{0:T(256)}, u32[]{:S(2)}) copy-start(s32[256]{0:T(256)} %param.11) | copy-start | bytes 3076
  4.3 2.6 %copy-start.3 = (s32[1,4]{1,0:T(1,128)S(1)}, s32[1,4]{1,0:T(1,128)}, u32[]{:S(2)}) copy-start(s32[1,4]{1,0:T(1,128)} %counts.1) | copy-start | bytes 52
  4.3 2.9 %copy-start = (bf16[1024,1024]{1,0:T(8,128)(2,1)S(1)}, bf16[1024,1024]{1,0:T(8,128)(2,1)}, u32[]{:S(2)}) copy-start(bf16[1024,1024]{1,0:T(8,128)(2,1)} %w_in.3) | copy-start | bytes 6291460
  9.9 9.3 %collective-permute-start.5 = (bf16[264,512]{1,0:T(8,128)(2,1)S(1)}, bf16[264,512]{1,0:T(8,128)(2,1)S(1)}, u32[]{:S(2)}, u32[]{:S(2)}) collective-permute-start(bf16[264,512]{1,0:T(8,128)(2,1)S(1)} %get-tuple-element.29.send_1), channel_id=1, source_target_pairs={{0,8},{8,16},{16,24},{24,26},{2,0},{10,2},{18,10},{26,18},{4,12},{... | collective-permute-start | bytes 811016 | tf_op jit(solution)/shard_map/ppermute | solution.py:430
  10.5 8.7 %collective-permute-start.4 = (bf16[264,512]{1,0:T(8,128)(2,1)S(1)}, bf16[264,512]{1,0:T(8,128)(2,1)S(1)}, u32[]{:S(2)}, u32[]{:S(2)}) collective-permute-start(bf16[264,512]{1,0:T(8,128)(2,1)S(1)} %get-tuple-element.30.send_2), channel_id=1, source_target_pairs={{0,2},{8,0},{16,8},{24,16},{2,10},{10,18},{18,26},{26,24},{4,6},{1... | collective-permute-start | bytes 811016 | tf_op jit(solution)/shard_map/ppermute | solution.py:430
  12.7 6.8 %collective-permute-start.7 = (bf16[264,256]{1,0:T(8,128)(2,1)S(1)}, bf16[264,256]{1,0:T(8,128)(2,1)S(1)}, u32[]{:S(2)}, u32[]{:S(2)}) collective-permute-start(bf16[264,256]{1,0:T(8,128)(2,1)S(1)} %shard_map.68.send_f), channel_id=1, source_target_pairs={{24,8},{25,9},{26,10},{27,11},{28,12},{29,13},{30,14},{31,15}} | collective-permute-start | bytes 405512 | tf_op jit(solution)/shard_map/ppermute | solution.py:471
  15.4 5.6 %collective-permute-start.3 = (bf16[264,512]{1,0:T(8,128)(2,1)S(1)}, bf16[264,512]{1,0:T(8,128)(2,1)S(1)}, u32[]{:S(2)}, u32[]{:S(2)}) collective-permute-start(bf16[264,512]{1,0:T(8,128)(2,1)S(1)} %get-tuple-element.33.send_a), channel_id=1, source_target_pairs={{0,16},{1,17},{2,18},{3,19},{4,20},{5,21},{6,22},{7,23}} | collective-permute-start | bytes 811016 | tf_op jit(solution)/shard_map/ppermute | solution.py:481
  19.5 11.9 %copy-start.1 = (bf16[512,1024]{1,0:T(8,128)(2,1)S(1)}, bf16[512,1024]{1,0:T(8,128)(2,1)}, u32[]{:S(2)}) copy-start(bf16[512,1024]{1,0:T(8,128)(2,1)} %w_out.1) | copy-start | bytes 3145732
  19.5 10.4 %collective-permute-start.8 = (bf16[256,256]{1,0:T(8,128)(2,1)S(1)}, bf16[256,256]{1,0:T(8,128)(2,1)S(1)}, u32[]{:S(2)}, u32[]{:S(2)}) collective-permute-start(bf16[256,256]{1,0:T(8,128)(2,1)S(1)} %get-tuple-element.43), channel_id=1, source_target_pairs={{8,24},{0,8},{9,25},{1,9},{10,26},{2,10},{11,27},{3,11},{12,28},{4... | collective-permute-start | bytes 393224 | tf_op jit(solution)/shard_map/ppermute | solution.py:502
  20.9 9.0 %collective-permute-start.9 = (bf16[256,256]{1,0:T(8,128)(2,1)S(1)}, bf16[256,256]{1,0:T(8,128)(2,1)S(1)}, u32[]{:S(2)}, u32[]{:S(2)}) collective-permute-start(bf16[256,256]{1,0:T(8,128)(2,1)S(1)} %get-tuple-element.44), channel_id=1, source_target_pairs={{0,2},{8,16},{16,8},{24,26},{2,0},{10,18},{18,10},{26,24},{4,6},{1... | collective-permute-start | bytes 393224 | tf_op jit(solution)/shard_map/ppermute | solution.py:438
  21.0 10.3 %collective-permute-start.6 = (bf16[256,256]{1,0:T(8,128)(2,1)S(1)}, bf16[256,256]{1,0:T(8,128)(2,1)S(1)}, u32[]{:S(2)}, u32[]{:S(2)}) collective-permute-start(bf16[256,256]{1,0:T(8,128)(2,1)S(1)} %shard_map.74), channel_id=1, source_target_pairs={{0,2},{8,10},{16,24},{24,16},{2,0},{10,8},{18,26},{26,18},{4,6},{1... | collective-permute-start | bytes 393224 | tf_op jit(solution)/shard_map/ppermute | solution.py:438

commit v10 on v9

--- a/solution.py
+++ b/solution.py
@@ -8,6 +8,7 @@
 HEADS = 4
 HEAD_DIM = 128
 SEG_ROWS = 8
+OUT_PARTS = 2
 
 eps_norm = 1e-06
 
@@ -343,7 +344,7 @@
         add_near(send_f, column, got_a, mixed.at[0])
 
 
-def finish_kernel(mixed, got_d, got_eg, gate, hidden, w_out, out):
+def finish_kernel(mixed, got_d, got_eg, gate, hidden, w_out, out, staged, sems):
     near = batch_index() % 2
     last = is_last()
     got = got_eg[...].astype(F32)
@@ -356,13 +357,22 @@
     sides = [side - total / (2 * group) for side in sides]
     total = sum(jnp.sum(side * side, axis=-1, keepdims=True) for side in sides)
     scale = lax.rsqrt(total / (2 * group) + eps_norm)
-    branch = None
-    for index, (which, side) in enumerate(zip((near, 1 - near), sides)):
-        gated = (side * scale * gate[index].astype(F32)).astype(BF16)
-        start = pl.multiple_of(which * group, group)
-        term = jnp.dot(gated, w_out[pl.ds(start, group), :], preferred_element_type=F32)
-        branch = term if branch is None else branch + term
-    out[...] = (hidden[...].astype(F32) + branch.astype(BF16).astype(F32)).astype(BF16)
+    gates = [(side * scale * gate[i].astype(F32)).astype(BF16) for i, side in enumerate(sides)]
+    columns = hidden.shape[1] // OUT_PARTS
+    copies = []
+    for part in range(OUT_PARTS):
+        at = slice(part * columns, (part + 1) * columns)
+        branch = None
+        for which, gated in zip((near, 1 - near), gates):
+            start = pl.multiple_of(which * group, group)
+            term = jnp.dot(gated, w_out[pl.ds(start, group), at], preferred_element_type=F32)
+            branch = term if branch is None else branch + term
+        total = hidden[:, at].astype(F32) + branch.astype(BF16).astype(F32)
+        staged[:, at] = total.astype(BF16)
+        copies.append(pltpu.make_async_copy(staged.at[:, at], out.at[:, at], sems.at[part]))
+        copies[-1].start()
+    for copy in copies:
+        copy.wait()
 
 
 VMEM = pl.BlockSpec(memory_space=pltpu.VMEM)
@@ -518,14 +528,18 @@
         rows,
         aliases={10: 0, 11: 1},
     )
-    (out,) = call(
+    return pl.pallas_call(
         finish_kernel,
-        [VMEM] * 6,
-        [((rows, features), BF16)],
-        (mixed, got_d, got_e + got_g, gate, hidden, output_weight),
-        rows,
-    )
-    return out
+        out_shape=jax.ShapeDtypeStruct((rows, features), BF16),
+        in_specs=[VMEM] * 6,
+        out_specs=pl.BlockSpec(memory_space=pl.ANY),
+        scratch_shapes=[
+            pltpu.VMEM((rows, features), BF16),
+            pltpu.SemaphoreType.DMA((OUT_PARTS,)),
+        ],
+        compiler_params=pltpu.CompilerParams(vmem_limit_bytes=32 << 20),
+        cost_estimate=pl.CostEstimate(flops=rows, bytes_accessed=0, transcendentals=0),
+    )(mixed, got_d, got_e + got_g, gate, hidden, output_weight)
 
 
 def solution(mesh):

time: 33.2 us -> 33.1 us (level)
    pallas_call x13 -> x12, Pallas kernels: 5.99 us -> 4.58 us  [call(): pl.pallas_call(kernel, out_shape=[jax.ShapeDtypeStruct(shape, dtype) for...]
    pallas_call x0 -> x1, Pallas kernels: none -> 1.35 us  [chain_plan(): pl.pallas_call(finish_kernel, out_shape=jax.ShapeDtypeStruct((rows, featu...]
where the time goes in v10:
time: 33.1 us; the launch traced here: 32.7 us
  starting transfers between devices  14.7 us (44%)
  waiting for transfers between devices  7.05 us (21%)
  Pallas kernels  5.93 us (18%)
  local copies, waits for them, and re-layouts  4.75 us (14%)
    ppermute x2, starting transfers between devices, closed(): return lax.ppermute(block, ('batch', 'col'), perm)  6.06 us
    pallas_call x12, Pallas kernels, call(): pl.pallas_call(kernel, out_shape=[jax.ShapeDtypeStruct(shape, dtype) for...  4.58 us
    ppermute x2, waiting for transfers between devices, up_and_down(): return lax.ppermute(block, ('batch', 'col'), perm)  3.18 us
    dynamic_slice x1, local copies, waits for them, and re-layouts, weight_of(): lax.dynamic_slice_in_dim(joined_weight, block * width + index * group, gr...  2.63 us
    ppermute x3, starting transfers between devices, exchange(): return lax.ppermute(block, 'col', [(i, i ^ shift) for i in range(cols)])  2.28 us
    ppermute x1, starting transfers between devices, chain_plan(): got_f = lax.ppermute(send_f, 'batch', [(3, 1)])  2.25 us
    ppermute x2, starting transfers between devices, up_and_down(): return lax.ppermute(block, ('batch', 'col'), perm)  2.06 us
    squeeze x2, local copies, waits for them, and re-layouts, piece(): return lax.dynamic_index_in_dim(source, col_at ^ shift, 0, keepdims=False)  1.97 us
  transfers between devices with their start and end apart: 10, of which 5 were waited for; matrix products, arithmetic and copies ran while one was open for 11% of the time, Pallas kernels for 11%

profile of v10, /device:TPU:24, one launch (start us, length us, event | category | flops | bytes accessed | tf_op | source)
XLA Modules:
  0.0 32.7 jit_solution(12627591387451514007)
XLA Ops:
  0.0 0.9 %dynamic-slice_bitcast_fusion.3 = bf16[256,256]{1,0:T(8,128)(2,1)S(1)} fusion(bf16[4,256,256]{2,1,0:T(8,128)(2,1)} %bitcast.11, s32[]{:T(128)S(6)} %select_n.44), kind=kLoop, calls=%fused_computation.3 | loop fusion | bytes 262148 | tf_op jit(solution)/shard_map/jit(dynamic_index_in_dim)/squeeze | solution.py:402
  0.9 1.6 %collective-permute-start.1 = (bf16[256,256]{1,0:T(8,128)(2,1)S(1)}, bf16[256,256]{1,0:T(8,128)(2,1)S(1)}, u32[]{:S(2)}, u32[]{:S(2)}) collective-permute-start(bf16[256,256]{1,0:T(8,128)(2,1)S(1)} %dynamic-slice_bitcast_fusion.3), channel_id=1, source_target_pairs={{0,4},{2,6},{4,0},{6,2},{1,5},{3,7},{5,1},{7,3},{8,12},{10,14},{12... | collective-permute-start | bytes 393224 | tf_op jit(solution)/shard_map/ppermute | solution.py:405
  2.5 1.1 %dynamic-slice_bitcast_fusion = (bf16[256,256]{1,0:T(8,128)(2,1)S(1)}, bf16[256,256]{1,0:T(8,128)(2,1)S(1)}, bf16[256,256]{1,0:T(8,128)(2,1)S(1)}) fusion(bf16[4,256,256]{2,1,0:T(8,128)(2,1)} %bitcast.12, s32[]{:T(128)S(6)} %select_n.47, s32[]{:T(128)S(6)} %select_n.46, s32[]{:T(128)S(6)} %select_n.45), kind=kLoop, calls=%fused_computation | loop fusion | bytes 786444 | tf_op jit(solution)/shard_map/jit(dynamic_index_in_dim)/squeeze | solution.py:402
  3.5 0.1 collective-permute-start.2
  3.6 0.7 %collective-permute-start = (bf16[256,256]{1,0:T(8,128)(2,1)S(1)}, bf16[256,256]{1,0:T(8,128)(2,1)S(1)}, u32[]{:S(2)}, u32[]{:S(2)}) collective-permute-start(bf16[256,256]{1,0:T(8,128)(2,1)S(1)} %get-tuple-element.57), channel_id=1, source_target_pairs={{0,6},{2,4},{4,2},{6,0},{1,7},{3,5},{5,3},{7,1},{8,14},{10,12},{12... | collective-permute-start | bytes 393224 | tf_op jit(solution)/shard_map/ppermute | solution.py:405
  4.3 0.0 copy-start.2
  4.3 0.0 copy-start.3
  4.3 0.0 copy-start
  4.3 2.6 %constant_dynamic-slice_fusion = (bf16[1024,256]{1,0:T(8,128)(2,1)S(1)}, bf16[1024,256]{1,0:T(8,128)(2,1)S(1)}, bf16[1024,256]{1,0:T(8,128)(2,1)S(1)}, bf16[1024...) fusion(bf16[1024,2048]{1,0:T(8,128)(2,1)} %param.8, ...), kind=kLoop, calls=%fused_computation.4 | loop fusion | bytes 8388640 | tf_op jit(solution)/shard_map/dynamic_slice | solution.py:428
  6.9 0.0 copy-done.2
  6.9 0.0 copy-done.3
  6.9 0.1 shard_map.65.seg
  7.1 0.0 collective-permute-done.1.part2
  7.1 0.0 collective-permute-done.2.part1
  7.1 0.1 copy-done
  7.2 0.6 %shard_map.64.partial = f32[256,1024]{1,0:T(8,128)S(1)} custom-call(bf16[256,256]{1,0:T(8,128)(2,1)S(1)} %collective-permute-done.1.part2, bf16[256,256]{1,0:T(8,128)(2,1)S(1)} %collective-permute-done.2.part1, bf16[256,256]{1,0:T(8,128)(2,1)S(1)} %get-tuple-element.55.own, bf16[1024,1024]{1,0:T(8,128)(2,1)S(1)} %copy-done), custom_call_target="tpu_custom_call" | custom-call | flops 256 | tf_op jit(solution)/shard_map/pallas_call | solution.py:382
  7.8 1.1 %collective-permute-done.part3 = bf16[256,256]{1,0:T(8,128)(2,1)S(1)} collective-permute-done((bf16[256,256]{1,0:T(8,128)(2,1)S(1)}, bf16[256,256]{1,0:T(8,128)(2,1)S(1)}, u32[]{:S(2)}, u32[]{:S(2)}) %collective-permute-start) | collective-permute-done | bytes 131104 | tf_op jit(solution)/shard_map/ppermute | solution.py:405
  8.9 1.0 %shard_map.66 = (bf16[256,1024]{1,0:T(8,128)(2,1)S(1)}, bf16[256,1024]{1,0:T(8,128)(2,1)S(1)}, bf16[264,512]{1,0:T(8,128)(2,1)S(1)}) custom-call(bf16[256,256]{1,0:T(8,128)(2,1)S(1)} %collective-permute-done.part3, f32[256,1024]{1,0:T(8,128)S(1)} %shard_map.64.partial, bf16[1024,1024]{1,0:T(8,128)(2,1)S(1)} %copy-done, ...), custom_call_target="tpu_custom_call" | custom-call | flops 805306368 | tf_op jit(solution)/shard_map/pallas_call | solution.py:382
  9.9 0.3 collective-permute-start.5
  10.2 0.3 shard_map.67
  10.5 1.8 %collective-permute-start.4 = (bf16[264,512]{1,0:T(8,128)(2,1)S(1)}, bf16[264,512]{1,0:T(8,128)(2,1)S(1)}, u32[]{:S(2)}, u32[]{:S(2)}) collective-permute-start(bf16[264,512]{1,0:T(8,128)(2,1)S(1)} %get-tuple-element.30.send_2), channel_id=1, source_target_pairs={{0,2},{8,0},{16,8},{24,16},{2,10},{10,18},{18,26},{26,24},{4,6},{1... | collective-permute-start | bytes 811016 | tf_op jit(solution)/shard_map/ppermute | solution.py:440
  12.3 0.3 shard_map.68.send_f
  12.7 2.2 %collective-permute-start.7 = (bf16[264,256]{1,0:T(8,128)(2,1)S(1)}, bf16[264,256]{1,0:T(8,128)(2,1)S(1)}, u32[]{:S(2)}, u32[]{:S(2)}) collective-permute-start(bf16[264,256]{1,0:T(8,128)(2,1)S(1)} %shard_map.68.send_f), channel_id=1, source_target_pairs={{24,8},{25,9},{26,10},{27,11},{28,12},{29,13},{30,14},{31,15}} | collective-permute-start | bytes 405512 | tf_op jit(solution)/shard_map/ppermute | solution.py:481
  14.9 0.5 %shard_map.69 = (bf16[264,512]{1,0:T(8,128)(2,1)S(1)}, f32[2,256,256]{2,1,0:T(8,128)S(1)}, bf16[2,256,256]{2,1,0:T(8,128)(2,1)S(1)}) custom-call(bf16[264,256]{1,0:T(8,128)(2,1)S(1)} %shard_map.68.send_f, bf16[256,512]{1,0:T(8,128)(2,1)S(1)} %get-tuple-element.31.far_keys, bf16[256,256]{1,0:T(8,128)(2,1)S(1)} %get-tuple-element.32.far_query, ...), custom_call_target="tpu_custom_call" | custom-call | flops 268435456 | tf_op jit(solution)/shard_map/pallas_call | solution.py:382
  15.4 0.7 %collective-permute-start.3 = (bf16[264,512]{1,0:T(8,128)(2,1)S(1)}, bf16[264,512]{1,0:T(8,128)(2,1)S(1)}, u32[]{:S(2)}, u32[]{:S(2)}) collective-permute-start(bf16[264,512]{1,0:T(8,128)(2,1)S(1)} %get-tuple-element.33.send_a), channel_id=1, source_target_pairs={{0,16},{1,17},{2,18},{3,19},{4,20},{5,21},{6,22},{7,23}} | collective-permute-start | bytes 811016 | tf_op jit(solution)/shard_map/ppermute | solution.py:491
  16.1 3.2 %collective-permute-done.5.got_1 = bf16[264,512]{1,0:T(8,128)(2,1)S(1)} collective-permute-done((bf16[264,512]{1,0:T(8,128)(2,1)S(1)}, bf16[264,512]{1,0:T(8,128)(2,1)S(1)}, u32[]{:S(2)}, u32[]{:S(2)}) %collective-permute-start.5) | collective-permute-done | bytes 270368 | tf_op jit(solution)/shard_map/ppermute | solution.py:440
  19.3 0.0 collective-permute-done.4.got_2
  19.4 0.1 collective-permute-done.7.got_f
  19.5 0.0 copy-start.1
  19.5 1.4 %collective-permute-start.8 = (bf16[256,256]{1,0:T(8,128)(2,1)S(1)}, bf16[256,256]{1,0:T(8,128)(2,1)S(1)}, u32[]{:S(2)}, u32[]{:S(2)}) collective-permute-start(bf16[256,256]{1,0:T(8,128)(2,1)S(1)} %get-tuple-element.43), channel_id=1, source_target_pairs={{8,24},{0,8},{9,25},{1,9},{10,26},{2,10},{11,27},{3,11},{12,28},{4... | collective-permute-start | bytes 393224 | tf_op jit(solution)/shard_map/ppermute | solution.py:512
  20.9 0.1 collective-permute-start.9
  21.0 0.0 collective-permute-done.3.got_a
  21.0 6.0 %collective-permute-start.6 = (bf16[256,256]{1,0:T(8,128)(2,1)S(1)}, bf16[256,256]{1,0:T(8,128)(2,1)S(1)}, u32[]{:S(2)}, u32[]{:S(2)}) collective-permute-start(bf16[256,256]{1,0:T(8,128)(2,1)S(1)} %shard_map.74), channel_id=1, source_target_pairs={{0,2},{8,10},{16,24},{24,16},{2,0},{10,8},{18,26},{26,18},{4,6},{1... | collective-permute-start | bytes 393224 | tf_op jit(solution)/shard_map/ppermute | solution.py:448
  27.0 1.6 %shard_map.72 = (f32[2,256,256]{2,1,0:T(8,128)S(1)}, bf16[2,256,256]{2,1,0:T(8,128)(2,1)S(1)}) custom-call(bf16[264,512]{1,0:T(8,128)(2,1)S(1)} %collective-permute-done.3.got_a, bf16[264,512]{1,0:T(8,128)(2,1)S(1)} %get-tuple-element.36.got_b, bf16[264,512]{1,0:T(8,128)(2,1)S(1)} %get-tuple-element.33.send_a, ...), custom_call_target="tpu_custom_call", output_to_operand_aliasing={{0}: (10, {}), {1}: (11, {})} | custom-call | flops 256 | tf_op jit(solution)/shard_map/pallas_call | solution.py:382
  28.6 1.2 %collective-permute-done.8 = bf16[256,256]{1,0:T(8,128)(2,1)S(1)} collective-permute-done((bf16[256,256]{1,0:T(8,128)(2,1)S(1)}, bf16[256,256]{1,0:T(8,128)(2,1)S(1)}, u32[]{:S(2)}, u32[]{:S(2)}) %collective-permute-start.8) | collective-permute-done | bytes 131104 | tf_op jit(solution)/shard_map/ppermute | solution.py:512
  29.9 0.0 collective-permute-done.9
  29.9 1.4 %collective-permute-done.6.got_d = bf16[256,256]{1,0:T(8,128)(2,1)S(1)} collective-permute-done((bf16[256,256]{1,0:T(8,128)(2,1)S(1)}, bf16[256,256]{1,0:T(8,128)(2,1)S(1)}, u32[]{:S(2)}, u32[]{:S(2)}) %collective-permute-start.6) | collective-permute-done | bytes 131104 | tf_op jit(solution)/shard_map/ppermute | solution.py:448
  31.3 0.0 copy-done.1
  31.3 1.3 %shard_map.76 = bf16[256,1024]{1,0:T(8,128)(2,1)} custom-call(f32[2,256,256]{2,1,0:T(8,128)S(1)} %get-tuple-element.39.mixed, bf16[256,256]{1,0:T(8,128)(2,1)S(1)} %collective-permute-done.6.got_d, bf16[256,256]{1,0:T(8,128)(2,1)S(1)} %add.93.got_eg, bf16[2,256,256]{2,1,0:T(8,128)(2,1)S(1)} %get-tuple-element.45.gate, ...), custom_call_target="tpu_custom_call" | custom-call | flops 256 | tf_op jit(solution)/shard_map/pallas_call | solution.py:531
  (6 shorter events, 0.2 us)
Async XLA Ops:
  0.9 6.2 %collective-permute-start.1 = (bf16[256,256]{1,0:T(8,128)(2,1)S(1)}, bf16[256,256]{1,0:T(8,128)(2,1)S(1)}, u32[]{:S(2)}, u32[]{:S(2)}) collective-permute-start(bf16[256,256]{1,0:T(8,128)(2,1)S(1)} %dynamic-slice_bitcast_fusion.3), channel_id=1, source_target_pairs={{0,4},{2,6},{4,0},{6,2},{1,5},{3,7},{5,1},{7,3},{8,12},{10,14},{12... | collective-permute-start | bytes 393224 | tf_op jit(solution)/shard_map/ppermute | solution.py:405
  3.5 3.5 %collective-permute-start.2 = (bf16[256,256]{1,0:T(8,128)(2,1)S(1)}, bf16[256,256]{1,0:T(8,128)(2,1)S(1)}, u32[]{:S(2)}, u32[]{:S(2)}) collective-permute-start(bf16[256,256]{1,0:T(8,128)(2,1)S(1)} %get-tuple-element.56), channel_id=1, source_target_pairs={{0,2},{2,0},{4,6},{6,4},{1,3},{3,1},{5,7},{7,5},{8,10},{10,8},{12,... | collective-permute-start | bytes 393224 | tf_op jit(solution)/shard_map/ppermute | solution.py:405
  3.6 5.3 %collective-permute-start = (bf16[256,256]{1,0:T(8,128)(2,1)S(1)}, bf16[256,256]{1,0:T(8,128)(2,1)S(1)}, u32[]{:S(2)}, u32[]{:S(2)}) collective-permute-start(bf16[256,256]{1,0:T(8,128)(2,1)S(1)} %get-tuple-element.57), channel_id=1, source_target_pairs={{0,6},{2,4},{4,2},{6,0},{1,7},{3,5},{5,3},{7,1},{8,14},{10,12},{12... | collective-permute-start | bytes 393224 | tf_op jit(solution)/shard_map/ppermute | solution.py:405
  4.3 2.6 %copy-start.2 = (s32[256]{0:T(256)S(1)}, s32[256]{0:T(256)}, u32[]{:S(2)}) copy-start(s32[256]{0:T(256)} %param.11) | copy-start | bytes 3076
  4.3 2.6 %copy-start.3 = (s32[1,4]{1,0:T(1,128)S(1)}, s32[1,4]{1,0:T(1,128)}, u32[]{:S(2)}) copy-start(s32[1,4]{1,0:T(1,128)} %counts.1) | copy-start | bytes 52
  4.3 2.9 %copy-start = (bf16[1024,1024]{1,0:T(8,128)(2,1)S(1)}, bf16[1024,1024]{1,0:T(8,128)(2,1)}, u32[]{:S(2)}) copy-start(bf16[1024,1024]{1,0:T(8,128)(2,1)} %w_in.3) | copy-start | bytes 6291460
  9.9 9.3 %collective-permute-start.5 = (bf16[264,512]{1,0:T(8,128)(2,1)S(1)}, bf16[264,512]{1,0:T(8,128)(2,1)S(1)}, u32[]{:S(2)}, u32[]{:S(2)}) collective-permute-start(bf16[264,512]{1,0:T(8,128)(2,1)S(1)} %get-tuple-element.29.send_1), channel_id=1, source_target_pairs={{0,8},{8,16},{16,24},{24,26},{2,0},{10,2},{18,10},{26,18},{4,12},{... | collective-permute-start | bytes 811016 | tf_op jit(solution)/shard_map/ppermute | solution.py:440
  10.5 8.7 %collective-permute-start.4 = (bf16[264,512]{1,0:T(8,128)(2,1)S(1)}, bf16[264,512]{1,0:T(8,128)(2,1)S(1)}, u32[]{:S(2)}, u32[]{:S(2)}) collective-permute-start(bf16[264,512]{1,0:T(8,128)(2,1)S(1)} %get-tuple-element.30.send_2), channel_id=1, source_target_pairs={{0,2},{8,0},{16,8},{24,16},{2,10},{10,18},{18,26},{26,24},{4,6},{1... | collective-permute-start | bytes 811016 | tf_op jit(solution)/shard_map/ppermute | solution.py:440
  12.7 6.8 %collective-permute-start.7 = (bf16[264,256]{1,0:T(8,128)(2,1)S(1)}, bf16[264,256]{1,0:T(8,128)(2,1)S(1)}, u32[]{:S(2)}, u32[]{:S(2)}) collective-permute-start(bf16[264,256]{1,0:T(8,128)(2,1)S(1)} %shard_map.68.send_f), channel_id=1, source_target_pairs={{24,8},{25,9},{26,10},{27,11},{28,12},{29,13},{30,14},{31,15}} | collective-permute-start | bytes 405512 | tf_op jit(solution)/shard_map/ppermute | solution.py:481
  15.4 5.6 %collective-permute-start.3 = (bf16[264,512]{1,0:T(8,128)(2,1)S(1)}, bf16[264,512]{1,0:T(8,128)(2,1)S(1)}, u32[]{:S(2)}, u32[]{:S(2)}) collective-permute-start(bf16[264,512]{1,0:T(8,128)(2,1)S(1)} %get-tuple-element.33.send_a), channel_id=1, source_target_pairs={{0,16},{1,17},{2,18},{3,19},{4,20},{5,21},{6,22},{7,23}} | collective-permute-start | bytes 811016 | tf_op jit(solution)/shard_map/ppermute | solution.py:491
  19.5 11.9 %copy-start.1 = (bf16[512,1024]{1,0:T(8,128)(2,1)S(1)}, bf16[512,1024]{1,0:T(8,128)(2,1)}, u32[]{:S(2)}) copy-start(bf16[512,1024]{1,0:T(8,128)(2,1)} %w_out.1) | copy-start | bytes 3145732
  19.5 10.4 %collective-permute-start.8 = (bf16[256,256]{1,0:T(8,128)(2,1)S(1)}, bf16[256,256]{1,0:T(8,128)(2,1)S(1)}, u32[]{:S(2)}, u32[]{:S(2)}) collective-permute-start(bf16[256,256]{1,0:T(8,128)(2,1)S(1)} %get-tuple-element.43), channel_id=1, source_target_pairs={{8,24},{0,8},{9,25},{1,9},{10,26},{2,10},{11,27},{3,11},{12,28},{4... | collective-permute-start | bytes 393224 | tf_op jit(solution)/shard_map/ppermute | solution.py:512
  20.9 9.0 %collective-permute-start.9 = (bf16[256,256]{1,0:T(8,128)(2,1)S(1)}, bf16[256,256]{1,0:T(8,128)(2,1)S(1)}, u32[]{:S(2)}, u32[]{:S(2)}) collective-permute-start(bf16[256,256]{1,0:T(8,128)(2,1)S(1)} %get-tuple-element.44), channel_id=1, source_target_pairs={{0,2},{8,16},{16,8},{24,26},{2,0},{10,18},{18,10},{26,24},{4,6},{1... | collective-permute-start | bytes 393224 | tf_op jit(solution)/shard_map/ppermute | solution.py:448
  21.0 10.3 %collective-permute-start.6 = (bf16[256,256]{1,0:T(8,128)(2,1)S(1)}, bf16[256,256]{1,0:T(8,128)(2,1)S(1)}, u32[]{:S(2)}, u32[]{:S(2)}) collective-permute-start(bf16[256,256]{1,0:T(8,128)(2,1)S(1)} %shard_map.74), channel_id=1, source_target_pairs={{0,2},{8,10},{16,24},{24,16},{2,0},{10,8},{18,26},{26,18},{4,6},{1... | collective-permute-start | bytes 393224 | tf_op jit(solution)/shard_map/ppermute | solution.py:448

commit v11 on v10

--- a/solution.py
+++ b/solution.py
@@ -236,8 +236,6 @@
             mixed[side, :, lo:hi] = jnp.dot(
                 weights, key_value[:rows, group + lo : group + hi], preferred_element_type=F32
             )
-    gate[0] = silu_dot(normed, w_near)
-    gate[1] = silu_dot(normed, w_far)
 
 
 def project_near_kernel(
@@ -330,6 +328,8 @@
     mixed_in, gate_in, mixed, gate,
 ):
     column = seg_column(seg[0:1, :])
+    gate[0] = silu_dot(normed, w_near)
+    gate[1] = silu_dot(normed, w_far)
 
     @pl.when(is_last())
     def _():

time: 33.1 us -> 32.9 us (level)
  no operation moved by 1% of the time
where the time goes in v11:
time: 32.9 us; the launch traced here: 32.4 us
  starting transfers between devices  14.5 us (44%)
  waiting for transfers between devices  6.82 us (21%)
  Pallas kernels  6.09 us (19%)
  local copies, waits for them, and re-layouts  4.75 us (14%)
    ppermute x2, starting transfers between devices, closed(): return lax.ppermute(block, ('batch', 'col'), perm)  5.83 us
    pallas_call x12, Pallas kernels, call(): pl.pallas_call(kernel, out_shape=[jax.ShapeDtypeStruct(shape, dtype) for...  4.75 us
    ppermute x2, waiting for transfers between devices, up_and_down(): return lax.ppermute(block, ('batch', 'col'), perm)  3.18 us
    dynamic_slice x1, local copies, waits for them, and re-layouts, weight_of(): lax.dynamic_slice_in_dim(joined_weight, block * width + index * group, gr...  2.63 us
    ppermute x3, starting transfers between devices, exchange(): return lax.ppermute(block, 'col', [(i, i ^ shift) for i in range(cols)])  2.28 us
    ppermute x1, starting transfers between devices, chain_plan(): got_f = lax.ppermute(send_f, 'batch', [(3, 1)])  2.25 us
    ppermute x2, starting transfers between devices, up_and_down(): return lax.ppermute(block, ('batch', 'col'), perm)  2.06 us
    squeeze x2, local copies, waits for them, and re-layouts, piece(): return lax.dynamic_index_in_dim(source, col_at ^ shift, 0, keepdims=False)  1.97 us
  transfers between devices with their start and end apart: 10, of which 5 were waited for; matrix products, arithmetic and copies ran while one was open for 11% of the time, Pallas kernels for 11%

profile of v11, /device:TPU:24, one launch (start us, length us, event | category | flops | bytes accessed | tf_op | source)
XLA Modules:
  0.0 32.4 jit_solution(5278725098264442794)
XLA Ops:
  0.0 0.9 %dynamic-slice_bitcast_fusion.3 = bf16[256,256]{1,0:T(8,128)(2,1)S(1)} fusion(bf16[4,256,256]{2,1,0:T(8,128)(2,1)} %bitcast.11, s32[]{:T(128)S(6)} %select_n.44), kind=kLoop, calls=%fused_computation.3 | loop fusion | bytes 262148 | tf_op jit(solution)/shard_map/jit(dynamic_index_in_dim)/squeeze | solution.py:402
  0.9 1.6 %collective-permute-start.1 = (bf16[256,256]{1,0:T(8,128)(2,1)S(1)}, bf16[256,256]{1,0:T(8,128)(2,1)S(1)}, u32[]{:S(2)}, u32[]{:S(2)}) collective-permute-start(bf16[256,256]{1,0:T(8,128)(2,1)S(1)} %dynamic-slice_bitcast_fusion.3), channel_id=1, source_target_pairs={{0,4},{2,6},{4,0},{6,2},{1,5},{3,7},{5,1},{7,3},{8,12},{10,14},{12... | collective-permute-start | bytes 393224 | tf_op jit(solution)/shard_map/ppermute | solution.py:405
  2.5 1.1 %dynamic-slice_bitcast_fusion = (bf16[256,256]{1,0:T(8,128)(2,1)S(1)}, bf16[256,256]{1,0:T(8,128)(2,1)S(1)}, bf16[256,256]{1,0:T(8,128)(2,1)S(1)}) fusion(bf16[4,256,256]{2,1,0:T(8,128)(2,1)} %bitcast.12, s32[]{:T(128)S(6)} %select_n.47, s32[]{:T(128)S(6)} %select_n.46, s32[]{:T(128)S(6)} %select_n.45), kind=kLoop, calls=%fused_computation | loop fusion | bytes 786444 | tf_op jit(solution)/shard_map/jit(dynamic_index_in_dim)/squeeze | solution.py:402
  3.5 0.1 collective-permute-start.2
  3.6 0.7 %collective-permute-start = (bf16[256,256]{1,0:T(8,128)(2,1)S(1)}, bf16[256,256]{1,0:T(8,128)(2,1)S(1)}, u32[]{:S(2)}, u32[]{:S(2)}) collective-permute-start(bf16[256,256]{1,0:T(8,128)(2,1)S(1)} %get-tuple-element.57), channel_id=1, source_target_pairs={{0,6},{2,4},{4,2},{6,0},{1,7},{3,5},{5,3},{7,1},{8,14},{10,12},{12... | collective-permute-start | bytes 393224 | tf_op jit(solution)/shard_map/ppermute | solution.py:405
  4.3 0.0 copy-start.2
  4.3 0.0 copy-start.3
  4.3 0.0 copy-start
  4.3 2.6 %constant_dynamic-slice_fusion = (bf16[1024,256]{1,0:T(8,128)(2,1)S(1)}, bf16[1024,256]{1,0:T(8,128)(2,1)S(1)}, bf16[1024,256]{1,0:T(8,128)(2,1)S(1)}, bf16[1024...) fusion(bf16[1024,2048]{1,0:T(8,128)(2,1)} %param.8, ...), kind=kLoop, calls=%fused_computation.4 | loop fusion | bytes 8388640 | tf_op jit(solution)/shard_map/dynamic_slice | solution.py:428
  6.9 0.0 copy-done.2
  6.9 0.0 copy-done.3
  6.9 0.1 shard_map.65.seg
  7.1 0.0 collective-permute-done.1.part2
  7.1 0.0 collective-permute-done.2.part1
  7.1 0.1 copy-done
  7.2 0.6 %shard_map.64.partial = f32[256,1024]{1,0:T(8,128)S(1)} custom-call(bf16[256,256]{1,0:T(8,128)(2,1)S(1)} %collective-permute-done.1.part2, bf16[256,256]{1,0:T(8,128)(2,1)S(1)} %collective-permute-done.2.part1, bf16[256,256]{1,0:T(8,128)(2,1)S(1)} %get-tuple-element.55.own, bf16[1024,1024]{1,0:T(8,128)(2,1)S(1)} %copy-done), custom_call_target="tpu_custom_call" | custom-call | flops 256 | tf_op jit(solution)/shard_map/pallas_call | solution.py:382
  7.8 1.1 %collective-permute-done.part3 = bf16[256,256]{1,0:T(8,128)(2,1)S(1)} collective-permute-done((bf16[256,256]{1,0:T(8,128)(2,1)S(1)}, bf16[256,256]{1,0:T(8,128)(2,1)S(1)}, u32[]{:S(2)}, u32[]{:S(2)}) %collective-permute-start) | collective-permute-done | bytes 131104 | tf_op jit(solution)/shard_map/ppermute | solution.py:405
  8.9 1.0 %shard_map.66 = (bf16[256,1024]{1,0:T(8,128)(2,1)S(1)}, bf16[256,1024]{1,0:T(8,128)(2,1)S(1)}, bf16[264,512]{1,0:T(8,128)(2,1)S(1)}) custom-call(bf16[256,256]{1,0:T(8,128)(2,1)S(1)} %collective-permute-done.part3, f32[256,1024]{1,0:T(8,128)S(1)} %shard_map.64.partial, bf16[1024,1024]{1,0:T(8,128)(2,1)S(1)} %copy-done, ...), custom_call_target="tpu_custom_call" | custom-call | flops 805306368 | tf_op jit(solution)/shard_map/pallas_call | solution.py:382
  9.9 0.3 collective-permute-start.5
  10.2 0.3 shard_map.67
  10.5 1.8 %collective-permute-start.4 = (bf16[264,512]{1,0:T(8,128)(2,1)S(1)}, bf16[264,512]{1,0:T(8,128)(2,1)S(1)}, u32[]{:S(2)}, u32[]{:S(2)}) collective-permute-start(bf16[264,512]{1,0:T(8,128)(2,1)S(1)} %get-tuple-element.30.send_2), channel_id=1, source_target_pairs={{0,2},{8,0},{16,8},{24,16},{2,10},{10,18},{18,26},{26,24},{4,6},{1... | collective-permute-start | bytes 811016 | tf_op jit(solution)/shard_map/ppermute | solution.py:440
  12.3 0.3 shard_map.68.send_f
  12.7 2.2 %collective-permute-start.7 = (bf16[264,256]{1,0:T(8,128)(2,1)S(1)}, bf16[264,256]{1,0:T(8,128)(2,1)S(1)}, u32[]{:S(2)}, u32[]{:S(2)}) collective-permute-start(bf16[264,256]{1,0:T(8,128)(2,1)S(1)} %shard_map.68.send_f), channel_id=1, source_target_pairs={{24,8},{25,9},{26,10},{27,11},{28,12},{29,13},{30,14},{31,15}} | collective-permute-start | bytes 405512 | tf_op jit(solution)/shard_map/ppermute | solution.py:481
  14.9 0.5 %shard_map.69 = (bf16[264,512]{1,0:T(8,128)(2,1)S(1)}, f32[2,256,256]{2,1,0:T(8,128)S(1)}, bf16[2,256,256]{2,1,0:T(8,128)(2,1)S(1)}) custom-call(bf16[264,256]{1,0:T(8,128)(2,1)S(1)} %shard_map.68.send_f, bf16[256,512]{1,0:T(8,128)(2,1)S(1)} %get-tuple-element.31.far_keys, bf16[256,256]{1,0:T(8,128)(2,1)S(1)} %get-tuple-element.32.far_query, ...), custom_call_target="tpu_custom_call" | custom-call | flops 268435456 | tf_op jit(solution)/shard_map/pallas_call | solution.py:382
  15.4 0.7 %collective-permute-start.3 = (bf16[264,512]{1,0:T(8,128)(2,1)S(1)}, bf16[264,512]{1,0:T(8,128)(2,1)S(1)}, u32[]{:S(2)}, u32[]{:S(2)}) collective-permute-start(bf16[264,512]{1,0:T(8,128)(2,1)S(1)} %get-tuple-element.33.send_a), channel_id=1, source_target_pairs={{0,16},{1,17},{2,18},{3,19},{4,20},{5,21},{6,22},{7,23}} | collective-permute-start | bytes 811016 | tf_op jit(solution)/shard_map/ppermute | solution.py:491
  16.1 3.2 %collective-permute-done.5.got_1 = bf16[264,512]{1,0:T(8,128)(2,1)S(1)} collective-permute-done((bf16[264,512]{1,0:T(8,128)(2,1)S(1)}, bf16[264,512]{1,0:T(8,128)(2,1)S(1)}, u32[]{:S(2)}, u32[]{:S(2)}) %collective-permute-start.5) | collective-permute-done | bytes 270368 | tf_op jit(solution)/shard_map/ppermute | solution.py:440
  19.3 0.0 collective-permute-done.4.got_2
  19.4 0.1 collective-permute-done.7.got_f
  19.5 0.0 copy-start.1
  19.5 1.4 %collective-permute-start.8 = (bf16[256,256]{1,0:T(8,128)(2,1)S(1)}, bf16[256,256]{1,0:T(8,128)(2,1)S(1)}, u32[]{:S(2)}, u32[]{:S(2)}) collective-permute-start(bf16[256,256]{1,0:T(8,128)(2,1)S(1)} %get-tuple-element.43), channel_id=1, source_target_pairs={{8,24},{0,8},{9,25},{1,9},{10,26},{2,10},{11,27},{3,11},{12,28},{4... | collective-permute-start | bytes 393224 | tf_op jit(solution)/shard_map/ppermute | solution.py:512
  20.9 0.1 collective-permute-start.9
  21.0 0.0 collective-permute-done.3.got_a
  21.0 5.8 %collective-permute-start.6 = (bf16[256,256]{1,0:T(8,128)(2,1)S(1)}, bf16[256,256]{1,0:T(8,128)(2,1)S(1)}, u32[]{:S(2)}, u32[]{:S(2)}) collective-permute-start(bf16[256,256]{1,0:T(8,128)(2,1)S(1)} %shard_map.74), channel_id=1, source_target_pairs={{0,2},{8,10},{16,24},{24,16},{2,0},{10,8},{18,26},{26,18},{4,6},{1... | collective-permute-start | bytes 393224 | tf_op jit(solution)/shard_map/ppermute | solution.py:448
  26.8 1.8 %shard_map.72 = (f32[2,256,256]{2,1,0:T(8,128)S(1)}, bf16[2,256,256]{2,1,0:T(8,128)(2,1)S(1)}) custom-call(bf16[264,512]{1,0:T(8,128)(2,1)S(1)} %collective-permute-done.3.got_a, bf16[264,512]{1,0:T(8,128)(2,1)S(1)} %get-tuple-element.36.got_b, bf16[264,512]{1,0:T(8,128)(2,1)S(1)} %get-tuple-element.33.send_a, ...), custom_call_target="tpu_custom_call", output_to_operand_aliasing={{0}: (10, {}), {1}: (11, {})} | custom-call | flops 256 | tf_op jit(solution)/shard_map/pallas_call | solution.py:382
  28.6 1.1 %collective-permute-done.8 = bf16[256,256]{1,0:T(8,128)(2,1)S(1)} collective-permute-done((bf16[256,256]{1,0:T(8,128)(2,1)S(1)}, bf16[256,256]{1,0:T(8,128)(2,1)S(1)}, u32[]{:S(2)}, u32[]{:S(2)}) %collective-permute-start.8) | collective-permute-done | bytes 131104 | tf_op jit(solution)/shard_map/ppermute | solution.py:512
  29.7 0.0 collective-permute-done.9
  29.7 1.3 %collective-permute-done.6.got_d = bf16[256,256]{1,0:T(8,128)(2,1)S(1)} collective-permute-done((bf16[256,256]{1,0:T(8,128)(2,1)S(1)}, bf16[256,256]{1,0:T(8,128)(2,1)S(1)}, u32[]{:S(2)}, u32[]{:S(2)}) %collective-permute-start.6) | collective-permute-done | bytes 131104 | tf_op jit(solution)/shard_map/ppermute | solution.py:448
  31.0 0.0 copy-done.1
  31.0 1.3 %shard_map.76 = bf16[256,1024]{1,0:T(8,128)(2,1)} custom-call(f32[2,256,256]{2,1,0:T(8,128)S(1)} %get-tuple-element.39.mixed, bf16[256,256]{1,0:T(8,128)(2,1)S(1)} %collective-permute-done.6.got_d, bf16[256,256]{1,0:T(8,128)(2,1)S(1)} %add.93.got_eg, bf16[2,256,256]{2,1,0:T(8,128)(2,1)S(1)} %get-tuple-element.45.gate, ...), custom_call_target="tpu_custom_call" | custom-call | flops 256 | tf_op jit(solution)/shard_map/pallas_call | solution.py:531
  (6 shorter events, 0.2 us)
Async XLA Ops:
  0.9 6.2 %collective-permute-start.1 = (bf16[256,256]{1,0:T(8,128)(2,1)S(1)}, bf16[256,256]{1,0:T(8,128)(2,1)S(1)}, u32[]{:S(2)}, u32[]{:S(2)}) collective-permute-start(bf16[256,256]{1,0:T(8,128)(2,1)S(1)} %dynamic-slice_bitcast_fusion.3), channel_id=1, source_target_pairs={{0,4},{2,6},{4,0},{6,2},{1,5},{3,7},{5,1},{7,3},{8,12},{10,14},{12... | collective-permute-start | bytes 393224 | tf_op jit(solution)/shard_map/ppermute | solution.py:405
  3.5 3.5 %collective-permute-start.2 = (bf16[256,256]{1,0:T(8,128)(2,1)S(1)}, bf16[256,256]{1,0:T(8,128)(2,1)S(1)}, u32[]{:S(2)}, u32[]{:S(2)}) collective-permute-start(bf16[256,256]{1,0:T(8,128)(2,1)S(1)} %get-tuple-element.56), channel_id=1, source_target_pairs={{0,2},{2,0},{4,6},{6,4},{1,3},{3,1},{5,7},{7,5},{8,10},{10,8},{12,... | collective-permute-start | bytes 393224 | tf_op jit(solution)/shard_map/ppermute | solution.py:405
  3.6 5.3 %collective-permute-start = (bf16[256,256]{1,0:T(8,128)(2,1)S(1)}, bf16[256,256]{1,0:T(8,128)(2,1)S(1)}, u32[]{:S(2)}, u32[]{:S(2)}) collective-permute-start(bf16[256,256]{1,0:T(8,128)(2,1)S(1)} %get-tuple-element.57), channel_id=1, source_target_pairs={{0,6},{2,4},{4,2},{6,0},{1,7},{3,5},{5,3},{7,1},{8,14},{10,12},{12... | collective-permute-start | bytes 393224 | tf_op jit(solution)/shard_map/ppermute | solution.py:405
  4.3 2.6 %copy-start.2 = (s32[256]{0:T(256)S(1)}, s32[256]{0:T(256)}, u32[]{:S(2)}) copy-start(s32[256]{0:T(256)} %param.11) | copy-start | bytes 3076
  4.3 2.6 %copy-start.3 = (s32[1,4]{1,0:T(1,128)S(1)}, s32[1,4]{1,0:T(1,128)}, u32[]{:S(2)}) copy-start(s32[1,4]{1,0:T(1,128)} %counts.1) | copy-start | bytes 52
  4.3 2.9 %copy-start = (bf16[1024,1024]{1,0:T(8,128)(2,1)S(1)}, bf16[1024,1024]{1,0:T(8,128)(2,1)}, u32[]{:S(2)}) copy-start(bf16[1024,1024]{1,0:T(8,128)(2,1)} %w_in.3) | copy-start | bytes 6291460
  9.9 9.3 %collective-permute-start.5 = (bf16[264,512]{1,0:T(8,128)(2,1)S(1)}, bf16[264,512]{1,0:T(8,128)(2,1)S(1)}, u32[]{:S(2)}, u32[]{:S(2)}) collective-permute-start(bf16[264,512]{1,0:T(8,128)(2,1)S(1)} %get-tuple-element.29.send_1), channel_id=1, source_target_pairs={{0,8},{8,16},{16,24},{24,26},{2,0},{10,2},{18,10},{26,18},{4,12},{... | collective-permute-start | bytes 811016 | tf_op jit(solution)/shard_map/ppermute | solution.py:440
  10.5 8.7 %collective-permute-start.4 = (bf16[264,512]{1,0:T(8,128)(2,1)S(1)}, bf16[264,512]{1,0:T(8,128)(2,1)S(1)}, u32[]{:S(2)}, u32[]{:S(2)}) collective-permute-start(bf16[264,512]{1,0:T(8,128)(2,1)S(1)} %get-tuple-element.30.send_2), channel_id=1, source_target_pairs={{0,2},{8,0},{16,8},{24,16},{2,10},{10,18},{18,26},{26,24},{4,6},{1... | collective-permute-start | bytes 811016 | tf_op jit(solution)/shard_map/ppermute | solution.py:440
  12.7 6.8 %collective-permute-start.7 = (bf16[264,256]{1,0:T(8,128)(2,1)S(1)}, bf16[264,256]{1,0:T(8,128)(2,1)S(1)}, u32[]{:S(2)}, u32[]{:S(2)}) collective-permute-start(bf16[264,256]{1,0:T(8,128)(2,1)S(1)} %shard_map.68.send_f), channel_id=1, source_target_pairs={{24,8},{25,9},{26,10},{27,11},{28,12},{29,13},{30,14},{31,15}} | collective-permute-start | bytes 405512 | tf_op jit(solution)/shard_map/ppermute | solution.py:481
  15.4 5.6 %collective-permute-start.3 = (bf16[264,512]{1,0:T(8,128)(2,1)S(1)}, bf16[264,512]{1,0:T(8,128)(2,1)S(1)}, u32[]{:S(2)}, u32[]{:S(2)}) collective-permute-start(bf16[264,512]{1,0:T(8,128)(2,1)S(1)} %get-tuple-element.33.send_a), channel_id=1, source_target_pairs={{0,16},{1,17},{2,18},{3,19},{4,20},{5,21},{6,22},{7,23}} | collective-permute-start | bytes 811016 | tf_op jit(solution)/shard_map/ppermute | solution.py:491
  19.5 11.6 %copy-start.1 = (bf16[512,1024]{1,0:T(8,128)(2,1)S(1)}, bf16[512,1024]{1,0:T(8,128)(2,1)}, u32[]{:S(2)}) copy-start(bf16[512,1024]{1,0:T(8,128)(2,1)} %w_out.1) | copy-start | bytes 3145732
  19.5 10.2 %collective-permute-start.8 = (bf16[256,256]{1,0:T(8,128)(2,1)S(1)}, bf16[256,256]{1,0:T(8,128)(2,1)S(1)}, u32[]{:S(2)}, u32[]{:S(2)}) collective-permute-start(bf16[256,256]{1,0:T(8,128)(2,1)S(1)} %get-tuple-element.43), channel_id=1, source_target_pairs={{8,24},{0,8},{9,25},{1,9},{10,26},{2,10},{11,27},{3,11},{12,28},{4... | collective-permute-start | bytes 393224 | tf_op jit(solution)/shard_map/ppermute | solution.py:512
  20.9 8.7 %collective-permute-start.9 = (bf16[256,256]{1,0:T(8,128)(2,1)S(1)}, bf16[256,256]{1,0:T(8,128)(2,1)S(1)}, u32[]{:S(2)}, u32[]{:S(2)}) collective-permute-start(bf16[256,256]{1,0:T(8,128)(2,1)S(1)} %get-tuple-element.44), channel_id=1, source_target_pairs={{0,2},{8,16},{16,8},{24,26},{2,0},{10,18},{18,10},{26,24},{4,6},{1... | collective-permute-start | bytes 393224 | tf_op jit(solution)/shard_map/ppermute | solution.py:448
  21.0 10.0 %collective-permute-start.6 = (bf16[256,256]{1,0:T(8,128)(2,1)S(1)}, bf16[256,256]{1,0:T(8,128)(2,1)S(1)}, u32[]{:S(2)}, u32[]{:S(2)}) collective-permute-start(bf16[256,256]{1,0:T(8,128)(2,1)S(1)} %shard_map.74), channel_id=1, source_target_pairs={{0,2},{8,10},{16,24},{24,16},{2,0},{10,8},{18,26},{26,18},{4,6},{1... | collective-permute-start | bytes 393224 | tf_op jit(solution)/shard_map/ppermute | solution.py:448

commit v12 on v11

--- a/solution.py
+++ b/solution.py
@@ -282,6 +282,10 @@
 
 
 def early_kernel(got_b, got_c, send_a, early_1, early_2):
+    @pl.when(batch_index() == 0)
+    def _():
+        add_blocks(got_c, [send_a], early_1)
+
     @pl.when(batch_index() == 1)
     def _():
         add_blocks(got_c, [send_a, got_b], early_1)
@@ -292,25 +296,22 @@
 
 
 def far_kernel(got_b, got_c, got_f, send_a, early_1, send_e, send_g):
-    @pl.when(batch_index() == 0)
-    def _():
-        add_blocks(got_c, [send_a], send_e)
-
     @pl.when(batch_index() == 1)
     def _():
         add_blocks(got_f, [send_a, got_b], send_e)
         send_g[...] = early_1[...]
 
-    @pl.when(batch_index() > 1)
+    @pl.when(batch_index() != 1)
     def _():
         send_e[...] = jnp.zeros_like(send_e)
-
-    @pl.when(batch_index() != 1)
-    def _():
         send_g[...] = jnp.zeros_like(send_g)
 
 
-def far_d_kernel(early_2, got_c, got_a, send_d, total):
+def far_d_kernel(early_1, early_2, got_c, got_a, send_d, total):
+    @pl.when(batch_index() == 0)
+    def _():
+        send_d[...] = early_1[...]
+
     @pl.when(batch_index() == 2)
     def _():
         rows = total.shape[0]
@@ -318,7 +319,7 @@
         add_near(got_c, seg_column(seg_row_of(got_c, rows)), got_a, total)
         send_d[...] = total[...].astype(BF16)
 
-    @pl.when(batch_index() != 2)
+    @pl.when((batch_index() != 0) & (batch_index() != 2))
     def _():
         send_d[...] = jnp.zeros_like(send_d)
 
@@ -509,17 +510,17 @@
         (got_b, got_c, got_f, send_a, early_1),
         1 << 30,
     )
-    got_e = lax.ppermute(send_e, "batch", [(1, 3), (0, 1)])
+    got_e = lax.ppermute(send_e, "batch", [(1, 3)])
     got_g = closed(send_g, {1: 2, 2: 1})
     (send_d,) = call(
         far_d_kernel,
-        [VMEM] * 3,
+        [VMEM] * 4,
         [((rows, group), BF16)],
-        (early_2, got_c, got_a),
+        (early_1, early_2, got_c, got_a),
         rows,
         [pltpu.VMEM((rows, group), F32)],
     )
-    got_d = closed(send_d, {2: 3, 3: 2})
+    got_d = closed(send_d, {0: 1, 1: 0, 2: 3, 3: 2})
     mixed, gate = call(
         near_kernel,
         [VMEM] * 12,

time: 32.9 us -> 32.8 us (level)
    ppermute x2, waiting for transfers between devices: 1.34 us -> 1.74 us  [closed(): return lax.ppermute(block, ('batch', 'col'), perm)]
where the time goes in v12:
time: 32.8 us; the launch traced here: 32.4 us
  starting transfers between devices  14.4 us (44%)
  waiting for transfers between devices  6.91 us (21%)
  Pallas kernels  6.1 us (19%)
  local copies, waits for them, and re-layouts  4.75 us (14%)
    ppermute x2, starting transfers between devices, closed(): return lax.ppermute(block, ('batch', 'col'), perm)  5.72 us
    pallas_call x12, Pallas kernels, call(): pl.pallas_call(kernel, out_shape=[jax.ShapeDtypeStruct(shape, dtype) for...  4.76 us
    ppermute x2, waiting for transfers between devices, up_and_down(): return lax.ppermute(block, ('batch', 'col'), perm)  3.18 us
    dynamic_slice x1, local copies, waits for them, and re-layouts, weight_of(): lax.dynamic_slice_in_dim(joined_weight, block * width + index * group, gr...  2.63 us
    ppermute x3, starting transfers between devices, exchange(): return lax.ppermute(block, 'col', [(i, i ^ shift) for i in range(cols)])  2.28 us
    ppermute x1, starting transfers between devices, chain_plan(): got_f = lax.ppermute(send_f, 'batch', [(3, 1)])  2.25 us
    ppermute x2, starting transfers between devices, up_and_down(): return lax.ppermute(block, ('batch', 'col'), perm)  2.06 us
    squeeze x2, local copies, waits for them, and re-layouts, piece(): return lax.dynamic_index_in_dim(source, col_at ^ shift, 0, keepdims=False)  1.97 us
  transfers between devices with their start and end apart: 10, of which 5 were waited for; matrix products, arithmetic and copies ran while one was open for 11% of the time, Pallas kernels for 11%

profile of v12, /device:TPU:24, one launch (start us, length us, event | category | flops | bytes accessed | tf_op | source)
XLA Modules:
  0.0 32.4 jit_solution(4133340604029567168)
XLA Ops:
  0.0 0.9 %dynamic-slice_bitcast_fusion.3 = bf16[256,256]{1,0:T(8,128)(2,1)S(1)} fusion(bf16[4,256,256]{2,1,0:T(8,128)(2,1)} %bitcast.11, s32[]{:T(128)S(6)} %select_n.44), kind=kLoop, calls=%fused_computation.3 | loop fusion | bytes 262148 | tf_op jit(solution)/shard_map/jit(dynamic_index_in_dim)/squeeze | solution.py:403
  0.9 1.6 %collective-permute-start.1 = (bf16[256,256]{1,0:T(8,128)(2,1)S(1)}, bf16[256,256]{1,0:T(8,128)(2,1)S(1)}, u32[]{:S(2)}, u32[]{:S(2)}) collective-permute-start(bf16[256,256]{1,0:T(8,128)(2,1)S(1)} %dynamic-slice_bitcast_fusion.3), channel_id=1, source_target_pairs={{0,4},{2,6},{4,0},{6,2},{1,5},{3,7},{5,1},{7,3},{8,12},{10,14},{12... | collective-permute-start | bytes 393224 | tf_op jit(solution)/shard_map/ppermute | solution.py:406
  2.5 1.1 %dynamic-slice_bitcast_fusion = (bf16[256,256]{1,0:T(8,128)(2,1)S(1)}, bf16[256,256]{1,0:T(8,128)(2,1)S(1)}, bf16[256,256]{1,0:T(8,128)(2,1)S(1)}) fusion(bf16[4,256,256]{2,1,0:T(8,128)(2,1)} %bitcast.12, s32[]{:T(128)S(6)} %select_n.47, s32[]{:T(128)S(6)} %select_n.46, s32[]{:T(128)S(6)} %select_n.45), kind=kLoop, calls=%fused_computation | loop fusion | bytes 786444 | tf_op jit(solution)/shard_map/jit(dynamic_index_in_dim)/squeeze | solution.py:403
  3.5 0.1 collective-permute-start.2
  3.6 0.7 %collective-permute-start = (bf16[256,256]{1,0:T(8,128)(2,1)S(1)}, bf16[256,256]{1,0:T(8,128)(2,1)S(1)}, u32[]{:S(2)}, u32[]{:S(2)}) collective-permute-start(bf16[256,256]{1,0:T(8,128)(2,1)S(1)} %get-tuple-element.57), channel_id=1, source_target_pairs={{0,6},{2,4},{4,2},{6,0},{1,7},{3,5},{5,3},{7,1},{8,14},{10,12},{12... | collective-permute-start | bytes 393224 | tf_op jit(solution)/shard_map/ppermute | solution.py:406
  4.3 0.0 copy-start.2
  4.3 0.0 copy-start.3
  4.3 0.0 copy-start
  4.3 2.6 %constant_dynamic-slice_fusion = (bf16[1024,256]{1,0:T(8,128)(2,1)S(1)}, bf16[1024,256]{1,0:T(8,128)(2,1)S(1)}, bf16[1024,256]{1,0:T(8,128)(2,1)S(1)}, bf16[1024...) fusion(bf16[1024,2048]{1,0:T(8,128)(2,1)} %param.8, ...), kind=kLoop, calls=%fused_computation.4 | loop fusion | bytes 8388640 | tf_op jit(solution)/shard_map/dynamic_slice | solution.py:429
  6.9 0.0 copy-done.2
  6.9 0.0 copy-done.3
  6.9 0.1 shard_map.65.seg
  7.1 0.0 collective-permute-done.1.part2
  7.1 0.0 collective-permute-done.2.part1
  7.1 0.1 copy-done
  7.2 0.6 %shard_map.64.partial = f32[256,1024]{1,0:T(8,128)S(1)} custom-call(bf16[256,256]{1,0:T(8,128)(2,1)S(1)} %collective-permute-done.1.part2, bf16[256,256]{1,0:T(8,128)(2,1)S(1)} %collective-permute-done.2.part1, bf16[256,256]{1,0:T(8,128)(2,1)S(1)} %get-tuple-element.55.own, bf16[1024,1024]{1,0:T(8,128)(2,1)S(1)} %copy-done), custom_call_target="tpu_custom_call" | custom-call | flops 256 | tf_op jit(solution)/shard_map/pallas_call | solution.py:383
  7.8 1.1 %collective-permute-done.part3 = bf16[256,256]{1,0:T(8,128)(2,1)S(1)} collective-permute-done((bf16[256,256]{1,0:T(8,128)(2,1)S(1)}, bf16[256,256]{1,0:T(8,128)(2,1)S(1)}, u32[]{:S(2)}, u32[]{:S(2)}) %collective-permute-start) | collective-permute-done | bytes 131104 | tf_op jit(solution)/shard_map/ppermute | solution.py:406
  8.9 1.0 %shard_map.66 = (bf16[256,1024]{1,0:T(8,128)(2,1)S(1)}, bf16[256,1024]{1,0:T(8,128)(2,1)S(1)}, bf16[264,512]{1,0:T(8,128)(2,1)S(1)}) custom-call(bf16[256,256]{1,0:T(8,128)(2,1)S(1)} %collective-permute-done.part3, f32[256,1024]{1,0:T(8,128)S(1)} %shard_map.64.partial, bf16[1024,1024]{1,0:T(8,128)(2,1)S(1)} %copy-done, ...), custom_call_target="tpu_custom_call" | custom-call | flops 805306368 | tf_op jit(solution)/shard_map/pallas_call | solution.py:383
  9.9 0.3 collective-permute-start.5
  10.2 0.3 shard_map.67
  10.5 1.8 %collective-permute-start.4 = (bf16[264,512]{1,0:T(8,128)(2,1)S(1)}, bf16[264,512]{1,0:T(8,128)(2,1)S(1)}, u32[]{:S(2)}, u32[]{:S(2)}) collective-permute-start(bf16[264,512]{1,0:T(8,128)(2,1)S(1)} %get-tuple-element.30.send_2), channel_id=1, source_target_pairs={{0,2},{8,0},{16,8},{24,16},{2,10},{10,18},{18,26},{26,24},{4,6},{1... | collective-permute-start | bytes 811016 | tf_op jit(solution)/shard_map/ppermute | solution.py:441
  12.3 0.3 shard_map.68.send_f
  12.7 2.2 %collective-permute-start.7 = (bf16[264,256]{1,0:T(8,128)(2,1)S(1)}, bf16[264,256]{1,0:T(8,128)(2,1)S(1)}, u32[]{:S(2)}, u32[]{:S(2)}) collective-permute-start(bf16[264,256]{1,0:T(8,128)(2,1)S(1)} %shard_map.68.send_f), channel_id=1, source_target_pairs={{24,8},{25,9},{26,10},{27,11},{28,12},{29,13},{30,14},{31,15}} | collective-permute-start | bytes 405512 | tf_op jit(solution)/shard_map/ppermute | solution.py:482
  14.9 0.5 %shard_map.69 = (bf16[264,512]{1,0:T(8,128)(2,1)S(1)}, f32[2,256,256]{2,1,0:T(8,128)S(1)}, bf16[2,256,256]{2,1,0:T(8,128)(2,1)S(1)}) custom-call(bf16[264,256]{1,0:T(8,128)(2,1)S(1)} %shard_map.68.send_f, bf16[256,512]{1,0:T(8,128)(2,1)S(1)} %get-tuple-element.31.far_keys, bf16[256,256]{1,0:T(8,128)(2,1)S(1)} %get-tuple-element.32.far_query, ...), custom_call_target="tpu_custom_call" | custom-call | flops 268435456 | tf_op jit(solution)/shard_map/pallas_call | solution.py:383
  15.4 0.7 %collective-permute-start.3 = (bf16[264,512]{1,0:T(8,128)(2,1)S(1)}, bf16[264,512]{1,0:T(8,128)(2,1)S(1)}, u32[]{:S(2)}, u32[]{:S(2)}) collective-permute-start(bf16[264,512]{1,0:T(8,128)(2,1)S(1)} %get-tuple-element.33.send_a), channel_id=1, source_target_pairs={{0,16},{1,17},{2,18},{3,19},{4,20},{5,21},{6,22},{7,23}} | collective-permute-start | bytes 811016 | tf_op jit(solution)/shard_map/ppermute | solution.py:492
  16.1 3.2 %collective-permute-done.5.got_1 = bf16[264,512]{1,0:T(8,128)(2,1)S(1)} collective-permute-done((bf16[264,512]{1,0:T(8,128)(2,1)S(1)}, bf16[264,512]{1,0:T(8,128)(2,1)S(1)}, u32[]{:S(2)}, u32[]{:S(2)}) %collective-permute-start.5) | collective-permute-done | bytes 270368 | tf_op jit(solution)/shard_map/ppermute | solution.py:441
  19.3 0.0 collective-permute-done.4.got_2
  19.4 0.1 collective-permute-done.7.got_f
  19.5 0.0 copy-start.1
  19.5 1.4 %collective-permute-start.8 = (bf16[256,256]{1,0:T(8,128)(2,1)S(1)}, bf16[256,256]{1,0:T(8,128)(2,1)S(1)}, u32[]{:S(2)}, u32[]{:S(2)}) collective-permute-start(bf16[256,256]{1,0:T(8,128)(2,1)S(1)} %get-tuple-element.43), channel_id=1, source_target_pairs={{8,24},{9,25},{10,26},{11,27},{12,28},{13,29},{14,30},{15,31}} | collective-permute-start | bytes 393224 | tf_op jit(solution)/shard_map/ppermute | solution.py:513
  20.9 0.1 collective-permute-start.9
  21.0 0.0 collective-permute-done.3.got_a
  21.0 5.7 %collective-permute-start.6 = (bf16[256,256]{1,0:T(8,128)(2,1)S(1)}, bf16[256,256]{1,0:T(8,128)(2,1)S(1)}, u32[]{:S(2)}, u32[]{:S(2)}) collective-permute-start(bf16[256,256]{1,0:T(8,128)(2,1)S(1)} %shard_map.74), channel_id=1, source_target_pairs={{0,8},{8,0},{16,24},{24,16},{2,10},{10,2},{18,26},{26,18},{4,12},{... | collective-permute-start | bytes 393224 | tf_op jit(solution)/shard_map/ppermute | solution.py:449
  26.7 1.8 %shard_map.72 = (f32[2,256,256]{2,1,0:T(8,128)S(1)}, bf16[2,256,256]{2,1,0:T(8,128)(2,1)S(1)}) custom-call(bf16[264,512]{1,0:T(8,128)(2,1)S(1)} %collective-permute-done.3.got_a, bf16[264,512]{1,0:T(8,128)(2,1)S(1)} %get-tuple-element.36.got_b, bf16[264,512]{1,0:T(8,128)(2,1)S(1)} %get-tuple-element.33.send_a, ...), custom_call_target="tpu_custom_call", output_to_operand_aliasing={{0}: (10, {}), {1}: (11, {})} | custom-call | flops 256 | tf_op jit(solution)/shard_map/pallas_call | solution.py:383
  28.5 0.8 %collective-permute-done.8 = bf16[256,256]{1,0:T(8,128)(2,1)S(1)} collective-permute-done((bf16[256,256]{1,0:T(8,128)(2,1)S(1)}, bf16[256,256]{1,0:T(8,128)(2,1)S(1)}, u32[]{:S(2)}, u32[]{:S(2)}) %collective-permute-start.8) | collective-permute-done | bytes 131104 | tf_op jit(solution)/shard_map/ppermute | solution.py:513
  29.2 0.0 collective-permute-done.9
  29.3 1.7 %collective-permute-done.6.got_d = bf16[256,256]{1,0:T(8,128)(2,1)S(1)} collective-permute-done((bf16[256,256]{1,0:T(8,128)(2,1)S(1)}, bf16[256,256]{1,0:T(8,128)(2,1)S(1)}, u32[]{:S(2)}, u32[]{:S(2)}) %collective-permute-start.6) | collective-permute-done | bytes 131104 | tf_op jit(solution)/shard_map/ppermute | solution.py:449
  31.0 0.0 copy-done.1
  31.0 1.3 %shard_map.76 = bf16[256,1024]{1,0:T(8,128)(2,1)} custom-call(f32[2,256,256]{2,1,0:T(8,128)S(1)} %get-tuple-element.39.mixed, bf16[256,256]{1,0:T(8,128)(2,1)S(1)} %collective-permute-done.6.got_d, bf16[256,256]{1,0:T(8,128)(2,1)S(1)} %add.93.got_eg, bf16[2,256,256]{2,1,0:T(8,128)(2,1)S(1)} %get-tuple-element.45.gate, ...), custom_call_target="tpu_custom_call" | custom-call | flops 256 | tf_op jit(solution)/shard_map/pallas_call | solution.py:532
  (6 shorter events, 0.2 us)
Async XLA Ops:
  0.9 6.2 %collective-permute-start.1 = (bf16[256,256]{1,0:T(8,128)(2,1)S(1)}, bf16[256,256]{1,0:T(8,128)(2,1)S(1)}, u32[]{:S(2)}, u32[]{:S(2)}) collective-permute-start(bf16[256,256]{1,0:T(8,128)(2,1)S(1)} %dynamic-slice_bitcast_fusion.3), channel_id=1, source_target_pairs={{0,4},{2,6},{4,0},{6,2},{1,5},{3,7},{5,1},{7,3},{8,12},{10,14},{12... | collective-permute-start | bytes 393224 | tf_op jit(solution)/shard_map/ppermute | solution.py:406
  3.5 3.5 %collective-permute-start.2 = (bf16[256,256]{1,0:T(8,128)(2,1)S(1)}, bf16[256,256]{1,0:T(8,128)(2,1)S(1)}, u32[]{:S(2)}, u32[]{:S(2)}) collective-permute-start(bf16[256,256]{1,0:T(8,128)(2,1)S(1)} %get-tuple-element.56), channel_id=1, source_target_pairs={{0,2},{2,0},{4,6},{6,4},{1,3},{3,1},{5,7},{7,5},{8,10},{10,8},{12,... | collective-permute-start | bytes 393224 | tf_op jit(solution)/shard_map/ppermute | solution.py:406
  3.6 5.3 %collective-permute-start = (bf16[256,256]{1,0:T(8,128)(2,1)S(1)}, bf16[256,256]{1,0:T(8,128)(2,1)S(1)}, u32[]{:S(2)}, u32[]{:S(2)}) collective-permute-start(bf16[256,256]{1,0:T(8,128)(2,1)S(1)} %get-tuple-element.57), channel_id=1, source_target_pairs={{0,6},{2,4},{4,2},{6,0},{1,7},{3,5},{5,3},{7,1},{8,14},{10,12},{12... | collective-permute-start | bytes 393224 | tf_op jit(solution)/shard_map/ppermute | solution.py:406
  4.3 2.6 %copy-start.2 = (s32[256]{0:T(256)S(1)}, s32[256]{0:T(256)}, u32[]{:S(2)}) copy-start(s32[256]{0:T(256)} %param.11) | copy-start | bytes 3076
  4.3 2.6 %copy-start.3 = (s32[1,4]{1,0:T(1,128)S(1)}, s32[1,4]{1,0:T(1,128)}, u32[]{:S(2)}) copy-start(s32[1,4]{1,0:T(1,128)} %counts.1) | copy-start | bytes 52
  4.3 2.9 %copy-start = (bf16[1024,1024]{1,0:T(8,128)(2,1)S(1)}, bf16[1024,1024]{1,0:T(8,128)(2,1)}, u32[]{:S(2)}) copy-start(bf16[1024,1024]{1,0:T(8,128)(2,1)} %w_in.3) | copy-start | bytes 6291460
  9.9 9.3 %collective-permute-start.5 = (bf16[264,512]{1,0:T(8,128)(2,1)S(1)}, bf16[264,512]{1,0:T(8,128)(2,1)S(1)}, u32[]{:S(2)}, u32[]{:S(2)}) collective-permute-start(bf16[264,512]{1,0:T(8,128)(2,1)S(1)} %get-tuple-element.29.send_1), channel_id=1, source_target_pairs={{0,8},{8,16},{16,24},{24,26},{2,0},{10,2},{18,10},{26,18},{4,12},{... | collective-permute-start | bytes 811016 | tf_op jit(solution)/shard_map/ppermute | solution.py:441
  10.5 8.7 %collective-permute-start.4 = (bf16[264,512]{1,0:T(8,128)(2,1)S(1)}, bf16[264,512]{1,0:T(8,128)(2,1)S(1)}, u32[]{:S(2)}, u32[]{:S(2)}) collective-permute-start(bf16[264,512]{1,0:T(8,128)(2,1)S(1)} %get-tuple-element.30.send_2), channel_id=1, source_target_pairs={{0,2},{8,0},{16,8},{24,16},{2,10},{10,18},{18,26},{26,24},{4,6},{1... | collective-permute-start | bytes 811016 | tf_op jit(solution)/shard_map/ppermute | solution.py:441
  12.7 6.8 %collective-permute-start.7 = (bf16[264,256]{1,0:T(8,128)(2,1)S(1)}, bf16[264,256]{1,0:T(8,128)(2,1)S(1)}, u32[]{:S(2)}, u32[]{:S(2)}) collective-permute-start(bf16[264,256]{1,0:T(8,128)(2,1)S(1)} %shard_map.68.send_f), channel_id=1, source_target_pairs={{24,8},{25,9},{26,10},{27,11},{28,12},{29,13},{30,14},{31,15}} | collective-permute-start | bytes 405512 | tf_op jit(solution)/shard_map/ppermute | solution.py:482
  15.4 5.6 %collective-permute-start.3 = (bf16[264,512]{1,0:T(8,128)(2,1)S(1)}, bf16[264,512]{1,0:T(8,128)(2,1)S(1)}, u32[]{:S(2)}, u32[]{:S(2)}) collective-permute-start(bf16[264,512]{1,0:T(8,128)(2,1)S(1)} %get-tuple-element.33.send_a), channel_id=1, source_target_pairs={{0,16},{1,17},{2,18},{3,19},{4,20},{5,21},{6,22},{7,23}} | collective-permute-start | bytes 811016 | tf_op jit(solution)/shard_map/ppermute | solution.py:492
  19.5 11.6 %copy-start.1 = (bf16[512,1024]{1,0:T(8,128)(2,1)S(1)}, bf16[512,1024]{1,0:T(8,128)(2,1)}, u32[]{:S(2)}) copy-start(bf16[512,1024]{1,0:T(8,128)(2,1)} %w_out.1) | copy-start | bytes 3145732
  19.5 9.8 %collective-permute-start.8 = (bf16[256,256]{1,0:T(8,128)(2,1)S(1)}, bf16[256,256]{1,0:T(8,128)(2,1)S(1)}, u32[]{:S(2)}, u32[]{:S(2)}) collective-permute-start(bf16[256,256]{1,0:T(8,128)(2,1)S(1)} %get-tuple-element.43), channel_id=1, source_target_pairs={{8,24},{9,25},{10,26},{11,27},{12,28},{13,29},{14,30},{15,31}} | collective-permute-start | bytes 393224 | tf_op jit(solution)/shard_map/ppermute | solution.py:513
  20.9 8.3 %collective-permute-start.9 = (bf16[256,256]{1,0:T(8,128)(2,1)S(1)}, bf16[256,256]{1,0:T(8,128)(2,1)S(1)}, u32[]{:S(2)}, u32[]{:S(2)}) collective-permute-start(bf16[256,256]{1,0:T(8,128)(2,1)S(1)} %get-tuple-element.44), channel_id=1, source_target_pairs={{0,2},{8,16},{16,8},{24,26},{2,0},{10,18},{18,10},{26,24},{4,6},{1... | collective-permute-start | bytes 393224 | tf_op jit(solution)/shard_map/ppermute | solution.py:449
  21.0 10.0 %collective-permute-start.6 = (bf16[256,256]{1,0:T(8,128)(2,1)S(1)}, bf16[256,256]{1,0:T(8,128)(2,1)S(1)}, u32[]{:S(2)}, u32[]{:S(2)}) collective-permute-start(bf16[256,256]{1,0:T(8,128)(2,1)S(1)} %shard_map.74), channel_id=1, source_target_pairs={{0,8},{8,0},{16,24},{24,16},{2,10},{10,2},{18,26},{26,18},{4,12},{... | collective-permute-start | bytes 393224 | tf_op jit(solution)/shard_map/ppermute | solution.py:449
